TPU v7x, 32 devices: a whole 2x2x4 slice. The times are simulated.
32 devices in a mesh: lon: 2 (over x), lat: 4 (over z), head: 4 (over y, core).
Axes of the slice: x: 2, y: 2, z: 4, core: 2. Of those that a mesh axis runs over, the one named last changes fastest.
Arguments:
- tokens: bfloat16 [2, 24, 48, 1024], P(None, 'lat', 'lon'), may hold values from -6 to 6
- norm_gain: float32 [1024], replicated, may hold values from 0.5 to 1.5
- w_qkv: bfloat16 [1024, 3072], P(None, 'head'), may hold values from -0.1875 to 0.1875
- w_out: bfloat16 [1024, 1024], P('head'), may hold values from -0.1875 to 0.1875
- bias_table: float32 [759, 16], P(None, 'head'), may hold values from -3 to 300
- cotangent: bfloat16 [2, 24, 48, 1024], P(None, 'lat', 'lon'), may hold values from -6 to 6
Outputs:
- layer_out: bfloat16 [2, 24, 48, 1024], P(None, 'lat', 'lon')
- grad_tokens: bfloat16 [2, 24, 48, 1024], P(None, 'lat', 'lon')
- grad_qkv: float32 [1024, 3072], P(('lon', 'lat'), 'head')
- grad_out: float32 [1024, 1024], P('head', ('lon', 'lat'))
All inputs are finite; a program needn't handle non-finite values.
Results may differ from a plain program's by a relative error of at most 0.013.
Values may be sent and summed in bfloat16 or wider, within the bound.
No kernel may reach another device: no remote copies, remote signals or barrier semaphores. Data moves between devices by JAX's collectives and lax.ppermute only.
A program may use at most 64 MiB of HBM per device.

v0:
```python
import functools

import jax
import jax.numpy as jnp
import numpy as np
from jax import lax
from jax.experimental import pallas as pl
from jax.experimental.pallas import tpu as pltpu
from jax.sharding import PartitionSpec as P

HEAD_DIM = 64
LEV = 2
WLAT = 6
WLON = 12
TILE_LON = 24
WINDOW = LEV * WLAT * WLON
WINDOWS = TILE_LON // WLON
CELLS = WINDOWS * WINDOW
QUARTERS = 4
PART = 80
MID_LAT = WLAT // 2
MID_LON = WLON // 2
SPAN_LAT = 2 * WLAT - 1
SPAN_LON = 2 * WLON - 1
EPSILON = 1e-05
NEG_FILL = -1e30
F32 = jnp.float32
BF16 = jnp.bfloat16

RIM_Z, RIM_X, RIM_D = 112, 48, 48
RIM = RIM_Z + RIM_X + RIM_D
OUT_OWN, OUT_Z, OUT_X, OUT_D = 32, 32, 16, 16
OUT_STARTS = (0, 32, 64, 80)
OUT_ROWS = 96


def own_row(level, lat, lon):
    return (level * WLAT + lat) * TILE_LON + lon


def rim_source():
    rows = np.full(RIM, -1)
    z_width = TILE_LON - MID_LON
    for level in range(LEV):
        for lat in range(MID_LAT):
            for lon in range(z_width):
                rows[(level * MID_LAT + lat) * z_width + lon] = own_row(level, lat, lon + MID_LON)
            for lon in range(MID_LON):
                at = (level * MID_LAT + lat) * MID_LON + lon
                rows[RIM_Z + at] = own_row(level, lat + MID_LAT, lon)
                rows[RIM_Z + RIM_X + at] = own_row(level, lat, lon)
    return rows


def window_cells():
    cells = []
    for window in range(WINDOWS):
        for quarter in range(QUARTERS):
            for lat in range(WLAT):
                for half in range(2):
                    for third in range(3):
                        lon = half * MID_LON + (quarter % 2) * 3 + third
                        cells.append((window, quarter // 2, lat, lon))
    return cells


CELL_LIST = window_cells()
CELL_AT = {cell: at for at, cell in enumerate(CELL_LIST)}


def shifted_source():
    z_width = TILE_LON - MID_LON
    rows = []
    for window, level, lat, lon in CELL_LIST:
        column = window * WLON + lon + MID_LON
        if lat < MID_LAT and column < TILE_LON:
            rows.append(own_row(level, lat + MID_LAT, column))
        elif column < TILE_LON:
            rows.append(CELLS + (level * MID_LAT + lat - MID_LAT) * z_width + column - MID_LON)
        else:
            base = CELLS + RIM_Z + (RIM_X if lat >= MID_LAT else 0)
            rows.append(base + (level * MID_LAT + lat % MID_LAT) * MID_LON + column - TILE_LON)
    return np.array(rows)


def quarter_cells(quarter):
    groups = [[], [], [], []]
    for cell in CELL_LIST:
        window, level, lat, lon = cell
        if level != quarter // 2 or lon % MID_LON // 3 != quarter % 2:
            continue
        beyond = window * WLON + lon + MID_LON >= TILE_LON
        groups[2 * beyond + (lat >= MID_LAT)].append(cell)
    return groups


def one_hot(rows, count):
    picked = np.zeros((len(rows), count), np.float32)
    for at, row in enumerate(rows):
        if row >= 0:
            picked[at, row] = 1.0
    return picked.astype(BF16)


def quarter_pick():
    rows = []
    for quarter in range(QUARTERS):
        cells = sum(quarter_cells(quarter), [])
        rows += [CELL_AT[cell] for cell in cells] + [-1] * (PART - len(cells))
    return one_hot(rows, CELLS)


def group_pick():
    rows = []
    start = 0
    for group, padded in zip(quarter_cells(0), (OUT_OWN, OUT_Z, OUT_X, OUT_D)):
        rows += list(range(start, start + len(group))) + [-1] * (padded - len(group))
        start += len(group)
    return one_hot(rows, PART)


def own_pick():
    place = {}
    for quarter in range(QUARTERS):
        for at, (window, level, lat, lon) in enumerate(sum(quarter_cells(quarter), [])):
            column = (window * WLON + lon + MID_LON) % TILE_LON
            row = own_row(level, (lat + MID_LAT) % WLAT, column)
            place[row] = quarter * PART + at
    return one_hot([place[row] for row in range(CELLS)], QUARTERS * PART)


def bias_rows():
    rows = []
    for window, level, lat, lon in CELL_LIST[:WINDOW]:
        rows.append((level * WLAT + lat) * 16 + WLON - 1 - lon)
    single = one_hot(rows, LEV * WLAT * 16)
    return np.concatenate([single] * 3, axis=1)


def bias_columns():
    return np.array(
        [
            [
                SPAN_LAT * SPAN_LON * (LEV - 1 - level)
                + SPAN_LON * (WLAT - 1 - lat)
                + 2 * (WLON - 1)
                - lon
                for _, level, lat, lon in CELL_LIST[:WINDOW]
            ]
        ],
        np.int32,
    )


def pole_mask():
    side = np.array([lat < MID_LAT for _, _, lat, _ in CELL_LIST[:WINDOW]])
    return np.where(side[:, None] == side[None, :], 0.0, NEG_FILL).astype(np.float32)


def dot(left, right):
    return lax.dot_general(left, right, (((1,), (0,)), ((), ())), preferred_element_type=F32)


def dot_rows(left, right):
    return lax.dot_general(left, right, (((1,), (1,)), ((), ())), preferred_element_type=F32)


def dot_columns(left, right):
    return lax.dot_general(left, right, (((0,), (0,)), ((), ())), preferred_element_type=F32)


def call(kernel, outs, scratch=(), cost=None, name=None):
    return pl.pallas_call(
        kernel,
        out_shape=outs,
        scratch_shapes=scratch,
        name=name,
        cost_estimate=cost,
        compiler_params=pltpu.CompilerParams(vmem_limit_bytes=48 * 1024 * 1024),
    )


def cost(flops, moved):
    return pl.CostEstimate(flops=flops, bytes_accessed=moved, transcendentals=0)


def pack_kernel(pick, tokens, cotangent, rim_z, rim_x, rim_d):
    core = lax.rem(lax.axis_index("head"), 2)
    source = jnp.where(core == 0, tokens[...], cotangent[...])
    rim = dot(pick[...], source).astype(BF16)
    rim_z[...] = rim[:RIM_Z]
    rim_x[...] = rim[RIM_Z : RIM_Z + RIM_X]
    rim_d[...] = rim[RIM_Z + RIM_X :]


def bias_kernel(table, columns, rows, mask, bias, shifted, parts):
    heads = bias.shape[0]
    width = shifted.shape[1]
    for head in range(heads):
        spread = jnp.broadcast_to(table[head : head + 1, :], (16, table.shape[1]))
        rolled = pltpu.roll(spread, 0, 1, stride=1, stride_axis=0)[:, :width]
        high = rolled.astype(BF16)
        rest = rolled - high.astype(F32)
        middle = rest.astype(BF16)
        low = (rest - middle.astype(F32)).astype(BF16)
        for split, value in enumerate((high, middle, low)):
            shifted[(head * 3 + split) * 16 : (head * 3 + split + 1) * 16, :] = value
    place = lax.broadcasted_iota(jnp.int32, (width, WINDOW), 0)
    count = LEV * WLAT * 16
    for level in range(LEV):
        for lat in range(WLAT):
            offset = SPAN_LAT * SPAN_LON * level + SPAN_LON * lat
            wanted = (place == columns[...] + offset).astype(F32).astype(BF16)
            block = dot(shifted[...], wanted).astype(BF16)
            start = (level * WLAT + lat) * 16
            for head in range(heads):
                for split in range(3):
                    first = (head * 3 + split) * 16
                    parts[head, split * count + start : split * count + start + 16, :] = block[
                        first : first + 16
                    ]
    last = lax.axis_index("lat") == lax.axis_size("lat") - 1
    added = jnp.where(last, mask[...], 0.0)
    for head in range(heads):
        bias[head] = dot(rows[...], parts[head]) + added


def scaled_rows(values):
    floats = values.astype(F32)
    center = floats - jnp.mean(floats, axis=-1, keepdims=True)
    inverse = lax.rsqrt(jnp.mean(center * center, axis=-1, keepdims=True) + EPSILON)
    return center * inverse, inverse


def attend(window, head, offset, projected, d_attended, bias, merged, group):
    cells = slice(window * WINDOW, (window + 1) * WINDOW)
    scale = HEAD_DIM**-0.5
    at = head - offset
    first = 3 * HEAD_DIM * at
    query = projected[cells, first : first + HEAD_DIM]
    key = projected[cells, first + HEAD_DIM : first + 2 * HEAD_DIM]
    value = projected[cells, first + 2 * HEAD_DIM : first + 3 * HEAD_DIM]
    grad = d_attended[cells, HEAD_DIM * at : HEAD_DIM * (at + 1)]
    scores = dot_rows(query, key) * scale + bias[head]
    raised = jnp.exp(scores - jnp.max(scores, axis=-1, keepdims=True))
    prob = raised / jnp.sum(raised, axis=-1, keepdims=True)
    half = prob.astype(BF16)
    grad_prob = dot_rows(grad, value)
    row_term = jnp.sum(prob * grad_prob, axis=-1, keepdims=True)
    grad_score = (prob * (grad_prob - row_term) * scale).astype(BF16)
    attended = dot(half, value)
    grad_query = dot(grad_score, key)
    grad_key = dot_columns(grad_score, query)
    grad_value = dot_columns(half, grad)
    merged[cells, HEAD_DIM * at : HEAD_DIM * (at + 1)] = attended.astype(BF16)
    merged[cells, group + first : group + first + 3 * HEAD_DIM] = jnp.concatenate(
        [grad_query, grad_key, grad_value], axis=1
    ).astype(BF16)


def weight_terms(lon_count, normed, near_grad, merged, group, grads, whole):
    here = lax.axis_index("lon")
    rows = grads[0].shape[0]
    if rows % 128:
        whole[:, : 3 * group] = dot_columns(normed[...], merged[:, group:]).astype(BF16)
        whole[:, 3 * group :] = dot_columns(near_grad[...], merged[:, :group]).astype(BF16)
    for step in range(lon_count):
        there = lax.rem(here + step, lon_count)
        part = pl.ds(pl.multiple_of(there * rows, rows), rows)
        if rows % 128:
            grads[step][...] = whole[part, :]
            continue
        grads[step][:, : 3 * group] = dot_columns(normed[:, part], merged[:, group:]).astype(BF16)
        grads[step][:, 3 * group :] = dot_columns(near_grad[:, part], merged[:, :group]).astype(BF16)


def first_kernel(
    lon_count,
    tokens,
    cotangent,
    rim_here,
    rim_there,
    gain,
    w_qkv,
    w_out,
    bias,
    shift_pick,
    *refs,
):
    grads = refs[:lon_count]
    near_tokens, near_grad, normed, projected, d_attended, merged = refs[lon_count : lon_count + 6]
    source, whole, project, d_attend = refs[lon_count + 6 :]
    core = lax.rem(lax.axis_index("head"), 2)
    heads = bias.shape[0] // 2
    group = heads * HEAD_DIM
    source[CELLS:, :] = jnp.where(core == 0, rim_here[...], rim_there[...])
    source[:CELLS, :] = tokens[...]
    near_tokens[...] = dot(shift_pick[...], source[...]).astype(BF16)
    source[CELLS:, :] = jnp.where(core == 0, rim_there[...], rim_here[...])
    source[:CELLS, :] = cotangent[...]
    near_grad[...] = dot(shift_pick[...], source[...]).astype(BF16)
    scaled, _ = scaled_rows(near_tokens[...])
    normed[...] = (scaled * gain[...]).astype(BF16)
    project[...] = dot(normed[...], w_qkv[...]).astype(BF16)
    d_attend[...] = dot_rows(near_grad[...], w_out[...]).astype(BF16)
    projected[...] = project[:, 3 * group :]
    d_attended[...] = d_attend[:, group:]
    for window in range(WINDOWS):
        for head in range(heads):
            attend(window, head, 0, project, d_attend, bias, merged, group)
    weight_terms(lon_count, normed, near_grad, merged, group, grads, whole)


def second_kernel(
    lon_count,
    near_tokens,
    near_grad,
    normed,
    projected,
    d_attended,
    merged_first,
    w_qkv,
    w_out,
    bias,
    quarter,
    *refs,
):
    grads = refs[:lon_count]
    stay, over, swap, part_tokens, part_cotangent = refs[lon_count : lon_count + 5]
    merged, ordered, terms, whole = refs[lon_count + 5 :]
    head_index = lax.axis_index("head")
    core = lax.rem(head_index, 2)
    heads = bias.shape[0] // 2
    group = heads * HEAD_DIM
    for window in range(WINDOWS):
        for head in range(heads):
            attend(window, heads + head, heads, projected, d_attended, bias, merged, group)
    weight_terms(lon_count, normed, near_grad, merged, group, grads, whole)
    pick = quarter[...]
    for half, part in enumerate((merged_first, merged)):
        ordered[:, half * group : (half + 1) * group] = dot(pick, part[:, :group]).astype(BF16)
        start = 2 * group + half * 3 * group
        ordered[:, start : start + 3 * group] = dot(pick, part[:, group:]).astype(BF16)
    terms[0] = dot(ordered[:, : 2 * group], w_out[...]).astype(BF16)
    terms[1] = dot_rows(ordered[:, 2 * group :], w_qkv[...]).astype(BF16)

    def term(owner):
        return terms[:, pl.ds(pl.multiple_of(owner * PART, 16), PART), :]

    far = lax.rem(head_index + 2, QUARTERS)
    stay[...] = term(head_index)
    over[...] = term(far)
    swap[0] = term(head_index + 1 - 2 * core)
    swap[1] = term(far + 1 - 2 * core)
    mine = quarter[pl.ds(pl.multiple_of(head_index * PART, 16), PART), :]
    part_tokens[...] = dot(mine, near_tokens[...]).astype(BF16)
    part_cotangent[...] = dot(mine, near_grad[...]).astype(BF16)


def cores_kernel(over, swapped, total):
    total[...] = (over[...].astype(F32) + swapped[1].astype(F32)).astype(BF16)


def regroup_kernel(*refs):
    arrived, blocks = refs[:-1], refs[-1]
    total = arrived[0][...].astype(F32)
    for other in arrived[1:]:
        total = total + other[...].astype(F32)
    blocks[...] = total.astype(BF16)


def finish_kernel(group, flip, first, second, grad_qkv, grad_out):
    for half, arrived in enumerate((first, second)):
        total = jnp.sum(arrived[...].astype(F32), axis=0)
        grad_qkv[:, half * 3 * group : (half + 1) * 3 * group] = total[:, : 3 * group]
        out = total[:, 3 * group :]
        if flip:
            grad_out[half * group : (half + 1) * group, :] = out.T
        else:
            grad_out[:, half * group : (half + 1) * group] = out


def norm_kernel(part_tokens, part_cotangent, gain, pick, stay, swapped, crossed, *outs):
    layer = part_tokens[...].astype(F32)
    attn = stay[0].astype(F32) + swapped[0, 0].astype(F32) + crossed[0].astype(F32)
    d_normed = stay[1].astype(F32) + swapped[0, 1].astype(F32) + crossed[1].astype(F32)
    scaled, inverse = scaled_rows(part_tokens[...])
    grad = d_normed * gain[...]
    mean_grad = jnp.mean(grad, axis=-1, keepdims=True)
    mean_mixed = jnp.mean(grad * scaled, axis=-1, keepdims=True)
    change = (grad - mean_grad - scaled * mean_mixed) * inverse
    for at, value in enumerate((layer + attn, part_cotangent[...].astype(F32) + change)):
        rows = dot(pick[...], value.astype(BF16)).astype(BF16)
        for start, out in zip(OUT_STARTS, outs):
            out[at] = rows[start : start + out.shape[1]]


def join_kernel(pick, own, z_rows, x_rows, d_rows, joined, rows):
    for start, piece in zip(OUT_STARTS, (own, z_rows, x_rows, d_rows)):
        rows[:, start : start + piece.shape[1], :] = piece[...]
    for at in range(2):
        joined[at] = dot_columns(pick[...], rows[at]).astype(BF16)


def spread_kernel(pick, mine, far, near, across, layer_out, grad_tokens, gathered):
    head_index = lax.axis_index("head")
    sibling = 1 - 2 * lax.rem(head_index, 2)
    over = lax.rem(head_index + 2, QUARTERS)
    owners = (head_index, over, head_index + sibling, over + sibling)
    for owner, piece in zip(owners, (mine, far, near, across)):
        at = pl.ds(pl.multiple_of(owner * PART, 16), PART)
        gathered[:, at, :] = piece[...]
    layer_out[...] = dot(pick[...], gathered[0]).astype(BF16)
    grad_tokens[...] = dot(pick[...], gathered[1]).astype(BF16)


def shaped(*shape, dtype=BF16):
    return jax.ShapeDtypeStruct(shape, dtype)


def rotated(value, axis, step):
    count = lax.axis_size(axis)
    return lax.ppermute(value, axis, [(i, (i + step) % count) for i in range(count)])


def moved(value, lat_step, lon_step):
    lon_count, lat_count = lax.axis_size("lon"), lax.axis_size("lat")
    pairs = []
    for lon in range(lon_count):
        for lat in range(lat_count):
            target = (lon + lon_step) % lon_count * lat_count + (lat + lat_step) % lat_count
            pairs.append((lon * lat_count + lat, target))
    return lax.ppermute(value, ("lon", "lat"), pairs)


def body(tokens, norm_gain, w_qkv, w_out, bias_table, cotangent):
    level_count, lat_cells, lon_cells, width = tokens.shape
    heads = bias_table.shape[1]
    group = w_out.shape[0]
    lon_count, lat_count = lax.axis_size("lon"), lax.axis_size("lat")
    flat_tokens = tokens.reshape(CELLS, width)
    flat_grad = cotangent.reshape(CELLS, width)
    gain = norm_gain.reshape(1, width)
    rims = call(
        pack_kernel,
        [shaped(RIM_Z, width), shaped(RIM_X, width), shaped(RIM_D, width)],
        cost=cost(2 * RIM * CELLS * width, 4 * CELLS * width),
        name="pack_rims",
    )(one_hot(rim_source(), CELLS), flat_tokens, flat_grad)
    arrived = [moved(rims[0], -1, 0), moved(rims[1], 0, -1), moved(rims[2], -1, -1)]
    rim_here = jnp.concatenate(arrived, axis=0)
    pairs = [(i, i ^ 1) for i in range(QUARTERS)]
    rim_there = lax.ppermute(rim_here, "head", pairs)
    table = jnp.pad(bias_table.T, ((0, 0), (0, 1024 - bias_table.shape[0])))
    bias = call(
        bias_kernel,
        shaped(heads, WINDOW, WINDOW, dtype=F32),
        [pltpu.VMEM((heads * 48, 768), BF16), pltpu.VMEM((heads, 576, WINDOW), BF16)],
        cost=cost(2 * 192 * 768 * 144 * 12 * 2, 1000000),
        name="window_bias",
    )(table, bias_columns(), bias_rows(), pole_mask())
    lon_rows = width // lon_count
    half_group = group // 2
    row_scratch = pltpu.VMEM((width, 4 * half_group), BF16)
    first = call(
        functools.partial(first_kernel, lon_count),
        [shaped(lon_rows, 4 * half_group)] * lon_count
        + [shaped(CELLS, width)] * 3
        + [shaped(CELLS, 3 * half_group), shaped(CELLS, half_group), shaped(CELLS, 4 * half_group)],
        [
            pltpu.VMEM((CELLS + RIM, width), BF16),
            row_scratch,
            pltpu.VMEM((CELLS, 3 * group), BF16),
            pltpu.VMEM((CELLS, group), BF16),
        ],
        cost=cost(3 * CELLS * width * width, 8000000),
        name="layer_first_heads",
    )(
        flat_tokens,
        flat_grad,
        rim_here,
        rim_there,
        gain,
        w_qkv,
        w_out,
        bias,
        one_hot(shifted_source(), CELLS + RIM),
    )
    near_tokens, near_grad, normed, projected, d_attended, merged = first[lon_count:]

    def lon_exchange(grads):
        return [grads[0]] + [rotated(grads[step], "lon", step) for step in range(1, lon_count)]

    def lat_exchange(arrived):
        rows = lon_rows // lat_count
        total = call(
            regroup_kernel,
            shaped(lon_rows, 4 * half_group),
            cost=cost(4 * lon_rows * 4 * half_group, 6 * lon_rows * 4 * half_group),
            name="sum_over_lon",
        )(*arrived)
        moved_rows = lax.all_to_all(total, "lat", 0, 0, tiled=True)
        return moved_rows.reshape(lat_count, rows, 4 * half_group)

    from_lon_first = lon_exchange(first[:lon_count])
    second = call(
        functools.partial(second_kernel, lon_count),
        [shaped(lon_rows, 4 * half_group)] * lon_count
        + [shaped(2, PART, width)] * 2
        + [shaped(2, 2, PART, width)]
        + [shaped(PART, width)] * 2,
        [
            pltpu.VMEM((CELLS, 4 * half_group), BF16),
            pltpu.VMEM((QUARTERS * PART, 4 * group), BF16),
            pltpu.VMEM((2, QUARTERS * PART, width), BF16),
            row_scratch,
        ],
        cost=cost(4 * CELLS * width * width, 8000000),
        name="layer_second_heads",
    )(
        near_tokens,
        near_grad,
        normed,
        projected,
        d_attended,
        merged,
        w_qkv,
        w_out,
        bias,
        quarter_pick(),
    )
    stay, over, swap, part_tokens, part_cotangent = second[lon_count:]
    swapped = lax.ppermute(swap, "head", pairs)
    from_lon_second = lon_exchange(second[:lon_count])
    across = call(
        cores_kernel, shaped(2, PART, width), cost=cost(0, 8 * PART * width), name="sum_over_cores"
    )(over, swapped)
    chips = [(i, i ^ 2) for i in range(QUARTERS)]
    crossed = lax.ppermute(across, "head", chips)
    from_lat_first = lat_exchange(from_lon_first)
    pieces = call(
        norm_kernel,
        [shaped(2, count, width) for count in (OUT_OWN, OUT_Z, OUT_X, OUT_D)],
        cost=cost(2 * 2 * OUT_ROWS * PART * width, 12 * PART * width),
        name="sum_over_heads",
    )(part_tokens, part_cotangent, gain, group_pick(), stay, swapped, crossed)
    home = [pieces[0], moved(pieces[1], 1, 0), moved(pieces[2], 0, 1), moved(pieces[3], 1, 1)]
    mine = call(
        join_kernel,
        shaped(2, PART, width),
        [pltpu.VMEM((2, OUT_ROWS, width), BF16)],
        cost=cost(2 * 2 * OUT_ROWS * PART * width, 8 * OUT_ROWS * width),
        name="join_home",
    )(group_pick(), *home)
    far = lax.ppermute(mine, "head", chips)
    near = lax.ppermute(mine, "head", pairs)
    from_lat_second = lat_exchange(from_lon_second)
    beyond = lax.ppermute(far, "head", pairs)
    layer_out, grad_tokens = call(
        spread_kernel,
        [shaped(CELLS, width)] * 2,
        [pltpu.VMEM((2, QUARTERS * PART, width), BF16)],
        cost=cost(2 * 2 * CELLS * CELLS * width, 8 * CELLS * width),
        name="spread_outputs",
    )(own_pick(), mine, far, near, beyond)
    rows = lon_rows // lat_count
    flip = rows % 128 == 0
    grad_qkv, grad_out = call(
        functools.partial(finish_kernel, half_group, flip),
        [
            shaped(rows, 3 * group, dtype=F32),
            shaped(*((group, rows) if flip else (rows, group)), dtype=F32),
        ],
        cost=cost(4 * rows * 4 * group, 16 * rows * 4 * group),
        name="sum_over_lat",
    )(from_lat_first, from_lat_second)
    return (
        layer_out.reshape(tokens.shape),
        grad_tokens.reshape(tokens.shape),
        grad_qkv,
        grad_out if flip else grad_out.T,
    )


def solution(mesh):
    in_specs = (
        P(None, "lat", "lon", None),
        P(),
        P(None, "head"),
        P("head", None),
        P(None, "head"),
        P(None, "lat", "lon", None),
    )
    out_specs = (
        P(None, "lat", "lon", None),
        P(None, "lat", "lon", None),
        P(("lon", "lat"), "head"),
        P("head", ("lon", "lat")),
    )
    return jax.shard_map(body, mesh=mesh, in_specs=in_specs, out_specs=out_specs, check_vma=False)
```

profile of v0, /device:TPU:0, one launch (start us, length us, event | category | flops | bytes accessed | tf_op | source)
XLA Modules:
  0.0 96.6 jit_solution(13234894824773457333)
XLA Ops:
  0.7 1.1 %copy-done.2 = bf16[2,6,24,1024]{3,2,1,0:T(8,128)(2,1)S(1)} copy-done((bf16[2,6,24,1024]{3,2,1,0:T(8,128)(2,1)S(1)}, bf16[2,6,24,1024]{3,2,1,0:T(8,128)(2,1)}, u32[]{:S(2)}) %copy-start.2) | copy-done | bytes 589848
  1.7 1.1 %copy-done.4 = bf16[2,6,24,1024]{3,2,1,0:T(8,128)(2,1)S(1)} copy-done((bf16[2,6,24,1024]{3,2,1,0:T(8,128)(2,1)S(1)}, bf16[2,6,24,1024]{3,2,1,0:T(8,128)(2,1)}, u32[]{:S(2)}) %copy-start.4) | copy-done | bytes 589848
  2.8 0.9 copy-done.9
  4.1 5.1 %collective-permute-start = (bf16[112,1024]{1,0:T(8,128)(2,1)S(1)}, bf16[112,1024]{1,0:T(8,128)(2,1)S(1)}, u32[]{:S(2)}, u32[]{:S(2)}) collective-permute-start(bf16[112,1024]{1,0:T(8,128)(2,1)S(1)} %get-tuple-element.30), channel_id=1, source_target_pairs={{0,12},{4,0},{8,4},{12,8},{16,28},{20,16},{24,20},{28,24},{1,13},{... | collective-permute-start | bytes 688136 | tf_op jit(solution)/shard_map/ppermute | solution.py:433
  9.2 1.5 %collective-permute-start.1 = (bf16[48,1024]{1,0:T(8,128)(2,1)S(1)}, bf16[48,1024]{1,0:T(8,128)(2,1)S(1)}, u32[]{:S(2)}, u32[]{:S(2)}) collective-permute-start(bf16[48,1024]{1,0:T(8,128)(2,1)S(1)} %get-tuple-element.31), channel_id=1, source_target_pairs={{0,16},{4,20},{8,24},{12,28},{16,0},{20,4},{24,8},{28,12},{1,17},{... | collective-permute-start | bytes 294920 | tf_op jit(solution)/shard_map/ppermute | solution.py:433
  11.1 4.0 %collective-permute-done = bf16[112,1024]{1,0:T(8,128)(2,1)S(1)} collective-permute-done((bf16[112,1024]{1,0:T(8,128)(2,1)S(1)}, bf16[112,1024]{1,0:T(8,128)(2,1)S(1)}, u32[]{:S(2)}, u32[]{:S(2)}) %collective-permute-start) | collective-permute-done | bytes 229408 | tf_op jit(solution)/shard_map/ppermute | solution.py:433
  15.2 1.0 %collective-permute-done.2 = bf16[48,1024]{1,0:T(8,128)(2,1)S(1)} collective-permute-done((bf16[48,1024]{1,0:T(8,128)(2,1)S(1)}, bf16[48,1024]{1,0:T(8,128)(2,1)S(1)}, u32[]{:S(2)}, u32[]{:S(2)}) %collective-permute-start.2) | collective-permute-done | bytes 98336 | tf_op jit(solution)/shard_map/ppermute | solution.py:433
  16.4 1.7 %window_bias.1.bias = f32[4,144,144]{2,1,0:T(8,128)S(1)} custom-call(f32[4,1024]{1,0:T(4,128)S(1)} %pad.4.table, s32[1,144]{1,0:T(1,128)S(1)} %copy-done.14, bf16[144,576]{1,0:T(8,128)(2,1)S(1)} %copy-done.12, f32[144,144]{1,0:T(8,128)S(1)} %copy-done.13), custom_call_target="tpu_custom_call" | custom-call | flops 1019215872 | bytes 1000000 | tf_op jit(solution)/shard_map/window_bias/pallas_call | solution.py:455
  18.1 0.8 copy-done
  18.9 6.5 %layer_first_heads.1 = (bf16[512,512]{1,0:T(8,128)(2,1)S(1)}, bf16[512,512]{1,0:T(8,128)(2,1)S(1)}, bf16[288,1024]{1,0:T(8,128)(2,1)S(1)}, bf16[288,1024]{1,0:T(...) custom-call(bf16[288,1024]{1,0:T(8,128)(2,1)S(1)} %bitcast.9, ...), custom_call_target="tpu_custom_call" | custom-call | flops 905969664 | bytes 8000000 | tf_op jit(solution)/shard_map/layer_first_heads/pallas_call | solution.py:465
  25.5 6.9 %layer_second_heads.1 = (bf16[512,512]{1,0:T(8,128)(2,1)S(1)}, bf16[512,512]{1,0:T(8,128)(2,1)S(1)}, bf16[2,80,1024]{2,1,0:T(8,128)(2,1)S(1)}, bf16[2,80,1024]{2...) custom-call(bf16[288,1024]{1,0:T(8,128)(2,1)S(1)} %get-tuple-element, ...), custom_call_target="tpu_custom_call" | custom-call | flops 1207959552 | bytes 8000000 | tf_op jit(solution)/shard_map/layer_second_heads/pallas_call | solution.py:506
  32.4 1.4 %collective-permute-start.13 = (bf16[512,512]{1,0:T(8,128)(2,1)S(1)}, bf16[512,512]{1,0:T(8,128)(2,1)S(1)}, u32[]{:S(2)}, u32[]{:S(2)}) collective-permute-start(bf16[512,512]{1,0:T(8,128)(2,1)S(1)} %get-tuple-element.53), channel_id=1, source_target_pairs={{0,16},{16,0},{1,17},{17,1},{2,18},{18,2},{3,19},{19,3},{4,20},{20... | collective-permute-start | bytes 1572872 | tf_op jit(solution)/shard_map/ppermute | solution.py:423
  33.9 12.7 %collective-permute-done.13.refs_1_ = bf16[512,512]{1,0:T(8,128)(2,1)S(1)} collective-permute-done((bf16[512,512]{1,0:T(8,128)(2,1)S(1)}, bf16[512,512]{1,0:T(8,128)(2,1)S(1)}, u32[]{:S(2)}, u32[]{:S(2)}) %collective-permute-start.13) | collective-permute-done | bytes 524320 | tf_op jit(solution)/shard_map/ppermute | solution.py:423
  46.7 0.9 sum_over_lon.3
  47.6 6.6 %all-to-all-start.1 = ((bf16[4,128,512]{2,1,0:T(8,128)(2,1)}), bf16[4,128,512]{2,1,0:T(8,128)(2,1)S(1)}, u32[]{:S(2)}, u32[]{:S(2)}) async-start(bf16[4,128,512]{2,1,0:T(8,128)(2,1)} %bitcast.7), calls=%async_computation.1 | async-start | bytes 1048576 | tf_op jit(solution)/shard_map/all_to_all | solution.py:502
  54.2 0.5 collective-permute-start.12
  54.8 1.6 %collective-permute-start.5 = (bf16[2,80,1024]{2,1,0:T(8,128)(2,1)S(1)}, bf16[2,80,1024]{2,1,0:T(8,128)(2,1)S(1)}, u32[]{:S(2)}, u32[]{:S(2)}) collective-permute-start(bf16[2,80,1024]{2,1,0:T(8,128)(2,1)S(1)} %sum_over_cores.1), channel_id=1, source_target_pairs={{0,2},{1,3},{2,0},{3,1},{4,6},{5,7},{6,4},{7,5},{8,10},{9,11},{10,... | collective-permute-start | bytes 983048 | tf_op jit(solution)/shard_map/ppermute | solution.py:539
  56.4 7.2 %collective-permute-done.5.crossed = bf16[2,80,1024]{2,1,0:T(8,128)(2,1)S(1)} collective-permute-done((bf16[2,80,1024]{2,1,0:T(8,128)(2,1)S(1)}, bf16[2,80,1024]{2,1,0:T(8,128)(2,1)S(1)}, u32[]{:S(2)}, u32[]{:S(2)}) %collective-permute-start.5) | collective-permute-done | bytes 327712 | tf_op jit(solution)/shard_map/ppermute | solution.py:539
  63.6 0.6 sum_over_heads.1
  64.2 1.8 %collective-permute-start.6 = (bf16[2,32,1024]{2,1,0:T(8,128)(2,1)S(1)}, bf16[2,32,1024]{2,1,0:T(8,128)(2,1)S(1)}, u32[]{:S(2)}, u32[]{:S(2)}) collective-permute-start(bf16[2,32,1024]{2,1,0:T(8,128)(2,1)S(1)} %get-tuple-element.45), channel_id=1, source_target_pairs={{0,4},{4,8},{8,12},{12,0},{16,20},{20,24},{24,28},{28,16},{1,5},{5... | collective-permute-start | bytes 393224 | tf_op jit(solution)/shard_map/ppermute | solution.py:433
  66.0 1.5 %collective-permute-done.12.refs_1_ = bf16[512,512]{1,0:T(8,128)(2,1)S(1)} collective-permute-done((bf16[512,512]{1,0:T(8,128)(2,1)S(1)}, bf16[512,512]{1,0:T(8,128)(2,1)S(1)}, u32[]{:S(2)}, u32[]{:S(2)}) %collective-permute-start.12) | collective-permute-done | bytes 524320 | tf_op jit(solution)/shard_map/ppermute | solution.py:423
  67.4 0.9 sum_over_lon.2
  68.3 3.0 %all-to-all-done.1.second = bf16[4,128,512]{2,1,0:T(8,128)(2,1)S(1)} async-done(((bf16[4,128,512]{2,1,0:T(8,128)(2,1)}), bf16[4,128,512]{2,1,0:T(8,128)(2,1)S(1)}, u32[]{:S(2)}, u32[]{:S(2)}) %all-to-all-start.1) | async-done | bytes 524320 | tf_op jit(solution)/shard_map/all_to_all | solution.py:502
  71.3 3.5 %all-to-all-start = ((bf16[4,128,512]{2,1,0:T(8,128)(2,1)}), bf16[4,128,512]{2,1,0:T(8,128)(2,1)S(1)}, u32[]{:S(2)}, u32[]{:S(2)}) async-start(bf16[4,128,512]{2,1,0:T(8,128)(2,1)} %bitcast.6), calls=%async_computation | async-start | bytes 1048576 | tf_op jit(solution)/shard_map/all_to_all | solution.py:502
  74.9 3.4 %collective-permute-start.8 = (bf16[2,16,1024]{2,1,0:T(8,128)(2,1)S(1)}, bf16[2,16,1024]{2,1,0:T(8,128)(2,1)S(1)}, u32[]{:S(2)}, u32[]{:S(2)}) collective-permute-start(bf16[2,16,1024]{2,1,0:T(8,128)(2,1)S(1)} %get-tuple-element.47), channel_id=1, source_target_pairs={{0,20},{4,24},{8,28},{12,16},{16,4},{20,8},{24,12},{28,0},{1,21},{... | collective-permute-start | bytes 196616 | tf_op jit(solution)/shard_map/ppermute | solution.py:433
  78.3 0.9 collective-permute-done.7.x_rows
  79.1 6.7 %collective-permute-done.8.d_rows = bf16[2,16,1024]{2,1,0:T(8,128)(2,1)S(1)} collective-permute-done((bf16[2,16,1024]{2,1,0:T(8,128)(2,1)S(1)}, bf16[2,16,1024]{2,1,0:T(8,128)(2,1)S(1)}, u32[]{:S(2)}, u32[]{:S(2)}) %collective-permute-start.8) | collective-permute-done | bytes 65568 | tf_op jit(solution)/shard_map/ppermute | solution.py:433
  86.1 1.6 %collective-permute-start.9 = (bf16[2,80,1024]{2,1,0:T(8,128)(2,1)S(1)}, bf16[2,80,1024]{2,1,0:T(8,128)(2,1)S(1)}, u32[]{:S(2)}, u32[]{:S(2)}) collective-permute-start(bf16[2,80,1024]{2,1,0:T(8,128)(2,1)S(1)} %join_home.1.mine), channel_id=1, source_target_pairs={{0,2},{1,3},{2,0},{3,1},{4,6},{5,7},{6,4},{7,5},{8,10},{9,11},{10,... | collective-permute-start | bytes 983048 | tf_op jit(solution)/shard_map/ppermute | solution.py:555
  87.7 5.5 %collective-permute-done.9.far = bf16[2,80,1024]{2,1,0:T(8,128)(2,1)S(1)} collective-permute-done((bf16[2,80,1024]{2,1,0:T(8,128)(2,1)S(1)}, bf16[2,80,1024]{2,1,0:T(8,128)(2,1)S(1)}, u32[]{:S(2)}, u32[]{:S(2)}) %collective-permute-start.9) | collective-permute-done | bytes 327712 | tf_op jit(solution)/shard_map/ppermute | solution.py:555
  93.2 0.9 sum_over_lat.1
  94.2 0.7 collective-permute-done.11.across
  94.9 1.7 %spread_outputs.1 = (bf16[288,1024]{1,0:T(8,128)(2,1)}, bf16[288,1024]{1,0:T(8,128)(2,1)}) custom-call(bf16[288,320]{1,0:T(8,128)(2,1)S(1)} %copy-done.8, bf16[2,80,1024]{2,1,0:T(8,128)(2,1)S(1)} %join_home.1.mine, bf16[2,80,1024]{2,1,0:T(8,128)(2,1)S(1)} %collective-permute-done.9.far, bf16[2,80,1024]{2,1,0:T(8,128)(2,1)S(1)} %collective-permute-done.10.near, ...), custom_call_target="tpu_custom_call" | custom-call | flops 339738624 | bytes 2359296 | tf_op jit(solution)/shard_map/spread_outputs/pallas_call | solution.py:559
  (47 shorter events, 1.7 us)
Async XLA Ops:
  0.6 15.7 %copy-start.14 = (s32[1,144]{1,0:T(1,128)S(1)}, s32[1,144]{1,0:T(1,128)}, u32[]{:S(2)}) copy-start(s32[1,144]{1,0:T(1,128)} %constant.20.clone.columns) | copy-start | bytes 1732
  0.6 1.1 %copy-start.2 = (bf16[2,6,24,1024]{3,2,1,0:T(8,128)(2,1)S(1)}, bf16[2,6,24,1024]{3,2,1,0:T(8,128)(2,1)}, u32[]{:S(2)}) copy-start(bf16[2,6,24,1024]{3,2,1,0:T(8,128)(2,1)} %param.15) | copy-start | bytes 1769476
  1.7 1.1 %copy-start.4 = (bf16[2,6,24,1024]{3,2,1,0:T(8,128)(2,1)S(1)}, bf16[2,6,24,1024]{3,2,1,0:T(8,128)(2,1)}, u32[]{:S(2)}) copy-start(bf16[2,6,24,1024]{3,2,1,0:T(8,128)(2,1)} %param.20) | copy-start | bytes 1769476
  2.8 0.9 copy-start.9
  3.7 12.6 %copy-start.15 = (f32[759,4]{0,1:T(4,128)S(1)}, f32[759,4]{0,1:T(4,128)}, u32[]{:S(2)}) copy-start(f32[759,4]{0,1:T(4,128)} %param.19) | copy-start | bytes 36436
  3.7 12.6 %copy-start.12 = (bf16[144,576]{1,0:T(8,128)(2,1)S(1)}, bf16[144,576]{1,0:T(8,128)(2,1)}, u32[]{:S(2)}) copy-start(bf16[144,576]{1,0:T(8,128)(2,1)} %constant.21.clone.rows) | copy-start | bytes 497668
  3.7 12.6 %copy-start.13 = (f32[144,144]{1,0:T(8,128)S(1)}, f32[144,144]{1,0:T(8,128)}, u32[]{:S(2)}) copy-start(f32[144,144]{1,0:T(8,128)} %constant.22.clone.mask) | copy-start | bytes 248836
  4.1 11.0 %collective-permute-start = (bf16[112,1024]{1,0:T(8,128)(2,1)S(1)}, bf16[112,1024]{1,0:T(8,128)(2,1)S(1)}, u32[]{:S(2)}, u32[]{:S(2)}) collective-permute-start(bf16[112,1024]{1,0:T(8,128)(2,1)S(1)} %get-tuple-element.30), channel_id=1, source_target_pairs={{0,12},{4,0},{8,4},{12,8},{16,28},{20,16},{24,20},{28,24},{1,13},{... | collective-permute-start | bytes 688136 | tf_op jit(solution)/shard_map/ppermute | solution.py:433
  9.2 5.9 %collective-permute-start.1 = (bf16[48,1024]{1,0:T(8,128)(2,1)S(1)}, bf16[48,1024]{1,0:T(8,128)(2,1)S(1)}, u32[]{:S(2)}, u32[]{:S(2)}) collective-permute-start(bf16[48,1024]{1,0:T(8,128)(2,1)S(1)} %get-tuple-element.31), channel_id=1, source_target_pairs={{0,16},{4,20},{8,24},{12,28},{16,0},{20,4},{24,8},{28,12},{1,17},{... | collective-permute-start | bytes 294920 | tf_op jit(solution)/shard_map/ppermute | solution.py:433
  10.7 5.5 %collective-permute-start.2 = (bf16[48,1024]{1,0:T(8,128)(2,1)S(1)}, bf16[48,1024]{1,0:T(8,128)(2,1)S(1)}, u32[]{:S(2)}, u32[]{:S(2)}) collective-permute-start(bf16[48,1024]{1,0:T(8,128)(2,1)S(1)} %get-tuple-element.32), channel_id=1, source_target_pairs={{0,28},{4,16},{8,20},{12,24},{16,12},{20,0},{24,4},{28,8},{1,29},{... | collective-permute-start | bytes 294920 | tf_op jit(solution)/shard_map/ppermute | solution.py:433
  16.2 2.7 %collective-permute-start.3 = (bf16[208,1024]{1,0:T(8,128)(2,1)S(1)}, bf16[208,1024]{1,0:T(8,128)(2,1)S(1)}, u32[]{:S(2)}, u32[]{:S(2)}) collective-permute-start(bf16[208,1024]{1,0:T(8,128)(2,1)S(1)} %constant_dynamic-update-slice_fusion.rim_here), channel_id=1, source_target_pairs={{0,1},{1,0},{2,3},{3,2},{4,5},{5,4},{6,7},{7,6},{8,9},{9,8},{10,11... | collective-permute-start | bytes 1277960 | tf_op jit(solution)/shard_map/ppermute | solution.py:453
  16.3 2.5 %copy-start.3 = (bf16[2,6,24,1024]{3,2,1,0:T(8,128)(2,1)S(1)}, bf16[2,6,24,1024]{3,2,1,0:T(8,128)(2,1)}, u32[]{:S(2)}) copy-start(bf16[2,6,24,1024]{3,2,1,0:T(8,128)(2,1)} %param.15) | copy-start | bytes 1769476
  16.4 2.5 %copy-start.5 = (bf16[256,1024]{1,0:T(8,128)(2,1)S(1)}, bf16[256,1024]{1,0:T(8,128)(2,1)}, u32[]{:S(2)}) copy-start(bf16[256,1024]{1,0:T(8,128)(2,1)} %w_out.3) | copy-start | bytes 1572868
  16.4 2.5 %copy-start.6 = (bf16[288,496]{1,0:T(8,128)(2,1)S(1)}, bf16[288,496]{1,0:T(8,128)(2,1)}, u32[]{:S(2)}) copy-start(bf16[288,496]{1,0:T(8,128)(2,1)} %constant.23.clone.shift_pick) | copy-start | bytes 857092
  16.4 2.5 %copy-start.11 = (f32[1024]{0:T(1024)S(1)}, f32[1024]{0:T(1024)}, u32[]{:S(2)}) copy-start(f32[1024]{0:T(1024)} %param.16) | copy-start | bytes 12292
  18.1 0.8 copy-start
  18.9 6.5 %copy-start.1 = (f32[4,144,144]{2,1,0:T(8,128)S(1)}, f32[4,144,144]{2,1,0:T(8,128)}, u32[]{:S(2)}) copy-start(f32[4,144,144]{2,1,0:T(8,128)} %copy-done) | copy-start | bytes 995332
  18.9 6.5 %copy-start.7 = (bf16[320,288]{1,0:T(8,128)(2,1)S(1)}, bf16[320,288]{1,0:T(8,128)(2,1)}, u32[]{:S(2)}) copy-start(bf16[320,288]{1,0:T(8,128)(2,1)} %constant.24.clone.quarter) | copy-start | bytes 552964
  32.4 14.3 %collective-permute-start.13 = (bf16[512,512]{1,0:T(8,128)(2,1)S(1)}, bf16[512,512]{1,0:T(8,128)(2,1)S(1)}, u32[]{:S(2)}, u32[]{:S(2)}) collective-permute-start(bf16[512,512]{1,0:T(8,128)(2,1)S(1)} %get-tuple-element.53), channel_id=1, source_target_pairs={{0,16},{16,0},{1,17},{17,1},{2,18},{18,2},{3,19},{19,3},{4,20},{20... | collective-permute-start | bytes 1572872 | tf_op jit(solution)/shard_map/ppermute | solution.py:423
  33.7 21.0 %collective-permute-start.4 = (bf16[2,2,80,1024]{3,2,1,0:T(8,128)(2,1)}, bf16[2,2,80,1024]{3,2,1,0:T(8,128)(2,1)S(1)}, u32[]{:S(2)}, u32[]{:S(2)}) collective-permute-start(bf16[2,2,80,1024]{3,2,1,0:T(8,128)(2,1)} %get-tuple-element.42), channel_id=1, source_target_pairs={{0,1},{1,0},{2,3},{3,2},{4,5},{5,4},{6,7},{7,6},{8,9},{9,8},{10,11... | collective-permute-start | bytes 1966088 | tf_op jit(solution)/shard_map/ppermute | solution.py:533
  47.6 16.0 %copy-start.10 = (bf16[96,80]{1,0:T(8,128)(2,1)S(1)}, bf16[96,80]{1,0:T(8,128)(2,1)}, u32[]{:S(2)}) copy-start(bf16[96,80]{1,0:T(8,128)(2,1)} %constant.25.clone.pick) | copy-start | bytes 46084
  47.6 23.8 %all-to-all-start.1 = ((bf16[4,128,512]{2,1,0:T(8,128)(2,1)}), bf16[4,128,512]{2,1,0:T(8,128)(2,1)S(1)}, u32[]{:S(2)}, u32[]{:S(2)}) async-start(bf16[4,128,512]{2,1,0:T(8,128)(2,1)} %bitcast.7), calls=%async_computation.1 | async-start | bytes 1048576 | tf_op jit(solution)/shard_map/all_to_all | solution.py:502
  54.2 13.3 %collective-permute-start.12 = (bf16[512,512]{1,0:T(8,128)(2,1)S(1)}, bf16[512,512]{1,0:T(8,128)(2,1)S(1)}, u32[]{:S(2)}, u32[]{:S(2)}) collective-permute-start(bf16[512,512]{1,0:T(8,128)(2,1)S(1)} %get-tuple-element.51), channel_id=1, source_target_pairs={{0,16},{16,0},{1,17},{17,1},{2,18},{18,2},{3,19},{19,3},{4,20},{20... | collective-permute-start | bytes 1572872 | tf_op jit(solution)/shard_map/ppermute | solution.py:423
  54.8 8.8 %collective-permute-start.5 = (bf16[2,80,1024]{2,1,0:T(8,128)(2,1)S(1)}, bf16[2,80,1024]{2,1,0:T(8,128)(2,1)S(1)}, u32[]{:S(2)}, u32[]{:S(2)}) collective-permute-start(bf16[2,80,1024]{2,1,0:T(8,128)(2,1)S(1)} %sum_over_cores.1), channel_id=1, source_target_pairs={{0,2},{1,3},{2,0},{3,1},{4,6},{5,7},{6,4},{7,5},{8,10},{9,11},{10,... | collective-permute-start | bytes 983048 | tf_op jit(solution)/shard_map/ppermute | solution.py:539
  64.2 21.6 %collective-permute-start.6 = (bf16[2,32,1024]{2,1,0:T(8,128)(2,1)S(1)}, bf16[2,32,1024]{2,1,0:T(8,128)(2,1)S(1)}, u32[]{:S(2)}, u32[]{:S(2)}) collective-permute-start(bf16[2,32,1024]{2,1,0:T(8,128)(2,1)S(1)} %get-tuple-element.45), channel_id=1, source_target_pairs={{0,4},{4,8},{8,12},{12,0},{16,20},{20,24},{24,28},{28,16},{1,5},{5... | collective-permute-start | bytes 393224 | tf_op jit(solution)/shard_map/ppermute | solution.py:433
  68.3 26.5 %copy-start.8 = (bf16[288,320]{1,0:T(8,128)(2,1)S(1)}, bf16[288,320]{1,0:T(8,128)(2,1)}, u32[]{:S(2)}) copy-start(bf16[288,320]{1,0:T(8,128)(2,1)} %constant.26.clone.pick) | copy-start | bytes 552964
  71.3 21.9 %all-to-all-start = ((bf16[4,128,512]{2,1,0:T(8,128)(2,1)}), bf16[4,128,512]{2,1,0:T(8,128)(2,1)S(1)}, u32[]{:S(2)}, u32[]{:S(2)}) async-start(bf16[4,128,512]{2,1,0:T(8,128)(2,1)} %bitcast.6), calls=%async_computation | async-start | bytes 1048576 | tf_op jit(solution)/shard_map/all_to_all | solution.py:502
  74.8 4.3 %collective-permute-start.7 = (bf16[2,16,1024]{2,1,0:T(8,128)(2,1)S(1)}, bf16[2,16,1024]{2,1,0:T(8,128)(2,1)S(1)}, u32[]{:S(2)}, u32[]{:S(2)}) collective-permute-start(bf16[2,16,1024]{2,1,0:T(8,128)(2,1)S(1)} %get-tuple-element.46), channel_id=1, source_target_pairs={{0,16},{4,20},{8,24},{12,28},{16,0},{20,4},{24,8},{28,12},{1,17},{... | collective-permute-start | bytes 196616 | tf_op jit(solution)/shard_map/ppermute | solution.py:433
  74.9 10.9 %collective-permute-start.8 = (bf16[2,16,1024]{2,1,0:T(8,128)(2,1)S(1)}, bf16[2,16,1024]{2,1,0:T(8,128)(2,1)S(1)}, u32[]{:S(2)}, u32[]{:S(2)}) collective-permute-start(bf16[2,16,1024]{2,1,0:T(8,128)(2,1)S(1)} %get-tuple-element.47), channel_id=1, source_target_pairs={{0,20},{4,24},{8,28},{12,16},{16,4},{20,8},{24,12},{28,0},{1,21},{... | collective-permute-start | bytes 196616 | tf_op jit(solution)/shard_map/ppermute | solution.py:433
  86.1 7.1 %collective-permute-start.9 = (bf16[2,80,1024]{2,1,0:T(8,128)(2,1)S(1)}, bf16[2,80,1024]{2,1,0:T(8,128)(2,1)S(1)}, u32[]{:S(2)}, u32[]{:S(2)}) collective-permute-start(bf16[2,80,1024]{2,1,0:T(8,128)(2,1)S(1)} %join_home.1.mine), channel_id=1, source_target_pairs={{0,2},{1,3},{2,0},{3,1},{4,6},{5,7},{6,4},{7,5},{8,10},{9,11},{10,... | collective-permute-start | bytes 983048 | tf_op jit(solution)/shard_map/ppermute | solution.py:555
  87.7 6.4 %collective-permute-start.10 = (bf16[2,80,1024]{2,1,0:T(8,128)(2,1)S(1)}, bf16[2,80,1024]{2,1,0:T(8,128)(2,1)S(1)}, u32[]{:S(2)}, u32[]{:S(2)}) collective-permute-start(bf16[2,80,1024]{2,1,0:T(8,128)(2,1)S(1)} %join_home.1.mine), channel_id=1, source_target_pairs={{0,1},{1,0},{2,3},{3,2},{4,5},{5,4},{6,7},{7,6},{8,9},{9,8},{10,11... | collective-permute-start | bytes 983048 | tf_op jit(solution)/shard_map/ppermute | solution.py:556
  93.2 1.6 %collective-permute-start.11 = (bf16[2,80,1024]{2,1,0:T(8,128)(2,1)S(1)}, bf16[2,80,1024]{2,1,0:T(8,128)(2,1)S(1)}, u32[]{:S(2)}, u32[]{:S(2)}) collective-permute-start(bf16[2,80,1024]{2,1,0:T(8,128)(2,1)S(1)} %collective-permute-done.9.far), channel_id=1, source_target_pairs={{0,1},{1,0},{2,3},{3,2},{4,5},{5,4},{6,7},{7,6},{8,9},{9,8},{10,11... | collective-permute-start | bytes 983048 | tf_op jit(solution)/shard_map/ppermute | solution.py:558
where the time goes:
time: 97.6 us; the launch traced here: 96.6 us
  waiting for transfers between devices  43.2 us (44%)
  starting transfers between devices  27.7 us (28%)
  Pallas kernels  20.8 us (21%)
  local copies, waits for them, and re-layouts  3.95 us (4%)
    ppermute x2, waiting for transfers between devices, rotated(): lax.ppermute(value, axis, [(i, (i + step) % count) for i in range(count)])  14.2 us
    ppermute x6, waiting for transfers between devices, moved(): return lax.ppermute(value, ('lon', 'lat'), pairs)  12.6 us
    ppermute x6, starting transfers between devices, moved(): return lax.ppermute(value, ('lon', 'lat'), pairs)  12.2 us
    all_to_all x2, starting transfers between devices, lat_exchange(): moved_rows = lax.all_to_all(total, 'lat', 0, 0, tiled=True)  10 us
    ppermute x1, waiting for transfers between devices, body(): crossed = lax.ppermute(across, 'head', chips)  7.22 us
    pallas_call x1, Pallas kernels, body(): call(functools.partial(second_kernel, lon_count), [shaped(lon_rows, 4 * h...  6.91 us
    pallas_call x1, Pallas kernels, body(): call(functools.partial(first_kernel, lon_count), [shaped(lon_rows, 4 * ha...  6.5 us
    ppermute x1, waiting for transfers between devices, body(): far = lax.ppermute(mine, 'head', chips)  5.5 us
  transfers between devices with their start and end apart: 16, of which 10 were waited for; matrix products, arithmetic and copies ran while one was open for 0% of the time, Pallas kernels for 6%

commit v1 on v0

--- a/solution.py
+++ b/solution.py
@@ -169,15 +169,23 @@
     return lax.dot_general(left, right, (((0,), (0,)), ((), ())), preferred_element_type=F32)
 
 
-def call(kernel, outs, scratch=(), cost=None, name=None):
-    return pl.pallas_call(
-        kernel,
-        out_shape=outs,
-        scratch_shapes=scratch,
-        name=name,
-        cost_estimate=cost,
-        compiler_params=pltpu.CompilerParams(vmem_limit_bytes=48 * 1024 * 1024),
-    )
+def call(kernel, outs, scratch=(), cost=None, name=None, after=()):
+    def run(*args):
+        def body(*refs):
+            kernel(*refs[: len(args)], *refs[len(args) + len(after) :])
+
+        return pl.pallas_call(
+            body,
+            out_shape=outs,
+            in_specs=[pl.BlockSpec(memory_space=pltpu.VMEM)] * len(args)
+            + [pl.BlockSpec(memory_space=pl.ANY)] * len(after),
+            scratch_shapes=scratch,
+            name=name,
+            cost_estimate=cost,
+            compiler_params=pltpu.CompilerParams(vmem_limit_bytes=48 * 1024 * 1024),
+        )(*args, *after)
+
+    return run
 
 
 def cost(flops, moved):
@@ -232,50 +240,51 @@
     return center * inverse, inverse
 
 
-def attend(window, head, offset, projected, d_attended, bias, merged, group):
+def attend(window, head, projected, d_attended, bias, merged, group):
     cells = slice(window * WINDOW, (window + 1) * WINDOW)
     scale = HEAD_DIM**-0.5
-    at = head - offset
-    first = 3 * HEAD_DIM * at
-    query = projected[cells, first : first + HEAD_DIM]
+    first = 3 * HEAD_DIM * head
+    query = projected[cells, first : first + HEAD_DIM] * jnp.asarray(scale, BF16)
     key = projected[cells, first + HEAD_DIM : first + 2 * HEAD_DIM]
     value = projected[cells, first + 2 * HEAD_DIM : first + 3 * HEAD_DIM]
-    grad = d_attended[cells, HEAD_DIM * at : HEAD_DIM * (at + 1)]
-    scores = dot_rows(query, key) * scale + bias[head]
+    grad = d_attended[cells, HEAD_DIM * head : HEAD_DIM * (head + 1)]
+    scores = dot_rows(query, key) + bias[head]
     raised = jnp.exp(scores - jnp.max(scores, axis=-1, keepdims=True))
-    prob = raised / jnp.sum(raised, axis=-1, keepdims=True)
+    prob = raised * (1.0 / jnp.sum(raised, axis=-1, keepdims=True))
     half = prob.astype(BF16)
     grad_prob = dot_rows(grad, value)
     row_term = jnp.sum(prob * grad_prob, axis=-1, keepdims=True)
-    grad_score = (prob * (grad_prob - row_term) * scale).astype(BF16)
+    grad_score = (prob * (grad_prob - row_term)).astype(BF16)
     attended = dot(half, value)
-    grad_query = dot(grad_score, key)
+    grad_query = dot(grad_score, key) * scale
     grad_key = dot_columns(grad_score, query)
     grad_value = dot_columns(half, grad)
-    merged[cells, HEAD_DIM * at : HEAD_DIM * (at + 1)] = attended.astype(BF16)
+    merged[cells, HEAD_DIM * head : HEAD_DIM * (head + 1)] = attended.astype(BF16)
     merged[cells, group + first : group + first + 3 * HEAD_DIM] = jnp.concatenate(
         [grad_query, grad_key, grad_value], axis=1
     ).astype(BF16)
 
 
-def weight_terms(lon_count, normed, near_grad, merged, group, grads, whole):
+def weight_terms(half, normed, near_grad, merged, grads, whole):
     here = lax.axis_index("lon")
     rows = grads[0].shape[0]
+    group = merged.shape[1] // 8
+    attended = slice(half * group, (half + 1) * group)
+    d_qkv = slice((2 + 3 * half) * group, (5 + 3 * half) * group)
     if rows % 128:
-        whole[:, : 3 * group] = dot_columns(normed[...], merged[:, group:]).astype(BF16)
-        whole[:, 3 * group :] = dot_columns(near_grad[...], merged[:, :group]).astype(BF16)
-    for step in range(lon_count):
-        there = lax.rem(here + step, lon_count)
+        whole[:, : 3 * group] = dot_columns(normed[...], merged[:, d_qkv]).astype(BF16)
+        whole[:, 3 * group :] = dot_columns(near_grad[...], merged[:, attended]).astype(BF16)
+    for step, grad in enumerate(grads):
+        there = lax.rem(here + step, len(grads))
         part = pl.ds(pl.multiple_of(there * rows, rows), rows)
         if rows % 128:
-            grads[step][...] = whole[part, :]
+            grad[...] = whole[part, :]
             continue
-        grads[step][:, : 3 * group] = dot_columns(normed[:, part], merged[:, group:]).astype(BF16)
-        grads[step][:, 3 * group :] = dot_columns(near_grad[:, part], merged[:, :group]).astype(BF16)
-
-
-def first_kernel(
-    lon_count,
+        grad[:, : 3 * group] = dot_columns(normed[:, part], merged[:, d_qkv]).astype(BF16)
+        grad[:, 3 * group :] = dot_columns(near_grad[:, part], merged[:, attended]).astype(BF16)
+
+
+def layer_kernel(
     tokens,
     cotangent,
     rim_here,
@@ -285,13 +294,14 @@
     w_out,
     bias,
     shift_pick,
+    quarter,
     *refs,
 ):
-    grads = refs[:lon_count]
-    near_tokens, near_grad, normed, projected, d_attended, merged = refs[lon_count : lon_count + 6]
-    source, whole, project, d_attend = refs[lon_count + 6 :]
-    core = lax.rem(lax.axis_index("head"), 2)
-    heads = bias.shape[0] // 2
+    *grads, normed, near_grad, merged, stay, over, swap, part_tokens, part_cotangent = refs[:-7]
+    source, near_tokens, projected, d_attended, ordered, terms, whole = refs[-7:]
+    head_index = lax.axis_index("head")
+    core = lax.rem(head_index, 2)
+    heads = bias.shape[0]
     group = heads * HEAD_DIM
     source[CELLS:, :] = jnp.where(core == 0, rim_here[...], rim_there[...])
     source[:CELLS, :] = tokens[...]
@@ -301,48 +311,15 @@
     near_grad[...] = dot(shift_pick[...], source[...]).astype(BF16)
     scaled, _ = scaled_rows(near_tokens[...])
     normed[...] = (scaled * gain[...]).astype(BF16)
-    project[...] = dot(normed[...], w_qkv[...]).astype(BF16)
-    d_attend[...] = dot_rows(near_grad[...], w_out[...]).astype(BF16)
-    projected[...] = project[:, 3 * group :]
-    d_attended[...] = d_attend[:, group:]
+    projected[...] = dot(normed[...], w_qkv[...]).astype(BF16)
+    d_attended[...] = dot_rows(near_grad[...], w_out[...]).astype(BF16)
     for window in range(WINDOWS):
         for head in range(heads):
-            attend(window, head, 0, project, d_attend, bias, merged, group)
-    weight_terms(lon_count, normed, near_grad, merged, group, grads, whole)
-
-
-def second_kernel(
-    lon_count,
-    near_tokens,
-    near_grad,
-    normed,
-    projected,
-    d_attended,
-    merged_first,
-    w_qkv,
-    w_out,
-    bias,
-    quarter,
-    *refs,
-):
-    grads = refs[:lon_count]
-    stay, over, swap, part_tokens, part_cotangent = refs[lon_count : lon_count + 5]
-    merged, ordered, terms, whole = refs[lon_count + 5 :]
-    head_index = lax.axis_index("head")
-    core = lax.rem(head_index, 2)
-    heads = bias.shape[0] // 2
-    group = heads * HEAD_DIM
-    for window in range(WINDOWS):
-        for head in range(heads):
-            attend(window, heads + head, heads, projected, d_attended, bias, merged, group)
-    weight_terms(lon_count, normed, near_grad, merged, group, grads, whole)
-    pick = quarter[...]
-    for half, part in enumerate((merged_first, merged)):
-        ordered[:, half * group : (half + 1) * group] = dot(pick, part[:, :group]).astype(BF16)
-        start = 2 * group + half * 3 * group
-        ordered[:, start : start + 3 * group] = dot(pick, part[:, group:]).astype(BF16)
-    terms[0] = dot(ordered[:, : 2 * group], w_out[...]).astype(BF16)
-    terms[1] = dot_rows(ordered[:, 2 * group :], w_qkv[...]).astype(BF16)
+            attend(window, head, projected, d_attended, bias, merged, group)
+    weight_terms(0, normed, near_grad, merged, grads, whole)
+    ordered[...] = dot(quarter[...], merged[...]).astype(BF16)
+    terms[0] = dot(ordered[:, :group], w_out[...]).astype(BF16)
+    terms[1] = dot_rows(ordered[:, group:], w_qkv[...]).astype(BF16)
 
     def term(owner):
         return terms[:, pl.ds(pl.multiple_of(owner * PART, 16), PART), :]
@@ -357,21 +334,34 @@
     part_cotangent[...] = dot(mine, near_grad[...]).astype(BF16)
 
 
+def weights_kernel(normed, near_grad, merged, *refs):
+    weight_terms(1, normed, near_grad, merged, refs[:-1], refs[-1])
+
+
 def cores_kernel(over, swapped, total):
     total[...] = (over[...].astype(F32) + swapped[1].astype(F32)).astype(BF16)
 
 
-def regroup_kernel(*refs):
-    arrived, blocks = refs[:-1], refs[-1]
-    total = arrived[0][...].astype(F32)
-    for other in arrived[1:]:
-        total = total + other[...].astype(F32)
-    blocks[...] = total.astype(BF16)
-
-
-def finish_kernel(group, flip, first, second, grad_qkv, grad_out):
-    for half, arrived in enumerate((first, second)):
-        total = jnp.sum(arrived[...].astype(F32), axis=0)
+def regroup_kernel(lat_count, *refs):
+    arrived, blocks = refs[:-lat_count], refs[-lat_count:]
+    here = lax.axis_index("lat")
+    rows = blocks[0].shape[0]
+    for step, block in enumerate(blocks):
+        there = lax.rem(here + step, lat_count)
+        part = pl.ds(pl.multiple_of(there * rows, rows), rows)
+        total = arrived[0][part, :].astype(F32)
+        for other in arrived[1:]:
+            total = total + other[part, :].astype(F32)
+        block[...] = total.astype(block.dtype)
+
+
+def finish_kernel(group, flip, *refs):
+    arrived, (grad_qkv, grad_out) = refs[:-2], refs[-2:]
+    count = len(arrived) // 2
+    for half in range(2):
+        total = arrived[half * count][...]
+        for other in arrived[half * count + 1 : (half + 1) * count]:
+            total = total + other[...].astype(F32)
         grad_qkv[:, half * 3 * group : (half + 1) * 3 * group] = total[:, : 3 * group]
         out = total[:, 3 * group :]
         if flip:
@@ -460,21 +450,26 @@
         name="window_bias",
     )(table, bias_columns(), bias_rows(), pole_mask())
     lon_rows = width // lon_count
-    half_group = group // 2
-    row_scratch = pltpu.VMEM((width, 4 * half_group), BF16)
-    first = call(
-        functools.partial(first_kernel, lon_count),
-        [shaped(lon_rows, 4 * half_group)] * lon_count
-        + [shaped(CELLS, width)] * 3
-        + [shaped(CELLS, 3 * half_group), shaped(CELLS, half_group), shaped(CELLS, 4 * half_group)],
+    columns = 2 * group
+    row_scratch = pltpu.VMEM((width, columns), BF16)
+    *first, normed, near_grad, merged, stay, over, swap, part_tokens, part_cotangent = call(
+        layer_kernel,
+        [shaped(lon_rows, columns)] * lon_count
+        + [shaped(CELLS, width), shaped(CELLS, width), shaped(CELLS, 4 * group)]
+        + [shaped(2, PART, width)] * 2
+        + [shaped(2, 2, PART, width)]
+        + [shaped(PART, width)] * 2,
         [
             pltpu.VMEM((CELLS + RIM, width), BF16),
-            row_scratch,
+            pltpu.VMEM((CELLS, width), BF16),
             pltpu.VMEM((CELLS, 3 * group), BF16),
             pltpu.VMEM((CELLS, group), BF16),
+            pltpu.VMEM((QUARTERS * PART, 4 * group), BF16),
+            pltpu.VMEM((2, QUARTERS * PART, width), BF16),
+            row_scratch,
         ],
-        cost=cost(3 * CELLS * width * width, 8000000),
-        name="layer_first_heads",
+        cost=cost(6 * CELLS * width * width, 8000000),
+        name="window_layer",
     )(
         flat_tokens,
         flat_grad,
@@ -485,59 +480,31 @@
         w_out,
         bias,
         one_hot(shifted_source(), CELLS + RIM),
+        quarter_pick(),
     )
-    near_tokens, near_grad, normed, projected, d_attended, merged = first[lon_count:]
 
     def lon_exchange(grads):
         return [grads[0]] + [rotated(grads[step], "lon", step) for step in range(1, lon_count)]
 
-    def lat_exchange(arrived):
+    def lat_exchange(arrived, after):
         rows = lon_rows // lat_count
-        total = call(
-            regroup_kernel,
-            shaped(lon_rows, 4 * half_group),
-            cost=cost(4 * lon_rows * 4 * half_group, 6 * lon_rows * 4 * half_group),
+        blocks = call(
+            functools.partial(regroup_kernel, lat_count),
+            [shaped(rows, columns, dtype=F32)] + [shaped(rows, columns)] * (lat_count - 1),
+            cost=cost(4 * lon_rows * columns, 6 * lon_rows * columns),
             name="sum_over_lon",
+            after=after,
         )(*arrived)
-        moved_rows = lax.all_to_all(total, "lat", 0, 0, tiled=True)
-        return moved_rows.reshape(lat_count, rows, 4 * half_group)
-
-    from_lon_first = lon_exchange(first[:lon_count])
-    second = call(
-        functools.partial(second_kernel, lon_count),
-        [shaped(lon_rows, 4 * half_group)] * lon_count
-        + [shaped(2, PART, width)] * 2
-        + [shaped(2, 2, PART, width)]
-        + [shaped(PART, width)] * 2,
-        [
-            pltpu.VMEM((CELLS, 4 * half_group), BF16),
-            pltpu.VMEM((QUARTERS * PART, 4 * group), BF16),
-            pltpu.VMEM((2, QUARTERS * PART, width), BF16),
-            row_scratch,
-        ],
-        cost=cost(4 * CELLS * width * width, 8000000),
-        name="layer_second_heads",
-    )(
-        near_tokens,
-        near_grad,
-        normed,
-        projected,
-        d_attended,
-        merged,
-        w_qkv,
-        w_out,
-        bias,
-        quarter_pick(),
-    )
-    stay, over, swap, part_tokens, part_cotangent = second[lon_count:]
+        arrived = [rotated(blocks[step], "lat", step) for step in range(1, lat_count)]
+        return blocks[0], [blocks[0]] + arrived
+
     swapped = lax.ppermute(swap, "head", pairs)
-    from_lon_second = lon_exchange(second[:lon_count])
+    from_lon_first = lon_exchange(first)
     across = call(
         cores_kernel, shaped(2, PART, width), cost=cost(0, 8 * PART * width), name="sum_over_cores"
     )(over, swapped)
     chips = [(i, i ^ 2) for i in range(QUARTERS)]
     crossed = lax.ppermute(across, "head", chips)
-    from_lat_first = lat_exchange(from_lon_first)
     pieces = call(
         norm_kernel,
         [shaped(2, count, width) for count in (OUT_OWN, OUT_Z, OUT_X, OUT_D)],
@@ -545,16 +512,27 @@
         name="sum_over_heads",
     )(part_tokens, part_cotangent, gain, group_pick(), stay, swapped, crossed)
     home = [pieces[0], moved(pieces[1], 1, 0), moved(pieces[2], 0, 1), moved(pieces[3], 1, 1)]
+    second = call(
+        weights_kernel,
+        [shaped(lon_rows, columns)] * lon_count,
+        [row_scratch],
+        cost=cost(CELLS * width * width, 8000000),
+        name="second_weights",
+        after=(pieces[0],),
+    )(normed, near_grad, merged)
+    from_lon_second = lon_exchange(second)
+    done_first, from_lat_first = lat_exchange(from_lon_first, (second[0],))
     mine = call(
         join_kernel,
         shaped(2, PART, width),
         [pltpu.VMEM((2, OUT_ROWS, width), BF16)],
         cost=cost(2 * 2 * OUT_ROWS * PART * width, 8 * OUT_ROWS * width),
         name="join_home",
+        after=(done_first,),
     )(group_pick(), *home)
     far = lax.ppermute(mine, "head", chips)
     near = lax.ppermute(mine, "head", pairs)
-    from_lat_second = lat_exchange(from_lon_second)
+    done_second, from_lat_second = lat_exchange(from_lon_second, (mine,))
     beyond = lax.ppermute(far, "head", pairs)
     layer_out, grad_tokens = call(
         spread_kernel,
@@ -562,18 +540,20 @@
         [pltpu.VMEM((2, QUARTERS * PART, width), BF16)],
         cost=cost(2 * 2 * CELLS * CELLS * width, 8 * CELLS * width),
         name="spread_outputs",
+        after=(done_second,),
     )(own_pick(), mine, far, near, beyond)
     rows = lon_rows // lat_count
     flip = rows % 128 == 0
     grad_qkv, grad_out = call(
-        functools.partial(finish_kernel, half_group, flip),
+        functools.partial(finish_kernel, group // 2, flip),
         [
             shaped(rows, 3 * group, dtype=F32),
             shaped(*((group, rows) if flip else (rows, group)), dtype=F32),
         ],
         cost=cost(4 * rows * 4 * group, 16 * rows * 4 * group),
         name="sum_over_lat",
-    )(from_lat_first, from_lat_second)
+        after=(layer_out,),
+    )(*from_lat_first, *from_lat_second)
     return (
         layer_out.reshape(tokens.shape),
         grad_tokens.reshape(tokens.shape),

time: 97.6 us -> 87.5 us (0.90)
  waiting for transfers between devices: 43.2 us -> 38.6 us
  Pallas kernels: 20.8 us -> 17.3 us
  starting transfers between devices: 27.7 us -> 25.3 us
  local copies, waits for them, and re-layouts: 3.95 us -> 5.01 us
    all_to_all x2 -> x0, starting transfers between devices: 10 us -> none  [lat_exchange(): moved_rows = lax.all_to_all(total, 'lat', 0, 0, tiled=True)]
    ppermute x2 -> x8, starting transfers between devices: 1.88 us -> 10.2 us  [rotated(): lax.ppermute(value, axis, [(i, (i + step) % count) for i in range(count)])]
    pallas_call x11, Pallas kernels: 20.8 us -> 17.3 us  [run(): pl.pallas_call(body, out_shape=outs, in_specs=[pl.BlockSpec(memory_space=...]
    ppermute x6, waiting for transfers between devices: 12.6 us -> 9.38 us  [moved(): return lax.ppermute(value, ('lon', 'lat'), pairs)]
    all_to_all x2 -> x0, waiting for transfers between devices: 3 us -> none  [lat_exchange(): moved_rows = lax.all_to_all(total, 'lat', 0, 0, tiled=True)]
    ppermute x1, waiting for transfers between devices: 7.22 us -> 8.46 us  [body(): crossed = lax.ppermute(across, 'head', chips)]
    unnamed x34 -> x32, local copies, waits for them, and re-layouts: 3.94 us -> 5 us
    ppermute x2 -> x8, waiting for transfers between devices: 14.2 us -> 15 us  [rotated(): lax.ppermute(value, axis, [(i, (i + step) % count) for i in range(count)])]
  transfers between devices with their start and end apart: 16 -> 20, of which waited for: 10 -> 11; matrix products, arithmetic and copies ran while one was open for 0% -> 0% of each run, Pallas kernels for 6% -> 6%
where the time goes in v1:
time: 87.5 us; the launch traced here: 87.2 us
  waiting for transfers between devices  38.6 us (44%)
  starting transfers between devices  25.3 us (29%)
  Pallas kernels  17.3 us (20%)
  local copies, waits for them, and re-layouts  5.01 us (6%)
    pallas_call x11, Pallas kernels, run(): pl.pallas_call(body, out_shape=outs, in_specs=[pl.BlockSpec(memory_space=...  17.3 us
    ppermute x8, waiting for transfers between devices, rotated(): lax.ppermute(value, axis, [(i, (i + step) % count) for i in range(count)])  15 us
    ppermute x6, starting transfers between devices, moved(): return lax.ppermute(value, ('lon', 'lat'), pairs)  11.4 us
    ppermute x8, starting transfers between devices, rotated(): lax.ppermute(value, axis, [(i, (i + step) % count) for i in range(count)])  10.2 us
    ppermute x6, waiting for transfers between devices, moved(): return lax.ppermute(value, ('lon', 'lat'), pairs)  9.38 us
    ppermute x1, waiting for transfers between devices, body(): crossed = lax.ppermute(across, 'head', chips)  8.46 us
    ppermute x1, waiting for transfers between devices, body(): far = lax.ppermute(mine, 'head', chips)  5.29 us
    unnamed x32, local copies, waits for them, and re-layouts  5 us
  transfers between devices with their start and end apart: 20, of which 11 were waited for; matrix products, arithmetic and copies ran while one was open for 0% of the time, Pallas kernels for 6%

profile of v1, /device:TPU:0, one launch (start us, length us, event | category | flops | bytes accessed | tf_op | source)
XLA Modules:
  0.0 87.2 jit_solution(703689520850552967)
XLA Ops:
  0.7 1.1 %copy-done = bf16[2,6,24,1024]{3,2,1,0:T(8,128)(2,1)S(1)} copy-done((bf16[2,6,24,1024]{3,2,1,0:T(8,128)(2,1)S(1)}, bf16[2,6,24,1024]{3,2,1,0:T(8,128)(2,1)}, u32[]{:S(2)}) %copy-start) | copy-done | bytes 589848
  1.7 1.1 %copy-done.1 = bf16[2,6,24,1024]{3,2,1,0:T(8,128)(2,1)S(1)} copy-done((bf16[2,6,24,1024]{3,2,1,0:T(8,128)(2,1)S(1)}, bf16[2,6,24,1024]{3,2,1,0:T(8,128)(2,1)}, u32[]{:S(2)}) %copy-start.1) | copy-done | bytes 589848
  2.8 0.9 %copy-done.4 = bf16[208,288]{1,0:T(8,128)(2,1)S(1)} copy-done((bf16[208,288]{1,0:T(8,128)(2,1)S(1)}, bf16[208,288]{1,0:T(8,128)(2,1)}, u32[]{:S(2)}) %copy-start.4) | copy-done | bytes 119832
  4.1 5.1 %collective-permute-start = (bf16[112,1024]{1,0:T(8,128)(2,1)S(1)}, bf16[112,1024]{1,0:T(8,128)(2,1)S(1)}, u32[]{:S(2)}, u32[]{:S(2)}) collective-permute-start(bf16[112,1024]{1,0:T(8,128)(2,1)S(1)} %get-tuple-element.35), channel_id=1, source_target_pairs={{0,12},{4,0},{8,4},{12,8},{16,28},{20,16},{24,20},{28,24},{1,13},{... | collective-permute-start | bytes 688136 | tf_op jit(solution)/shard_map/ppermute | solution.py:423
  9.2 1.5 %collective-permute-start.1 = (bf16[48,1024]{1,0:T(8,128)(2,1)S(1)}, bf16[48,1024]{1,0:T(8,128)(2,1)S(1)}, u32[]{:S(2)}, u32[]{:S(2)}) collective-permute-start(bf16[48,1024]{1,0:T(8,128)(2,1)S(1)} %get-tuple-element.36), channel_id=1, source_target_pairs={{0,16},{4,20},{8,24},{12,28},{16,0},{20,4},{24,8},{28,12},{1,17},{... | collective-permute-start | bytes 294920 | tf_op jit(solution)/shard_map/ppermute | solution.py:423
  11.1 4.0 %collective-permute-done = bf16[112,1024]{1,0:T(8,128)(2,1)S(1)} collective-permute-done((bf16[112,1024]{1,0:T(8,128)(2,1)S(1)}, bf16[112,1024]{1,0:T(8,128)(2,1)S(1)}, u32[]{:S(2)}, u32[]{:S(2)}) %collective-permute-start) | collective-permute-done | bytes 229408 | tf_op jit(solution)/shard_map/ppermute | solution.py:423
  15.2 1.0 %collective-permute-done.2 = bf16[48,1024]{1,0:T(8,128)(2,1)S(1)} collective-permute-done((bf16[48,1024]{1,0:T(8,128)(2,1)S(1)}, bf16[48,1024]{1,0:T(8,128)(2,1)S(1)}, u32[]{:S(2)}, u32[]{:S(2)}) %collective-permute-start.2) | collective-permute-done | bytes 98336 | tf_op jit(solution)/shard_map/ppermute | solution.py:423
  16.4 1.7 %window_bias.1.refs_7_ = f32[4,144,144]{2,1,0:T(8,128)S(1)} custom-call(f32[4,1024]{1,0:T(4,128)S(1)} %pad.4.refs_0_, s32[1,144]{1,0:T(1,128)S(1)} %copy-done.12, bf16[144,576]{1,0:T(8,128)(2,1)S(1)} %copy-done.10, f32[144,144]{1,0:T(8,128)S(1)} %copy-done.11), custom_call_target="tpu_custom_call" | custom-call | flops 1019215872 | bytes 1000000 | tf_op jit(solution)/shard_map/window_bias/pallas_call | solution.py:177
  18.1 0.8 copy-done.13
  18.9 10.6 %window_layer.1 = (bf16[512,512]{1,0:T(8,128)(2,1)S(1)}, bf16[512,512]{1,0:T(8,128)(2,1)S(1)}, bf16[288,1024]{1,0:T(8,128)(2,1)S(1)}, bf16[288,1024]{1,0:T(8,128...) custom-call(bf16[288,1024]{1,0:T(8,128)(2,1)} %bitcast.6, ...), custom_call_target="tpu_custom_call" | custom-call | flops 1811939328 | bytes 8000000 | tf_op jit(solution)/shard_map/window_layer/pallas_call | solution.py:177
  30.0 1.4 %collective-permute-start.9 = (bf16[512,512]{1,0:T(8,128)(2,1)S(1)}, bf16[512,512]{1,0:T(8,128)(2,1)S(1)}, u32[]{:S(2)}, u32[]{:S(2)}) collective-permute-start(bf16[512,512]{1,0:T(8,128)(2,1)S(1)} %get-tuple-element.48), channel_id=1, source_target_pairs={{0,16},{16,0},{1,17},{17,1},{2,18},{18,2},{3,19},{19,3},{4,20},{20... | collective-permute-start | bytes 1572872 | tf_op jit(solution)/shard_map/ppermute | solution.py:413
  31.4 0.5 collective-permute-done.4.refs_1_.refs_5_
  32.0 1.6 %collective-permute-start.5 = (bf16[2,80,1024]{2,1,0:T(8,128)(2,1)S(1)}, bf16[2,80,1024]{2,1,0:T(8,128)(2,1)S(1)}, u32[]{:S(2)}, u32[]{:S(2)}) collective-permute-start(bf16[2,80,1024]{2,1,0:T(8,128)(2,1)S(1)} %sum_over_cores.1), channel_id=1, source_target_pairs={{0,2},{1,3},{2,0},{3,1},{4,6},{5,7},{6,4},{7,5},{8,10},{9,11},{10,... | collective-permute-start | bytes 983048 | tf_op jit(solution)/shard_map/ppermute | solution.py:507
  33.6 8.5 %collective-permute-done.5.refs_6_ = bf16[2,80,1024]{2,1,0:T(8,128)(2,1)S(1)} collective-permute-done((bf16[2,80,1024]{2,1,0:T(8,128)(2,1)S(1)}, bf16[2,80,1024]{2,1,0:T(8,128)(2,1)S(1)}, u32[]{:S(2)}, u32[]{:S(2)}) %collective-permute-start.5) | collective-permute-done | bytes 327712 | tf_op jit(solution)/shard_map/ppermute | solution.py:507
  42.1 0.6 sum_over_heads.1
  42.6 1.4 %collective-permute-start.6 = (bf16[2,32,1024]{2,1,0:T(8,128)(2,1)S(1)}, bf16[2,32,1024]{2,1,0:T(8,128)(2,1)S(1)}, u32[]{:S(2)}, u32[]{:S(2)}) collective-permute-start(bf16[2,32,1024]{2,1,0:T(8,128)(2,1)S(1)} %get-tuple-element.44), channel_id=1, source_target_pairs={{0,4},{4,8},{8,12},{12,0},{16,20},{20,24},{24,28},{28,16},{1,5},{5... | collective-permute-start | bytes 393224 | tf_op jit(solution)/shard_map/ppermute | solution.py:423
  44.6 2.5 %collective-permute-start.8 = (bf16[2,16,1024]{2,1,0:T(8,128)(2,1)S(1)}, bf16[2,16,1024]{2,1,0:T(8,128)(2,1)S(1)}, u32[]{:S(2)}, u32[]{:S(2)}) collective-permute-start(bf16[2,16,1024]{2,1,0:T(8,128)(2,1)S(1)} %get-tuple-element.46), channel_id=1, source_target_pairs={{0,20},{4,24},{8,28},{12,16},{16,4},{20,8},{24,12},{28,0},{1,21},{... | collective-permute-start | bytes 196616 | tf_op jit(solution)/shard_map/ppermute | solution.py:423
  47.1 0.9 %second_weights.1 = (bf16[512,512]{1,0:T(8,128)(2,1)S(1)}, bf16[512,512]{1,0:T(8,128)(2,1)S(1)}) custom-call(bf16[288,1024]{1,0:T(8,128)(2,1)S(1)} %get-tuple-element.49.refs_0_, bf16[288,1024]{1,0:T(8,128)(2,1)S(1)} %get-tuple-element.50.refs_1_, bf16[288,1024]{1,0:T(8,128)(2,1)S(1)} %get-tuple-element.51.refs_2_, ...), custom_call_target="tpu_custom_call" | custom-call | flops 301989888 | bytes 8000000 | tf_op jit(solution)/shard_map/second_weights/pallas_call | solution.py:177
  48.3 4.2 %collective-permute-done.8.refs_4_ = bf16[2,16,1024]{2,1,0:T(8,128)(2,1)S(1)} collective-permute-done((bf16[2,16,1024]{2,1,0:T(8,128)(2,1)S(1)}, bf16[2,16,1024]{2,1,0:T(8,128)(2,1)S(1)}, u32[]{:S(2)}, u32[]{:S(2)}) %collective-permute-start.8) | collective-permute-done | bytes 65568 | tf_op jit(solution)/shard_map/ppermute | solution.py:423
  52.8 1.6 %collective-permute-start.10 = (bf16[2,80,1024]{2,1,0:T(8,128)(2,1)S(1)}, bf16[2,80,1024]{2,1,0:T(8,128)(2,1)S(1)}, u32[]{:S(2)}, u32[]{:S(2)}) collective-permute-start(bf16[2,80,1024]{2,1,0:T(8,128)(2,1)S(1)} %join_home.1.refs_2_.refs_1_), channel_id=1, source_target_pairs={{0,2},{1,3},{2,0},{3,1},{4,6},{5,7},{6,4},{7,5},{8,10},{9,11},{10,... | collective-permute-start | bytes 983048 | tf_op jit(solution)/shard_map/ppermute | solution.py:533
  54.3 1.5 %collective-permute-start.13 = (bf16[512,512]{1,0:T(8,128)(2,1)S(1)}, bf16[512,512]{1,0:T(8,128)(2,1)S(1)}, u32[]{:S(2)}, u32[]{:S(2)}) collective-permute-start(bf16[512,512]{1,0:T(8,128)(2,1)S(1)} %get-tuple-element.54), channel_id=1, source_target_pairs={{0,16},{16,0},{1,17},{17,1},{2,18},{18,2},{3,19},{19,3},{4,20},{20... | collective-permute-start | bytes 1572872 | tf_op jit(solution)/shard_map/ppermute | solution.py:413
  55.8 5.3 %collective-permute-done.10.refs_2_ = bf16[2,80,1024]{2,1,0:T(8,128)(2,1)S(1)} collective-permute-done((bf16[2,80,1024]{2,1,0:T(8,128)(2,1)S(1)}, bf16[2,80,1024]{2,1,0:T(8,128)(2,1)S(1)}, u32[]{:S(2)}, u32[]{:S(2)}) %collective-permute-start.10) | collective-permute-done | bytes 327712 | tf_op jit(solution)/shard_map/ppermute | solution.py:533
  61.1 2.0 %collective-permute-start.15 = (bf16[128,512]{1,0:T(8,128)(2,1)S(1)}, bf16[128,512]{1,0:T(8,128)(2,1)S(1)}, u32[]{:S(2)}, u32[]{:S(2)}) collective-permute-start(bf16[128,512]{1,0:T(8,128)(2,1)S(1)} %get-tuple-element.59), channel_id=1, source_target_pairs={{0,8},{4,12},{8,0},{12,4},{1,9},{5,13},{9,1},{13,5},{2,10},{6,14},... | collective-permute-start | bytes 393224 | tf_op jit(solution)/shard_map/ppermute | solution.py:413
  63.1 3.5 %collective-permute-done.13.refs_1_ = bf16[512,512]{1,0:T(8,128)(2,1)S(1)} collective-permute-done((bf16[512,512]{1,0:T(8,128)(2,1)S(1)}, bf16[512,512]{1,0:T(8,128)(2,1)S(1)}, u32[]{:S(2)}, u32[]{:S(2)}) %collective-permute-start.13) | collective-permute-done | bytes 524320 | tf_op jit(solution)/shard_map/ppermute | solution.py:413
  66.6 1.4 %collective-permute-start.16 = (bf16[128,512]{1,0:T(8,128)(2,1)S(1)}, bf16[128,512]{1,0:T(8,128)(2,1)S(1)}, u32[]{:S(2)}, u32[]{:S(2)}) collective-permute-start(bf16[128,512]{1,0:T(8,128)(2,1)S(1)} %get-tuple-element.60), channel_id=1, source_target_pairs={{0,12},{4,0},{8,4},{12,8},{1,13},{5,1},{9,5},{13,9},{2,14},{6,2},{... | collective-permute-start | bytes 393224 | tf_op jit(solution)/shard_map/ppermute | solution.py:413
  68.1 1.3 %collective-permute-done.14.refs_1_ = bf16[128,512]{1,0:T(8,128)(2,1)S(1)} collective-permute-done((bf16[128,512]{1,0:T(8,128)(2,1)S(1)}, bf16[128,512]{1,0:T(8,128)(2,1)S(1)}, u32[]{:S(2)}, u32[]{:S(2)}) %collective-permute-start.14) | collective-permute-done | bytes 131104 | tf_op jit(solution)/shard_map/ppermute | solution.py:413
  69.6 3.6 %collective-permute-start.19 = (bf16[128,512]{1,0:T(8,128)(2,1)S(1)}, bf16[128,512]{1,0:T(8,128)(2,1)S(1)}, u32[]{:S(2)}, u32[]{:S(2)}) collective-permute-start(bf16[128,512]{1,0:T(8,128)(2,1)S(1)} %get-tuple-element.63), channel_id=1, source_target_pairs={{0,12},{4,0},{8,4},{12,8},{1,13},{5,1},{9,5},{13,9},{2,14},{6,2},{... | collective-permute-start | bytes 393224 | tf_op jit(solution)/shard_map/ppermute | solution.py:413
  73.2 1.7 %spread_outputs.1 = (bf16[288,1024]{1,0:T(8,128)(2,1)}, bf16[288,1024]{1,0:T(8,128)(2,1)}) custom-call(bf16[288,320]{1,0:T(8,128)(2,1)S(1)} %copy-done.3, bf16[2,80,1024]{2,1,0:T(8,128)(2,1)S(1)} %join_home.1.refs_2_.refs_1_, bf16[2,80,1024]{2,1,0:T(8,128)(2,1)S(1)} %collective-permute-done.10.refs_2_, ...), custom_call_target="tpu_custom_call" | custom-call | flops 339738624 | bytes 2359296 | tf_op jit(solution)/shard_map/spread_outputs/pallas_call | solution.py:177
  75.0 2.9 %collective-permute-done.17.refs_5_ = bf16[128,512]{1,0:T(8,128)(2,1)S(1)} collective-permute-done((bf16[128,512]{1,0:T(8,128)(2,1)S(1)}, bf16[128,512]{1,0:T(8,128)(2,1)S(1)}, u32[]{:S(2)}, u32[]{:S(2)}) %collective-permute-start.17) | collective-permute-done | bytes 131104 | tf_op jit(solution)/shard_map/ppermute | solution.py:413
  77.8 7.4 %collective-permute-done.18.refs_6_ = bf16[128,512]{1,0:T(8,128)(2,1)S(1)} collective-permute-done((bf16[128,512]{1,0:T(8,128)(2,1)S(1)}, bf16[128,512]{1,0:T(8,128)(2,1)S(1)}, u32[]{:S(2)}, u32[]{:S(2)}) %collective-permute-start.18) | collective-permute-done | bytes 131104 | tf_op jit(solution)/shard_map/ppermute | solution.py:413
  85.2 1.1 %copy-done.2 = bf16[288,1024]{1,0:T(8,128)(2,1)S(1)} copy-done((bf16[288,1024]{1,0:T(8,128)(2,1)S(1)}, bf16[288,1024]{1,0:T(8,128)(2,1)}, u32[]{:S(2)}) %copy-start.2) | copy-done | bytes 589848
  86.3 0.9 %sum_over_lat.1 = (f32[128,768]{1,0:T(8,128)}, f32[256,128]{1,0:T(8,128)}) custom-call(f32[128,512]{1,0:T(8,128)S(1)} %get-tuple-element.53.refs_5_.refs_0_, bf16[128,512]{1,0:T(8,128)(2,1)S(1)} %collective-permute-done.14.refs_1_, bf16[128,512]{1,0:T(8,128)(2,1)S(1)} %collective-permute-done.15.refs_2_, ...), custom_call_target="tpu_custom_call" | custom-call | flops 524288 | bytes 2097152 | tf_op jit(solution)/shard_map/sum_over_lat/pallas_call | solution.py:177
  (53 shorter events, 3.1 us)
Async XLA Ops:
  0.6 15.7 %copy-start.12 = (s32[1,144]{1,0:T(1,128)S(1)}, s32[1,144]{1,0:T(1,128)}, u32[]{:S(2)}) copy-start(s32[1,144]{1,0:T(1,128)} %constant.20.clone.refs_1_) | copy-start | bytes 1732
  0.6 1.1 %copy-start = (bf16[2,6,24,1024]{3,2,1,0:T(8,128)(2,1)S(1)}, bf16[2,6,24,1024]{3,2,1,0:T(8,128)(2,1)}, u32[]{:S(2)}) copy-start(bf16[2,6,24,1024]{3,2,1,0:T(8,128)(2,1)} %param.15) | copy-start | bytes 1769476
  3.7 12.6 %copy-start.14 = (f32[759,4]{0,1:T(4,128)S(1)}, f32[759,4]{0,1:T(4,128)}, u32[]{:S(2)}) copy-start(f32[759,4]{0,1:T(4,128)} %param.19) | copy-start | bytes 36436
  3.7 12.6 %copy-start.10 = (bf16[144,576]{1,0:T(8,128)(2,1)S(1)}, bf16[144,576]{1,0:T(8,128)(2,1)}, u32[]{:S(2)}) copy-start(bf16[144,576]{1,0:T(8,128)(2,1)} %constant.21.clone.refs_2_) | copy-start | bytes 497668
  3.7 12.6 %copy-start.11 = (f32[144,144]{1,0:T(8,128)S(1)}, f32[144,144]{1,0:T(8,128)}, u32[]{:S(2)}) copy-start(f32[144,144]{1,0:T(8,128)} %constant.22.clone.refs_3_) | copy-start | bytes 248836
  4.1 11.0 %collective-permute-start = (bf16[112,1024]{1,0:T(8,128)(2,1)S(1)}, bf16[112,1024]{1,0:T(8,128)(2,1)S(1)}, u32[]{:S(2)}, u32[]{:S(2)}) collective-permute-start(bf16[112,1024]{1,0:T(8,128)(2,1)S(1)} %get-tuple-element.35), channel_id=1, source_target_pairs={{0,12},{4,0},{8,4},{12,8},{16,28},{20,16},{24,20},{28,24},{1,13},{... | collective-permute-start | bytes 688136 | tf_op jit(solution)/shard_map/ppermute | solution.py:423
  9.2 5.9 %collective-permute-start.1 = (bf16[48,1024]{1,0:T(8,128)(2,1)S(1)}, bf16[48,1024]{1,0:T(8,128)(2,1)S(1)}, u32[]{:S(2)}, u32[]{:S(2)}) collective-permute-start(bf16[48,1024]{1,0:T(8,128)(2,1)S(1)} %get-tuple-element.36), channel_id=1, source_target_pairs={{0,16},{4,20},{8,24},{12,28},{16,0},{20,4},{24,8},{28,12},{1,17},{... | collective-permute-start | bytes 294920 | tf_op jit(solution)/shard_map/ppermute | solution.py:423
  10.7 5.5 %collective-permute-start.2 = (bf16[48,1024]{1,0:T(8,128)(2,1)S(1)}, bf16[48,1024]{1,0:T(8,128)(2,1)S(1)}, u32[]{:S(2)}, u32[]{:S(2)}) collective-permute-start(bf16[48,1024]{1,0:T(8,128)(2,1)S(1)} %get-tuple-element.37), channel_id=1, source_target_pairs={{0,28},{4,16},{8,20},{12,24},{16,12},{20,0},{24,4},{28,8},{1,29},{... | collective-permute-start | bytes 294920 | tf_op jit(solution)/shard_map/ppermute | solution.py:423
  16.2 2.7 %collective-permute-start.3 = (bf16[208,1024]{1,0:T(8,128)(2,1)S(1)}, bf16[208,1024]{1,0:T(8,128)(2,1)S(1)}, u32[]{:S(2)}, u32[]{:S(2)}) collective-permute-start(bf16[208,1024]{1,0:T(8,128)(2,1)S(1)} %constant_dynamic-update-slice_fusion.refs_2_), channel_id=1, source_target_pairs={{0,1},{1,0},{2,3},{3,2},{4,5},{5,4},{6,7},{7,6},{8,9},{9,8},{10,11... | collective-permute-start | bytes 1277960 | tf_op jit(solution)/shard_map/ppermute | solution.py:443
  16.3 2.5 %copy-start.6 = (f32[1024]{0:T(1024)S(1)}, f32[1024]{0:T(1024)}, u32[]{:S(2)}) copy-start(f32[1024]{0:T(1024)} %param.16) | copy-start | bytes 12292
  16.4 2.5 %copy-start.7 = (bf16[256,1024]{1,0:T(8,128)(2,1)S(1)}, bf16[256,1024]{1,0:T(8,128)(2,1)}, u32[]{:S(2)}) copy-start(bf16[256,1024]{1,0:T(8,128)(2,1)} %refs_6_.1) | copy-start | bytes 1572868
  16.4 2.5 %copy-start.8 = (bf16[288,496]{1,0:T(8,128)(2,1)S(1)}, bf16[288,496]{1,0:T(8,128)(2,1)}, u32[]{:S(2)}) copy-start(bf16[288,496]{1,0:T(8,128)(2,1)} %constant.23.clone.refs_8_) | copy-start | bytes 857092
  16.4 2.5 %copy-start.9 = (bf16[320,288]{1,0:T(8,128)(2,1)S(1)}, bf16[320,288]{1,0:T(8,128)(2,1)}, u32[]{:S(2)}) copy-start(bf16[320,288]{1,0:T(8,128)(2,1)} %constant.24.clone.refs_9_) | copy-start | bytes 552964
  18.9 23.2 %copy-start.5 = (bf16[96,80]{1,0:T(8,128)(2,1)S(1)}, bf16[96,80]{1,0:T(8,128)(2,1)}, u32[]{:S(2)}) copy-start(bf16[96,80]{1,0:T(8,128)(2,1)} %constant.25.clone.refs_3_.refs_0_) | copy-start | bytes 46084
  29.5 2.4 %collective-permute-start.4 = (bf16[2,2,80,1024]{3,2,1,0:T(8,128)(2,1)}, bf16[2,2,80,1024]{3,2,1,0:T(8,128)(2,1)S(1)}, u32[]{:S(2)}, u32[]{:S(2)}) collective-permute-start(bf16[2,2,80,1024]{3,2,1,0:T(8,128)(2,1)} %get-tuple-element.41), channel_id=1, source_target_pairs={{0,1},{1,0},{2,3},{3,2},{4,5},{5,4},{6,7},{7,6},{8,9},{9,8},{10,11... | collective-permute-start | bytes 1966088 | tf_op jit(solution)/shard_map/ppermute | solution.py:501
  30.0 18.0 %collective-permute-start.9 = (bf16[512,512]{1,0:T(8,128)(2,1)S(1)}, bf16[512,512]{1,0:T(8,128)(2,1)S(1)}, u32[]{:S(2)}, u32[]{:S(2)}) collective-permute-start(bf16[512,512]{1,0:T(8,128)(2,1)S(1)} %get-tuple-element.48), channel_id=1, source_target_pairs={{0,16},{16,0},{1,17},{17,1},{2,18},{18,2},{3,19},{19,3},{4,20},{20... | collective-permute-start | bytes 1572872 | tf_op jit(solution)/shard_map/ppermute | solution.py:413
  32.0 10.1 %collective-permute-start.5 = (bf16[2,80,1024]{2,1,0:T(8,128)(2,1)S(1)}, bf16[2,80,1024]{2,1,0:T(8,128)(2,1)S(1)}, u32[]{:S(2)}, u32[]{:S(2)}) collective-permute-start(bf16[2,80,1024]{2,1,0:T(8,128)(2,1)S(1)} %sum_over_cores.1), channel_id=1, source_target_pairs={{0,2},{1,3},{2,0},{3,1},{4,6},{5,7},{6,4},{7,5},{8,10},{9,11},{10,... | collective-permute-start | bytes 983048 | tf_op jit(solution)/shard_map/ppermute | solution.py:507
  42.6 9.8 %collective-permute-start.6 = (bf16[2,32,1024]{2,1,0:T(8,128)(2,1)S(1)}, bf16[2,32,1024]{2,1,0:T(8,128)(2,1)S(1)}, u32[]{:S(2)}, u32[]{:S(2)}) collective-permute-start(bf16[2,32,1024]{2,1,0:T(8,128)(2,1)S(1)} %get-tuple-element.44), channel_id=1, source_target_pairs={{0,4},{4,8},{8,12},{12,0},{16,20},{20,24},{24,28},{28,16},{1,5},{5... | collective-permute-start | bytes 393224 | tf_op jit(solution)/shard_map/ppermute | solution.py:423
  44.0 4.3 %collective-permute-start.7 = (bf16[2,16,1024]{2,1,0:T(8,128)(2,1)S(1)}, bf16[2,16,1024]{2,1,0:T(8,128)(2,1)S(1)}, u32[]{:S(2)}, u32[]{:S(2)}) collective-permute-start(bf16[2,16,1024]{2,1,0:T(8,128)(2,1)S(1)} %get-tuple-element.45), channel_id=1, source_target_pairs={{0,16},{4,20},{8,24},{12,28},{16,0},{20,4},{24,8},{28,12},{1,17},{... | collective-permute-start | bytes 196616 | tf_op jit(solution)/shard_map/ppermute | solution.py:423
  44.6 7.9 %collective-permute-start.8 = (bf16[2,16,1024]{2,1,0:T(8,128)(2,1)S(1)}, bf16[2,16,1024]{2,1,0:T(8,128)(2,1)S(1)}, u32[]{:S(2)}, u32[]{:S(2)}) collective-permute-start(bf16[2,16,1024]{2,1,0:T(8,128)(2,1)S(1)} %get-tuple-element.46), channel_id=1, source_target_pairs={{0,20},{4,24},{8,28},{12,16},{16,4},{20,8},{24,12},{28,0},{1,21},{... | collective-permute-start | bytes 196616 | tf_op jit(solution)/shard_map/ppermute | solution.py:423
  48.1 25.1 %copy-start.3 = (bf16[288,320]{1,0:T(8,128)(2,1)S(1)}, bf16[288,320]{1,0:T(8,128)(2,1)}, u32[]{:S(2)}) copy-start(bf16[288,320]{1,0:T(8,128)(2,1)} %constant.26.clone.refs_0_) | copy-start | bytes 552964
  52.8 8.3 %collective-permute-start.10 = (bf16[2,80,1024]{2,1,0:T(8,128)(2,1)S(1)}, bf16[2,80,1024]{2,1,0:T(8,128)(2,1)S(1)}, u32[]{:S(2)}, u32[]{:S(2)}) collective-permute-start(bf16[2,80,1024]{2,1,0:T(8,128)(2,1)S(1)} %join_home.1.refs_2_.refs_1_), channel_id=1, source_target_pairs={{0,2},{1,3},{2,0},{3,1},{4,6},{5,7},{6,4},{7,5},{8,10},{9,11},{10,... | collective-permute-start | bytes 983048 | tf_op jit(solution)/shard_map/ppermute | solution.py:533
  54.3 12.2 %collective-permute-start.13 = (bf16[512,512]{1,0:T(8,128)(2,1)S(1)}, bf16[512,512]{1,0:T(8,128)(2,1)S(1)}, u32[]{:S(2)}, u32[]{:S(2)}) collective-permute-start(bf16[512,512]{1,0:T(8,128)(2,1)S(1)} %get-tuple-element.54), channel_id=1, source_target_pairs={{0,16},{16,0},{1,17},{17,1},{2,18},{18,2},{3,19},{19,3},{4,20},{20... | collective-permute-start | bytes 1572872 | tf_op jit(solution)/shard_map/ppermute | solution.py:413
  55.8 13.5 %collective-permute-start.11 = (bf16[2,80,1024]{2,1,0:T(8,128)(2,1)S(1)}, bf16[2,80,1024]{2,1,0:T(8,128)(2,1)S(1)}, u32[]{:S(2)}, u32[]{:S(2)}) collective-permute-start(bf16[2,80,1024]{2,1,0:T(8,128)(2,1)S(1)} %join_home.1.refs_2_.refs_1_), channel_id=1, source_target_pairs={{0,1},{1,0},{2,3},{3,2},{4,5},{5,4},{6,7},{7,6},{8,9},{9,8},{10,11... | collective-permute-start | bytes 983048 | tf_op jit(solution)/shard_map/ppermute | solution.py:534
  61.1 8.5 %collective-permute-start.12 = (bf16[2,80,1024]{2,1,0:T(8,128)(2,1)S(1)}, bf16[2,80,1024]{2,1,0:T(8,128)(2,1)S(1)}, u32[]{:S(2)}, u32[]{:S(2)}) collective-permute-start(bf16[2,80,1024]{2,1,0:T(8,128)(2,1)S(1)} %collective-permute-done.10.refs_2_), channel_id=1, source_target_pairs={{0,1},{1,0},{2,3},{3,2},{4,5},{5,4},{6,7},{7,6},{8,9},{9,8},{10,11... | collective-permute-start | bytes 983048 | tf_op jit(solution)/shard_map/ppermute | solution.py:536
  61.1 8.2 %collective-permute-start.14 = (bf16[128,512]{1,0:T(8,128)(2,1)S(1)}, bf16[128,512]{1,0:T(8,128)(2,1)S(1)}, u32[]{:S(2)}, u32[]{:S(2)}) collective-permute-start(bf16[128,512]{1,0:T(8,128)(2,1)S(1)} %get-tuple-element.58), channel_id=1, source_target_pairs={{0,4},{4,8},{8,12},{12,0},{1,5},{5,9},{9,13},{13,1},{2,6},{6,10},{... | collective-permute-start | bytes 393224 | tf_op jit(solution)/shard_map/ppermute | solution.py:413
  61.1 13.8 %collective-permute-start.15 = (bf16[128,512]{1,0:T(8,128)(2,1)S(1)}, bf16[128,512]{1,0:T(8,128)(2,1)S(1)}, u32[]{:S(2)}, u32[]{:S(2)}) collective-permute-start(bf16[128,512]{1,0:T(8,128)(2,1)S(1)} %get-tuple-element.59), channel_id=1, source_target_pairs={{0,8},{4,12},{8,0},{12,4},{1,9},{5,13},{9,1},{13,5},{2,10},{6,14},... | collective-permute-start | bytes 393224 | tf_op jit(solution)/shard_map/ppermute | solution.py:413
  66.6 8.4 %collective-permute-start.16 = (bf16[128,512]{1,0:T(8,128)(2,1)S(1)}, bf16[128,512]{1,0:T(8,128)(2,1)S(1)}, u32[]{:S(2)}, u32[]{:S(2)}) collective-permute-start(bf16[128,512]{1,0:T(8,128)(2,1)S(1)} %get-tuple-element.60), channel_id=1, source_target_pairs={{0,12},{4,0},{8,4},{12,8},{1,13},{5,1},{9,5},{13,9},{2,14},{6,2},{... | collective-permute-start | bytes 393224 | tf_op jit(solution)/shard_map/ppermute | solution.py:413
  69.4 8.5 %collective-permute-start.17 = (bf16[128,512]{1,0:T(8,128)(2,1)S(1)}, bf16[128,512]{1,0:T(8,128)(2,1)S(1)}, u32[]{:S(2)}, u32[]{:S(2)}) collective-permute-start(bf16[128,512]{1,0:T(8,128)(2,1)S(1)} %get-tuple-element.61), channel_id=1, source_target_pairs={{0,4},{4,8},{8,12},{12,0},{1,5},{5,9},{9,13},{13,1},{2,6},{6,10},{... | collective-permute-start | bytes 393224 | tf_op jit(solution)/shard_map/ppermute | solution.py:413
  69.4 15.8 %collective-permute-start.18 = (bf16[128,512]{1,0:T(8,128)(2,1)S(1)}, bf16[128,512]{1,0:T(8,128)(2,1)S(1)}, u32[]{:S(2)}, u32[]{:S(2)}) collective-permute-start(bf16[128,512]{1,0:T(8,128)(2,1)S(1)} %get-tuple-element.62), channel_id=1, source_target_pairs={{0,8},{4,12},{8,0},{12,4},{1,9},{5,13},{9,1},{13,5},{2,10},{6,14},... | collective-permute-start | bytes 393224 | tf_op jit(solution)/shard_map/ppermute | solution.py:413
  69.6 15.6 %collective-permute-start.19 = (bf16[128,512]{1,0:T(8,128)(2,1)S(1)}, bf16[128,512]{1,0:T(8,128)(2,1)S(1)}, u32[]{:S(2)}, u32[]{:S(2)}) collective-permute-start(bf16[128,512]{1,0:T(8,128)(2,1)S(1)} %get-tuple-element.63), channel_id=1, source_target_pairs={{0,12},{4,0},{8,4},{12,8},{1,13},{5,1},{9,5},{13,9},{2,14},{6,2},{... | collective-permute-start | bytes 393224 | tf_op jit(solution)/shard_map/ppermute | solution.py:413
  85.2 1.1 %copy-start.2 = (bf16[288,1024]{1,0:T(8,128)(2,1)S(1)}, bf16[288,1024]{1,0:T(8,128)(2,1)}, u32[]{:S(2)}) copy-start(bf16[288,1024]{1,0:T(8,128)(2,1)} %get-tuple-element.56.refs_8_) | copy-start | bytes 1769476
  (3 other events, 2.8 us)

commit v2 on v1

--- a/solution.py
+++ b/solution.py
@@ -265,23 +265,19 @@
     ).astype(BF16)
 
 
-def weight_terms(half, normed, near_grad, merged, grads, whole):
-    here = lax.axis_index("lon")
-    rows = grads[0].shape[0]
+def weight_terms(half, normed, near_grad, merged, whole):
     group = merged.shape[1] // 8
     attended = slice(half * group, (half + 1) * group)
     d_qkv = slice((2 + 3 * half) * group, (5 + 3 * half) * group)
-    if rows % 128:
-        whole[:, : 3 * group] = dot_columns(normed[...], merged[:, d_qkv]).astype(BF16)
-        whole[:, 3 * group :] = dot_columns(near_grad[...], merged[:, attended]).astype(BF16)
-    for step, grad in enumerate(grads):
-        there = lax.rem(here + step, len(grads))
-        part = pl.ds(pl.multiple_of(there * rows, rows), rows)
-        if rows % 128:
-            grad[...] = whole[part, :]
-            continue
-        grad[:, : 3 * group] = dot_columns(normed[:, part], merged[:, d_qkv]).astype(BF16)
-        grad[:, 3 * group :] = dot_columns(near_grad[:, part], merged[:, attended]).astype(BF16)
+    whole[:, : 3 * group] = dot_columns(normed[...], merged[:, d_qkv]).astype(BF16)
+    whole[:, 3 * group :] = dot_columns(near_grad[...], merged[:, attended]).astype(BF16)
+
+
+def lat_rows(whole, out, lon_count, parity):
+    rows = whole.shape[0] // (4 * lon_count)
+    for block in range(2 * lon_count):
+        start = pl.multiple_of((2 * block + parity) * rows, rows)
+        out[block * rows : (block + 1) * rows, :] = whole[pl.ds(start, rows), :]
 
 
 def layer_kernel(
@@ -297,8 +293,9 @@
     quarter,
     *refs,
 ):
-    *grads, normed, near_grad, merged, stay, over, swap, part_tokens, part_cotangent = refs[:-7]
-    source, near_tokens, projected, d_attended, ordered, terms, whole = refs[-7:]
+    *by_lon, lat_keep, lat_send, stay, over, swap, part_tokens, part_cotangent = refs[:-10]
+    source, near_tokens, near_grad, normed, projected, d_attended, merged = refs[-10:-3]
+    ordered, terms, whole = refs[-3:]
     head_index = lax.axis_index("head")
     core = lax.rem(head_index, 2)
     heads = bias.shape[0]
@@ -316,7 +313,16 @@
     for window in range(WINDOWS):
         for head in range(heads):
             attend(window, head, projected, d_attended, bias, merged, group)
-    weight_terms(0, normed, near_grad, merged, grads, whole)
+    weight_terms(0, normed, near_grad, merged, whole)
+    lon, lon_count = lax.axis_index("lon"), len(by_lon)
+    rows = by_lon[0].shape[0]
+    for step, block in enumerate(by_lon):
+        start = pl.multiple_of(lax.rem(lon + step, lon_count) * rows, rows)
+        block[...] = whole[pl.ds(start, rows), :]
+    weight_terms(1, normed, near_grad, merged, whole)
+    parity = lax.rem(lax.axis_index("lat"), 2)
+    lat_rows(whole, lat_keep, lon_count, parity)
+    lat_rows(whole, lat_send, lon_count, 1 - parity)
     ordered[...] = dot(quarter[...], merged[...]).astype(BF16)
     terms[0] = dot(ordered[:, :group], w_out[...]).astype(BF16)
     terms[1] = dot_rows(ordered[:, group:], w_qkv[...]).astype(BF16)
@@ -334,34 +340,46 @@
     part_cotangent[...] = dot(mine, near_grad[...]).astype(BF16)
 
 
-def weights_kernel(normed, near_grad, merged, *refs):
-    weight_terms(1, normed, near_grad, merged, refs[:-1], refs[-1])
-
-
 def cores_kernel(over, swapped, total):
     total[...] = (over[...].astype(F32) + swapped[1].astype(F32)).astype(BF16)
 
 
-def regroup_kernel(lat_count, *refs):
-    arrived, blocks = refs[:-lat_count], refs[-lat_count:]
-    here = lax.axis_index("lat")
-    rows = blocks[0].shape[0]
-    for step, block in enumerate(blocks):
-        there = lax.rem(here + step, lat_count)
-        part = pl.ds(pl.multiple_of(there * rows, rows), rows)
-        total = arrived[0][part, :].astype(F32)
-        for other in arrived[1:]:
-            total = total + other[part, :].astype(F32)
-        block[...] = total.astype(block.dtype)
-
-
-def finish_kernel(group, flip, *refs):
-    arrived, (grad_qkv, grad_out) = refs[:-2], refs[-2:]
-    count = len(arrived) // 2
+def total_of(parts):
+    total = parts[0].astype(F32)
+    for part in parts[1:]:
+        total = total + part.astype(F32)
+    return total
+
+
+def second_step_kernel(lon_count, *refs):
+    from_lon, (lat_keep, from_lat) = refs[:lon_count], refs[lon_count : lon_count + 2]
+    keep_first, send_first, *by_lon = refs[lon_count + 2 :]
+    rows = keep_first.shape[0] // 2
+    lon, parity = lax.axis_index("lon"), lax.rem(lax.axis_index("lat"), 2)
+    for out, wanted in ((keep_first, parity), (send_first, 1 - parity)):
+        for block in range(2):
+            part = pl.ds(pl.multiple_of((2 * block + wanted) * rows, rows), rows)
+            total = total_of([piece[part, :] for piece in from_lon])
+            out[block * rows : (block + 1) * rows, :] = total.astype(out.dtype)
+    for step, out in enumerate(by_lon):
+        start = lax.rem(lon + step, lon_count) * 2 * rows
+        part = pl.ds(pl.multiple_of(start, rows), 2 * rows)
+        out[...] = total_of([lat_keep[part, :], from_lat[part, :]]).astype(out.dtype)
+
+
+def third_step_kernel(keep_first, from_lat, *refs):
+    from_lon, (keep, send) = refs[:-2], refs[-2:]
+    rows = keep.shape[1]
+    mine = lax.div(lax.axis_index("lat"), 2)
+    for half, parts in enumerate(((keep_first, from_lat), from_lon)):
+        for out, block in ((keep, mine), (send, 1 - mine)):
+            part = pl.ds(pl.multiple_of(block * rows, rows), rows)
+            out[half] = total_of([piece[part, :] for piece in parts]).astype(out.dtype)
+
+
+def finish_kernel(group, flip, keep, arrived, grad_qkv, grad_out):
     for half in range(2):
-        total = arrived[half * count][...]
-        for other in arrived[half * count + 1 : (half + 1) * count]:
-            total = total + other[...].astype(F32)
+        total = keep[half] + arrived[half].astype(F32)
         grad_qkv[:, half * 3 * group : (half + 1) * 3 * group] = total[:, : 3 * group]
         out = total[:, 3 * group :]
         if flip:
@@ -450,23 +468,26 @@
         name="window_bias",
     )(table, bias_columns(), bias_rows(), pole_mask())
     lon_rows = width // lon_count
+    rows = lon_rows // lat_count
     columns = 2 * group
-    row_scratch = pltpu.VMEM((width, columns), BF16)
-    *first, normed, near_grad, merged, stay, over, swap, part_tokens, part_cotangent = call(
+    *by_lon, lat_keep, lat_send, stay, over, swap, part_tokens, part_cotangent = call(
         layer_kernel,
         [shaped(lon_rows, columns)] * lon_count
-        + [shaped(CELLS, width), shaped(CELLS, width), shaped(CELLS, 4 * group)]
+        + [shaped(2 * lon_count * rows, columns)] * 2
         + [shaped(2, PART, width)] * 2
         + [shaped(2, 2, PART, width)]
         + [shaped(PART, width)] * 2,
         [
             pltpu.VMEM((CELLS + RIM, width), BF16),
             pltpu.VMEM((CELLS, width), BF16),
+            pltpu.VMEM((CELLS, width), BF16),
+            pltpu.VMEM((CELLS, width), BF16),
             pltpu.VMEM((CELLS, 3 * group), BF16),
             pltpu.VMEM((CELLS, group), BF16),
+            pltpu.VMEM((CELLS, 4 * group), BF16),
             pltpu.VMEM((QUARTERS * PART, 4 * group), BF16),
             pltpu.VMEM((2, QUARTERS * PART, width), BF16),
-            row_scratch,
+            pltpu.VMEM((width, columns), BF16),
         ],
         cost=cost(6 * CELLS * width * width, 8000000),
         name="window_layer",
@@ -482,24 +503,10 @@
         one_hot(shifted_source(), CELLS + RIM),
         quarter_pick(),
     )
-
-    def lon_exchange(grads):
-        return [grads[0]] + [rotated(grads[step], "lon", step) for step in range(1, lon_count)]
-
-    def lat_exchange(arrived, after):
-        rows = lon_rows // lat_count
-        blocks = call(
-            functools.partial(regroup_kernel, lat_count),
-            [shaped(rows, columns, dtype=F32)] + [shaped(rows, columns)] * (lat_count - 1),
-            cost=cost(4 * lon_rows * columns, 6 * lon_rows * columns),
-            name="sum_over_lon",
-            after=after,
-        )(*arrived)
-        arrived = [rotated(blocks[step], "lat", step) for step in range(1, lat_count)]
-        return blocks[0], [blocks[0]] + arrived
-
+    from_lon = [by_lon[0]] + [rotated(by_lon[step], "lon", step) for step in range(1, lon_count)]
+    neighbours = [(i, i ^ 1) for i in range(lat_count)]
+    from_lat = lax.ppermute(lat_send, "lat", neighbours)
     swapped = lax.ppermute(swap, "head", pairs)
-    from_lon_first = lon_exchange(first)
     across = call(
         cores_kernel, shaped(2, PART, width), cost=cost(0, 8 * PART * width), name="sum_over_cores"
     )(over, swapped)
@@ -512,27 +519,35 @@
         name="sum_over_heads",
     )(part_tokens, part_cotangent, gain, group_pick(), stay, swapped, crossed)
     home = [pieces[0], moved(pieces[1], 1, 0), moved(pieces[2], 0, 1), moved(pieces[3], 1, 1)]
-    second = call(
-        weights_kernel,
-        [shaped(lon_rows, columns)] * lon_count,
-        [row_scratch],
-        cost=cost(CELLS * width * width, 8000000),
-        name="second_weights",
+    keep_first, send_first, *by_lon = call(
+        functools.partial(second_step_kernel, lon_count),
+        [shaped(2 * rows, columns, dtype=F32), shaped(2 * rows, columns)]
+        + [shaped(2 * rows, columns, dtype=F32)]
+        + [shaped(2 * rows, columns)] * (lon_count - 1),
+        cost=cost(4 * lon_rows * columns, 6 * lon_rows * columns),
+        name="second_step",
         after=(pieces[0],),
-    )(normed, near_grad, merged)
-    from_lon_second = lon_exchange(second)
-    done_first, from_lat_first = lat_exchange(from_lon_first, (second[0],))
+    )(*from_lon, lat_keep, from_lat)
+    from_lat = lax.ppermute(send_first, "lat", neighbours)
+    from_lon = [by_lon[0]] + [rotated(by_lon[step], "lon", step) for step in range(1, lon_count)]
     mine = call(
         join_kernel,
         shaped(2, PART, width),
         [pltpu.VMEM((2, OUT_ROWS, width), BF16)],
         cost=cost(2 * 2 * OUT_ROWS * PART * width, 8 * OUT_ROWS * width),
         name="join_home",
-        after=(done_first,),
+        after=(keep_first,),
     )(group_pick(), *home)
     far = lax.ppermute(mine, "head", chips)
     near = lax.ppermute(mine, "head", pairs)
-    done_second, from_lat_second = lat_exchange(from_lon_second, (mine,))
+    keep, send = call(
+        third_step_kernel,
+        [shaped(2, rows, columns, dtype=F32), shaped(2, rows, columns)],
+        cost=cost(4 * rows * columns, 6 * rows * columns),
+        name="third_step",
+        after=(mine,),
+    )(keep_first, from_lat, *from_lon)
+    last = lax.ppermute(send, "lat", [(i, i ^ 2) for i in range(lat_count)])
     beyond = lax.ppermute(far, "head", pairs)
     layer_out, grad_tokens = call(
         spread_kernel,
@@ -540,9 +555,8 @@
         [pltpu.VMEM((2, QUARTERS * PART, width), BF16)],
         cost=cost(2 * 2 * CELLS * CELLS * width, 8 * CELLS * width),
         name="spread_outputs",
-        after=(done_second,),
+        after=(keep,),
     )(own_pick(), mine, far, near, beyond)
-    rows = lon_rows // lat_count
     flip = rows % 128 == 0
     grad_qkv, grad_out = call(
         functools.partial(finish_kernel, group // 2, flip),
@@ -553,7 +567,7 @@
         cost=cost(4 * rows * 4 * group, 16 * rows * 4 * group),
         name="sum_over_lat",
         after=(layer_out,),
-    )(*from_lat_first, *from_lat_second)
+    )(keep, last)
     return (
         layer_out.reshape(tokens.shape),
         grad_tokens.reshape(tokens.shape),

time: 87.5 us -> 78.8 us (0.901)
  waiting for transfers between devices: 38.6 us -> 34.2 us
  starting transfers between devices: 25.3 us -> 21.1 us
    ppermute x8 -> x2, waiting for transfers between devices: 15 us -> 0.1 us  [rotated(): lax.ppermute(value, axis, [(i, (i + step) % count) for i in range(count)])]
    ppermute x0 -> x3, waiting for transfers between devices: none -> 10.6 us  [the longest x1 10.6 us: body(): last = lax.ppermute(send, 'lat', [(i, i ^ 2) for i in range(lat_count)])]
    ppermute x8 -> x2, starting transfers between devices: 10.2 us -> 1.98 us  [rotated(): lax.ppermute(value, axis, [(i, (i + step) % count) for i in range(count)])]
    ppermute x0 -> x3, starting transfers between devices: none -> 2.87 us  [the longest x1 1.69 us: body(): last = lax.ppermute(send, 'lat', [(i, i ^ 2) for i in range(lat_count)])]
    ppermute x6, starting transfers between devices: 11.4 us -> 12.5 us  [moved(): return lax.ppermute(value, ('lon', 'lat'), pairs)]
    pallas_call x11 -> x10, Pallas kernels: 17.3 us -> 17.3 us  [run(): pl.pallas_call(body, out_shape=outs, in_specs=[pl.BlockSpec(memory_space=...]
    unnamed x32 -> x36, local copies, waits for them, and re-layouts: 5 us -> 5.01 us
  transfers between devices with their start and end apart: 20 -> 17, of which waited for: 11 -> 8; matrix products, arithmetic and copies ran while one was open for 0% -> 0% of each run, Pallas kernels for 6% -> 6%
where the time goes in v2:
time: 78.8 us; the launch traced here: 78.5 us
  waiting for transfers between devices  34.2 us (43%)
  starting transfers between devices  21.1 us (27%)
  Pallas kernels  17.3 us (22%)
  local copies, waits for them, and re-layouts  5.02 us (6%)
  between operations  0.88 us (1%)
    pallas_call x10, Pallas kernels, run(): pl.pallas_call(body, out_shape=outs, in_specs=[pl.BlockSpec(memory_space=...  17.3 us
    ppermute x6, starting transfers between devices, moved(): return lax.ppermute(value, ('lon', 'lat'), pairs)  12.5 us
    ppermute x1, waiting for transfers between devices, body(): last = lax.ppermute(send, 'lat', [(i, i ^ 2) for i in range(lat_count)])  10.6 us
    ppermute x6, waiting for transfers between devices, moved(): return lax.ppermute(value, ('lon', 'lat'), pairs)  9.31 us
    ppermute x1, waiting for transfers between devices, body(): crossed = lax.ppermute(across, 'head', chips)  8.47 us
    ppermute x1, waiting for transfers between devices, body(): far = lax.ppermute(mine, 'head', chips)  5.66 us
    unnamed x36, local copies, waits for them, and re-layouts  5.01 us
    ppermute x2, starting transfers between devices, rotated(): lax.ppermute(value, axis, [(i, (i + step) % count) for i in range(count)])  1.98 us
  transfers between devices with their start and end apart: 17, of which 8 were waited for; matrix products, arithmetic and copies ran while one was open for 0% of the time, Pallas kernels for 6%

profile of v2, /device:TPU:0, one launch (start us, length us, event | category | flops | bytes accessed | tf_op | source)
XLA Modules:
  0.0 78.5 jit_solution(10245544937103907204)
XLA Ops:
  0.7 1.1 %copy-done = bf16[2,6,24,1024]{3,2,1,0:T(8,128)(2,1)S(1)} copy-done((bf16[2,6,24,1024]{3,2,1,0:T(8,128)(2,1)S(1)}, bf16[2,6,24,1024]{3,2,1,0:T(8,128)(2,1)}, u32[]{:S(2)}) %copy-start) | copy-done | bytes 589848
  1.7 1.1 %copy-done.2 = bf16[2,6,24,1024]{3,2,1,0:T(8,128)(2,1)S(1)} copy-done((bf16[2,6,24,1024]{3,2,1,0:T(8,128)(2,1)S(1)}, bf16[2,6,24,1024]{3,2,1,0:T(8,128)(2,1)}, u32[]{:S(2)}) %copy-start.2) | copy-done | bytes 589848
  2.8 0.9 %copy-done.6 = bf16[208,288]{1,0:T(8,128)(2,1)S(1)} copy-done((bf16[208,288]{1,0:T(8,128)(2,1)S(1)}, bf16[208,288]{1,0:T(8,128)(2,1)}, u32[]{:S(2)}) %copy-start.6) | copy-done | bytes 119832
  3.7 0.4 pack_rims.1
  4.1 5.1 %collective-permute-start = (bf16[112,1024]{1,0:T(8,128)(2,1)S(1)}, bf16[112,1024]{1,0:T(8,128)(2,1)S(1)}, u32[]{:S(2)}, u32[]{:S(2)}) collective-permute-start(bf16[112,1024]{1,0:T(8,128)(2,1)S(1)} %get-tuple-element.30), channel_id=1, source_target_pairs={{0,12},{4,0},{8,4},{12,8},{16,28},{20,16},{24,20},{28,24},{1,13},{... | collective-permute-start | bytes 688136 | tf_op jit(solution)/shard_map/ppermute | solution.py:441
  9.2 1.5 %collective-permute-start.1 = (bf16[48,1024]{1,0:T(8,128)(2,1)S(1)}, bf16[48,1024]{1,0:T(8,128)(2,1)S(1)}, u32[]{:S(2)}, u32[]{:S(2)}) collective-permute-start(bf16[48,1024]{1,0:T(8,128)(2,1)S(1)} %get-tuple-element.31), channel_id=1, source_target_pairs={{0,16},{4,20},{8,24},{12,28},{16,0},{20,4},{24,8},{28,12},{1,17},{... | collective-permute-start | bytes 294920 | tf_op jit(solution)/shard_map/ppermute | solution.py:441
  10.7 0.4 collective-permute-start.2
  11.1 4.0 %collective-permute-done = bf16[112,1024]{1,0:T(8,128)(2,1)S(1)} collective-permute-done((bf16[112,1024]{1,0:T(8,128)(2,1)S(1)}, bf16[112,1024]{1,0:T(8,128)(2,1)S(1)}, u32[]{:S(2)}, u32[]{:S(2)}) %collective-permute-start) | collective-permute-done | bytes 229408 | tf_op jit(solution)/shard_map/ppermute | solution.py:441
  15.2 1.0 %collective-permute-done.2 = bf16[48,1024]{1,0:T(8,128)(2,1)S(1)} collective-permute-done((bf16[48,1024]{1,0:T(8,128)(2,1)S(1)}, bf16[48,1024]{1,0:T(8,128)(2,1)S(1)}, u32[]{:S(2)}, u32[]{:S(2)}) %collective-permute-start.2) | collective-permute-done | bytes 98336 | tf_op jit(solution)/shard_map/ppermute | solution.py:441
  16.4 1.7 %window_bias.1.refs_7_ = f32[4,144,144]{2,1,0:T(8,128)S(1)} custom-call(f32[4,1024]{1,0:T(4,128)S(1)} %pad.4.refs_0_, s32[1,144]{1,0:T(1,128)S(1)} %copy-done.14, bf16[144,576]{1,0:T(8,128)(2,1)S(1)} %copy-done.12, f32[144,144]{1,0:T(8,128)S(1)} %copy-done.13), custom_call_target="tpu_custom_call" | custom-call | flops 1019215872 | bytes 1000000 | tf_op jit(solution)/shard_map/window_bias/pallas_call | solution.py:177
  18.1 0.8 %copy-done.15 = f32[4,144,144]{2,1,0:T(8,128)} copy-done((f32[4,144,144]{2,1,0:T(8,128)}, f32[4,144,144]{2,1,0:T(8,128)S(1)}, u32[]{:S(2)}) %copy-start.15) | copy-done | bytes 331800
  19.0 11.5 %window_layer.1 = (bf16[512,512]{1,0:T(8,128)(2,1)S(1)}, bf16[512,512]{1,0:T(8,128)(2,1)S(1)}, bf16[512,512]{1,0:T(8,128)(2,1)S(1)}, bf16[512,512]{1,0:T(8,128)(...) custom-call(bf16[288,1024]{1,0:T(8,128)(2,1)S(1)} %bitcast.7, ...), custom_call_target="tpu_custom_call" | custom-call | flops 1811939328 | bytes 8000000 | tf_op jit(solution)/shard_map/window_layer/pallas_call | solution.py:177
  30.5 0.5 collective-permute-start.4
  30.9 1.4 %collective-permute-start.9 = (bf16[512,512]{1,0:T(8,128)(2,1)S(1)}, bf16[512,512]{1,0:T(8,128)(2,1)S(1)}, u32[]{:S(2)}, u32[]{:S(2)}) collective-permute-start(bf16[512,512]{1,0:T(8,128)(2,1)S(1)} %get-tuple-element.43), channel_id=1, source_target_pairs={{0,16},{16,0},{1,17},{17,1},{2,18},{18,2},{3,19},{19,3},{4,20},{20... | collective-permute-start | bytes 1572872 | tf_op jit(solution)/shard_map/ppermute | solution.py:431
  32.3 0.5 collective-permute-start.10
  33.0 1.6 %collective-permute-start.5 = (bf16[2,80,1024]{2,1,0:T(8,128)(2,1)S(1)}, bf16[2,80,1024]{2,1,0:T(8,128)(2,1)S(1)}, u32[]{:S(2)}, u32[]{:S(2)}) collective-permute-start(bf16[2,80,1024]{2,1,0:T(8,128)(2,1)S(1)} %sum_over_cores.1), channel_id=1, source_target_pairs={{0,2},{1,3},{2,0},{3,1},{4,6},{5,7},{6,4},{7,5},{8,10},{9,11},{10,... | collective-permute-start | bytes 983048 | tf_op jit(solution)/shard_map/ppermute | solution.py:514
  34.5 8.5 %collective-permute-done.5.refs_6_ = bf16[2,80,1024]{2,1,0:T(8,128)(2,1)S(1)} collective-permute-done((bf16[2,80,1024]{2,1,0:T(8,128)(2,1)S(1)}, bf16[2,80,1024]{2,1,0:T(8,128)(2,1)S(1)}, u32[]{:S(2)}, u32[]{:S(2)}) %collective-permute-start.5) | collective-permute-done | bytes 327712 | tf_op jit(solution)/shard_map/ppermute | solution.py:514
  43.0 0.6 sum_over_heads.1
  43.6 1.4 %collective-permute-start.6 = (bf16[2,32,1024]{2,1,0:T(8,128)(2,1)S(1)}, bf16[2,32,1024]{2,1,0:T(8,128)(2,1)S(1)}, u32[]{:S(2)}, u32[]{:S(2)}) collective-permute-start(bf16[2,32,1024]{2,1,0:T(8,128)(2,1)S(1)} %get-tuple-element.39), channel_id=1, source_target_pairs={{0,4},{4,8},{8,12},{12,0},{16,20},{20,24},{24,28},{28,16},{1,5},{5... | collective-permute-start | bytes 393224 | tf_op jit(solution)/shard_map/ppermute | solution.py:441
  45.0 0.5 collective-permute-start.7
  45.5 3.6 %collective-permute-start.8 = (bf16[2,16,1024]{2,1,0:T(8,128)(2,1)S(1)}, bf16[2,16,1024]{2,1,0:T(8,128)(2,1)S(1)}, u32[]{:S(2)}, u32[]{:S(2)}) collective-permute-start(bf16[2,16,1024]{2,1,0:T(8,128)(2,1)S(1)} %get-tuple-element.41), channel_id=1, source_target_pairs={{0,20},{4,24},{8,28},{12,16},{16,4},{20,8},{24,12},{28,0},{1,21},{... | collective-permute-start | bytes 196616 | tf_op jit(solution)/shard_map/ppermute | solution.py:441
  49.4 4.3 %collective-permute-done.8.refs_4_ = bf16[2,16,1024]{2,1,0:T(8,128)(2,1)S(1)} collective-permute-done((bf16[2,16,1024]{2,1,0:T(8,128)(2,1)S(1)}, bf16[2,16,1024]{2,1,0:T(8,128)(2,1)S(1)}, u32[]{:S(2)}, u32[]{:S(2)}) %collective-permute-start.8) | collective-permute-done | bytes 65568 | tf_op jit(solution)/shard_map/ppermute | solution.py:441
  53.6 0.3 join_home.1.refs_4_.refs_1_
  53.9 1.6 %collective-permute-start.11 = (bf16[2,80,1024]{2,1,0:T(8,128)(2,1)S(1)}, bf16[2,80,1024]{2,1,0:T(8,128)(2,1)S(1)}, u32[]{:S(2)}, u32[]{:S(2)}) collective-permute-start(bf16[2,80,1024]{2,1,0:T(8,128)(2,1)S(1)} %join_home.1.refs_4_.refs_1_), channel_id=1, source_target_pairs={{0,2},{1,3},{2,0},{3,1},{4,6},{5,7},{6,4},{7,5},{8,10},{9,11},{10,... | collective-permute-start | bytes 983048 | tf_op jit(solution)/shard_map/ppermute | solution.py:541
  55.5 0.7 collective-permute-start.14
  56.2 0.6 collective-permute-start.15
  56.8 5.7 %collective-permute-done.11.refs_2_ = bf16[2,80,1024]{2,1,0:T(8,128)(2,1)S(1)} collective-permute-done((bf16[2,80,1024]{2,1,0:T(8,128)(2,1)S(1)}, bf16[2,80,1024]{2,1,0:T(8,128)(2,1)S(1)}, u32[]{:S(2)}, u32[]{:S(2)}) %collective-permute-start.11) | collective-permute-done | bytes 327712 | tf_op jit(solution)/shard_map/ppermute | solution.py:541
  62.6 1.7 %collective-permute-start.16 = (bf16[2,128,512]{2,1,0:T(8,128)(2,1)S(1)}, bf16[2,128,512]{2,1,0:T(8,128)(2,1)S(1)}, u32[]{:S(2)}, u32[]{:S(2)}) collective-permute-start(bf16[2,128,512]{2,1,0:T(8,128)(2,1)S(1)} %get-tuple-element.53), channel_id=1, source_target_pairs={{0,8},{4,12},{8,0},{12,4},{1,9},{5,13},{9,1},{13,5},{2,10},{6,14},... | collective-permute-start | bytes 786440 | tf_op jit(solution)/shard_map/ppermute | solution.py:550
  64.3 1.7 %spread_outputs.1 = (bf16[288,1024]{1,0:T(8,128)(2,1)}, bf16[288,1024]{1,0:T(8,128)(2,1)}) custom-call(bf16[288,320]{1,0:T(8,128)(2,1)S(1)} %copy-done.5, bf16[2,80,1024]{2,1,0:T(8,128)(2,1)S(1)} %join_home.1.refs_4_.refs_1_, bf16[2,80,1024]{2,1,0:T(8,128)(2,1)S(1)} %collective-permute-done.11.refs_2_, ...), custom_call_target="tpu_custom_call" | custom-call | flops 339738624 | bytes 2359296 | tf_op jit(solution)/shard_map/spread_outputs/pallas_call | solution.py:177
  66.1 10.6 %collective-permute-done.16.refs_1_ = bf16[2,128,512]{2,1,0:T(8,128)(2,1)S(1)} collective-permute-done((bf16[2,128,512]{2,1,0:T(8,128)(2,1)S(1)}, bf16[2,128,512]{2,1,0:T(8,128)(2,1)S(1)}, u32[]{:S(2)}, u32[]{:S(2)}) %collective-permute-start.16) | collective-permute-done | bytes 262176 | tf_op jit(solution)/shard_map/ppermute | solution.py:550
  76.6 1.1 %copy-done.4 = bf16[288,1024]{1,0:T(8,128)(2,1)S(1)} copy-done((bf16[288,1024]{1,0:T(8,128)(2,1)S(1)}, bf16[288,1024]{1,0:T(8,128)(2,1)}, u32[]{:S(2)}) %copy-start.4) | copy-done | bytes 589848
  77.7 0.8 %sum_over_lat.1 = (f32[128,768]{1,0:T(8,128)}, f32[256,128]{1,0:T(8,128)}) custom-call(f32[2,128,512]{2,1,0:T(8,128)S(1)} %get-tuple-element.50.refs_5_.refs_0_, bf16[2,128,512]{2,1,0:T(8,128)(2,1)S(1)} %collective-permute-done.16.refs_1_, bf16[288,1024]{1,0:T(8,128)(2,1)S(1)} %copy-done.4), custom_call_target="tpu_custom_call" | custom-call | flops 524288 | bytes 2097152 | tf_op jit(solution)/shard_map/sum_over_lat/pallas_call | solution.py:177
  (50 shorter events, 0.8 us)
Async XLA Ops:
  0.6 15.7 %copy-start.14 = (s32[1,144]{1,0:T(1,128)S(1)}, s32[1,144]{1,0:T(1,128)}, u32[]{:S(2)}) copy-start(s32[1,144]{1,0:T(1,128)} %constant.20.clone.refs_1_) | copy-start | bytes 1732
  0.6 1.1 %copy-start = (bf16[2,6,24,1024]{3,2,1,0:T(8,128)(2,1)S(1)}, bf16[2,6,24,1024]{3,2,1,0:T(8,128)(2,1)}, u32[]{:S(2)}) copy-start(bf16[2,6,24,1024]{3,2,1,0:T(8,128)(2,1)} %param.15) | copy-start | bytes 1769476
  1.7 1.1 %copy-start.2 = (bf16[2,6,24,1024]{3,2,1,0:T(8,128)(2,1)S(1)}, bf16[2,6,24,1024]{3,2,1,0:T(8,128)(2,1)}, u32[]{:S(2)}) copy-start(bf16[2,6,24,1024]{3,2,1,0:T(8,128)(2,1)} %param.20) | copy-start | bytes 1769476
  3.7 12.6 %copy-start.16 = (f32[759,4]{0,1:T(4,128)S(1)}, f32[759,4]{0,1:T(4,128)}, u32[]{:S(2)}) copy-start(f32[759,4]{0,1:T(4,128)} %param.19) | copy-start | bytes 36436
  3.7 12.6 %copy-start.12 = (bf16[144,576]{1,0:T(8,128)(2,1)S(1)}, bf16[144,576]{1,0:T(8,128)(2,1)}, u32[]{:S(2)}) copy-start(bf16[144,576]{1,0:T(8,128)(2,1)} %constant.21.clone.refs_2_) | copy-start | bytes 497668
  3.7 12.6 %copy-start.13 = (f32[144,144]{1,0:T(8,128)S(1)}, f32[144,144]{1,0:T(8,128)}, u32[]{:S(2)}) copy-start(f32[144,144]{1,0:T(8,128)} %constant.22.clone.refs_3_) | copy-start | bytes 248836
  4.1 11.0 %collective-permute-start = (bf16[112,1024]{1,0:T(8,128)(2,1)S(1)}, bf16[112,1024]{1,0:T(8,128)(2,1)S(1)}, u32[]{:S(2)}, u32[]{:S(2)}) collective-permute-start(bf16[112,1024]{1,0:T(8,128)(2,1)S(1)} %get-tuple-element.30), channel_id=1, source_target_pairs={{0,12},{4,0},{8,4},{12,8},{16,28},{20,16},{24,20},{28,24},{1,13},{... | collective-permute-start | bytes 688136 | tf_op jit(solution)/shard_map/ppermute | solution.py:441
  9.2 5.9 %collective-permute-start.1 = (bf16[48,1024]{1,0:T(8,128)(2,1)S(1)}, bf16[48,1024]{1,0:T(8,128)(2,1)S(1)}, u32[]{:S(2)}, u32[]{:S(2)}) collective-permute-start(bf16[48,1024]{1,0:T(8,128)(2,1)S(1)} %get-tuple-element.31), channel_id=1, source_target_pairs={{0,16},{4,20},{8,24},{12,28},{16,0},{20,4},{24,8},{28,12},{1,17},{... | collective-permute-start | bytes 294920 | tf_op jit(solution)/shard_map/ppermute | solution.py:441
  10.7 5.5 %collective-permute-start.2 = (bf16[48,1024]{1,0:T(8,128)(2,1)S(1)}, bf16[48,1024]{1,0:T(8,128)(2,1)S(1)}, u32[]{:S(2)}, u32[]{:S(2)}) collective-permute-start(bf16[48,1024]{1,0:T(8,128)(2,1)S(1)} %get-tuple-element.32), channel_id=1, source_target_pairs={{0,28},{4,16},{8,20},{12,24},{16,12},{20,0},{24,4},{28,8},{1,29},{... | collective-permute-start | bytes 294920 | tf_op jit(solution)/shard_map/ppermute | solution.py:441
  16.2 2.7 %collective-permute-start.3 = (bf16[208,1024]{1,0:T(8,128)(2,1)S(1)}, bf16[208,1024]{1,0:T(8,128)(2,1)S(1)}, u32[]{:S(2)}, u32[]{:S(2)}) collective-permute-start(bf16[208,1024]{1,0:T(8,128)(2,1)S(1)} %constant_dynamic-update-slice_fusion.refs_2_), channel_id=1, source_target_pairs={{0,1},{1,0},{2,3},{3,2},{4,5},{5,4},{6,7},{7,6},{8,9},{9,8},{10,11... | collective-permute-start | bytes 1277960 | tf_op jit(solution)/shard_map/ppermute | solution.py:461
  16.3 2.6 %copy-start.1 = (bf16[2,6,24,1024]{3,2,1,0:T(8,128)(2,1)S(1)}, bf16[2,6,24,1024]{3,2,1,0:T(8,128)(2,1)}, u32[]{:S(2)}) copy-start(bf16[2,6,24,1024]{3,2,1,0:T(8,128)(2,1)} %param.15) | copy-start | bytes 1769476
  16.4 2.6 %copy-start.3 = (bf16[2,6,24,1024]{3,2,1,0:T(8,128)(2,1)S(1)}, bf16[2,6,24,1024]{3,2,1,0:T(8,128)(2,1)}, u32[]{:S(2)}) copy-start(bf16[2,6,24,1024]{3,2,1,0:T(8,128)(2,1)} %param.20) | copy-start | bytes 1769476
  16.4 2.5 %copy-start.8 = (f32[1024]{0:T(1024)S(1)}, f32[1024]{0:T(1024)}, u32[]{:S(2)}) copy-start(f32[1024]{0:T(1024)} %param.16) | copy-start | bytes 12292
  16.4 2.5 %copy-start.9 = (bf16[256,1024]{1,0:T(8,128)(2,1)S(1)}, bf16[256,1024]{1,0:T(8,128)(2,1)}, u32[]{:S(2)}) copy-start(bf16[256,1024]{1,0:T(8,128)(2,1)} %refs_6_.1) | copy-start | bytes 1572868
  16.4 2.5 %copy-start.10 = (bf16[288,496]{1,0:T(8,128)(2,1)S(1)}, bf16[288,496]{1,0:T(8,128)(2,1)}, u32[]{:S(2)}) copy-start(bf16[288,496]{1,0:T(8,128)(2,1)} %constant.23.clone.refs_8_) | copy-start | bytes 857092
  16.4 2.5 %copy-start.11 = (bf16[320,288]{1,0:T(8,128)(2,1)S(1)}, bf16[320,288]{1,0:T(8,128)(2,1)}, u32[]{:S(2)}) copy-start(bf16[320,288]{1,0:T(8,128)(2,1)} %constant.24.clone.refs_9_) | copy-start | bytes 552964
  19.0 24.1 %copy-start.7 = (bf16[96,80]{1,0:T(8,128)(2,1)S(1)}, bf16[96,80]{1,0:T(8,128)(2,1)}, u32[]{:S(2)}) copy-start(bf16[96,80]{1,0:T(8,128)(2,1)} %constant.25.clone.refs_3_.refs_0_) | copy-start | bytes 46084
  30.5 2.4 %collective-permute-start.4 = (bf16[2,2,80,1024]{3,2,1,0:T(8,128)(2,1)}, bf16[2,2,80,1024]{3,2,1,0:T(8,128)(2,1)S(1)}, u32[]{:S(2)}, u32[]{:S(2)}) collective-permute-start(bf16[2,2,80,1024]{3,2,1,0:T(8,128)(2,1)} %get-tuple-element.36), channel_id=1, source_target_pairs={{0,1},{1,0},{2,3},{3,2},{4,5},{5,4},{6,7},{7,6},{8,9},{9,8},{10,11... | collective-permute-start | bytes 1966088 | tf_op jit(solution)/shard_map/ppermute | solution.py:509
  30.9 18.2 %collective-permute-start.9 = (bf16[512,512]{1,0:T(8,128)(2,1)S(1)}, bf16[512,512]{1,0:T(8,128)(2,1)S(1)}, u32[]{:S(2)}, u32[]{:S(2)}) collective-permute-start(bf16[512,512]{1,0:T(8,128)(2,1)S(1)} %get-tuple-element.43), channel_id=1, source_target_pairs={{0,16},{16,0},{1,17},{17,1},{2,18},{18,2},{3,19},{19,3},{4,20},{20... | collective-permute-start | bytes 1572872 | tf_op jit(solution)/shard_map/ppermute | solution.py:431
  32.3 16.8 %collective-permute-start.10 = (bf16[512,512]{1,0:T(8,128)(2,1)S(1)}, bf16[512,512]{1,0:T(8,128)(2,1)S(1)}, u32[]{:S(2)}, u32[]{:S(2)}) collective-permute-start(bf16[512,512]{1,0:T(8,128)(2,1)S(1)} %get-tuple-element.45), channel_id=1, source_target_pairs={{0,4},{4,0},{8,12},{12,8},{1,5},{5,1},{9,13},{13,9},{2,6},{6,2},{1... | collective-permute-start | bytes 1572872 | tf_op jit(solution)/shard_map/ppermute | solution.py:508
  33.0 10.1 %collective-permute-start.5 = (bf16[2,80,1024]{2,1,0:T(8,128)(2,1)S(1)}, bf16[2,80,1024]{2,1,0:T(8,128)(2,1)S(1)}, u32[]{:S(2)}, u32[]{:S(2)}) collective-permute-start(bf16[2,80,1024]{2,1,0:T(8,128)(2,1)S(1)} %sum_over_cores.1), channel_id=1, source_target_pairs={{0,2},{1,3},{2,0},{3,1},{4,6},{5,7},{6,4},{7,5},{8,10},{9,11},{10,... | collective-permute-start | bytes 983048 | tf_op jit(solution)/shard_map/ppermute | solution.py:514
  43.6 10.0 %collective-permute-start.6 = (bf16[2,32,1024]{2,1,0:T(8,128)(2,1)S(1)}, bf16[2,32,1024]{2,1,0:T(8,128)(2,1)S(1)}, u32[]{:S(2)}, u32[]{:S(2)}) collective-permute-start(bf16[2,32,1024]{2,1,0:T(8,128)(2,1)S(1)} %get-tuple-element.39), channel_id=1, source_target_pairs={{0,4},{4,8},{8,12},{12,0},{16,20},{20,24},{24,28},{28,16},{1,5},{5... | collective-permute-start | bytes 393224 | tf_op jit(solution)/shard_map/ppermute | solution.py:441
  45.0 4.4 %collective-permute-start.7 = (bf16[2,16,1024]{2,1,0:T(8,128)(2,1)S(1)}, bf16[2,16,1024]{2,1,0:T(8,128)(2,1)S(1)}, u32[]{:S(2)}, u32[]{:S(2)}) collective-permute-start(bf16[2,16,1024]{2,1,0:T(8,128)(2,1)S(1)} %get-tuple-element.40), channel_id=1, source_target_pairs={{0,16},{4,20},{8,24},{12,28},{16,0},{20,4},{24,8},{28,12},{1,17},{... | collective-permute-start | bytes 196616 | tf_op jit(solution)/shard_map/ppermute | solution.py:441
  45.5 8.1 %collective-permute-start.8 = (bf16[2,16,1024]{2,1,0:T(8,128)(2,1)S(1)}, bf16[2,16,1024]{2,1,0:T(8,128)(2,1)S(1)}, u32[]{:S(2)}, u32[]{:S(2)}) collective-permute-start(bf16[2,16,1024]{2,1,0:T(8,128)(2,1)S(1)} %get-tuple-element.41), channel_id=1, source_target_pairs={{0,20},{4,24},{8,28},{12,16},{16,4},{20,8},{24,12},{28,0},{1,21},{... | collective-permute-start | bytes 196616 | tf_op jit(solution)/shard_map/ppermute | solution.py:441
  53.6 10.7 %copy-start.5 = (bf16[288,320]{1,0:T(8,128)(2,1)S(1)}, bf16[288,320]{1,0:T(8,128)(2,1)}, u32[]{:S(2)}) copy-start(bf16[288,320]{1,0:T(8,128)(2,1)} %constant.26.clone.refs_0_) | copy-start | bytes 552964
  53.9 8.5 %collective-permute-start.11 = (bf16[2,80,1024]{2,1,0:T(8,128)(2,1)S(1)}, bf16[2,80,1024]{2,1,0:T(8,128)(2,1)S(1)}, u32[]{:S(2)}, u32[]{:S(2)}) collective-permute-start(bf16[2,80,1024]{2,1,0:T(8,128)(2,1)S(1)} %join_home.1.refs_4_.refs_1_), channel_id=1, source_target_pairs={{0,2},{1,3},{2,0},{3,1},{4,6},{5,7},{6,4},{7,5},{8,10},{9,11},{10,... | collective-permute-start | bytes 983048 | tf_op jit(solution)/shard_map/ppermute | solution.py:541
  55.5 7.0 %collective-permute-start.14 = (bf16[256,512]{1,0:T(8,128)(2,1)S(1)}, bf16[256,512]{1,0:T(8,128)(2,1)S(1)}, u32[]{:S(2)}, u32[]{:S(2)}) collective-permute-start(bf16[256,512]{1,0:T(8,128)(2,1)S(1)} %get-tuple-element.47), channel_id=1, source_target_pairs={{0,4},{4,0},{8,12},{12,8},{1,5},{5,1},{9,13},{13,9},{2,6},{6,2},{1... | collective-permute-start | bytes 786440 | tf_op jit(solution)/shard_map/ppermute | solution.py:531
  56.2 6.4 %collective-permute-start.15 = (bf16[256,512]{1,0:T(8,128)(2,1)S(1)}, bf16[256,512]{1,0:T(8,128)(2,1)S(1)}, u32[]{:S(2)}, u32[]{:S(2)}) collective-permute-start(bf16[256,512]{1,0:T(8,128)(2,1)S(1)} %get-tuple-element.49), channel_id=1, source_target_pairs={{0,16},{16,0},{1,17},{17,1},{2,18},{18,2},{3,19},{19,3},{4,20},{20... | collective-permute-start | bytes 786440 | tf_op jit(solution)/shard_map/ppermute | solution.py:431
  56.8 7.6 %collective-permute-start.12 = (bf16[2,80,1024]{2,1,0:T(8,128)(2,1)S(1)}, bf16[2,80,1024]{2,1,0:T(8,128)(2,1)S(1)}, u32[]{:S(2)}, u32[]{:S(2)}) collective-permute-start(bf16[2,80,1024]{2,1,0:T(8,128)(2,1)S(1)} %join_home.1.refs_4_.refs_1_), channel_id=1, source_target_pairs={{0,1},{1,0},{2,3},{3,2},{4,5},{5,4},{6,7},{7,6},{8,9},{9,8},{10,11... | collective-permute-start | bytes 983048 | tf_op jit(solution)/shard_map/ppermute | solution.py:542
  62.4 1.9 %collective-permute-start.13 = (bf16[2,80,1024]{2,1,0:T(8,128)(2,1)S(1)}, bf16[2,80,1024]{2,1,0:T(8,128)(2,1)S(1)}, u32[]{:S(2)}, u32[]{:S(2)}) collective-permute-start(bf16[2,80,1024]{2,1,0:T(8,128)(2,1)S(1)} %collective-permute-done.11.refs_2_), channel_id=1, source_target_pairs={{0,1},{1,0},{2,3},{3,2},{4,5},{5,4},{6,7},{7,6},{8,9},{9,8},{10,11... | collective-permute-start | bytes 983048 | tf_op jit(solution)/shard_map/ppermute | solution.py:551
  62.6 14.0 %collective-permute-start.16 = (bf16[2,128,512]{2,1,0:T(8,128)(2,1)S(1)}, bf16[2,128,512]{2,1,0:T(8,128)(2,1)S(1)}, u32[]{:S(2)}, u32[]{:S(2)}) collective-permute-start(bf16[2,128,512]{2,1,0:T(8,128)(2,1)S(1)} %get-tuple-element.53), channel_id=1, source_target_pairs={{0,8},{4,12},{8,0},{12,4},{1,9},{5,13},{9,1},{13,5},{2,10},{6,14},... | collective-permute-start | bytes 786440 | tf_op jit(solution)/shard_map/ppermute | solution.py:550
  76.6 1.1 %copy-start.4 = (bf16[288,1024]{1,0:T(8,128)(2,1)S(1)}, bf16[288,1024]{1,0:T(8,128)(2,1)}, u32[]{:S(2)}) copy-start(bf16[288,1024]{1,0:T(8,128)(2,1)} %get-tuple-element.51.refs_2_) | copy-start | bytes 1769476
  (2 other events, 1.7 us)

commit v3 on v2

--- a/solution.py
+++ b/solution.py
@@ -38,20 +38,6 @@
     return (level * WLAT + lat) * TILE_LON + lon
 
 
-def rim_source():
-    rows = np.full(RIM, -1)
-    z_width = TILE_LON - MID_LON
-    for level in range(LEV):
-        for lat in range(MID_LAT):
-            for lon in range(z_width):
-                rows[(level * MID_LAT + lat) * z_width + lon] = own_row(level, lat, lon + MID_LON)
-            for lon in range(MID_LON):
-                at = (level * MID_LAT + lat) * MID_LON + lon
-                rows[RIM_Z + at] = own_row(level, lat + MID_LAT, lon)
-                rows[RIM_Z + RIM_X + at] = own_row(level, lat, lon)
-    return rows
-
-
 def window_cells():
     cells = []
     for window in range(WINDOWS):
@@ -169,21 +155,26 @@
     return lax.dot_general(left, right, (((0,), (0,)), ((), ())), preferred_element_type=F32)
 
 
-def call(kernel, outs, scratch=(), cost=None, name=None, after=()):
+def call(kernel, outs, scratch=(), cost=None, name=None, after=(), far=(), far_outs=0, limit=16):
     def run(*args):
         def body(*refs):
-            kernel(*refs[: len(args)], *refs[len(args) + len(after) :])
-
+            count = len(args) + len(far)
+            kernel(*refs[:count], *refs[count + len(after) :])
+
+        near, outside = pl.BlockSpec(memory_space=pltpu.VMEM), pl.BlockSpec(memory_space=pl.ANY)
+        specs = near
+        if isinstance(outs, list):
+            specs = [outside] * far_outs + [near] * (len(outs) - far_outs)
         return pl.pallas_call(
             body,
             out_shape=outs,
-            in_specs=[pl.BlockSpec(memory_space=pltpu.VMEM)] * len(args)
-            + [pl.BlockSpec(memory_space=pl.ANY)] * len(after),
+            in_specs=[near] * len(args) + [outside] * (len(far) + len(after)),
+            out_specs=specs,
             scratch_shapes=scratch,
             name=name,
             cost_estimate=cost,
-            compiler_params=pltpu.CompilerParams(vmem_limit_bytes=48 * 1024 * 1024),
-        )(*args, *after)
+            compiler_params=pltpu.CompilerParams(vmem_limit_bytes=limit * 1024 * 1024),
+        )(*args, *far, *after)
 
     return run
 
@@ -192,16 +183,54 @@
     return pl.CostEstimate(flops=flops, bytes_accessed=moved, transcendentals=0)
 
 
-def pack_kernel(pick, tokens, cotangent, rim_z, rim_x, rim_d):
+def rim_rows(shape):
+    row = lax.broadcasted_iota(jnp.int32, shape, 1)
+    level = (row >= WLAT * TILE_LON).astype(jnp.int32)
+    row = row - level * WLAT * TILE_LON
+    lat = sum((row >= TILE_LON * count).astype(jnp.int32) for count in range(1, WLAT))
+    lon = row - lat * TILE_LON
+    line = level * MID_LAT + lat
+    z_row = line * (TILE_LON - MID_LON) + lon - MID_LON
+    d_row = RIM_Z + RIM_X + line * MID_LON + lon
+    x_row = RIM_Z + (line - MID_LAT) * MID_LON + lon
+    west = lon < MID_LON
+    return jnp.where(
+        lat < MID_LAT, jnp.where(west, d_row, z_row), jnp.where(west, x_row, -1)
+    )
+
+
+def pack_kernel(tokens, cotangent, rim_z, rim_x, rim_d, source, sems):
     core = lax.rem(lax.axis_index("head"), 2)
-    source = jnp.where(core == 0, tokens[...], cotangent[...])
-    rim = dot(pick[...], source).astype(BF16)
+    pieces = sems.shape[0]
+    rows = CELLS // pieces
+
+    def load(array):
+        copies = []
+        for piece in range(pieces):
+            part = pl.ds(piece * rows, rows)
+            copies.append(pltpu.make_async_copy(array.at[part], source.at[part], sems.at[piece]))
+        for copy in copies:
+            copy.start()
+        for copy in copies:
+            copy.wait()
+
+    pl.when(core == 0)(lambda: load(tokens))
+    pl.when(core != 0)(lambda: load(cotangent))
+    wanted = lax.broadcasted_iota(jnp.int32, (RIM, CELLS), 0) == rim_rows((RIM, CELLS))
+    rim = dot(wanted.astype(F32).astype(BF16), source[...]).astype(BF16)
     rim_z[...] = rim[:RIM_Z]
     rim_x[...] = rim[RIM_Z : RIM_Z + RIM_X]
     rim_d[...] = rim[RIM_Z + RIM_X :]
 
 
-def bias_kernel(table, columns, rows, mask, bias, shifted, parts):
+def rims_kernel(rim_z, rim_x, rim_d, rim):
+    rim[:RIM_Z] = rim_z[...]
+    rim[RIM_Z : RIM_Z + RIM_X] = rim_x[...]
+    rim[RIM_Z + RIM_X :] = rim_d[...]
+
+
+def bias_kernel(table, columns, rows, mask, bias, mark, shifted, parts):
+    mark[...] = jnp.zeros_like(mark)
     heads = bias.shape[0]
     width = shifted.shape[1]
     for head in range(heads):
@@ -273,11 +302,14 @@
     whole[:, 3 * group :] = dot_columns(near_grad[...], merged[:, attended]).astype(BF16)
 
 
-def lat_rows(whole, out, lon_count, parity):
+def lat_copies(whole, out, lon_count, parity, sems, first):
     rows = whole.shape[0] // (4 * lon_count)
+    copies = []
     for block in range(2 * lon_count):
         start = pl.multiple_of((2 * block + parity) * rows, rows)
-        out[block * rows : (block + 1) * rows, :] = whole[pl.ds(start, rows), :]
+        source, target = whole.at[pl.ds(start, rows)], out.at[pl.ds(block * rows, rows)]
+        copies.append(pltpu.make_async_copy(source, target, sems.at[first + block]))
+    return copies
 
 
 def layer_kernel(
@@ -286,16 +318,25 @@
     rim_here,
     rim_there,
     gain,
-    w_qkv,
     w_out,
     bias,
     shift_pick,
     quarter,
+    w_far,
     *refs,
 ):
-    *by_lon, lat_keep, lat_send, stay, over, swap, part_tokens, part_cotangent = refs[:-10]
-    source, near_tokens, near_grad, normed, projected, d_attended, merged = refs[-10:-3]
-    ordered, terms, whole = refs[-3:]
+    *by_lon, lat_keep, lat_send, stay, over, swap, part_tokens, part_cotangent = refs[:-14]
+    source, near_tokens, near_grad, normed, projected, d_attended, merged = refs[-14:-7]
+    ordered, terms, whole_first, whole_second, w_qkv, load_sems, store_sems = refs[-7:]
+    pieces = load_sems.shape[0]
+    loads = []
+    for piece in range(pieces):
+        count = w_qkv.shape[0] // pieces
+        part = pl.ds(piece * count, count)
+        loads.append(
+            pltpu.make_async_copy(w_far.at[part], w_qkv.at[part], load_sems.at[piece])
+        )
+        loads[-1].start()
     head_index = lax.axis_index("head")
     core = lax.rem(head_index, 2)
     heads = bias.shape[0]
@@ -308,21 +349,29 @@
     near_grad[...] = dot(shift_pick[...], source[...]).astype(BF16)
     scaled, _ = scaled_rows(near_tokens[...])
     normed[...] = (scaled * gain[...]).astype(BF16)
+    d_attended[...] = dot_rows(near_grad[...], w_out[...]).astype(BF16)
+    for load in loads:
+        load.wait()
     projected[...] = dot(normed[...], w_qkv[...]).astype(BF16)
-    d_attended[...] = dot_rows(near_grad[...], w_out[...]).astype(BF16)
     for window in range(WINDOWS):
         for head in range(heads):
             attend(window, head, projected, d_attended, bias, merged, group)
-    weight_terms(0, normed, near_grad, merged, whole)
+    weight_terms(0, normed, near_grad, merged, whole_first)
     lon, lon_count = lax.axis_index("lon"), len(by_lon)
     rows = by_lon[0].shape[0]
+    stores = []
     for step, block in enumerate(by_lon):
         start = pl.multiple_of(lax.rem(lon + step, lon_count) * rows, rows)
-        block[...] = whole[pl.ds(start, rows), :]
-    weight_terms(1, normed, near_grad, merged, whole)
+        source_rows = whole_first.at[pl.ds(start, rows)]
+        stores.append(pltpu.make_async_copy(source_rows, block, store_sems.at[step]))
+    for store in stores:
+        store.start()
+    weight_terms(1, normed, near_grad, merged, whole_second)
     parity = lax.rem(lax.axis_index("lat"), 2)
-    lat_rows(whole, lat_keep, lon_count, parity)
-    lat_rows(whole, lat_send, lon_count, 1 - parity)
+    late = lat_copies(whole_second, lat_keep, lon_count, parity, store_sems, lon_count)
+    late += lat_copies(whole_second, lat_send, lon_count, 1 - parity, store_sems, 3 * lon_count)
+    for store in late:
+        store.start()
     ordered[...] = dot(quarter[...], merged[...]).astype(BF16)
     terms[0] = dot(ordered[:, :group], w_out[...]).astype(BF16)
     terms[1] = dot_rows(ordered[:, group:], w_qkv[...]).astype(BF16)
@@ -338,6 +387,8 @@
     mine = quarter[pl.ds(pl.multiple_of(head_index * PART, 16), PART), :]
     part_tokens[...] = dot(mine, near_tokens[...]).astype(BF16)
     part_cotangent[...] = dot(mine, near_grad[...]).astype(BF16)
+    for store in stores + late:
+        store.wait()
 
 
 def cores_kernel(over, swapped, total):
@@ -353,7 +404,8 @@
 
 def second_step_kernel(lon_count, *refs):
     from_lon, (lat_keep, from_lat) = refs[:lon_count], refs[lon_count : lon_count + 2]
-    keep_first, send_first, *by_lon = refs[lon_count + 2 :]
+    keep_first, send_first, *by_lon, mark = refs[lon_count + 2 :]
+    mark[...] = jnp.zeros_like(mark)
     rows = keep_first.shape[0] // 2
     lon, parity = lax.axis_index("lon"), lax.rem(lax.axis_index("lat"), 2)
     for out, wanted in ((keep_first, parity), (send_first, 1 - parity)):
@@ -368,7 +420,8 @@
 
 
 def third_step_kernel(keep_first, from_lat, *refs):
-    from_lon, (keep, send) = refs[:-2], refs[-2:]
+    from_lon, (keep, send, mark) = refs[:-3], refs[-3:]
+    mark[...] = jnp.zeros_like(mark)
     rows = keep.shape[1]
     mine = lax.div(lax.axis_index("lat"), 2)
     for half, parts in enumerate(((keep_first, from_lat), from_lon)):
@@ -377,7 +430,8 @@
             out[half] = total_of([piece[part, :] for piece in parts]).astype(out.dtype)
 
 
-def finish_kernel(group, flip, keep, arrived, grad_qkv, grad_out):
+def finish_kernel(group, flip, keep, arrived, grad_qkv, grad_out, mark):
+    mark[...] = jnp.zeros_like(mark)
     for half in range(2):
         total = keep[half] + arrived[half].astype(F32)
         grad_qkv[:, half * 3 * group : (half + 1) * 3 * group] = total[:, : 3 * group]
@@ -403,6 +457,10 @@
             out[at] = rows[start : start + out.shape[1]]
 
 
+def pass_kernel(arrived, passed):
+    passed[...] = arrived[...]
+
+
 def join_kernel(pick, own, z_rows, x_rows, d_rows, joined, rows):
     for start, piece in zip(OUT_STARTS, (own, z_rows, x_rows, d_rows)):
         rows[:, start : start + piece.shape[1], :] = piece[...]
@@ -449,24 +507,32 @@
     flat_tokens = tokens.reshape(CELLS, width)
     flat_grad = cotangent.reshape(CELLS, width)
     gain = norm_gain.reshape(1, width)
+    mark = shaped(8, 128, dtype=F32)
     rims = call(
         pack_kernel,
         [shaped(RIM_Z, width), shaped(RIM_X, width), shaped(RIM_D, width)],
+        [pltpu.VMEM((CELLS, width), BF16), pltpu.SemaphoreType.DMA((6,))],
         cost=cost(2 * RIM * CELLS * width, 4 * CELLS * width),
         name="pack_rims",
-    )(one_hot(rim_source(), CELLS), flat_tokens, flat_grad)
+        far=tuple(
+            pltpu.with_memory_space_constraint(array, pltpu.HBM)
+            for array in (flat_tokens, flat_grad)
+        ),
+    )()
     arrived = [moved(rims[0], -1, 0), moved(rims[1], 0, -1), moved(rims[2], -1, -1)]
-    rim_here = jnp.concatenate(arrived, axis=0)
-    pairs = [(i, i ^ 1) for i in range(QUARTERS)]
-    rim_there = lax.ppermute(rim_here, "head", pairs)
     table = jnp.pad(bias_table.T, ((0, 0), (0, 1024 - bias_table.shape[0])))
-    bias = call(
+    bias, bias_mark = call(
         bias_kernel,
-        shaped(heads, WINDOW, WINDOW, dtype=F32),
+        [shaped(heads, WINDOW, WINDOW, dtype=F32), mark],
         [pltpu.VMEM((heads * 48, 768), BF16), pltpu.VMEM((heads, 576, WINDOW), BF16)],
         cost=cost(2 * 192 * 768 * 144 * 12 * 2, 1000000),
         name="window_bias",
     )(table, bias_columns(), bias_rows(), pole_mask())
+    rim_here = call(
+        rims_kernel, shaped(RIM, width), name="join_rims", cost=cost(0, 4 * RIM * width), after=(bias_mark,)
+    )(*arrived)
+    pairs = [(i, i ^ 1) for i in range(QUARTERS)]
+    rim_there = lax.ppermute(rim_here, "head", pairs)
     lon_rows = width // lon_count
     rows = lon_rows // lat_count
     columns = 2 * group
@@ -488,16 +554,22 @@
             pltpu.VMEM((QUARTERS * PART, 4 * group), BF16),
             pltpu.VMEM((2, QUARTERS * PART, width), BF16),
             pltpu.VMEM((width, columns), BF16),
+            pltpu.VMEM((width, columns), BF16),
+            pltpu.VMEM((width, 3 * group), BF16),
+            pltpu.SemaphoreType.DMA((4,)),
+            pltpu.SemaphoreType.DMA((5 * lon_count,)),
         ],
         cost=cost(6 * CELLS * width * width, 8000000),
         name="window_layer",
+        far=(w_qkv,),
+        far_outs=lon_count + 2,
+        limit=32,
     )(
         flat_tokens,
         flat_grad,
         rim_here,
         rim_there,
         gain,
-        w_qkv,
         w_out,
         bias,
         one_hot(shifted_source(), CELLS + RIM),
@@ -512,62 +584,64 @@
     )(over, swapped)
     chips = [(i, i ^ 2) for i in range(QUARTERS)]
     crossed = lax.ppermute(across, "head", chips)
+    keep_first, send_first, *by_lon, second_mark = call(
+        functools.partial(second_step_kernel, lon_count),
+        [shaped(2 * rows, columns, dtype=F32), shaped(2 * rows, columns)]
+        + [shaped(2 * rows, columns, dtype=F32)]
+        + [shaped(2 * rows, columns)] * (lon_count - 1)
+        + [mark],
+        cost=cost(4 * lon_rows * columns, 6 * lon_rows * columns),
+        name="second_step",
+    )(*from_lon, lat_keep, from_lat)
+    from_lat = lax.ppermute(send_first, "lat", neighbours)
+    from_lon = [by_lon[0]] + [rotated(by_lon[step], "lon", step) for step in range(1, lon_count)]
     pieces = call(
         norm_kernel,
         [shaped(2, count, width) for count in (OUT_OWN, OUT_Z, OUT_X, OUT_D)],
         cost=cost(2 * 2 * OUT_ROWS * PART * width, 12 * PART * width),
         name="sum_over_heads",
+        after=(second_mark,),
     )(part_tokens, part_cotangent, gain, group_pick(), stay, swapped, crossed)
     home = [pieces[0], moved(pieces[1], 1, 0), moved(pieces[2], 0, 1), moved(pieces[3], 1, 1)]
-    keep_first, send_first, *by_lon = call(
-        functools.partial(second_step_kernel, lon_count),
-        [shaped(2 * rows, columns, dtype=F32), shaped(2 * rows, columns)]
-        + [shaped(2 * rows, columns, dtype=F32)]
-        + [shaped(2 * rows, columns)] * (lon_count - 1),
-        cost=cost(4 * lon_rows * columns, 6 * lon_rows * columns),
-        name="second_step",
-        after=(pieces[0],),
-    )(*from_lon, lat_keep, from_lat)
-    from_lat = lax.ppermute(send_first, "lat", neighbours)
-    from_lon = [by_lon[0]] + [rotated(by_lon[step], "lon", step) for step in range(1, lon_count)]
+    keep, send, third_mark = call(
+        third_step_kernel,
+        [shaped(2, rows, columns, dtype=F32), shaped(2, rows, columns), mark],
+        cost=cost(4 * rows * columns, 6 * rows * columns),
+        name="third_step",
+    )(keep_first, from_lat, *from_lon)
+    last = lax.ppermute(send, "lat", [(i, i ^ 2) for i in range(lat_count)])
     mine = call(
         join_kernel,
         shaped(2, PART, width),
         [pltpu.VMEM((2, OUT_ROWS, width), BF16)],
         cost=cost(2 * 2 * OUT_ROWS * PART * width, 8 * OUT_ROWS * width),
         name="join_home",
-        after=(keep_first,),
+        after=(third_mark,),
     )(group_pick(), *home)
     far = lax.ppermute(mine, "head", chips)
     near = lax.ppermute(mine, "head", pairs)
-    keep, send = call(
-        third_step_kernel,
-        [shaped(2, rows, columns, dtype=F32), shaped(2, rows, columns)],
-        cost=cost(4 * rows * columns, 6 * rows * columns),
-        name="third_step",
-        after=(mine,),
-    )(keep_first, from_lat, *from_lon)
-    last = lax.ppermute(send, "lat", [(i, i ^ 2) for i in range(lat_count)])
-    beyond = lax.ppermute(far, "head", pairs)
+    flip = rows % 128 == 0
+    grad_qkv, grad_out, finish_mark = call(
+        functools.partial(finish_kernel, group // 2, flip),
+        [
+            shaped(rows, 3 * group, dtype=F32),
+            shaped(*((group, rows) if flip else (rows, group)), dtype=F32),
+            mark,
+        ],
+        cost=cost(4 * rows * 4 * group, 16 * rows * 4 * group),
+        name="sum_over_lat",
+    )(keep, last)
+    passed = call(
+        pass_kernel, shaped(2, PART, width), name="pass_on", after=(finish_mark,), cost=cost(0, 8 * PART * width)
+    )(far)
+    beyond = lax.ppermute(passed, "head", pairs)
     layer_out, grad_tokens = call(
         spread_kernel,
         [shaped(CELLS, width)] * 2,
         [pltpu.VMEM((2, QUARTERS * PART, width), BF16)],
         cost=cost(2 * 2 * CELLS * CELLS * width, 8 * CELLS * width),
         name="spread_outputs",
-        after=(keep,),
     )(own_pick(), mine, far, near, beyond)
-    flip = rows % 128 == 0
-    grad_qkv, grad_out = call(
-        functools.partial(finish_kernel, group // 2, flip),
-        [
-            shaped(rows, 3 * group, dtype=F32),
-            shaped(*((group, rows) if flip else (rows, group)), dtype=F32),
-        ],
-        cost=cost(4 * rows * 4 * group, 16 * rows * 4 * group),
-        name="sum_over_lat",
-        after=(layer_out,),
-    )(keep, last)
     return (
         layer_out.reshape(tokens.shape),
         grad_tokens.reshape(tokens.shape),

time: 78.8 us -> 77.2 us (0.980)
  waiting for transfers between devices: 34.2 us -> 31.7 us
  local copies, waits for them, and re-layouts: 5.02 us -> 3.26 us
  Pallas kernels: 17.3 us -> 18.7 us
  starting transfers between devices: 21.1 us -> 22.4 us
    ppermute x2, waiting for transfers between devices: 0.1 us -> 9.93 us  [rotated(): lax.ppermute(value, axis, [(i, (i + step) % count) for i in range(count)])]
    ppermute x1, waiting for transfers between devices: 8.47 us -> 0.01 us  [body(): crossed = lax.ppermute(across, 'head', chips)]
    ppermute x1, waiting for transfers between devices: 5.66 us -> 0.01 us  [body(): far = lax.ppermute(mine, 'head', chips)]
    ppermute x6, waiting for transfers between devices: 9.31 us -> 6.11 us  [moved(): return lax.ppermute(value, ('lon', 'lat'), pairs)]
    unnamed x36 -> x24, local copies, waits for them, and re-layouts: 5.01 us -> 2.55 us
    ppermute x1, waiting for transfers between devices: 0.01 us -> 1.76 us  [body(): rim_there = lax.ppermute(rim_here, 'head', pairs)]
    ppermute x1, starting transfers between devices: 1.69 us -> 0.01 us  [body(): last = lax.ppermute(send, 'lat', [(i, i ^ 2) for i in range(lat_count)])]
    pallas_call x10 -> x12, Pallas kernels: 17.3 us -> 18.7 us  [run(): pl.pallas_call(body, out_shape=outs, in_specs=[near] * len(args) + [outsi...]
  transfers between devices with their start and end apart: 17 -> 17, of which waited for: 8 -> 10; matrix products, arithmetic and copies ran while one was open for 0% -> 1% of each run, Pallas kernels for 6% -> 5%
where the time goes in v3:
time: 77.2 us; the launch traced here: 76.9 us
  waiting for transfers between devices  31.7 us (41%)
  starting transfers between devices  22.4 us (29%)
  Pallas kernels  18.7 us (24%)
  local copies, waits for them, and re-layouts  3.26 us (4%)
  between operations  0.78 us (1%)
    pallas_call x12, Pallas kernels, run(): pl.pallas_call(body, out_shape=outs, in_specs=[near] * len(args) + [outsi...  18.7 us
    ppermute x6, starting transfers between devices, moved(): return lax.ppermute(value, ('lon', 'lat'), pairs)  13.4 us
    ppermute x1, waiting for transfers between devices, body(): last = lax.ppermute(send, 'lat', [(i, i ^ 2) for i in range(lat_count)])  11.2 us
    ppermute x2, waiting for transfers between devices, rotated(): lax.ppermute(value, axis, [(i, (i + step) % count) for i in range(count)])  9.93 us
    ppermute x6, waiting for transfers between devices, moved(): return lax.ppermute(value, ('lon', 'lat'), pairs)  6.11 us
    unnamed x24, local copies, waits for them, and re-layouts  2.55 us
    ppermute x2, starting transfers between devices, rotated(): lax.ppermute(value, axis, [(i, (i + step) % count) for i in range(count)])  2.02 us
    ppermute x1, waiting for transfers between devices, body(): rim_there = lax.ppermute(rim_here, 'head', pairs)  1.76 us
  transfers between devices with their start and end apart: 17, of which 10 were waited for; matrix products, arithmetic and copies ran while one was open for 1% of the time, Pallas kernels for 5%

profile of v3, /device:TPU:0, one launch (start us, length us, event | category | flops | bytes accessed | tf_op | source)
XLA Modules:
  0.0 76.9 jit_solution(9543021411621238768)
XLA Ops:
  0.6 1.6 %pack_rims.1 = (bf16[112,1024]{1,0:T(8,128)(2,1)S(1)}, bf16[48,1024]{1,0:T(8,128)(2,1)S(1)}, bf16[48,1024]{1,0:T(8,128)(2,1)S(1)}) custom-call(bf16[288,1024]{1,0:T(8,128)(2,1)} %bitcast.6, bf16[288,1024]{1,0:T(8,128)(2,1)} %bitcast.8), custom_call_target="tpu_custom_call" | custom-call | flops 122683392 | bytes 1179648 | tf_op jit(solution)/shard_map/pack_rims/pallas_call | solution.py:168
  2.2 5.1 %collective-permute-start = (bf16[112,1024]{1,0:T(8,128)(2,1)S(1)}, bf16[112,1024]{1,0:T(8,128)(2,1)S(1)}, u32[]{:S(2)}, u32[]{:S(2)}) collective-permute-start(bf16[112,1024]{1,0:T(8,128)(2,1)S(1)} %get-tuple-element.35), channel_id=1, source_target_pairs={{0,12},{4,0},{8,4},{12,8},{16,28},{20,16},{24,20},{28,24},{1,13},{... | collective-permute-start | bytes 688136 | tf_op jit(solution)/shard_map/ppermute | solution.py:499
  7.3 1.5 %collective-permute-start.1 = (bf16[48,1024]{1,0:T(8,128)(2,1)S(1)}, bf16[48,1024]{1,0:T(8,128)(2,1)S(1)}, u32[]{:S(2)}, u32[]{:S(2)}) collective-permute-start(bf16[48,1024]{1,0:T(8,128)(2,1)S(1)} %get-tuple-element.36), channel_id=1, source_target_pairs={{0,16},{4,20},{8,24},{12,28},{16,0},{20,4},{24,8},{28,12},{1,17},{... | collective-permute-start | bytes 294920 | tf_op jit(solution)/shard_map/ppermute | solution.py:499
  8.8 0.4 collective-permute-start.2
  9.2 0.7 pad.4.refs_0_
  9.9 0.9 %copy-done.9 = bf16[144,576]{1,0:T(8,128)(2,1)S(1)} copy-done((bf16[144,576]{1,0:T(8,128)(2,1)S(1)}, bf16[144,576]{1,0:T(8,128)(2,1)}, u32[]{:S(2)}) %copy-start.9) | copy-done | bytes 165912
  10.9 0.9 %copy-done.10 = f32[144,144]{1,0:T(8,128)S(1)} copy-done((f32[144,144]{1,0:T(8,128)S(1)}, f32[144,144]{1,0:T(8,128)}, u32[]{:S(2)}) %copy-start.10) | copy-done | bytes 82968
  11.8 0.7 copy-done.11
  12.5 1.7 %window_bias.1 = (f32[4,144,144]{2,1,0:T(8,128)S(1)}, f32[8,128]{1,0:T(8,128)S(1)}) custom-call(f32[4,1024]{1,0:T(4,128)S(1)} %pad.4.refs_0_, s32[1,144]{1,0:T(1,128)S(1)} %copy-done.11, bf16[144,576]{1,0:T(8,128)(2,1)S(1)} %copy-done.9, f32[144,144]{1,0:T(8,128)S(1)} %copy-done.10), custom_call_target="tpu_custom_call" | custom-call | flops 1019215872 | bytes 1000000 | tf_op jit(solution)/shard_map/window_bias/pallas_call | solution.py:168
  14.4 1.8 %collective-permute-done.3.refs_3_ = bf16[208,1024]{1,0:T(8,128)(2,1)S(1)} collective-permute-done((bf16[208,1024]{1,0:T(8,128)(2,1)S(1)}, bf16[208,1024]{1,0:T(8,128)(2,1)S(1)}, u32[]{:S(2)}, u32[]{:S(2)}) %collective-permute-start.3) | collective-permute-done | bytes 426016 | tf_op jit(solution)/shard_map/ppermute | solution.py:535
  16.2 11.6 %window_layer.1 = (bf16[512,512]{1,0:T(8,128)(2,1)S(1)}, bf16[512,512]{1,0:T(8,128)(2,1)S(1)}, bf16[512,512]{1,0:T(8,128)(2,1)S(1)}, bf16[512,512]{1,0:T(8,128)(...) custom-call(bf16[288,1024]{1,0:T(8,128)(2,1)S(1)} %bitcast.7, ...), custom_call_target="tpu_custom_call" | custom-call | flops 1811939328 | bytes 8000000 | tf_op jit(solution)/shard_map/window_layer/pallas_call | solution.py:168
  28.0 1.5 %collective-permute-start.6 = (bf16[512,512]{1,0:T(8,128)(2,1)S(1)}, bf16[512,512]{1,0:T(8,128)(2,1)S(1)}, u32[]{:S(2)}, u32[]{:S(2)}) collective-permute-start(bf16[512,512]{1,0:T(8,128)(2,1)S(1)} %get-tuple-element.46), channel_id=1, source_target_pairs={{0,16},{16,0},{1,17},{17,1},{2,18},{18,2},{3,19},{19,3},{4,20},{20... | collective-permute-start | bytes 1572872 | tf_op jit(solution)/shard_map/ppermute | solution.py:489
  29.5 1.5 %collective-permute-start.7 = (bf16[512,512]{1,0:T(8,128)(2,1)S(1)}, bf16[512,512]{1,0:T(8,128)(2,1)S(1)}, u32[]{:S(2)}, u32[]{:S(2)}) collective-permute-start(bf16[512,512]{1,0:T(8,128)(2,1)S(1)} %get-tuple-element.48), channel_id=1, source_target_pairs={{0,4},{4,0},{8,12},{12,8},{1,5},{5,1},{9,13},{13,9},{2,6},{6,2},{1... | collective-permute-start | bytes 1572872 | tf_op jit(solution)/shard_map/ppermute | solution.py:580
  31.1 1.6 %collective-permute-start.5 = (bf16[2,80,1024]{2,1,0:T(8,128)(2,1)S(1)}, bf16[2,80,1024]{2,1,0:T(8,128)(2,1)S(1)}, u32[]{:S(2)}, u32[]{:S(2)}) collective-permute-start(bf16[2,80,1024]{2,1,0:T(8,128)(2,1)S(1)} %sum_over_cores.1), channel_id=1, source_target_pairs={{0,2},{1,3},{2,0},{3,1},{4,6},{5,7},{6,4},{7,5},{8,10},{9,11},{10,... | collective-permute-start | bytes 983048 | tf_op jit(solution)/shard_map/ppermute | solution.py:586
  32.7 9.6 %collective-permute-done.6.refs_1_ = bf16[512,512]{1,0:T(8,128)(2,1)S(1)} collective-permute-done((bf16[512,512]{1,0:T(8,128)(2,1)S(1)}, bf16[512,512]{1,0:T(8,128)(2,1)S(1)}, u32[]{:S(2)}, u32[]{:S(2)}) %collective-permute-start.6) | collective-permute-done | bytes 524320 | tf_op jit(solution)/shard_map/ppermute | solution.py:489
  42.2 1.2 %collective-permute-done.7.refs_3_ = bf16[512,512]{1,0:T(8,128)(2,1)S(1)} collective-permute-done((bf16[512,512]{1,0:T(8,128)(2,1)S(1)}, bf16[512,512]{1,0:T(8,128)(2,1)S(1)}, u32[]{:S(2)}, u32[]{:S(2)}) %collective-permute-start.7) | collective-permute-done | bytes 524320 | tf_op jit(solution)/shard_map/ppermute | solution.py:580
  43.7 1.6 %collective-permute-start.11 = (bf16[256,512]{1,0:T(8,128)(2,1)S(1)}, bf16[256,512]{1,0:T(8,128)(2,1)S(1)}, u32[]{:S(2)}, u32[]{:S(2)}) collective-permute-start(bf16[256,512]{1,0:T(8,128)(2,1)S(1)} %get-tuple-element.55), channel_id=1, source_target_pairs={{0,4},{4,0},{8,12},{12,8},{1,5},{5,1},{9,13},{13,9},{2,6},{6,2},{1... | collective-permute-start | bytes 786440 | tf_op jit(solution)/shard_map/ppermute | solution.py:596
  45.2 0.5 collective-permute-start.12
  45.7 0.6 sum_over_heads.1
  46.3 0.6 collective-permute-start.8
  47.0 1.5 %collective-permute-start.9 = (bf16[2,16,1024]{2,1,0:T(8,128)(2,1)S(1)}, bf16[2,16,1024]{2,1,0:T(8,128)(2,1)S(1)}, u32[]{:S(2)}, u32[]{:S(2)}) collective-permute-start(bf16[2,16,1024]{2,1,0:T(8,128)(2,1)S(1)} %get-tuple-element.52), channel_id=1, source_target_pairs={{0,16},{4,20},{8,24},{12,28},{16,0},{20,4},{24,8},{28,12},{1,17},{... | collective-permute-start | bytes 196616 | tf_op jit(solution)/shard_map/ppermute | solution.py:499
  48.4 4.3 %collective-permute-start.10 = (bf16[2,16,1024]{2,1,0:T(8,128)(2,1)S(1)}, bf16[2,16,1024]{2,1,0:T(8,128)(2,1)S(1)}, u32[]{:S(2)}, u32[]{:S(2)}) collective-permute-start(bf16[2,16,1024]{2,1,0:T(8,128)(2,1)S(1)} %get-tuple-element.53), channel_id=1, source_target_pairs={{0,20},{4,24},{8,28},{12,16},{16,4},{20,8},{24,12},{28,0},{1,21},{... | collective-permute-start | bytes 196616 | tf_op jit(solution)/shard_map/ppermute | solution.py:499
  52.7 0.4 collective-permute-done.12.refs_3_
  53.2 0.6 collective-permute-done.9.refs_3_
  53.8 5.4 %collective-permute-done.10.refs_4_ = bf16[2,16,1024]{2,1,0:T(8,128)(2,1)S(1)} collective-permute-done((bf16[2,16,1024]{2,1,0:T(8,128)(2,1)S(1)}, bf16[2,16,1024]{2,1,0:T(8,128)(2,1)S(1)}, u32[]{:S(2)}, u32[]{:S(2)}) %collective-permute-start.10) | collective-permute-done | bytes 65568 | tf_op jit(solution)/shard_map/ppermute | solution.py:499
  59.4 1.6 %collective-permute-start.13 = (bf16[2,80,1024]{2,1,0:T(8,128)(2,1)S(1)}, bf16[2,80,1024]{2,1,0:T(8,128)(2,1)S(1)}, u32[]{:S(2)}, u32[]{:S(2)}) collective-permute-start(bf16[2,80,1024]{2,1,0:T(8,128)(2,1)S(1)} %join_home.1.refs_1_), channel_id=1, source_target_pairs={{0,2},{1,3},{2,0},{3,1},{4,6},{5,7},{6,4},{7,5},{8,10},{9,11},{10,... | collective-permute-start | bytes 983048 | tf_op jit(solution)/shard_map/ppermute | solution.py:621
  61.0 11.2 %collective-permute-done.15.refs_1_ = bf16[2,128,512]{2,1,0:T(8,128)(2,1)S(1)} collective-permute-done((bf16[2,128,512]{2,1,0:T(8,128)(2,1)S(1)}, bf16[2,128,512]{2,1,0:T(8,128)(2,1)S(1)}, u32[]{:S(2)}, u32[]{:S(2)}) %collective-permute-start.15) | collective-permute-done | bytes 262176 | tf_op jit(solution)/shard_map/ppermute | solution.py:612
  72.2 0.8 %sum_over_lat.1 = (f32[128,768]{1,0:T(8,128)}, f32[256,128]{1,0:T(8,128)}, f32[8,128]{1,0:T(8,128)S(1)}) custom-call(f32[2,128,512]{2,1,0:T(8,128)S(1)} %get-tuple-element.59.refs_0_, bf16[2,128,512]{2,1,0:T(8,128)(2,1)S(1)} %collective-permute-done.15.refs_1_), custom_call_target="tpu_custom_call" | custom-call | flops 524288 | bytes 2097152 | tf_op jit(solution)/shard_map/sum_over_lat/pallas_call | solution.py:168
  73.1 0.6 collective-permute-start.16
  73.7 1.0 %collective-permute-done.14.refs_3_ = bf16[2,80,1024]{2,1,0:T(8,128)(2,1)S(1)} collective-permute-done((bf16[2,80,1024]{2,1,0:T(8,128)(2,1)S(1)}, bf16[2,80,1024]{2,1,0:T(8,128)(2,1)S(1)}, u32[]{:S(2)}, u32[]{:S(2)}) %collective-permute-start.14) | collective-permute-done | bytes 327712 | tf_op jit(solution)/shard_map/ppermute | solution.py:622
  74.7 0.5 collective-permute-done.16.refs_4_
  75.2 1.7 %spread_outputs.1 = (bf16[288,1024]{1,0:T(8,128)(2,1)}, bf16[288,1024]{1,0:T(8,128)(2,1)}) custom-call(bf16[288,320]{1,0:T(8,128)(2,1)S(1)} %copy-done.2, bf16[2,80,1024]{2,1,0:T(8,128)(2,1)S(1)} %join_home.1.refs_1_, bf16[2,80,1024]{2,1,0:T(8,128)(2,1)S(1)} %collective-permute-done.13.refs_0_.refs_2_, ...), custom_call_target="tpu_custom_call" | custom-call | flops 339738624 | bytes 2359296 | tf_op jit(solution)/shard_map/spread_outputs/pallas_call | solution.py:168
  (39 shorter events, 1.2 us)
Async XLA Ops:
  2.2 12.1 %collective-permute-start = (bf16[112,1024]{1,0:T(8,128)(2,1)S(1)}, bf16[112,1024]{1,0:T(8,128)(2,1)S(1)}, u32[]{:S(2)}, u32[]{:S(2)}) collective-permute-start(bf16[112,1024]{1,0:T(8,128)(2,1)S(1)} %get-tuple-element.35), channel_id=1, source_target_pairs={{0,12},{4,0},{8,4},{12,8},{16,28},{20,16},{24,20},{28,24},{1,13},{... | collective-permute-start | bytes 688136 | tf_op jit(solution)/shard_map/ppermute | solution.py:499
  7.3 6.8 %collective-permute-start.1 = (bf16[48,1024]{1,0:T(8,128)(2,1)S(1)}, bf16[48,1024]{1,0:T(8,128)(2,1)S(1)}, u32[]{:S(2)}, u32[]{:S(2)}) collective-permute-start(bf16[48,1024]{1,0:T(8,128)(2,1)S(1)} %get-tuple-element.36), channel_id=1, source_target_pairs={{0,16},{4,20},{8,24},{12,28},{16,0},{20,4},{24,8},{28,12},{1,17},{... | collective-permute-start | bytes 294920 | tf_op jit(solution)/shard_map/ppermute | solution.py:499
  8.8 5.5 %collective-permute-start.2 = (bf16[48,1024]{1,0:T(8,128)(2,1)S(1)}, bf16[48,1024]{1,0:T(8,128)(2,1)S(1)}, u32[]{:S(2)}, u32[]{:S(2)}) collective-permute-start(bf16[48,1024]{1,0:T(8,128)(2,1)S(1)} %get-tuple-element.37), channel_id=1, source_target_pairs={{0,28},{4,16},{8,20},{12,24},{16,12},{20,0},{24,4},{28,8},{1,29},{... | collective-permute-start | bytes 294920 | tf_op jit(solution)/shard_map/ppermute | solution.py:499
  9.9 0.9 %copy-start.9 = (bf16[144,576]{1,0:T(8,128)(2,1)S(1)}, bf16[144,576]{1,0:T(8,128)(2,1)}, u32[]{:S(2)}) copy-start(bf16[144,576]{1,0:T(8,128)(2,1)} %constant.18.clone.refs_2_) | copy-start | bytes 497668
  10.9 0.9 %copy-start.10 = (f32[144,144]{1,0:T(8,128)S(1)}, f32[144,144]{1,0:T(8,128)}, u32[]{:S(2)}) copy-start(f32[144,144]{1,0:T(8,128)} %constant.19.clone.refs_3_) | copy-start | bytes 248836
  11.8 0.7 copy-start.11
  12.5 3.7 %copy-start = (bf16[2,6,24,1024]{3,2,1,0:T(8,128)(2,1)S(1)}, bf16[2,6,24,1024]{3,2,1,0:T(8,128)(2,1)}, u32[]{:S(2)}) copy-start(bf16[2,6,24,1024]{3,2,1,0:T(8,128)(2,1)} %param.14) | copy-start | bytes 1769476
  12.5 3.7 %copy-start.1 = (bf16[2,6,24,1024]{3,2,1,0:T(8,128)(2,1)S(1)}, bf16[2,6,24,1024]{3,2,1,0:T(8,128)(2,1)}, u32[]{:S(2)}) copy-start(bf16[2,6,24,1024]{3,2,1,0:T(8,128)(2,1)} %param.19) | copy-start | bytes 1769476
  12.5 3.7 %copy-start.4 = (f32[1024]{0:T(1024)S(1)}, f32[1024]{0:T(1024)}, u32[]{:S(2)}) copy-start(f32[1024]{0:T(1024)} %param.15) | copy-start | bytes 12292
  12.5 3.7 %copy-start.5 = (bf16[1024,768]{1,0:T(8,128)(2,1)S(1)}, bf16[1024,768]{1,0:T(8,128)(2,1)}, u32[]{:S(2)}) copy-start(bf16[1024,768]{1,0:T(8,128)(2,1)} %refs_9_.1) | copy-start | bytes 4718596
  12.5 3.8 %copy-start.6 = (bf16[256,1024]{1,0:T(8,128)(2,1)S(1)}, bf16[256,1024]{1,0:T(8,128)(2,1)}, u32[]{:S(2)}) copy-start(bf16[256,1024]{1,0:T(8,128)(2,1)} %refs_5_.1) | copy-start | bytes 1572868
  12.5 3.8 %copy-start.7 = (bf16[288,496]{1,0:T(8,128)(2,1)S(1)}, bf16[288,496]{1,0:T(8,128)(2,1)}, u32[]{:S(2)}) copy-start(bf16[288,496]{1,0:T(8,128)(2,1)} %constant.20.clone.refs_7_) | copy-start | bytes 857092
  12.5 3.7 %copy-start.8 = (bf16[320,288]{1,0:T(8,128)(2,1)S(1)}, bf16[320,288]{1,0:T(8,128)(2,1)}, u32[]{:S(2)}) copy-start(bf16[320,288]{1,0:T(8,128)(2,1)} %constant.21.clone.refs_8_) | copy-start | bytes 552964
  14.4 1.8 %collective-permute-start.3 = (bf16[208,1024]{1,0:T(8,128)(2,1)S(1)}, bf16[208,1024]{1,0:T(8,128)(2,1)S(1)}, u32[]{:S(2)}, u32[]{:S(2)}) collective-permute-start(bf16[208,1024]{1,0:T(8,128)(2,1)S(1)} %join_rims.1.refs_2_), channel_id=1, source_target_pairs={{0,1},{1,0},{2,3},{3,2},{4,5},{5,4},{6,7},{7,6},{8,9},{9,8},{10,11... | collective-permute-start | bytes 1277960 | tf_op jit(solution)/shard_map/ppermute | solution.py:535
  27.8 3.2 %collective-permute-start.4 = (bf16[2,2,80,1024]{3,2,1,0:T(8,128)(2,1)S(1)}, bf16[2,2,80,1024]{3,2,1,0:T(8,128)(2,1)S(1)}, u32[]{:S(2)}, u32[]{:S(2)}) collective-permute-start(bf16[2,2,80,1024]{3,2,1,0:T(8,128)(2,1)S(1)} %get-tuple-element.43), channel_id=1, source_target_pairs={{0,1},{1,0},{2,3},{3,2},{4,5},{5,4},{6,7},{7,6},{8,9},{9,8},{10,11... | collective-permute-start | bytes 1966088 | tf_op jit(solution)/shard_map/ppermute | solution.py:581
  28.0 14.2 %collective-permute-start.6 = (bf16[512,512]{1,0:T(8,128)(2,1)S(1)}, bf16[512,512]{1,0:T(8,128)(2,1)S(1)}, u32[]{:S(2)}, u32[]{:S(2)}) collective-permute-start(bf16[512,512]{1,0:T(8,128)(2,1)S(1)} %get-tuple-element.46), channel_id=1, source_target_pairs={{0,16},{16,0},{1,17},{17,1},{2,18},{18,2},{3,19},{19,3},{4,20},{20... | collective-permute-start | bytes 1572872 | tf_op jit(solution)/shard_map/ppermute | solution.py:489
  29.5 13.9 %collective-permute-start.7 = (bf16[512,512]{1,0:T(8,128)(2,1)S(1)}, bf16[512,512]{1,0:T(8,128)(2,1)S(1)}, u32[]{:S(2)}, u32[]{:S(2)}) collective-permute-start(bf16[512,512]{1,0:T(8,128)(2,1)S(1)} %get-tuple-element.48), channel_id=1, source_target_pairs={{0,4},{4,0},{8,12},{12,8},{1,5},{5,1},{9,13},{13,9},{2,6},{6,2},{1... | collective-permute-start | bytes 1572872 | tf_op jit(solution)/shard_map/ppermute | solution.py:580
  31.0 14.7 %copy-start.3 = (bf16[96,80]{1,0:T(8,128)(2,1)S(1)}, bf16[96,80]{1,0:T(8,128)(2,1)}, u32[]{:S(2)}) copy-start(bf16[96,80]{1,0:T(8,128)(2,1)} %constant.22.clone.refs_3_.refs_0_) | copy-start | bytes 46084
  31.1 14.7 %collective-permute-start.5 = (bf16[2,80,1024]{2,1,0:T(8,128)(2,1)S(1)}, bf16[2,80,1024]{2,1,0:T(8,128)(2,1)S(1)}, u32[]{:S(2)}, u32[]{:S(2)}) collective-permute-start(bf16[2,80,1024]{2,1,0:T(8,128)(2,1)S(1)} %sum_over_cores.1), channel_id=1, source_target_pairs={{0,2},{1,3},{2,0},{3,1},{4,6},{5,7},{6,4},{7,5},{8,10},{9,11},{10,... | collective-permute-start | bytes 983048 | tf_op jit(solution)/shard_map/ppermute | solution.py:586
  43.7 9.1 %collective-permute-start.11 = (bf16[256,512]{1,0:T(8,128)(2,1)S(1)}, bf16[256,512]{1,0:T(8,128)(2,1)S(1)}, u32[]{:S(2)}, u32[]{:S(2)}) collective-permute-start(bf16[256,512]{1,0:T(8,128)(2,1)S(1)} %get-tuple-element.55), channel_id=1, source_target_pairs={{0,4},{4,0},{8,12},{12,8},{1,5},{5,1},{9,13},{13,9},{2,6},{6,2},{1... | collective-permute-start | bytes 786440 | tf_op jit(solution)/shard_map/ppermute | solution.py:596
  45.2 7.9 %collective-permute-start.12 = (bf16[256,512]{1,0:T(8,128)(2,1)S(1)}, bf16[256,512]{1,0:T(8,128)(2,1)S(1)}, u32[]{:S(2)}, u32[]{:S(2)}) collective-permute-start(bf16[256,512]{1,0:T(8,128)(2,1)S(1)} %get-tuple-element.57), channel_id=1, source_target_pairs={{0,16},{16,0},{1,17},{17,1},{2,18},{18,2},{3,19},{19,3},{4,20},{20... | collective-permute-start | bytes 786440 | tf_op jit(solution)/shard_map/ppermute | solution.py:489
  46.3 12.8 %collective-permute-start.8 = (bf16[2,32,1024]{2,1,0:T(8,128)(2,1)S(1)}, bf16[2,32,1024]{2,1,0:T(8,128)(2,1)S(1)}, u32[]{:S(2)}, u32[]{:S(2)}) collective-permute-start(bf16[2,32,1024]{2,1,0:T(8,128)(2,1)S(1)} %get-tuple-element.51), channel_id=1, source_target_pairs={{0,4},{4,8},{8,12},{12,0},{16,20},{20,24},{24,28},{28,16},{1,5},{5... | collective-permute-start | bytes 393224 | tf_op jit(solution)/shard_map/ppermute | solution.py:499
  47.0 6.8 %collective-permute-start.9 = (bf16[2,16,1024]{2,1,0:T(8,128)(2,1)S(1)}, bf16[2,16,1024]{2,1,0:T(8,128)(2,1)S(1)}, u32[]{:S(2)}, u32[]{:S(2)}) collective-permute-start(bf16[2,16,1024]{2,1,0:T(8,128)(2,1)S(1)} %get-tuple-element.52), channel_id=1, source_target_pairs={{0,16},{4,20},{8,24},{12,28},{16,0},{20,4},{24,8},{28,12},{1,17},{... | collective-permute-start | bytes 196616 | tf_op jit(solution)/shard_map/ppermute | solution.py:499
  48.4 10.7 %collective-permute-start.10 = (bf16[2,16,1024]{2,1,0:T(8,128)(2,1)S(1)}, bf16[2,16,1024]{2,1,0:T(8,128)(2,1)S(1)}, u32[]{:S(2)}, u32[]{:S(2)}) collective-permute-start(bf16[2,16,1024]{2,1,0:T(8,128)(2,1)S(1)} %get-tuple-element.53), channel_id=1, source_target_pairs={{0,20},{4,24},{8,28},{12,16},{16,4},{20,8},{24,12},{28,0},{1,21},{... | collective-permute-start | bytes 196616 | tf_op jit(solution)/shard_map/ppermute | solution.py:499
  53.1 22.1 %copy-start.2 = (bf16[288,320]{1,0:T(8,128)(2,1)S(1)}, bf16[288,320]{1,0:T(8,128)(2,1)}, u32[]{:S(2)}) copy-start(bf16[288,320]{1,0:T(8,128)(2,1)} %constant.23.clone.refs_0_) | copy-start | bytes 552964
  59.4 13.6 %collective-permute-start.13 = (bf16[2,80,1024]{2,1,0:T(8,128)(2,1)S(1)}, bf16[2,80,1024]{2,1,0:T(8,128)(2,1)S(1)}, u32[]{:S(2)}, u32[]{:S(2)}) collective-permute-start(bf16[2,80,1024]{2,1,0:T(8,128)(2,1)S(1)} %join_home.1.refs_1_), channel_id=1, source_target_pairs={{0,2},{1,3},{2,0},{3,1},{4,6},{5,7},{6,4},{7,5},{8,10},{9,11},{10,... | collective-permute-start | bytes 983048 | tf_op jit(solution)/shard_map/ppermute | solution.py:621
  61.0 11.2 %collective-permute-start.15 = (bf16[2,128,512]{2,1,0:T(8,128)(2,1)S(1)}, bf16[2,128,512]{2,1,0:T(8,128)(2,1)S(1)}, u32[]{:S(2)}, u32[]{:S(2)}) collective-permute-start(bf16[2,128,512]{2,1,0:T(8,128)(2,1)S(1)} %get-tuple-element.60), channel_id=1, source_target_pairs={{0,8},{4,12},{8,0},{12,4},{1,9},{5,13},{9,1},{13,5},{2,10},{6,14},... | collective-permute-start | bytes 786440 | tf_op jit(solution)/shard_map/ppermute | solution.py:612
  73.1 1.6 %collective-permute-start.14 = (bf16[2,80,1024]{2,1,0:T(8,128)(2,1)S(1)}, bf16[2,80,1024]{2,1,0:T(8,128)(2,1)S(1)}, u32[]{:S(2)}, u32[]{:S(2)}) collective-permute-start(bf16[2,80,1024]{2,1,0:T(8,128)(2,1)S(1)} %join_home.1.refs_1_), channel_id=1, source_target_pairs={{0,1},{1,0},{2,3},{3,2},{4,5},{5,4},{6,7},{7,6},{8,9},{9,8},{10,11... | collective-permute-start | bytes 983048 | tf_op jit(solution)/shard_map/ppermute | solution.py:622
  73.1 2.1 %collective-permute-start.16 = (bf16[2,80,1024]{2,1,0:T(8,128)(2,1)S(1)}, bf16[2,80,1024]{2,1,0:T(8,128)(2,1)S(1)}, u32[]{:S(2)}, u32[]{:S(2)}) collective-permute-start(bf16[2,80,1024]{2,1,0:T(8,128)(2,1)S(1)} %pass_on.1), channel_id=1, source_target_pairs={{0,1},{1,0},{2,3},{3,2},{4,5},{5,4},{6,7},{7,6},{8,9},{9,8},{10,11... | collective-permute-start | bytes 983048 | tf_op jit(solution)/shard_map/ppermute | solution.py:637

commit v4 on v3

--- a/solution.py
+++ b/solution.py
@@ -30,7 +30,7 @@
 RIM_Z, RIM_X, RIM_D = 112, 48, 48
 RIM = RIM_Z + RIM_X + RIM_D
 OUT_OWN, OUT_Z, OUT_X, OUT_D = 32, 32, 16, 16
-OUT_STARTS = (0, 32, 64, 80)
+OUT_STARTS = (0, 32, 64)
 OUT_ROWS = 96
 
 
@@ -115,32 +115,19 @@
     return one_hot([place[row] for row in range(CELLS)], QUARTERS * PART)
 
 
-def bias_rows():
-    rows = []
-    for window, level, lat, lon in CELL_LIST[:WINDOW]:
-        rows.append((level * WLAT + lat) * 16 + WLON - 1 - lon)
-    single = one_hot(rows, LEV * WLAT * 16)
-    return np.concatenate([single] * 3, axis=1)
-
-
-def bias_columns():
-    return np.array(
-        [
-            [
-                SPAN_LAT * SPAN_LON * (LEV - 1 - level)
-                + SPAN_LON * (WLAT - 1 - lat)
-                + 2 * (WLON - 1)
-                - lon
-                for _, level, lat, lon in CELL_LIST[:WINDOW]
-            ]
-        ],
-        np.int32,
-    )
-
-
-def pole_mask():
-    side = np.array([lat < MID_LAT for _, _, lat, _ in CELL_LIST[:WINDOW]])
-    return np.where(side[:, None] == side[None, :], 0.0, NEG_FILL).astype(np.float32)
+def window_position(shape, dim):
+    def count(value, size, parts):
+        return sum((value >= size * step).astype(jnp.int32) for step in range(1, parts))
+
+    cell = lax.broadcasted_iota(jnp.int32, shape, dim)
+    quarter = count(cell, WINDOW // QUARTERS, QUARTERS)
+    cell = cell - quarter * (WINDOW // QUARTERS)
+    lat = count(cell, 6, WLAT)
+    cell = cell - lat * 6
+    half = count(cell, 3, 2)
+    level = count(quarter, 2, 2)
+    lon = half * MID_LON + (quarter - 2 * level) * 3 + cell - half * 3
+    return level, lat, lon
 
 
 def dot(left, right):
@@ -229,12 +216,14 @@
     rim[RIM_Z + RIM_X :] = rim_d[...]
 
 
-def bias_kernel(table, columns, rows, mask, bias, mark, shifted, parts):
+def bias_kernel(table, bias, mark, padded, shifted, parts):
     mark[...] = jnp.zeros_like(mark)
     heads = bias.shape[0]
     width = shifted.shape[1]
+    padded[...] = jnp.zeros_like(padded)
+    padded[:heads, : table.shape[1]] = table[...]
     for head in range(heads):
-        spread = jnp.broadcast_to(table[head : head + 1, :], (16, table.shape[1]))
+        spread = jnp.broadcast_to(padded[head : head + 1, :], (16, padded.shape[1]))
         rolled = pltpu.roll(spread, 0, 1, stride=1, stride_axis=0)[:, :width]
         high = rolled.astype(BF16)
         rest = rolled - high.astype(F32)
@@ -244,10 +233,12 @@
             shifted[(head * 3 + split) * 16 : (head * 3 + split + 1) * 16, :] = value
     place = lax.broadcasted_iota(jnp.int32, (width, WINDOW), 0)
     count = LEV * WLAT * 16
+    level_of, lat_of, lon_of = window_position((1, WINDOW), 1)
+    plane = SPAN_LAT * SPAN_LON
+    column = plane * (level_of + LEV - 1) + SPAN_LON * (lat_of + WLAT - 1) + lon_of + WLON - 1
     for level in range(LEV):
         for lat in range(WLAT):
-            offset = SPAN_LAT * SPAN_LON * level + SPAN_LON * lat
-            wanted = (place == columns[...] + offset).astype(F32).astype(BF16)
+            wanted = (place == column - (plane * level + SPAN_LON * lat)).astype(F32).astype(BF16)
             block = dot(shifted[...], wanted).astype(BF16)
             start = (level * WLAT + lat) * 16
             for head in range(heads):
@@ -256,10 +247,16 @@
                     parts[head, split * count + start : split * count + start + 16, :] = block[
                         first : first + 16
                     ]
+    level_in, lat_in, lon_in = window_position((WINDOW, 1), 0)
+    lane = lax.broadcasted_iota(jnp.int32, (WINDOW, 3 * count), 1)
+    lane = lane - count * ((lane >= count).astype(jnp.int32) + (lane >= 2 * count).astype(jnp.int32))
+    rows = (lane == (level_in * WLAT + lat_in) * 16 + lon_in).astype(F32).astype(BF16)
     last = lax.axis_index("lat") == lax.axis_size("lat") - 1
-    added = jnp.where(last, mask[...], 0.0)
+    south_in = (lat_in < MID_LAT).astype(jnp.int32)
+    south_of = (lat_of < MID_LAT).astype(jnp.int32)
+    added = jnp.where((south_in != south_of) & last, NEG_FILL, 0.0)
     for head in range(heads):
-        bias[head] = dot(rows[...], parts[head]) + added
+        bias[head] = dot(rows, parts[head]) + added
 
 
 def scaled_rows(values):
@@ -269,45 +266,46 @@
     return center * inverse, inverse
 
 
-def attend(window, head, projected, d_attended, bias, merged, group):
+def attend(window, projected, d_attended, bias, merged, group):
     cells = slice(window * WINDOW, (window + 1) * WINDOW)
     scale = HEAD_DIM**-0.5
-    first = 3 * HEAD_DIM * head
-    query = projected[cells, first : first + HEAD_DIM] * jnp.asarray(scale, BF16)
-    key = projected[cells, first + HEAD_DIM : first + 2 * HEAD_DIM]
-    value = projected[cells, first + 2 * HEAD_DIM : first + 3 * HEAD_DIM]
-    grad = d_attended[cells, HEAD_DIM * head : HEAD_DIM * (head + 1)]
-    scores = dot_rows(query, key) + bias[head]
-    raised = jnp.exp(scores - jnp.max(scores, axis=-1, keepdims=True))
-    prob = raised * (1.0 / jnp.sum(raised, axis=-1, keepdims=True))
-    half = prob.astype(BF16)
-    grad_prob = dot_rows(grad, value)
-    row_term = jnp.sum(prob * grad_prob, axis=-1, keepdims=True)
-    grad_score = (prob * (grad_prob - row_term)).astype(BF16)
-    attended = dot(half, value)
-    grad_query = dot(grad_score, key) * scale
-    grad_key = dot_columns(grad_score, query)
-    grad_value = dot_columns(half, grad)
-    merged[cells, HEAD_DIM * head : HEAD_DIM * (head + 1)] = attended.astype(BF16)
-    merged[cells, group + first : group + first + 3 * HEAD_DIM] = jnp.concatenate(
-        [grad_query, grad_key, grad_value], axis=1
-    ).astype(BF16)
-
-
-def weight_terms(half, normed, near_grad, merged, whole):
-    group = merged.shape[1] // 8
-    attended = slice(half * group, (half + 1) * group)
-    d_qkv = slice((2 + 3 * half) * group, (5 + 3 * half) * group)
-    whole[:, : 3 * group] = dot_columns(normed[...], merged[:, d_qkv]).astype(BF16)
-    whole[:, 3 * group :] = dot_columns(near_grad[...], merged[:, attended]).astype(BF16)
-
-
-def lat_copies(whole, out, lon_count, parity, sems, first):
+    heads = range(bias.shape[0])
+
+    def part(head, kind):
+        first = (3 * head + kind) * HEAD_DIM
+        return projected[cells, first : first + HEAD_DIM]
+
+    queries = [part(head, 0) * jnp.asarray(scale, BF16) for head in heads]
+    keys = [part(head, 1) for head in heads]
+    values = [part(head, 2) for head in heads]
+    grads = [d_attended[cells, HEAD_DIM * head : HEAD_DIM * (head + 1)] for head in heads]
+    scores = [dot_rows(keys[head], queries[head]) + bias[head] for head in heads]
+    grad_probs = [dot_rows(values[head], grads[head]) for head in heads]
+    halves, grad_scores = [], []
+    for head in heads:
+        raised = jnp.exp(scores[head] - jnp.max(scores[head], axis=0, keepdims=True))
+        prob = raised * (1.0 / jnp.sum(raised, axis=0, keepdims=True))
+        row_term = jnp.sum(prob * grad_probs[head], axis=0, keepdims=True)
+        halves.append(prob.astype(BF16))
+        grad_scores.append((prob * (grad_probs[head] - row_term)).astype(BF16))
+    for head in heads:
+        attended = dot_columns(halves[head], values[head])
+        grad_value = dot(halves[head], grads[head])
+        grad_query = dot_columns(grad_scores[head], keys[head]) * scale
+        grad_key = dot(grad_scores[head], queries[head])
+        merged[cells, HEAD_DIM * head : HEAD_DIM * (head + 1)] = attended.astype(BF16)
+        first = group + 3 * HEAD_DIM * head
+        merged[cells, first : first + 3 * HEAD_DIM] = jnp.concatenate(
+            [grad_query, grad_key, grad_value], axis=1
+        ).astype(BF16)
+
+
+def lat_copies(whole, columns, out, lon_count, parity, sems, first):
     rows = whole.shape[0] // (4 * lon_count)
     copies = []
     for block in range(2 * lon_count):
         start = pl.multiple_of((2 * block + parity) * rows, rows)
-        source, target = whole.at[pl.ds(start, rows)], out.at[pl.ds(block * rows, rows)]
+        source, target = whole.at[pl.ds(start, rows), columns], out.at[pl.ds(block * rows, rows)]
         copies.append(pltpu.make_async_copy(source, target, sems.at[first + block]))
     return copies
 
@@ -325,9 +323,9 @@
     w_far,
     *refs,
 ):
-    *by_lon, lat_keep, lat_send, stay, over, swap, part_tokens, part_cotangent = refs[:-14]
-    source, near_tokens, near_grad, normed, projected, d_attended, merged = refs[-14:-7]
-    ordered, terms, whole_first, whole_second, w_qkv, load_sems, store_sems = refs[-7:]
+    *by_lon, lat_keep, lat_send, stay, over, swap, part_tokens, part_cotangent = refs[:-13]
+    source, near_tokens, near_grad, normed, projected, d_attended, merged = refs[-13:-6]
+    ordered, terms, whole, w_qkv, load_sems, store_sems = refs[-6:]
     pieces = load_sems.shape[0]
     loads = []
     for piece in range(pieces):
@@ -354,23 +352,21 @@
         load.wait()
     projected[...] = dot(normed[...], w_qkv[...]).astype(BF16)
     for window in range(WINDOWS):
-        for head in range(heads):
-            attend(window, head, projected, d_attended, bias, merged, group)
-    weight_terms(0, normed, near_grad, merged, whole_first)
+        attend(window, projected, d_attended, bias, merged, group)
+    whole[:, : 3 * group] = dot_columns(normed[...], merged[:, group:]).astype(BF16)
+    whole[:, 3 * group :] = dot_columns(near_grad[...], merged[:, :group]).astype(BF16)
     lon, lon_count = lax.axis_index("lon"), len(by_lon)
     rows = by_lon[0].shape[0]
     stores = []
     for step, block in enumerate(by_lon):
         start = pl.multiple_of(lax.rem(lon + step, lon_count) * rows, rows)
-        source_rows = whole_first.at[pl.ds(start, rows)]
+        source_rows = whole.at[pl.ds(start, rows), pl.ds(0, 2 * group)]
         stores.append(pltpu.make_async_copy(source_rows, block, store_sems.at[step]))
+    parity = lax.rem(lax.axis_index("lat"), 2)
+    later = pl.ds(2 * group, 2 * group)
+    stores += lat_copies(whole, later, lat_keep, lon_count, parity, store_sems, lon_count)
+    stores += lat_copies(whole, later, lat_send, lon_count, 1 - parity, store_sems, 3 * lon_count)
     for store in stores:
-        store.start()
-    weight_terms(1, normed, near_grad, merged, whole_second)
-    parity = lax.rem(lax.axis_index("lat"), 2)
-    late = lat_copies(whole_second, lat_keep, lon_count, parity, store_sems, lon_count)
-    late += lat_copies(whole_second, lat_send, lon_count, 1 - parity, store_sems, 3 * lon_count)
-    for store in late:
         store.start()
     ordered[...] = dot(quarter[...], merged[...]).astype(BF16)
     terms[0] = dot(ordered[:, :group], w_out[...]).astype(BF16)
@@ -387,7 +383,7 @@
     mine = quarter[pl.ds(pl.multiple_of(head_index * PART, 16), PART), :]
     part_tokens[...] = dot(mine, near_tokens[...]).astype(BF16)
     part_cotangent[...] = dot(mine, near_grad[...]).astype(BF16)
-    for store in stores + late:
+    for store in stores:
         store.wait()
 
 
@@ -404,8 +400,7 @@
 
 def second_step_kernel(lon_count, *refs):
     from_lon, (lat_keep, from_lat) = refs[:lon_count], refs[lon_count : lon_count + 2]
-    keep_first, send_first, *by_lon, mark = refs[lon_count + 2 :]
-    mark[...] = jnp.zeros_like(mark)
+    keep_first, send_first, *by_lon = refs[lon_count + 2 :]
     rows = keep_first.shape[0] // 2
     lon, parity = lax.axis_index("lon"), lax.rem(lax.axis_index("lat"), 2)
     for out, wanted in ((keep_first, parity), (send_first, 1 - parity)):
@@ -420,8 +415,7 @@
 
 
 def third_step_kernel(keep_first, from_lat, *refs):
-    from_lon, (keep, send, mark) = refs[:-3], refs[-3:]
-    mark[...] = jnp.zeros_like(mark)
+    from_lon, (keep, send) = refs[:-2], refs[-2:]
     rows = keep.shape[1]
     mine = lax.div(lax.axis_index("lat"), 2)
     for half, parts in enumerate(((keep_first, from_lat), from_lon)):
@@ -430,16 +424,12 @@
             out[half] = total_of([piece[part, :] for piece in parts]).astype(out.dtype)
 
 
-def finish_kernel(group, flip, keep, arrived, grad_qkv, grad_out, mark):
-    mark[...] = jnp.zeros_like(mark)
-    for half in range(2):
-        total = keep[half] + arrived[half].astype(F32)
-        grad_qkv[:, half * 3 * group : (half + 1) * 3 * group] = total[:, : 3 * group]
-        out = total[:, 3 * group :]
-        if flip:
-            grad_out[half * group : (half + 1) * group, :] = out.T
-        else:
-            grad_out[:, half * group : (half + 1) * group] = out
+def finish_kernel(group, flip, keep, arrived, grad_qkv, grad_out):
+    grad_qkv[:, : 2 * group] = keep[0] + arrived[0].astype(F32)
+    total = keep[1] + arrived[1].astype(F32)
+    grad_qkv[:, 2 * group :] = total[:, :group]
+    out = total[:, group:]
+    grad_out[...] = out.T if flip else out
 
 
 def norm_kernel(part_tokens, part_cotangent, gain, pick, stay, swapped, crossed, *outs):
@@ -457,27 +447,39 @@
             out[at] = rows[start : start + out.shape[1]]
 
 
-def pass_kernel(arrived, passed):
-    passed[...] = arrived[...]
-
-
-def join_kernel(pick, own, z_rows, x_rows, d_rows, joined, rows):
-    for start, piece in zip(OUT_STARTS, (own, z_rows, x_rows, d_rows)):
-        rows[:, start : start + piece.shape[1], :] = piece[...]
-    for at in range(2):
-        joined[at] = dot_columns(pick[...], rows[at]).astype(BF16)
-
-
-def spread_kernel(pick, mine, far, near, across, layer_out, grad_tokens, gathered):
+def north_kernel(z_rows, x_rows, rows, mark):
+    mark[...] = jnp.zeros_like(mark)
+    rows[:, :OUT_Z, :] = z_rows[...]
+    rows[:, OUT_Z:, :] = x_rows[:, OUT_X:, :]
+
+
+def join_kernel(pick, own, z_rows, x_rows, joined, layer, grad, mark, rows):
+    mark[...] = jnp.zeros_like(mark)
+    rows[:, :OUT_OWN, :] = own[...]
+    rows[:, OUT_OWN : OUT_OWN + OUT_Z, :] = z_rows[:, :OUT_Z, :]
+    rows[:, OUT_OWN + OUT_Z : OUT_ROWS - OUT_D, :] = x_rows[:, :OUT_X, :]
+    rows[:, OUT_ROWS - OUT_D :, :] = z_rows[:, OUT_Z:, :]
+    for at, single in enumerate((layer, grad)):
+        single[...] = dot_columns(pick[...], rows[at]).astype(BF16)
+        joined[at] = single[...]
+
+
+def spread_kernel(pick, mine, near, *refs):
+    far, across, outs, (mark, gathered) = refs[:2], refs[2:4], refs[4:6], refs[6:]
+    mark[...] = jnp.zeros_like(mark)
     head_index = lax.axis_index("head")
     sibling = 1 - 2 * lax.rem(head_index, 2)
     over = lax.rem(head_index + 2, QUARTERS)
-    owners = (head_index, over, head_index + sibling, over + sibling)
-    for owner, piece in zip(owners, (mine, far, near, across)):
-        at = pl.ds(pl.multiple_of(owner * PART, 16), PART)
-        gathered[:, at, :] = piece[...]
-    layer_out[...] = dot(pick[...], gathered[0]).astype(BF16)
-    grad_tokens[...] = dot(pick[...], gathered[1]).astype(BF16)
+
+    def place(owner):
+        return pl.ds(pl.multiple_of(owner * PART, 16), PART)
+
+    for at, out in enumerate(outs):
+        gathered[at, place(head_index), :] = mine[at]
+        gathered[at, place(head_index + sibling), :] = near[at]
+        gathered[at, place(over), :] = far[at][...]
+        gathered[at, place(over + sibling), :] = across[at][...]
+        out[...] = dot(pick[...], gathered[at]).astype(BF16)
 
 
 def shaped(*shape, dtype=BF16):
@@ -520,14 +522,17 @@
         ),
     )()
     arrived = [moved(rims[0], -1, 0), moved(rims[1], 0, -1), moved(rims[2], -1, -1)]
-    table = jnp.pad(bias_table.T, ((0, 0), (0, 1024 - bias_table.shape[0])))
     bias, bias_mark = call(
         bias_kernel,
         [shaped(heads, WINDOW, WINDOW, dtype=F32), mark],
-        [pltpu.VMEM((heads * 48, 768), BF16), pltpu.VMEM((heads, 576, WINDOW), BF16)],
+        [
+            pltpu.VMEM((8, 1024), F32),
+            pltpu.VMEM((heads * 48, 768), BF16),
+            pltpu.VMEM((heads, 576, WINDOW), BF16),
+        ],
         cost=cost(2 * 192 * 768 * 144 * 12 * 2, 1000000),
         name="window_bias",
-    )(table, bias_columns(), bias_rows(), pole_mask())
+    )(bias_table.T)
     rim_here = call(
         rims_kernel, shaped(RIM, width), name="join_rims", cost=cost(0, 4 * RIM * width), after=(bias_mark,)
     )(*arrived)
@@ -553,8 +558,7 @@
             pltpu.VMEM((CELLS, 4 * group), BF16),
             pltpu.VMEM((QUARTERS * PART, 4 * group), BF16),
             pltpu.VMEM((2, QUARTERS * PART, width), BF16),
-            pltpu.VMEM((width, columns), BF16),
-            pltpu.VMEM((width, columns), BF16),
+            pltpu.VMEM((width, 4 * group), BF16),
             pltpu.VMEM((width, 3 * group), BF16),
             pltpu.SemaphoreType.DMA((4,)),
             pltpu.SemaphoreType.DMA((5 * lon_count,)),
@@ -584,64 +588,67 @@
     )(over, swapped)
     chips = [(i, i ^ 2) for i in range(QUARTERS)]
     crossed = lax.ppermute(across, "head", chips)
-    keep_first, send_first, *by_lon, second_mark = call(
+    pieces = call(
+        norm_kernel,
+        [shaped(2, count, width) for count in (OUT_OWN, OUT_Z, OUT_X + OUT_D)],
+        cost=cost(2 * 2 * OUT_ROWS * PART * width, 12 * PART * width),
+        name="sum_over_heads",
+    )(part_tokens, part_cotangent, gain, group_pick(), stay, swapped, crossed)
+    from_west = rotated(pieces[2], "lon", 1)
+    to_north, north_mark = call(
+        north_kernel,
+        [shaped(2, OUT_Z + OUT_D, width), mark],
+        cost=cost(0, 8 * (OUT_Z + OUT_D) * width),
+        name="rows_for_north",
+    )(pieces[1], from_west)
+    home = [pieces[0], rotated(to_north, "lat", 1), from_west]
+    keep_first, send_first, *by_lon = call(
         functools.partial(second_step_kernel, lon_count),
         [shaped(2 * rows, columns, dtype=F32), shaped(2 * rows, columns)]
         + [shaped(2 * rows, columns, dtype=F32)]
-        + [shaped(2 * rows, columns)] * (lon_count - 1)
-        + [mark],
+        + [shaped(2 * rows, columns)] * (lon_count - 1),
         cost=cost(4 * lon_rows * columns, 6 * lon_rows * columns),
         name="second_step",
+        after=(north_mark,),
     )(*from_lon, lat_keep, from_lat)
     from_lat = lax.ppermute(send_first, "lat", neighbours)
     from_lon = [by_lon[0]] + [rotated(by_lon[step], "lon", step) for step in range(1, lon_count)]
-    pieces = call(
-        norm_kernel,
-        [shaped(2, count, width) for count in (OUT_OWN, OUT_Z, OUT_X, OUT_D)],
-        cost=cost(2 * 2 * OUT_ROWS * PART * width, 12 * PART * width),
-        name="sum_over_heads",
-        after=(second_mark,),
-    )(part_tokens, part_cotangent, gain, group_pick(), stay, swapped, crossed)
-    home = [pieces[0], moved(pieces[1], 1, 0), moved(pieces[2], 0, 1), moved(pieces[3], 1, 1)]
-    keep, send, third_mark = call(
-        third_step_kernel,
-        [shaped(2, rows, columns, dtype=F32), shaped(2, rows, columns), mark],
-        cost=cost(4 * rows * columns, 6 * rows * columns),
-        name="third_step",
-    )(keep_first, from_lat, *from_lon)
-    last = lax.ppermute(send, "lat", [(i, i ^ 2) for i in range(lat_count)])
-    mine = call(
+    mine, *each, join_mark = call(
         join_kernel,
-        shaped(2, PART, width),
+        [shaped(2, PART, width)] + [shaped(PART, width)] * 2 + [mark],
         [pltpu.VMEM((2, OUT_ROWS, width), BF16)],
         cost=cost(2 * 2 * OUT_ROWS * PART * width, 8 * OUT_ROWS * width),
         name="join_home",
-        after=(third_mark,),
     )(group_pick(), *home)
-    far = lax.ppermute(mine, "head", chips)
+    keep, send = call(
+        third_step_kernel,
+        [shaped(2, rows, columns, dtype=F32), shaped(2, rows, columns)],
+        cost=cost(4 * rows * columns, 6 * rows * columns),
+        name="third_step",
+        after=(join_mark,),
+    )(keep_first, from_lat, *from_lon)
+    last = lax.ppermute(send, "lat", [(i, i ^ 2) for i in range(lat_count)])
+    far = [lax.ppermute(single, "head", chips) for single in each]
     near = lax.ppermute(mine, "head", pairs)
+    across = [lax.ppermute(single, "head", pairs) for single in far]
+    layer_out, grad_tokens, spread_mark = call(
+        spread_kernel,
+        [shaped(CELLS, width)] * 2 + [mark],
+        [pltpu.VMEM((2, QUARTERS * PART, width), BF16)],
+        cost=cost(2 * 2 * CELLS * CELLS * width, 8 * CELLS * width),
+        name="spread_outputs",
+    )(own_pick(), mine, near, *far, *across)
     flip = rows % 128 == 0
-    grad_qkv, grad_out, finish_mark = call(
-        functools.partial(finish_kernel, group // 2, flip),
+    grad_qkv, grad_out = call(
+        functools.partial(finish_kernel, group, flip),
         [
             shaped(rows, 3 * group, dtype=F32),
             shaped(*((group, rows) if flip else (rows, group)), dtype=F32),
-            mark,
         ],
         cost=cost(4 * rows * 4 * group, 16 * rows * 4 * group),
         name="sum_over_lat",
+        after=(spread_mark,),
     )(keep, last)
-    passed = call(
-        pass_kernel, shaped(2, PART, width), name="pass_on", after=(finish_mark,), cost=cost(0, 8 * PART * width)
-    )(far)
-    beyond = lax.ppermute(passed, "head", pairs)
-    layer_out, grad_tokens = call(
-        spread_kernel,
-        [shaped(CELLS, width)] * 2,
-        [pltpu.VMEM((2, QUARTERS * PART, width), BF16)],
-        cost=cost(2 * 2 * CELLS * CELLS * width, 8 * CELLS * width),
-        name="spread_outputs",
-    )(own_pick(), mine, far, near, beyond)
     return (
         layer_out.reshape(tokens.shape),
         grad_tokens.reshape(tokens.shape),

time: 77.2 us -> 70.6 us (0.915)
  Pallas kernels: 18.7 us -> 15.1 us
  local copies, waits for them, and re-layouts: 3.26 us -> 0.75 us
    ppermute x1, waiting for transfers between devices: 0.01 us -> 8.23 us  [body(): crossed = lax.ppermute(across, 'head', chips)]
    ppermute x1, waiting for transfers between devices: 11.2 us -> 4.56 us  [body(): last = lax.ppermute(send, 'lat', [(i, i ^ 2) for i in range(lat_count)])]
    ppermute x6 -> x3, starting transfers between devices: 13.4 us -> 7 us  [moved(): return lax.ppermute(value, ('lon', 'lat'), pairs)]
    ppermute x2 -> x4, waiting for transfers between devices: 0.47 us -> 6.79 us  [the longest x2 5.41 us: body(): far = [lax.ppermute(single, 'head', chips) for single in each]]
    ppermute x2 -> x4, starting transfers between devices: 2.02 us -> 5.86 us  [rotated(): lax.ppermute(value, axis, [(i, (i + step) % count) for i in range(count)])]
    ppermute x6 -> x3, waiting for transfers between devices: 6.11 us -> 2.36 us  [moved(): return lax.ppermute(value, ('lon', 'lat'), pairs)]
    pallas_call x12, Pallas kernels: 18.7 us -> 15.1 us  [run(): pl.pallas_call(body, out_shape=outs, in_specs=[near] * len(args) + [outsi...]
    unnamed x24 -> x20, local copies, waits for them, and re-layouts: 2.55 us -> 0.75 us
  transfers between devices with their start and end apart: 17 -> 18, of which waited for: 10 -> 11; matrix products, arithmetic and copies ran while one was open for 1% -> 0% of each run, Pallas kernels for 5% -> 7%
where the time goes in v4:
time: 70.6 us; the launch traced here: 70.4 us
  waiting for transfers between devices  31.9 us (45%)
  starting transfers between devices  21.8 us (31%)
  Pallas kernels  15.1 us (21%)
  between operations  0.79 us (1%)
  local copies, waits for them, and re-layouts  0.75 us (1%)
    pallas_call x12, Pallas kernels, run(): pl.pallas_call(body, out_shape=outs, in_specs=[near] * len(args) + [outsi...  15.1 us
    ppermute x1, waiting for transfers between devices, body(): crossed = lax.ppermute(across, 'head', chips)  8.23 us
    ppermute x4, waiting for transfers between devices, rotated(): lax.ppermute(value, axis, [(i, (i + step) % count) for i in range(count)])  8.15 us
    ppermute x3, starting transfers between devices, moved(): return lax.ppermute(value, ('lon', 'lat'), pairs)  7 us
    ppermute x4, starting transfers between devices, rotated(): lax.ppermute(value, axis, [(i, (i + step) % count) for i in range(count)])  5.86 us
    ppermute x2, waiting for transfers between devices, body(): far = [lax.ppermute(single, 'head', chips) for single in each]  5.41 us
    ppermute x1, waiting for transfers between devices, body(): last = lax.ppermute(send, 'lat', [(i, i ^ 2) for i in range(lat_count)])  4.56 us
    ppermute x1, starting transfers between devices, body(): from_lat = lax.ppermute(send_first, 'lat', neighbours)  3.26 us
  transfers between devices with their start and end apart: 18, of which 11 were waited for; matrix products, arithmetic and copies ran while one was open for 0% of the time, Pallas kernels for 7%

profile of v4, /device:TPU:0, one launch (start us, length us, event | category | flops | bytes accessed | tf_op | source)
XLA Modules:
  0.0 70.4 jit_solution(18036565099654609659)
XLA Ops:
  0.6 1.6 %pack_rims.1 = (bf16[112,1024]{1,0:T(8,128)(2,1)S(1)}, bf16[48,1024]{1,0:T(8,128)(2,1)S(1)}, bf16[48,1024]{1,0:T(8,128)(2,1)S(1)}) custom-call(bf16[288,1024]{1,0:T(8,128)(2,1)} %bitcast.6, bf16[288,1024]{1,0:T(8,128)(2,1)} %bitcast.8), custom_call_target="tpu_custom_call" | custom-call | flops 122683392 | bytes 1179648 | tf_op jit(solution)/shard_map/pack_rims/pallas_call | solution.py:155
  2.2 5.1 %collective-permute-start = (bf16[112,1024]{1,0:T(8,128)(2,1)S(1)}, bf16[112,1024]{1,0:T(8,128)(2,1)S(1)}, u32[]{:S(2)}, u32[]{:S(2)}) collective-permute-start(bf16[112,1024]{1,0:T(8,128)(2,1)S(1)} %get-tuple-element.38), channel_id=1, source_target_pairs={{0,12},{4,0},{8,4},{12,8},{16,28},{20,16},{24,20},{28,24},{1,13},{... | collective-permute-start | bytes 688136 | tf_op jit(solution)/shard_map/ppermute | solution.py:501
  7.3 1.5 %collective-permute-start.1 = (bf16[48,1024]{1,0:T(8,128)(2,1)S(1)}, bf16[48,1024]{1,0:T(8,128)(2,1)S(1)}, u32[]{:S(2)}, u32[]{:S(2)}) collective-permute-start(bf16[48,1024]{1,0:T(8,128)(2,1)S(1)} %get-tuple-element.39), channel_id=1, source_target_pairs={{0,16},{4,20},{8,24},{12,28},{16,0},{20,4},{24,8},{28,12},{1,17},{... | collective-permute-start | bytes 294920 | tf_op jit(solution)/shard_map/ppermute | solution.py:501
  8.8 0.4 collective-permute-start.2
  9.2 0.7 %copy-done.7 = f32[759,4]{0,1:T(4,128)S(1)} copy-done((f32[759,4]{0,1:T(4,128)S(1)}, f32[759,4]{0,1:T(4,128)}, u32[]{:S(2)}) %copy-start.7) | copy-done | bytes 12168
  10.0 2.0 %window_bias.1 = (f32[4,144,144]{2,1,0:T(8,128)S(1)}, f32[8,128]{1,0:T(8,128)S(1)}) custom-call(f32[4,759]{1,0:T(4,128)S(1)} %bitcast.12), custom_call_target="tpu_custom_call" | custom-call | flops 1019215872 | bytes 1000000 | tf_op jit(solution)/shard_map/window_bias/pallas_call | solution.py:155
  12.0 1.0 %collective-permute-done.1.refs_1_ = bf16[48,1024]{1,0:T(8,128)(2,1)S(1)} collective-permute-done((bf16[48,1024]{1,0:T(8,128)(2,1)S(1)}, bf16[48,1024]{1,0:T(8,128)(2,1)S(1)}, u32[]{:S(2)}, u32[]{:S(2)}) %collective-permute-start.1) | collective-permute-done | bytes 98336 | tf_op jit(solution)/shard_map/ppermute | solution.py:501
  13.0 1.3 %collective-permute-done.2.refs_2_ = bf16[48,1024]{1,0:T(8,128)(2,1)S(1)} collective-permute-done((bf16[48,1024]{1,0:T(8,128)(2,1)S(1)}, bf16[48,1024]{1,0:T(8,128)(2,1)S(1)}, u32[]{:S(2)}, u32[]{:S(2)}) %collective-permute-start.2) | collective-permute-done | bytes 98336 | tf_op jit(solution)/shard_map/ppermute | solution.py:501
  14.4 1.8 %collective-permute-done.3.refs_3_ = bf16[208,1024]{1,0:T(8,128)(2,1)S(1)} collective-permute-done((bf16[208,1024]{1,0:T(8,128)(2,1)S(1)}, bf16[208,1024]{1,0:T(8,128)(2,1)S(1)}, u32[]{:S(2)}, u32[]{:S(2)}) %collective-permute-start.3) | collective-permute-done | bytes 426016 | tf_op jit(solution)/shard_map/ppermute | solution.py:540
  16.3 7.7 %window_layer.1 = (bf16[512,512]{1,0:T(8,128)(2,1)S(1)}, bf16[512,512]{1,0:T(8,128)(2,1)S(1)}, bf16[512,512]{1,0:T(8,128)(2,1)S(1)}, bf16[512,512]{1,0:T(8,128)(...) custom-call(bf16[288,1024]{1,0:T(8,128)(2,1)S(1)} %bitcast.7, ...), custom_call_target="tpu_custom_call" | custom-call | flops 1811939328 | bytes 8000000 | tf_op jit(solution)/shard_map/window_layer/pallas_call | solution.py:155
  24.2 1.5 %collective-permute-start.13 = (bf16[512,512]{1,0:T(8,128)(2,1)S(1)}, bf16[512,512]{1,0:T(8,128)(2,1)S(1)}, u32[]{:S(2)}, u32[]{:S(2)}) collective-permute-start(bf16[512,512]{1,0:T(8,128)(2,1)S(1)} %get-tuple-element.58), channel_id=1, source_target_pairs={{0,16},{16,0},{1,17},{17,1},{2,18},{18,2},{3,19},{19,3},{4,20},{20... | collective-permute-start | bytes 1572872 | tf_op jit(solution)/shard_map/ppermute | solution.py:491
  25.6 0.4 collective-permute-start.14
  26.2 1.6 %collective-permute-start.5 = (bf16[2,80,1024]{2,1,0:T(8,128)(2,1)S(1)}, bf16[2,80,1024]{2,1,0:T(8,128)(2,1)S(1)}, u32[]{:S(2)}, u32[]{:S(2)}) collective-permute-start(bf16[2,80,1024]{2,1,0:T(8,128)(2,1)S(1)} %sum_over_cores.1), channel_id=1, source_target_pairs={{0,2},{1,3},{2,0},{3,1},{4,6},{5,7},{6,4},{7,5},{8,10},{9,11},{10,... | collective-permute-start | bytes 983048 | tf_op jit(solution)/shard_map/ppermute | solution.py:590
  27.8 8.2 %collective-permute-done.5.refs_6_ = bf16[2,80,1024]{2,1,0:T(8,128)(2,1)S(1)} collective-permute-done((bf16[2,80,1024]{2,1,0:T(8,128)(2,1)S(1)}, bf16[2,80,1024]{2,1,0:T(8,128)(2,1)S(1)}, u32[]{:S(2)}, u32[]{:S(2)}) %collective-permute-start.5) | collective-permute-done | bytes 327712 | tf_op jit(solution)/shard_map/ppermute | solution.py:590
  36.0 0.6 sum_over_heads.1
  36.6 1.5 %collective-permute-start.6 = (bf16[2,32,1024]{2,1,0:T(8,128)(2,1)S(1)}, bf16[2,32,1024]{2,1,0:T(8,128)(2,1)S(1)}, u32[]{:S(2)}, u32[]{:S(2)}) collective-permute-start(bf16[2,32,1024]{2,1,0:T(8,128)(2,1)S(1)} %get-tuple-element.50), channel_id=1, source_target_pairs={{0,16},{16,0},{1,17},{17,1},{2,18},{18,2},{3,19},{19,3},{4,20},{20... | collective-permute-start | bytes 393224 | tf_op jit(solution)/shard_map/ppermute | solution.py:491
  38.1 3.5 %collective-permute-done.6.refs_1_.refs_3_ = bf16[2,32,1024]{2,1,0:T(8,128)(2,1)S(1)} collective-permute-done((bf16[2,32,1024]{2,1,0:T(8,128)(2,1)S(1)}, bf16[2,32,1024]{2,1,0:T(8,128)(2,1)S(1)}, u32[]{:S(2)}, u32[]{:S(2)}) %collective-permute-start.6) | collective-permute-done | bytes 131104 | tf_op jit(solution)/shard_map/ppermute | solution.py:491
  41.7 1.4 %collective-permute-start.7 = (bf16[2,48,1024]{2,1,0:T(8,128)(2,1)S(1)}, bf16[2,48,1024]{2,1,0:T(8,128)(2,1)S(1)}, u32[]{:S(2)}, u32[]{:S(2)}) collective-permute-start(bf16[2,48,1024]{2,1,0:T(8,128)(2,1)S(1)} %get-tuple-element.51), channel_id=1, source_target_pairs={{0,4},{4,8},{8,12},{12,0},{1,5},{5,9},{9,13},{13,1},{2,6},{6,10},{... | collective-permute-start | bytes 589832 | tf_op jit(solution)/shard_map/ppermute | solution.py:491
  43.1 0.2 second_step.1
  43.3 3.3 %collective-permute-start.15 = (bf16[256,512]{1,0:T(8,128)(2,1)S(1)}, bf16[256,512]{1,0:T(8,128)(2,1)S(1)}, u32[]{:S(2)}, u32[]{:S(2)}) collective-permute-start(bf16[256,512]{1,0:T(8,128)(2,1)S(1)} %get-tuple-element.63), channel_id=1, source_target_pairs={{0,4},{4,0},{8,12},{12,8},{1,5},{5,1},{9,13},{13,9},{2,6},{6,2},{1... | collective-permute-start | bytes 786440 | tf_op jit(solution)/shard_map/ppermute | solution.py:614
  46.6 1.5 %collective-permute-start.16 = (bf16[256,512]{1,0:T(8,128)(2,1)S(1)}, bf16[256,512]{1,0:T(8,128)(2,1)S(1)}, u32[]{:S(2)}, u32[]{:S(2)}) collective-permute-start(bf16[256,512]{1,0:T(8,128)(2,1)S(1)} %get-tuple-element.65), channel_id=1, source_target_pairs={{0,16},{16,0},{1,17},{17,1},{2,18},{18,2},{3,19},{19,3},{4,20},{20... | collective-permute-start | bytes 786440 | tf_op jit(solution)/shard_map/ppermute | solution.py:491
  48.1 4.6 %collective-permute-done.7.refs_2_ = bf16[2,48,1024]{2,1,0:T(8,128)(2,1)S(1)} collective-permute-done((bf16[2,48,1024]{2,1,0:T(8,128)(2,1)S(1)}, bf16[2,48,1024]{2,1,0:T(8,128)(2,1)S(1)}, u32[]{:S(2)}, u32[]{:S(2)}) %collective-permute-start.7) | collective-permute-done | bytes 196640 | tf_op jit(solution)/shard_map/ppermute | solution.py:491
  52.7 0.3 join_home.1
  53.0 1.6 %collective-permute-start.9 = (bf16[80,1024]{1,0:T(8,128)(2,1)S(1)}, bf16[80,1024]{1,0:T(8,128)(2,1)S(1)}, u32[]{:S(2)}, u32[]{:S(2)}) collective-permute-start(bf16[80,1024]{1,0:T(8,128)(2,1)S(1)} %get-tuple-element.53), channel_id=1, source_target_pairs={{0,2},{1,3},{2,0},{3,1},{4,6},{5,7},{6,4},{7,5},{8,10},{9,11},{10,... | collective-permute-start | bytes 491528 | tf_op jit(solution)/shard_map/ppermute | solution.py:631
  54.6 0.5 collective-permute-start.10
  55.2 1.3 %collective-permute-start.17 = (bf16[2,128,512]{2,1,0:T(8,128)(2,1)S(1)}, bf16[2,128,512]{2,1,0:T(8,128)(2,1)S(1)}, u32[]{:S(2)}, u32[]{:S(2)}) collective-permute-start(bf16[2,128,512]{2,1,0:T(8,128)(2,1)S(1)} %get-tuple-element.68), channel_id=1, source_target_pairs={{0,8},{4,12},{8,0},{12,4},{1,9},{5,13},{9,1},{13,5},{2,10},{6,14},... | collective-permute-start | bytes 786440 | tf_op jit(solution)/shard_map/ppermute | solution.py:630
  56.4 2.7 %collective-permute-done.9.refs_3_ = bf16[80,1024]{1,0:T(8,128)(2,1)S(1)} collective-permute-done((bf16[80,1024]{1,0:T(8,128)(2,1)S(1)}, bf16[80,1024]{1,0:T(8,128)(2,1)S(1)}, u32[]{:S(2)}, u32[]{:S(2)}) %collective-permute-start.9) | collective-permute-done | bytes 163872 | tf_op jit(solution)/shard_map/ppermute | solution.py:631
  59.1 2.7 %collective-permute-done.10.refs_4_ = bf16[80,1024]{1,0:T(8,128)(2,1)S(1)} collective-permute-done((bf16[80,1024]{1,0:T(8,128)(2,1)S(1)}, bf16[80,1024]{1,0:T(8,128)(2,1)S(1)}, u32[]{:S(2)}, u32[]{:S(2)}) %collective-permute-start.10) | collective-permute-done | bytes 163872 | tf_op jit(solution)/shard_map/ppermute | solution.py:631
  61.9 1.4 %collective-permute-done.12.refs_6_ = bf16[80,1024]{1,0:T(8,128)(2,1)S(1)} collective-permute-done((bf16[80,1024]{1,0:T(8,128)(2,1)S(1)}, bf16[80,1024]{1,0:T(8,128)(2,1)S(1)}, u32[]{:S(2)}, u32[]{:S(2)}) %collective-permute-start.12) | collective-permute-done | bytes 163872 | tf_op jit(solution)/shard_map/ppermute | solution.py:633
  63.3 1.7 %spread_outputs.1 = (bf16[288,1024]{1,0:T(8,128)(2,1)}, bf16[288,1024]{1,0:T(8,128)(2,1)}, f32[8,128]{1,0:T(8,128)S(1)}) custom-call(bf16[288,320]{1,0:T(8,128)(2,1)S(1)} %copy-done.2, bf16[2,80,1024]{2,1,0:T(8,128)(2,1)S(1)} %get-tuple-element.52.refs_1_, bf16[2,80,1024]{2,1,0:T(8,128)(2,1)S(1)} %collective-permute-done.8.refs_2_, ...), custom_call_target="tpu_custom_call" | custom-call | flops 339738624 | bytes 2359296 | tf_op jit(solution)/shard_map/spread_outputs/pallas_call | solution.py:155
  64.9 4.6 %collective-permute-done.17.refs_1_ = bf16[2,128,512]{2,1,0:T(8,128)(2,1)S(1)} collective-permute-done((bf16[2,128,512]{2,1,0:T(8,128)(2,1)S(1)}, bf16[2,128,512]{2,1,0:T(8,128)(2,1)S(1)}, u32[]{:S(2)}, u32[]{:S(2)}) %collective-permute-start.17) | collective-permute-done | bytes 262176 | tf_op jit(solution)/shard_map/ppermute | solution.py:630
  69.5 0.8 %sum_over_lat.1 = (f32[128,768]{1,0:T(8,128)}, f32[256,128]{1,0:T(8,128)}) custom-call(f32[2,128,512]{2,1,0:T(8,128)S(1)} %get-tuple-element.67.refs_0_, bf16[2,128,512]{2,1,0:T(8,128)(2,1)S(1)} %collective-permute-done.17.refs_1_, f32[8,128]{1,0:T(8,128)S(1)} %get-tuple-element.69.refs_2_), custom_call_target="tpu_custom_call" | custom-call | flops 524288 | bytes 2097152 | tf_op jit(solution)/shard_map/sum_over_lat/pallas_call | solution.py:155
  (36 shorter events, 0.6 us)
Async XLA Ops:
  2.2 12.1 %collective-permute-start = (bf16[112,1024]{1,0:T(8,128)(2,1)S(1)}, bf16[112,1024]{1,0:T(8,128)(2,1)S(1)}, u32[]{:S(2)}, u32[]{:S(2)}) collective-permute-start(bf16[112,1024]{1,0:T(8,128)(2,1)S(1)} %get-tuple-element.38), channel_id=1, source_target_pairs={{0,12},{4,0},{8,4},{12,8},{16,28},{20,16},{24,20},{28,24},{1,13},{... | collective-permute-start | bytes 688136 | tf_op jit(solution)/shard_map/ppermute | solution.py:501
  7.3 5.7 %collective-permute-start.1 = (bf16[48,1024]{1,0:T(8,128)(2,1)S(1)}, bf16[48,1024]{1,0:T(8,128)(2,1)S(1)}, u32[]{:S(2)}, u32[]{:S(2)}) collective-permute-start(bf16[48,1024]{1,0:T(8,128)(2,1)S(1)} %get-tuple-element.39), channel_id=1, source_target_pairs={{0,16},{4,20},{8,24},{12,28},{16,0},{20,4},{24,8},{28,12},{1,17},{... | collective-permute-start | bytes 294920 | tf_op jit(solution)/shard_map/ppermute | solution.py:501
  8.8 5.5 %collective-permute-start.2 = (bf16[48,1024]{1,0:T(8,128)(2,1)S(1)}, bf16[48,1024]{1,0:T(8,128)(2,1)S(1)}, u32[]{:S(2)}, u32[]{:S(2)}) collective-permute-start(bf16[48,1024]{1,0:T(8,128)(2,1)S(1)} %get-tuple-element.40), channel_id=1, source_target_pairs={{0,28},{4,16},{8,20},{12,24},{16,12},{20,0},{24,4},{28,8},{1,29},{... | collective-permute-start | bytes 294920 | tf_op jit(solution)/shard_map/ppermute | solution.py:501
  9.2 0.7 %copy-start.7 = (f32[759,4]{0,1:T(4,128)S(1)}, f32[759,4]{0,1:T(4,128)}, u32[]{:S(2)}) copy-start(f32[759,4]{0,1:T(4,128)} %param.15) | copy-start | bytes 36436
  9.9 6.3 %copy-start = (bf16[2,6,24,1024]{3,2,1,0:T(8,128)(2,1)S(1)}, bf16[2,6,24,1024]{3,2,1,0:T(8,128)(2,1)}, u32[]{:S(2)}) copy-start(bf16[2,6,24,1024]{3,2,1,0:T(8,128)(2,1)} %param.11) | copy-start | bytes 1769476
  9.9 6.3 %copy-start.1 = (bf16[2,6,24,1024]{3,2,1,0:T(8,128)(2,1)S(1)}, bf16[2,6,24,1024]{3,2,1,0:T(8,128)(2,1)}, u32[]{:S(2)}) copy-start(bf16[2,6,24,1024]{3,2,1,0:T(8,128)(2,1)} %param.16) | copy-start | bytes 1769476
  9.9 6.3 %copy-start.4 = (f32[1024]{0:T(1024)S(1)}, f32[1024]{0:T(1024)}, u32[]{:S(2)}) copy-start(f32[1024]{0:T(1024)} %param.12) | copy-start | bytes 12292
  9.9 6.3 %copy-start.5 = (bf16[1024,768]{1,0:T(8,128)(2,1)S(1)}, bf16[1024,768]{1,0:T(8,128)(2,1)}, u32[]{:S(2)}) copy-start(bf16[1024,768]{1,0:T(8,128)(2,1)} %refs_9_.1) | copy-start | bytes 4718596
  9.9 6.3 %copy-start.6 = (bf16[256,1024]{1,0:T(8,128)(2,1)S(1)}, bf16[256,1024]{1,0:T(8,128)(2,1)}, u32[]{:S(2)}) copy-start(bf16[256,1024]{1,0:T(8,128)(2,1)} %refs_5_.1) | copy-start | bytes 1572868
  10.0 6.3 %copy-start.8 = (bf16[288,496]{1,0:T(8,128)(2,1)S(1)}, bf16[288,496]{1,0:T(8,128)(2,1)}, u32[]{:S(2)}) copy-start(bf16[288,496]{1,0:T(8,128)(2,1)} %constant.8.clone.refs_7_) | copy-start | bytes 857092
  10.0 6.3 %copy-start.9 = (bf16[320,288]{1,0:T(8,128)(2,1)S(1)}, bf16[320,288]{1,0:T(8,128)(2,1)}, u32[]{:S(2)}) copy-start(bf16[320,288]{1,0:T(8,128)(2,1)} %constant.9.clone.refs_8_) | copy-start | bytes 552964
  14.4 1.8 %collective-permute-start.3 = (bf16[208,1024]{1,0:T(8,128)(2,1)S(1)}, bf16[208,1024]{1,0:T(8,128)(2,1)S(1)}, u32[]{:S(2)}, u32[]{:S(2)}) collective-permute-start(bf16[208,1024]{1,0:T(8,128)(2,1)S(1)} %join_rims.1.refs_2_), channel_id=1, source_target_pairs={{0,1},{1,0},{2,3},{3,2},{4,5},{5,4},{6,7},{7,6},{8,9},{9,8},{10,11... | collective-permute-start | bytes 1277960 | tf_op jit(solution)/shard_map/ppermute | solution.py:540
  16.2 19.8 %copy-start.3 = (bf16[96,80]{1,0:T(8,128)(2,1)S(1)}, bf16[96,80]{1,0:T(8,128)(2,1)}, u32[]{:S(2)}) copy-start(bf16[96,80]{1,0:T(8,128)(2,1)} %constant.10.clone.refs_3_.refs_0_) | copy-start | bytes 46084
  23.9 2.2 %collective-permute-start.4 = (bf16[2,2,80,1024]{3,2,1,0:T(8,128)(2,1)S(1)}, bf16[2,2,80,1024]{3,2,1,0:T(8,128)(2,1)S(1)}, u32[]{:S(2)}, u32[]{:S(2)}) collective-permute-start(bf16[2,2,80,1024]{3,2,1,0:T(8,128)(2,1)S(1)} %get-tuple-element.46), channel_id=1, source_target_pairs={{0,1},{1,0},{2,3},{3,2},{4,5},{5,4},{6,7},{7,6},{8,9},{9,8},{10,11... | collective-permute-start | bytes 1966088 | tf_op jit(solution)/shard_map/ppermute | solution.py:585
  24.2 18.9 %collective-permute-start.13 = (bf16[512,512]{1,0:T(8,128)(2,1)S(1)}, bf16[512,512]{1,0:T(8,128)(2,1)S(1)}, u32[]{:S(2)}, u32[]{:S(2)}) collective-permute-start(bf16[512,512]{1,0:T(8,128)(2,1)S(1)} %get-tuple-element.58), channel_id=1, source_target_pairs={{0,16},{16,0},{1,17},{17,1},{2,18},{18,2},{3,19},{19,3},{4,20},{20... | collective-permute-start | bytes 1572872 | tf_op jit(solution)/shard_map/ppermute | solution.py:491
  25.6 17.4 %collective-permute-start.14 = (bf16[512,512]{1,0:T(8,128)(2,1)S(1)}, bf16[512,512]{1,0:T(8,128)(2,1)S(1)}, u32[]{:S(2)}, u32[]{:S(2)}) collective-permute-start(bf16[512,512]{1,0:T(8,128)(2,1)S(1)} %get-tuple-element.60), channel_id=1, source_target_pairs={{0,4},{4,0},{8,12},{12,8},{1,5},{5,1},{9,13},{13,9},{2,6},{6,2},{1... | collective-permute-start | bytes 1572872 | tf_op jit(solution)/shard_map/ppermute | solution.py:584
  26.2 9.8 %collective-permute-start.5 = (bf16[2,80,1024]{2,1,0:T(8,128)(2,1)S(1)}, bf16[2,80,1024]{2,1,0:T(8,128)(2,1)S(1)}, u32[]{:S(2)}, u32[]{:S(2)}) collective-permute-start(bf16[2,80,1024]{2,1,0:T(8,128)(2,1)S(1)} %sum_over_cores.1), channel_id=1, source_target_pairs={{0,2},{1,3},{2,0},{3,1},{4,6},{5,7},{6,4},{7,5},{8,10},{9,11},{10,... | collective-permute-start | bytes 983048 | tf_op jit(solution)/shard_map/ppermute | solution.py:590
  36.6 5.0 %collective-permute-start.6 = (bf16[2,32,1024]{2,1,0:T(8,128)(2,1)S(1)}, bf16[2,32,1024]{2,1,0:T(8,128)(2,1)S(1)}, u32[]{:S(2)}, u32[]{:S(2)}) collective-permute-start(bf16[2,32,1024]{2,1,0:T(8,128)(2,1)S(1)} %get-tuple-element.50), channel_id=1, source_target_pairs={{0,16},{16,0},{1,17},{17,1},{2,18},{18,2},{3,19},{19,3},{4,20},{20... | collective-permute-start | bytes 393224 | tf_op jit(solution)/shard_map/ppermute | solution.py:491
  41.7 11.0 %collective-permute-start.7 = (bf16[2,48,1024]{2,1,0:T(8,128)(2,1)S(1)}, bf16[2,48,1024]{2,1,0:T(8,128)(2,1)S(1)}, u32[]{:S(2)}, u32[]{:S(2)}) collective-permute-start(bf16[2,48,1024]{2,1,0:T(8,128)(2,1)S(1)} %get-tuple-element.51), channel_id=1, source_target_pairs={{0,4},{4,8},{8,12},{12,0},{1,5},{5,9},{9,13},{13,1},{2,6},{6,10},{... | collective-permute-start | bytes 589832 | tf_op jit(solution)/shard_map/ppermute | solution.py:491
  43.1 20.2 %copy-start.2 = (bf16[288,320]{1,0:T(8,128)(2,1)S(1)}, bf16[288,320]{1,0:T(8,128)(2,1)}, u32[]{:S(2)}) copy-start(bf16[288,320]{1,0:T(8,128)(2,1)} %constant.11.clone.refs_0_) | copy-start | bytes 552964
  43.3 11.7 %collective-permute-start.15 = (bf16[256,512]{1,0:T(8,128)(2,1)S(1)}, bf16[256,512]{1,0:T(8,128)(2,1)S(1)}, u32[]{:S(2)}, u32[]{:S(2)}) collective-permute-start(bf16[256,512]{1,0:T(8,128)(2,1)S(1)} %get-tuple-element.63), channel_id=1, source_target_pairs={{0,4},{4,0},{8,12},{12,8},{1,5},{5,1},{9,13},{13,9},{2,6},{6,2},{1... | collective-permute-start | bytes 786440 | tf_op jit(solution)/shard_map/ppermute | solution.py:614
  46.6 8.5 %collective-permute-start.16 = (bf16[256,512]{1,0:T(8,128)(2,1)S(1)}, bf16[256,512]{1,0:T(8,128)(2,1)S(1)}, u32[]{:S(2)}, u32[]{:S(2)}) collective-permute-start(bf16[256,512]{1,0:T(8,128)(2,1)S(1)} %get-tuple-element.65), channel_id=1, source_target_pairs={{0,16},{16,0},{1,17},{17,1},{2,18},{18,2},{3,19},{19,3},{4,20},{20... | collective-permute-start | bytes 786440 | tf_op jit(solution)/shard_map/ppermute | solution.py:491
  53.0 6.2 %collective-permute-start.9 = (bf16[80,1024]{1,0:T(8,128)(2,1)S(1)}, bf16[80,1024]{1,0:T(8,128)(2,1)S(1)}, u32[]{:S(2)}, u32[]{:S(2)}) collective-permute-start(bf16[80,1024]{1,0:T(8,128)(2,1)S(1)} %get-tuple-element.53), channel_id=1, source_target_pairs={{0,2},{1,3},{2,0},{3,1},{4,6},{5,7},{6,4},{7,5},{8,10},{9,11},{10,... | collective-permute-start | bytes 491528 | tf_op jit(solution)/shard_map/ppermute | solution.py:631
  54.6 7.3 %collective-permute-start.8 = (bf16[2,80,1024]{2,1,0:T(8,128)(2,1)S(1)}, bf16[2,80,1024]{2,1,0:T(8,128)(2,1)S(1)}, u32[]{:S(2)}, u32[]{:S(2)}) collective-permute-start(bf16[2,80,1024]{2,1,0:T(8,128)(2,1)S(1)} %get-tuple-element.52.refs_1_), channel_id=1, source_target_pairs={{0,1},{1,0},{2,3},{3,2},{4,5},{5,4},{6,7},{7,6},{8,9},{9,8},{10,11... | collective-permute-start | bytes 983048 | tf_op jit(solution)/shard_map/ppermute | solution.py:632
  54.6 7.3 %collective-permute-start.10 = (bf16[80,1024]{1,0:T(8,128)(2,1)S(1)}, bf16[80,1024]{1,0:T(8,128)(2,1)S(1)}, u32[]{:S(2)}, u32[]{:S(2)}) collective-permute-start(bf16[80,1024]{1,0:T(8,128)(2,1)S(1)} %get-tuple-element.54), channel_id=1, source_target_pairs={{0,2},{1,3},{2,0},{3,1},{4,6},{5,7},{6,4},{7,5},{8,10},{9,11},{10,... | collective-permute-start | bytes 491528 | tf_op jit(solution)/shard_map/ppermute | solution.py:631
  55.2 14.3 %collective-permute-start.17 = (bf16[2,128,512]{2,1,0:T(8,128)(2,1)S(1)}, bf16[2,128,512]{2,1,0:T(8,128)(2,1)S(1)}, u32[]{:S(2)}, u32[]{:S(2)}) collective-permute-start(bf16[2,128,512]{2,1,0:T(8,128)(2,1)S(1)} %get-tuple-element.68), channel_id=1, source_target_pairs={{0,8},{4,12},{8,0},{12,4},{1,9},{5,13},{9,1},{13,5},{2,10},{6,14},... | collective-permute-start | bytes 786440 | tf_op jit(solution)/shard_map/ppermute | solution.py:630
  59.1 2.7 %collective-permute-start.11 = (bf16[80,1024]{1,0:T(8,128)(2,1)S(1)}, bf16[80,1024]{1,0:T(8,128)(2,1)S(1)}, u32[]{:S(2)}, u32[]{:S(2)}) collective-permute-start(bf16[80,1024]{1,0:T(8,128)(2,1)S(1)} %collective-permute-done.9.refs_3_), channel_id=1, source_target_pairs={{0,1},{1,0},{2,3},{3,2},{4,5},{5,4},{6,7},{7,6},{8,9},{9,8},{10,11... | collective-permute-start | bytes 491528 | tf_op jit(solution)/shard_map/ppermute | solution.py:633
  61.9 1.4 %collective-permute-start.12 = (bf16[80,1024]{1,0:T(8,128)(2,1)S(1)}, bf16[80,1024]{1,0:T(8,128)(2,1)S(1)}, u32[]{:S(2)}, u32[]{:S(2)}) collective-permute-start(bf16[80,1024]{1,0:T(8,128)(2,1)S(1)} %collective-permute-done.10.refs_4_), channel_id=1, source_target_pairs={{0,1},{1,0},{2,3},{3,2},{4,5},{5,4},{6,7},{7,6},{8,9},{9,8},{10,11... | collective-permute-start | bytes 491528 | tf_op jit(solution)/shard_map/ppermute | solution.py:633

commit v5 on v4

--- a/solution.py
+++ b/solution.py
@@ -400,7 +400,8 @@
 
 def second_step_kernel(lon_count, *refs):
     from_lon, (lat_keep, from_lat) = refs[:lon_count], refs[lon_count : lon_count + 2]
-    keep_first, send_first, *by_lon = refs[lon_count + 2 :]
+    keep_first, send_first, *by_lon, mark = refs[lon_count + 2 :]
+    mark[...] = jnp.zeros_like(mark)
     rows = keep_first.shape[0] // 2
     lon, parity = lax.axis_index("lon"), lax.rem(lax.axis_index("lat"), 2)
     for out, wanted in ((keep_first, parity), (send_first, 1 - parity)):
@@ -415,7 +416,8 @@
 
 
 def third_step_kernel(keep_first, from_lat, *refs):
-    from_lon, (keep, send) = refs[:-2], refs[-2:]
+    from_lon, (keep, send, mark) = refs[:-3], refs[-3:]
+    mark[...] = jnp.zeros_like(mark)
     rows = keep.shape[1]
     mine = lax.div(lax.axis_index("lat"), 2)
     for half, parts in enumerate(((keep_first, from_lat), from_lon)):
@@ -432,7 +434,9 @@
     grad_out[...] = out.T if flip else out
 
 
-def norm_kernel(part_tokens, part_cotangent, gain, pick, stay, swapped, crossed, *outs):
+def norm_kernel(part_tokens, part_cotangent, gain, pick, stay, swapped, crossed, *refs):
+    *outs, mark = refs
+    mark[...] = jnp.zeros_like(mark)
     layer = part_tokens[...].astype(F32)
     attn = stay[0].astype(F32) + swapped[0, 0].astype(F32) + crossed[0].astype(F32)
     d_normed = stay[1].astype(F32) + swapped[0, 1].astype(F32) + crossed[1].astype(F32)
@@ -453,32 +457,25 @@
     rows[:, OUT_Z:, :] = x_rows[:, OUT_X:, :]
 
 
-def join_kernel(pick, own, z_rows, x_rows, joined, layer, grad, mark, rows):
-    mark[...] = jnp.zeros_like(mark)
+def join_kernel(pick, own, z_rows, x_rows, layer, grad, rows):
     rows[:, :OUT_OWN, :] = own[...]
     rows[:, OUT_OWN : OUT_OWN + OUT_Z, :] = z_rows[:, :OUT_Z, :]
     rows[:, OUT_OWN + OUT_Z : OUT_ROWS - OUT_D, :] = x_rows[:, :OUT_X, :]
     rows[:, OUT_ROWS - OUT_D :, :] = z_rows[:, OUT_Z:, :]
     for at, single in enumerate((layer, grad)):
         single[...] = dot_columns(pick[...], rows[at]).astype(BF16)
-        joined[at] = single[...]
-
-
-def spread_kernel(pick, mine, near, *refs):
-    far, across, outs, (mark, gathered) = refs[:2], refs[2:4], refs[4:6], refs[6:]
+
+
+def spread_kernel(pick, *refs):
+    arrived, outs, (mark, gathered) = refs[:8], refs[8:10], refs[10:]
     mark[...] = jnp.zeros_like(mark)
     head_index = lax.axis_index("head")
     sibling = 1 - 2 * lax.rem(head_index, 2)
     over = lax.rem(head_index + 2, QUARTERS)
-
-    def place(owner):
-        return pl.ds(pl.multiple_of(owner * PART, 16), PART)
-
+    owners = (head_index, head_index + sibling, over, over + sibling)
     for at, out in enumerate(outs):
-        gathered[at, place(head_index), :] = mine[at]
-        gathered[at, place(head_index + sibling), :] = near[at]
-        gathered[at, place(over), :] = far[at][...]
-        gathered[at, place(over + sibling), :] = across[at][...]
+        for owner, piece in zip(owners, arrived[at::2]):
+            gathered[at, pl.ds(pl.multiple_of(owner * PART, 16), PART), :] = piece[...]
         out[...] = dot(pick[...], gathered[at]).astype(BF16)
 
 
@@ -588,48 +585,51 @@
     )(over, swapped)
     chips = [(i, i ^ 2) for i in range(QUARTERS)]
     crossed = lax.ppermute(across, "head", chips)
-    pieces = call(
+    *pieces, norm_mark = call(
         norm_kernel,
-        [shaped(2, count, width) for count in (OUT_OWN, OUT_Z, OUT_X + OUT_D)],
+        [shaped(2, count, width) for count in (OUT_OWN, OUT_Z, OUT_X + OUT_D)] + [mark],
         cost=cost(2 * 2 * OUT_ROWS * PART * width, 12 * PART * width),
         name="sum_over_heads",
     )(part_tokens, part_cotangent, gain, group_pick(), stay, swapped, crossed)
+    keep_first, send_first, *by_lon, second_mark = call(
+        functools.partial(second_step_kernel, lon_count),
+        [shaped(2 * rows, columns, dtype=F32), shaped(2 * rows, columns)]
+        + [shaped(2 * rows, columns, dtype=F32)]
+        + [shaped(2 * rows, columns)] * (lon_count - 1)
+        + [mark],
+        cost=cost(4 * lon_rows * columns, 6 * lon_rows * columns),
+        name="second_step",
+        after=(norm_mark,),
+    )(*from_lon, lat_keep, from_lat)
+    from_lat = lax.ppermute(send_first, "lat", neighbours)
+    from_lon = [by_lon[0]] + [rotated(by_lon[step], "lon", step) for step in range(1, lon_count)]
     from_west = rotated(pieces[2], "lon", 1)
     to_north, north_mark = call(
         north_kernel,
         [shaped(2, OUT_Z + OUT_D, width), mark],
         cost=cost(0, 8 * (OUT_Z + OUT_D) * width),
         name="rows_for_north",
+        after=(second_mark,),
     )(pieces[1], from_west)
     home = [pieces[0], rotated(to_north, "lat", 1), from_west]
-    keep_first, send_first, *by_lon = call(
-        functools.partial(second_step_kernel, lon_count),
-        [shaped(2 * rows, columns, dtype=F32), shaped(2 * rows, columns)]
-        + [shaped(2 * rows, columns, dtype=F32)]
-        + [shaped(2 * rows, columns)] * (lon_count - 1),
-        cost=cost(4 * lon_rows * columns, 6 * lon_rows * columns),
-        name="second_step",
+    keep, send, third_mark = call(
+        third_step_kernel,
+        [shaped(2, rows, columns, dtype=F32), shaped(2, rows, columns), mark],
+        cost=cost(4 * rows * columns, 6 * rows * columns),
+        name="third_step",
         after=(north_mark,),
-    )(*from_lon, lat_keep, from_lat)
-    from_lat = lax.ppermute(send_first, "lat", neighbours)
-    from_lon = [by_lon[0]] + [rotated(by_lon[step], "lon", step) for step in range(1, lon_count)]
-    mine, *each, join_mark = call(
+    )(keep_first, from_lat, *from_lon)
+    last = lax.ppermute(send, "lat", [(i, i ^ 2) for i in range(lat_count)])
+    each = call(
         join_kernel,
-        [shaped(2, PART, width)] + [shaped(PART, width)] * 2 + [mark],
+        [shaped(PART, width)] * 2,
         [pltpu.VMEM((2, OUT_ROWS, width), BF16)],
         cost=cost(2 * 2 * OUT_ROWS * PART * width, 8 * OUT_ROWS * width),
         name="join_home",
+        after=(third_mark,),
     )(group_pick(), *home)
-    keep, send = call(
-        third_step_kernel,
-        [shaped(2, rows, columns, dtype=F32), shaped(2, rows, columns)],
-        cost=cost(4 * rows * columns, 6 * rows * columns),
-        name="third_step",
-        after=(join_mark,),
-    )(keep_first, from_lat, *from_lon)
-    last = lax.ppermute(send, "lat", [(i, i ^ 2) for i in range(lat_count)])
     far = [lax.ppermute(single, "head", chips) for single in each]
-    near = lax.ppermute(mine, "head", pairs)
+    near = [lax.ppermute(single, "head", pairs) for single in each]
     across = [lax.ppermute(single, "head", pairs) for single in far]
     layer_out, grad_tokens, spread_mark = call(
         spread_kernel,
@@ -637,7 +637,7 @@
         [pltpu.VMEM((2, QUARTERS * PART, width), BF16)],
         cost=cost(2 * 2 * CELLS * CELLS * width, 8 * CELLS * width),
         name="spread_outputs",
-    )(own_pick(), mine, near, *far, *across)
+    )(own_pick(), *each, *near, *far, *across)
     flip = rows % 128 == 0
     grad_qkv, grad_out = call(
         functools.partial(finish_kernel, group, flip),

time: 70.6 us -> 69.2 us (0.980)
  starting transfers between devices: 21.8 us -> 18.1 us
  waiting for transfers between devices: 31.9 us -> 34.2 us
    ppermute x1, waiting for transfers between devices: 0.01 us -> 4.24 us  [body(): from_lat = lax.ppermute(send_first, 'lat', neighbours)]
    ppermute x1, starting transfers between devices: 3.26 us -> 0.5 us  [body(): from_lat = lax.ppermute(send_first, 'lat', neighbours)]
    ppermute x1, waiting for transfers between devices: 4.56 us -> 2.07 us  [body(): last = lax.ppermute(send, 'lat', [(i, i ^ 2) for i in range(lat_count)])]
    ppermute x1, starting transfers between devices: 1.28 us -> 0.01 us  [body(): last = lax.ppermute(send, 'lat', [(i, i ^ 2) for i in range(lat_count)])]
    ppermute x1, waiting for transfers between devices: 0.01 us -> 1.18 us  [body(): from_lat = lax.ppermute(lat_send, 'lat', neighbours)]
    ppermute x4, waiting for transfers between devices: 8.15 us -> 7.17 us  [rotated(): lax.ppermute(value, axis, [(i, (i + step) % count) for i in range(count)])]
  transfers between devices with their start and end apart: 18 -> 19, of which waited for: 11 -> 14; matrix products, arithmetic and copies ran while one was open for 0% -> 0% of each run, Pallas kernels for 7% -> 7%
where the time goes in v5:
time: 69.2 us; the launch traced here: 68.9 us
  waiting for transfers between devices  34.2 us (49%)
  starting transfers between devices  18.1 us (26%)
  Pallas kernels  15.1 us (22%)
  between operations  0.8 us (1%)
  local copies, waits for them, and re-layouts  0.75 us (1%)
    pallas_call x12, Pallas kernels, run(): pl.pallas_call(body, out_shape=outs, in_specs=[near] * len(args) + [outsi...  15.1 us
    ppermute x1, waiting for transfers between devices, body(): crossed = lax.ppermute(across, 'head', chips)  8.23 us
    ppermute x4, waiting for transfers between devices, rotated(): lax.ppermute(value, axis, [(i, (i + step) % count) for i in range(count)])  7.17 us
    ppermute x3, starting transfers between devices, moved(): return lax.ppermute(value, ('lon', 'lat'), pairs)  7 us
    ppermute x2, waiting for transfers between devices, body(): far = [lax.ppermute(single, 'head', chips) for single in each]  5.72 us
    ppermute x4, starting transfers between devices, rotated(): lax.ppermute(value, axis, [(i, (i + step) % count) for i in range(count)])  5.71 us
    ppermute x1, waiting for transfers between devices, body(): from_lat = lax.ppermute(send_first, 'lat', neighbours)  4.24 us
    ppermute x3, waiting for transfers between devices, moved(): return lax.ppermute(value, ('lon', 'lat'), pairs)  2.36 us
  transfers between devices with their start and end apart: 19, of which 14 were waited for; matrix products, arithmetic and copies ran while one was open for 0% of the time, Pallas kernels for 7%

profile of v5, /device:TPU:0, one launch (start us, length us, event | category | flops | bytes accessed | tf_op | source)
XLA Modules:
  0.0 68.9 jit_solution(16889049448649537023)
XLA Ops:
  0.6 1.6 %pack_rims.1 = (bf16[112,1024]{1,0:T(8,128)(2,1)S(1)}, bf16[48,1024]{1,0:T(8,128)(2,1)S(1)}, bf16[48,1024]{1,0:T(8,128)(2,1)S(1)}) custom-call(bf16[288,1024]{1,0:T(8,128)(2,1)} %bitcast.6, bf16[288,1024]{1,0:T(8,128)(2,1)} %bitcast.8), custom_call_target="tpu_custom_call" | custom-call | flops 122683392 | bytes 1179648 | tf_op jit(solution)/shard_map/pack_rims/pallas_call | solution.py:155
  2.2 5.1 %collective-permute-start = (bf16[112,1024]{1,0:T(8,128)(2,1)S(1)}, bf16[112,1024]{1,0:T(8,128)(2,1)S(1)}, u32[]{:S(2)}, u32[]{:S(2)}) collective-permute-start(bf16[112,1024]{1,0:T(8,128)(2,1)S(1)} %get-tuple-element.39), channel_id=1, source_target_pairs={{0,12},{4,0},{8,4},{12,8},{16,28},{20,16},{24,20},{28,24},{1,13},{... | collective-permute-start | bytes 688136 | tf_op jit(solution)/shard_map/ppermute | solution.py:498
  7.3 1.5 %collective-permute-start.1 = (bf16[48,1024]{1,0:T(8,128)(2,1)S(1)}, bf16[48,1024]{1,0:T(8,128)(2,1)S(1)}, u32[]{:S(2)}, u32[]{:S(2)}) collective-permute-start(bf16[48,1024]{1,0:T(8,128)(2,1)S(1)} %get-tuple-element.40), channel_id=1, source_target_pairs={{0,16},{4,20},{8,24},{12,28},{16,0},{20,4},{24,8},{28,12},{1,17},{... | collective-permute-start | bytes 294920 | tf_op jit(solution)/shard_map/ppermute | solution.py:498
  8.8 0.4 collective-permute-start.2
  9.2 0.7 %copy-done.7 = f32[759,4]{0,1:T(4,128)S(1)} copy-done((f32[759,4]{0,1:T(4,128)S(1)}, f32[759,4]{0,1:T(4,128)}, u32[]{:S(2)}) %copy-start.7) | copy-done | bytes 12168
  10.0 2.0 %window_bias.1 = (f32[4,144,144]{2,1,0:T(8,128)S(1)}, f32[8,128]{1,0:T(8,128)S(1)}) custom-call(f32[4,759]{1,0:T(4,128)S(1)} %bitcast.12), custom_call_target="tpu_custom_call" | custom-call | flops 1019215872 | bytes 1000000 | tf_op jit(solution)/shard_map/window_bias/pallas_call | solution.py:155
  12.0 1.0 %collective-permute-done.1.refs_1_ = bf16[48,1024]{1,0:T(8,128)(2,1)S(1)} collective-permute-done((bf16[48,1024]{1,0:T(8,128)(2,1)S(1)}, bf16[48,1024]{1,0:T(8,128)(2,1)S(1)}, u32[]{:S(2)}, u32[]{:S(2)}) %collective-permute-start.1) | collective-permute-done | bytes 98336 | tf_op jit(solution)/shard_map/ppermute | solution.py:498
  13.0 1.3 %collective-permute-done.2.refs_2_ = bf16[48,1024]{1,0:T(8,128)(2,1)S(1)} collective-permute-done((bf16[48,1024]{1,0:T(8,128)(2,1)S(1)}, bf16[48,1024]{1,0:T(8,128)(2,1)S(1)}, u32[]{:S(2)}, u32[]{:S(2)}) %collective-permute-start.2) | collective-permute-done | bytes 98336 | tf_op jit(solution)/shard_map/ppermute | solution.py:498
  14.4 1.8 %collective-permute-done.3.refs_3_ = bf16[208,1024]{1,0:T(8,128)(2,1)S(1)} collective-permute-done((bf16[208,1024]{1,0:T(8,128)(2,1)S(1)}, bf16[208,1024]{1,0:T(8,128)(2,1)S(1)}, u32[]{:S(2)}, u32[]{:S(2)}) %collective-permute-start.3) | collective-permute-done | bytes 426016 | tf_op jit(solution)/shard_map/ppermute | solution.py:537
  16.3 7.7 %window_layer.1 = (bf16[512,512]{1,0:T(8,128)(2,1)S(1)}, bf16[512,512]{1,0:T(8,128)(2,1)S(1)}, bf16[512,512]{1,0:T(8,128)(2,1)S(1)}, bf16[512,512]{1,0:T(8,128)(...) custom-call(bf16[288,1024]{1,0:T(8,128)(2,1)S(1)} %bitcast.7, ...), custom_call_target="tpu_custom_call" | custom-call | flops 1811939328 | bytes 8000000 | tf_op jit(solution)/shard_map/window_layer/pallas_call | solution.py:155
  24.2 1.5 %collective-permute-start.7 = (bf16[512,512]{1,0:T(8,128)(2,1)S(1)}, bf16[512,512]{1,0:T(8,128)(2,1)S(1)}, u32[]{:S(2)}, u32[]{:S(2)}) collective-permute-start(bf16[512,512]{1,0:T(8,128)(2,1)S(1)} %get-tuple-element.53), channel_id=1, source_target_pairs={{0,16},{16,0},{1,17},{17,1},{2,18},{18,2},{3,19},{19,3},{4,20},{20... | collective-permute-start | bytes 1572872 | tf_op jit(solution)/shard_map/ppermute | solution.py:488
  25.6 0.4 collective-permute-start.8
  26.2 1.6 %collective-permute-start.5 = (bf16[2,80,1024]{2,1,0:T(8,128)(2,1)S(1)}, bf16[2,80,1024]{2,1,0:T(8,128)(2,1)S(1)}, u32[]{:S(2)}, u32[]{:S(2)}) collective-permute-start(bf16[2,80,1024]{2,1,0:T(8,128)(2,1)S(1)} %sum_over_cores.1), channel_id=1, source_target_pairs={{0,2},{1,3},{2,0},{3,1},{4,6},{5,7},{6,4},{7,5},{8,10},{9,11},{10,... | collective-permute-start | bytes 983048 | tf_op jit(solution)/shard_map/ppermute | solution.py:587
  27.8 8.2 %collective-permute-done.5.refs_6_ = bf16[2,80,1024]{2,1,0:T(8,128)(2,1)S(1)} collective-permute-done((bf16[2,80,1024]{2,1,0:T(8,128)(2,1)S(1)}, bf16[2,80,1024]{2,1,0:T(8,128)(2,1)S(1)}, u32[]{:S(2)}, u32[]{:S(2)}) %collective-permute-start.5) | collective-permute-done | bytes 327712 | tf_op jit(solution)/shard_map/ppermute | solution.py:587
  36.0 0.6 sum_over_heads.1
  36.6 1.5 %collective-permute-start.6 = (bf16[2,32,1024]{2,1,0:T(8,128)(2,1)S(1)}, bf16[2,32,1024]{2,1,0:T(8,128)(2,1)S(1)}, u32[]{:S(2)}, u32[]{:S(2)}) collective-permute-start(bf16[2,32,1024]{2,1,0:T(8,128)(2,1)S(1)} %get-tuple-element.51), channel_id=1, source_target_pairs={{0,16},{16,0},{1,17},{17,1},{2,18},{18,2},{3,19},{19,3},{4,20},{20... | collective-permute-start | bytes 393224 | tf_op jit(solution)/shard_map/ppermute | solution.py:488
  38.4 1.2 %collective-permute-done.8.refs_3_ = bf16[512,512]{1,0:T(8,128)(2,1)S(1)} collective-permute-done((bf16[512,512]{1,0:T(8,128)(2,1)S(1)}, bf16[512,512]{1,0:T(8,128)(2,1)S(1)}, u32[]{:S(2)}, u32[]{:S(2)}) %collective-permute-start.8) | collective-permute-done | bytes 524320 | tf_op jit(solution)/shard_map/ppermute | solution.py:581
  39.8 0.5 collective-permute-start.10
  40.3 1.5 %collective-permute-start.11 = (bf16[256,512]{1,0:T(8,128)(2,1)S(1)}, bf16[256,512]{1,0:T(8,128)(2,1)S(1)}, u32[]{:S(2)}, u32[]{:S(2)}) collective-permute-start(bf16[256,512]{1,0:T(8,128)(2,1)S(1)} %get-tuple-element.62), channel_id=1, source_target_pairs={{0,16},{16,0},{1,17},{17,1},{2,18},{18,2},{3,19},{19,3},{4,20},{20... | collective-permute-start | bytes 786440 | tf_op jit(solution)/shard_map/ppermute | solution.py:488
  41.8 1.2 %collective-permute-start.9 = (bf16[2,48,1024]{2,1,0:T(8,128)(2,1)S(1)}, bf16[2,48,1024]{2,1,0:T(8,128)(2,1)S(1)}, u32[]{:S(2)}, u32[]{:S(2)}) collective-permute-start(bf16[2,48,1024]{2,1,0:T(8,128)(2,1)S(1)} %get-tuple-element.58), channel_id=1, source_target_pairs={{0,4},{4,8},{8,12},{12,0},{1,5},{5,9},{9,13},{13,1},{2,6},{6,10},{... | collective-permute-start | bytes 589832 | tf_op jit(solution)/shard_map/ppermute | solution.py:488
  43.1 4.2 %collective-permute-done.10.refs_1_ = bf16[256,512]{1,0:T(8,128)(2,1)S(1)} collective-permute-done((bf16[256,512]{1,0:T(8,128)(2,1)S(1)}, bf16[256,512]{1,0:T(8,128)(2,1)S(1)}, u32[]{:S(2)}, u32[]{:S(2)}) %collective-permute-start.10) | collective-permute-done | bytes 262176 | tf_op jit(solution)/shard_map/ppermute | solution.py:604
  47.6 6.7 %collective-permute-done.9.refs_2_ = bf16[2,48,1024]{2,1,0:T(8,128)(2,1)S(1)} collective-permute-done((bf16[2,48,1024]{2,1,0:T(8,128)(2,1)S(1)}, bf16[2,48,1024]{2,1,0:T(8,128)(2,1)S(1)}, u32[]{:S(2)}, u32[]{:S(2)}) %collective-permute-start.9) | collective-permute-done | bytes 196640 | tf_op jit(solution)/shard_map/ppermute | solution.py:488
  54.3 0.3 join_home.1
  54.6 1.6 %collective-permute-start.14 = (bf16[80,1024]{1,0:T(8,128)(2,1)S(1)}, bf16[80,1024]{1,0:T(8,128)(2,1)S(1)}, u32[]{:S(2)}, u32[]{:S(2)}) collective-permute-start(bf16[80,1024]{1,0:T(8,128)(2,1)S(1)} %get-tuple-element.65.refs_1_), channel_id=1, source_target_pairs={{0,2},{1,3},{2,0},{3,1},{4,6},{5,7},{6,4},{7,5},{8,10},{9,11},{10,... | collective-permute-start | bytes 491528 | tf_op jit(solution)/shard_map/ppermute | solution.py:631
  56.2 0.5 collective-permute-start.15
  56.7 0.5 collective-permute-start.13
  57.2 4.0 %collective-permute-done.14.refs_5_ = bf16[80,1024]{1,0:T(8,128)(2,1)S(1)} collective-permute-done((bf16[80,1024]{1,0:T(8,128)(2,1)S(1)}, bf16[80,1024]{1,0:T(8,128)(2,1)S(1)}, u32[]{:S(2)}, u32[]{:S(2)}) %collective-permute-start.14) | collective-permute-done | bytes 163872 | tf_op jit(solution)/shard_map/ppermute | solution.py:631
  61.2 1.8 %collective-permute-done.15.refs_6_ = bf16[80,1024]{1,0:T(8,128)(2,1)S(1)} collective-permute-done((bf16[80,1024]{1,0:T(8,128)(2,1)S(1)}, bf16[80,1024]{1,0:T(8,128)(2,1)S(1)}, u32[]{:S(2)}, u32[]{:S(2)}) %collective-permute-start.15) | collective-permute-done | bytes 163872 | tf_op jit(solution)/shard_map/ppermute | solution.py:631
  63.0 1.4 %collective-permute-done.17.refs_8_ = bf16[80,1024]{1,0:T(8,128)(2,1)S(1)} collective-permute-done((bf16[80,1024]{1,0:T(8,128)(2,1)S(1)}, bf16[80,1024]{1,0:T(8,128)(2,1)S(1)}, u32[]{:S(2)}, u32[]{:S(2)}) %collective-permute-start.17) | collective-permute-done | bytes 163872 | tf_op jit(solution)/shard_map/ppermute | solution.py:633
  64.3 1.7 %spread_outputs.1 = (bf16[288,1024]{1,0:T(8,128)(2,1)}, bf16[288,1024]{1,0:T(8,128)(2,1)}, f32[8,128]{1,0:T(8,128)S(1)}) custom-call(bf16[288,320]{1,0:T(8,128)(2,1)S(1)} %copy-done.2, bf16[80,1024]{1,0:T(8,128)(2,1)S(1)} %get-tuple-element.65.refs_1_, bf16[80,1024]{1,0:T(8,128)(2,1)S(1)} %get-tuple-element.66.refs_2_, ...), custom_call_target="tpu_custom_call" | custom-call | flops 339738624 | bytes 2359296 | tf_op jit(solution)/shard_map/spread_outputs/pallas_call | solution.py:155
  66.0 2.1 %collective-permute-done.18.refs_1_ = bf16[2,128,512]{2,1,0:T(8,128)(2,1)S(1)} collective-permute-done((bf16[2,128,512]{2,1,0:T(8,128)(2,1)S(1)}, bf16[2,128,512]{2,1,0:T(8,128)(2,1)S(1)}, u32[]{:S(2)}, u32[]{:S(2)}) %collective-permute-start.18) | collective-permute-done | bytes 262176 | tf_op jit(solution)/shard_map/ppermute | solution.py:622
  68.1 0.8 %sum_over_lat.1 = (f32[128,768]{1,0:T(8,128)}, f32[256,128]{1,0:T(8,128)}) custom-call(f32[2,128,512]{2,1,0:T(8,128)S(1)} %get-tuple-element.69.refs_0_, bf16[2,128,512]{2,1,0:T(8,128)(2,1)S(1)} %collective-permute-done.18.refs_1_, f32[8,128]{1,0:T(8,128)S(1)} %get-tuple-element.71.refs_2_), custom_call_target="tpu_custom_call" | custom-call | flops 524288 | bytes 2097152 | tf_op jit(solution)/shard_map/sum_over_lat/pallas_call | solution.py:155
  (38 shorter events, 1.4 us)
Async XLA Ops:
  2.2 12.1 %collective-permute-start = (bf16[112,1024]{1,0:T(8,128)(2,1)S(1)}, bf16[112,1024]{1,0:T(8,128)(2,1)S(1)}, u32[]{:S(2)}, u32[]{:S(2)}) collective-permute-start(bf16[112,1024]{1,0:T(8,128)(2,1)S(1)} %get-tuple-element.39), channel_id=1, source_target_pairs={{0,12},{4,0},{8,4},{12,8},{16,28},{20,16},{24,20},{28,24},{1,13},{... | collective-permute-start | bytes 688136 | tf_op jit(solution)/shard_map/ppermute | solution.py:498
  7.3 5.7 %collective-permute-start.1 = (bf16[48,1024]{1,0:T(8,128)(2,1)S(1)}, bf16[48,1024]{1,0:T(8,128)(2,1)S(1)}, u32[]{:S(2)}, u32[]{:S(2)}) collective-permute-start(bf16[48,1024]{1,0:T(8,128)(2,1)S(1)} %get-tuple-element.40), channel_id=1, source_target_pairs={{0,16},{4,20},{8,24},{12,28},{16,0},{20,4},{24,8},{28,12},{1,17},{... | collective-permute-start | bytes 294920 | tf_op jit(solution)/shard_map/ppermute | solution.py:498
  8.8 5.5 %collective-permute-start.2 = (bf16[48,1024]{1,0:T(8,128)(2,1)S(1)}, bf16[48,1024]{1,0:T(8,128)(2,1)S(1)}, u32[]{:S(2)}, u32[]{:S(2)}) collective-permute-start(bf16[48,1024]{1,0:T(8,128)(2,1)S(1)} %get-tuple-element.41), channel_id=1, source_target_pairs={{0,28},{4,16},{8,20},{12,24},{16,12},{20,0},{24,4},{28,8},{1,29},{... | collective-permute-start | bytes 294920 | tf_op jit(solution)/shard_map/ppermute | solution.py:498
  9.2 0.7 %copy-start.7 = (f32[759,4]{0,1:T(4,128)S(1)}, f32[759,4]{0,1:T(4,128)}, u32[]{:S(2)}) copy-start(f32[759,4]{0,1:T(4,128)} %param.15) | copy-start | bytes 36436
  9.9 6.3 %copy-start = (bf16[2,6,24,1024]{3,2,1,0:T(8,128)(2,1)S(1)}, bf16[2,6,24,1024]{3,2,1,0:T(8,128)(2,1)}, u32[]{:S(2)}) copy-start(bf16[2,6,24,1024]{3,2,1,0:T(8,128)(2,1)} %param.11) | copy-start | bytes 1769476
  9.9 6.3 %copy-start.1 = (bf16[2,6,24,1024]{3,2,1,0:T(8,128)(2,1)S(1)}, bf16[2,6,24,1024]{3,2,1,0:T(8,128)(2,1)}, u32[]{:S(2)}) copy-start(bf16[2,6,24,1024]{3,2,1,0:T(8,128)(2,1)} %param.16) | copy-start | bytes 1769476
  9.9 6.3 %copy-start.4 = (f32[1024]{0:T(1024)S(1)}, f32[1024]{0:T(1024)}, u32[]{:S(2)}) copy-start(f32[1024]{0:T(1024)} %param.12) | copy-start | bytes 12292
  9.9 6.3 %copy-start.5 = (bf16[1024,768]{1,0:T(8,128)(2,1)S(1)}, bf16[1024,768]{1,0:T(8,128)(2,1)}, u32[]{:S(2)}) copy-start(bf16[1024,768]{1,0:T(8,128)(2,1)} %refs_9_.1) | copy-start | bytes 4718596
  9.9 6.3 %copy-start.6 = (bf16[256,1024]{1,0:T(8,128)(2,1)S(1)}, bf16[256,1024]{1,0:T(8,128)(2,1)}, u32[]{:S(2)}) copy-start(bf16[256,1024]{1,0:T(8,128)(2,1)} %refs_5_.1) | copy-start | bytes 1572868
  10.0 6.3 %copy-start.8 = (bf16[288,496]{1,0:T(8,128)(2,1)S(1)}, bf16[288,496]{1,0:T(8,128)(2,1)}, u32[]{:S(2)}) copy-start(bf16[288,496]{1,0:T(8,128)(2,1)} %constant.8.clone.refs_7_) | copy-start | bytes 857092
  10.0 6.3 %copy-start.9 = (bf16[320,288]{1,0:T(8,128)(2,1)S(1)}, bf16[320,288]{1,0:T(8,128)(2,1)}, u32[]{:S(2)}) copy-start(bf16[320,288]{1,0:T(8,128)(2,1)} %constant.9.clone.refs_8_) | copy-start | bytes 552964
  14.4 1.8 %collective-permute-start.3 = (bf16[208,1024]{1,0:T(8,128)(2,1)S(1)}, bf16[208,1024]{1,0:T(8,128)(2,1)S(1)}, u32[]{:S(2)}, u32[]{:S(2)}) collective-permute-start(bf16[208,1024]{1,0:T(8,128)(2,1)S(1)} %join_rims.1.refs_2_), channel_id=1, source_target_pairs={{0,1},{1,0},{2,3},{3,2},{4,5},{5,4},{6,7},{7,6},{8,9},{9,8},{10,11... | collective-permute-start | bytes 1277960 | tf_op jit(solution)/shard_map/ppermute | solution.py:537
  16.2 19.8 %copy-start.3 = (bf16[96,80]{1,0:T(8,128)(2,1)S(1)}, bf16[96,80]{1,0:T(8,128)(2,1)}, u32[]{:S(2)}) copy-start(bf16[96,80]{1,0:T(8,128)(2,1)} %constant.10.clone.refs_3_.refs_0_) | copy-start | bytes 46084
  23.9 2.2 %collective-permute-start.4 = (bf16[2,2,80,1024]{3,2,1,0:T(8,128)(2,1)S(1)}, bf16[2,2,80,1024]{3,2,1,0:T(8,128)(2,1)S(1)}, u32[]{:S(2)}, u32[]{:S(2)}) collective-permute-start(bf16[2,2,80,1024]{3,2,1,0:T(8,128)(2,1)S(1)} %get-tuple-element.47), channel_id=1, source_target_pairs={{0,1},{1,0},{2,3},{3,2},{4,5},{5,4},{6,7},{7,6},{8,9},{9,8},{10,11... | collective-permute-start | bytes 1966088 | tf_op jit(solution)/shard_map/ppermute | solution.py:582
  24.2 14.2 %collective-permute-start.7 = (bf16[512,512]{1,0:T(8,128)(2,1)S(1)}, bf16[512,512]{1,0:T(8,128)(2,1)S(1)}, u32[]{:S(2)}, u32[]{:S(2)}) collective-permute-start(bf16[512,512]{1,0:T(8,128)(2,1)S(1)} %get-tuple-element.53), channel_id=1, source_target_pairs={{0,16},{16,0},{1,17},{17,1},{2,18},{18,2},{3,19},{19,3},{4,20},{20... | collective-permute-start | bytes 1572872 | tf_op jit(solution)/shard_map/ppermute | solution.py:488
  25.6 13.9 %collective-permute-start.8 = (bf16[512,512]{1,0:T(8,128)(2,1)S(1)}, bf16[512,512]{1,0:T(8,128)(2,1)S(1)}, u32[]{:S(2)}, u32[]{:S(2)}) collective-permute-start(bf16[512,512]{1,0:T(8,128)(2,1)S(1)} %get-tuple-element.55), channel_id=1, source_target_pairs={{0,4},{4,0},{8,12},{12,8},{1,5},{5,1},{9,13},{13,9},{2,6},{6,2},{1... | collective-permute-start | bytes 1572872 | tf_op jit(solution)/shard_map/ppermute | solution.py:581
  26.2 9.8 %collective-permute-start.5 = (bf16[2,80,1024]{2,1,0:T(8,128)(2,1)S(1)}, bf16[2,80,1024]{2,1,0:T(8,128)(2,1)S(1)}, u32[]{:S(2)}, u32[]{:S(2)}) collective-permute-start(bf16[2,80,1024]{2,1,0:T(8,128)(2,1)S(1)} %sum_over_cores.1), channel_id=1, source_target_pairs={{0,2},{1,3},{2,0},{3,1},{4,6},{5,7},{6,4},{7,5},{8,10},{9,11},{10,... | collective-permute-start | bytes 983048 | tf_op jit(solution)/shard_map/ppermute | solution.py:587
  36.6 5.2 %collective-permute-start.6 = (bf16[2,32,1024]{2,1,0:T(8,128)(2,1)S(1)}, bf16[2,32,1024]{2,1,0:T(8,128)(2,1)S(1)}, u32[]{:S(2)}, u32[]{:S(2)}) collective-permute-start(bf16[2,32,1024]{2,1,0:T(8,128)(2,1)S(1)} %get-tuple-element.51), channel_id=1, source_target_pairs={{0,16},{16,0},{1,17},{17,1},{2,18},{18,2},{3,19},{19,3},{4,20},{20... | collective-permute-start | bytes 393224 | tf_op jit(solution)/shard_map/ppermute | solution.py:488
  39.8 24.6 %copy-start.2 = (bf16[288,320]{1,0:T(8,128)(2,1)S(1)}, bf16[288,320]{1,0:T(8,128)(2,1)}, u32[]{:S(2)}) copy-start(bf16[288,320]{1,0:T(8,128)(2,1)} %constant.11.clone.refs_0_) | copy-start | bytes 552964
  39.8 7.5 %collective-permute-start.10 = (bf16[256,512]{1,0:T(8,128)(2,1)S(1)}, bf16[256,512]{1,0:T(8,128)(2,1)S(1)}, u32[]{:S(2)}, u32[]{:S(2)}) collective-permute-start(bf16[256,512]{1,0:T(8,128)(2,1)S(1)} %get-tuple-element.60), channel_id=1, source_target_pairs={{0,4},{4,0},{8,12},{12,8},{1,5},{5,1},{9,13},{13,9},{2,6},{6,2},{1... | collective-permute-start | bytes 786440 | tf_op jit(solution)/shard_map/ppermute | solution.py:604
  40.3 7.3 %collective-permute-start.11 = (bf16[256,512]{1,0:T(8,128)(2,1)S(1)}, bf16[256,512]{1,0:T(8,128)(2,1)S(1)}, u32[]{:S(2)}, u32[]{:S(2)}) collective-permute-start(bf16[256,512]{1,0:T(8,128)(2,1)S(1)} %get-tuple-element.62), channel_id=1, source_target_pairs={{0,16},{16,0},{1,17},{17,1},{2,18},{18,2},{3,19},{19,3},{4,20},{20... | collective-permute-start | bytes 786440 | tf_op jit(solution)/shard_map/ppermute | solution.py:488
  41.8 12.5 %collective-permute-start.9 = (bf16[2,48,1024]{2,1,0:T(8,128)(2,1)S(1)}, bf16[2,48,1024]{2,1,0:T(8,128)(2,1)S(1)}, u32[]{:S(2)}, u32[]{:S(2)}) collective-permute-start(bf16[2,48,1024]{2,1,0:T(8,128)(2,1)S(1)} %get-tuple-element.58), channel_id=1, source_target_pairs={{0,4},{4,8},{8,12},{12,0},{1,5},{5,9},{9,13},{13,1},{2,6},{6,10},{... | collective-permute-start | bytes 589832 | tf_op jit(solution)/shard_map/ppermute | solution.py:488
  54.6 6.6 %collective-permute-start.14 = (bf16[80,1024]{1,0:T(8,128)(2,1)S(1)}, bf16[80,1024]{1,0:T(8,128)(2,1)S(1)}, u32[]{:S(2)}, u32[]{:S(2)}) collective-permute-start(bf16[80,1024]{1,0:T(8,128)(2,1)S(1)} %get-tuple-element.65.refs_1_), channel_id=1, source_target_pairs={{0,2},{1,3},{2,0},{3,1},{4,6},{5,7},{6,4},{7,5},{8,10},{9,11},{10,... | collective-permute-start | bytes 491528 | tf_op jit(solution)/shard_map/ppermute | solution.py:631
  56.2 6.7 %collective-permute-start.15 = (bf16[80,1024]{1,0:T(8,128)(2,1)S(1)}, bf16[80,1024]{1,0:T(8,128)(2,1)S(1)}, u32[]{:S(2)}, u32[]{:S(2)}) collective-permute-start(bf16[80,1024]{1,0:T(8,128)(2,1)S(1)} %get-tuple-element.66.refs_2_), channel_id=1, source_target_pairs={{0,2},{1,3},{2,0},{3,1},{4,6},{5,7},{6,4},{7,5},{8,10},{9,11},{10,... | collective-permute-start | bytes 491528 | tf_op jit(solution)/shard_map/ppermute | solution.py:631
  56.7 11.4 %collective-permute-start.18 = (bf16[2,128,512]{2,1,0:T(8,128)(2,1)S(1)}, bf16[2,128,512]{2,1,0:T(8,128)(2,1)S(1)}, u32[]{:S(2)}, u32[]{:S(2)}) collective-permute-start(bf16[2,128,512]{2,1,0:T(8,128)(2,1)S(1)} %get-tuple-element.70), channel_id=1, source_target_pairs={{0,8},{4,12},{8,0},{12,4},{1,9},{5,13},{9,1},{13,5},{2,10},{6,14},... | collective-permute-start | bytes 786440 | tf_op jit(solution)/shard_map/ppermute | solution.py:622
  56.7 6.2 %collective-permute-start.12 = (bf16[80,1024]{1,0:T(8,128)(2,1)S(1)}, bf16[80,1024]{1,0:T(8,128)(2,1)S(1)}, u32[]{:S(2)}, u32[]{:S(2)}) collective-permute-start(bf16[80,1024]{1,0:T(8,128)(2,1)S(1)} %get-tuple-element.65.refs_1_), channel_id=1, source_target_pairs={{0,1},{1,0},{2,3},{3,2},{4,5},{5,4},{6,7},{7,6},{8,9},{9,8},{10,11... | collective-permute-start | bytes 491528 | tf_op jit(solution)/shard_map/ppermute | solution.py:632
  56.7 6.2 %collective-permute-start.13 = (bf16[80,1024]{1,0:T(8,128)(2,1)S(1)}, bf16[80,1024]{1,0:T(8,128)(2,1)S(1)}, u32[]{:S(2)}, u32[]{:S(2)}) collective-permute-start(bf16[80,1024]{1,0:T(8,128)(2,1)S(1)} %get-tuple-element.66.refs_2_), channel_id=1, source_target_pairs={{0,1},{1,0},{2,3},{3,2},{4,5},{5,4},{6,7},{7,6},{8,9},{9,8},{10,11... | collective-permute-start | bytes 491528 | tf_op jit(solution)/shard_map/ppermute | solution.py:632
  61.2 1.8 %collective-permute-start.16 = (bf16[80,1024]{1,0:T(8,128)(2,1)S(1)}, bf16[80,1024]{1,0:T(8,128)(2,1)S(1)}, u32[]{:S(2)}, u32[]{:S(2)}) collective-permute-start(bf16[80,1024]{1,0:T(8,128)(2,1)S(1)} %collective-permute-done.14.refs_5_), channel_id=1, source_target_pairs={{0,1},{1,0},{2,3},{3,2},{4,5},{5,4},{6,7},{7,6},{8,9},{9,8},{10,11... | collective-permute-start | bytes 491528 | tf_op jit(solution)/shard_map/ppermute | solution.py:633
  62.9 1.4 %collective-permute-start.17 = (bf16[80,1024]{1,0:T(8,128)(2,1)S(1)}, bf16[80,1024]{1,0:T(8,128)(2,1)S(1)}, u32[]{:S(2)}, u32[]{:S(2)}) collective-permute-start(bf16[80,1024]{1,0:T(8,128)(2,1)S(1)} %collective-permute-done.15.refs_6_), channel_id=1, source_target_pairs={{0,1},{1,0},{2,3},{3,2},{4,5},{5,4},{6,7},{7,6},{8,9},{9,8},{10,11... | collective-permute-start | bytes 491528 | tf_op jit(solution)/shard_map/ppermute | solution.py:633

commit v6 on v5

--- a/solution.py
+++ b/solution.py
@@ -17,7 +17,8 @@
 WINDOWS = TILE_LON // WLON
 CELLS = WINDOWS * WINDOW
 QUARTERS = 4
-PART = 80
+PART = 72
+STRIDE = 80
 MID_LAT = WLAT // 2
 MID_LON = WLON // 2
 SPAN_LAT = 2 * WLAT - 1
@@ -29,9 +30,10 @@
 
 RIM_Z, RIM_X, RIM_D = 112, 48, 48
 RIM = RIM_Z + RIM_X + RIM_D
-OUT_OWN, OUT_Z, OUT_X, OUT_D = 32, 32, 16, 16
 OUT_STARTS = (0, 32, 64)
+OUT_SIZES = (32, 32, 32)
 OUT_ROWS = 96
+NORTH_ROWS = 40
 
 
 def own_row(level, lat, lon):
@@ -92,16 +94,19 @@
     rows = []
     for quarter in range(QUARTERS):
         cells = sum(quarter_cells(quarter), [])
-        rows += [CELL_AT[cell] for cell in cells] + [-1] * (PART - len(cells))
+        rows += [CELL_AT[cell] for cell in cells] + [-1] * (STRIDE - len(cells))
     return one_hot(rows, CELLS)
 
 
+def group_sizes():
+    return [len(group) for group in quarter_cells(0)]
+
+
 def group_pick():
-    rows = []
-    start = 0
-    for group, padded in zip(quarter_cells(0), (OUT_OWN, OUT_Z, OUT_X, OUT_D)):
-        rows += list(range(start, start + len(group))) + [-1] * (padded - len(group))
-        start += len(group)
+    stay, north, east, corner = group_sizes()
+    rows = list(range(stay)) + [-1] * (OUT_STARTS[1] - stay)
+    rows += list(range(stay, stay + north)) + [-1] * (OUT_STARTS[2] - OUT_STARTS[1] - north)
+    rows += list(range(stay + north, PART)) + [-1] * (OUT_ROWS - OUT_STARTS[2] - east - corner)
     return one_hot(rows, PART)
 
 
@@ -111,8 +116,8 @@
         for at, (window, level, lat, lon) in enumerate(sum(quarter_cells(quarter), [])):
             column = (window * WLON + lon + MID_LON) % TILE_LON
             row = own_row(level, (lat + MID_LAT) % WLAT, column)
-            place[row] = quarter * PART + at
-    return one_hot([place[row] for row in range(CELLS)], QUARTERS * PART)
+            place[row] = quarter * STRIDE + at
+    return one_hot([place[row] for row in range(CELLS)], QUARTERS * STRIDE)
 
 
 def window_position(shape, dim):
@@ -373,14 +378,14 @@
     terms[1] = dot_rows(ordered[:, group:], w_qkv[...]).astype(BF16)
 
     def term(owner):
-        return terms[:, pl.ds(pl.multiple_of(owner * PART, 16), PART), :]
+        return terms[:, pl.ds(pl.multiple_of(owner * STRIDE, 16), PART), :]
 
     far = lax.rem(head_index + 2, QUARTERS)
     stay[...] = term(head_index)
     over[...] = term(far)
     swap[0] = term(head_index + 1 - 2 * core)
     swap[1] = term(far + 1 - 2 * core)
-    mine = quarter[pl.ds(pl.multiple_of(head_index * PART, 16), PART), :]
+    mine = quarter[pl.ds(pl.multiple_of(head_index * STRIDE, 16), PART), :]
     part_tokens[...] = dot(mine, near_tokens[...]).astype(BF16)
     part_cotangent[...] = dot(mine, near_grad[...]).astype(BF16)
     for store in stores:
@@ -451,19 +456,37 @@
             out[at] = rows[start : start + out.shape[1]]
 
 
+def taken(count, source, spans):
+    row = lax.broadcasted_iota(jnp.int32, (count, source.shape[0]), 0)
+    column = lax.broadcasted_iota(jnp.int32, (count, source.shape[0]), 1)
+    wanted = jnp.zeros((count, source.shape[0]), F32)
+    for start, first, rows in spans:
+        inside = (row >= start) & (row < start + rows)
+        wanted = jnp.where(inside & (column == row + (first - start)), 1.0, wanted)
+    return dot(wanted.astype(BF16), source)
+
+
 def north_kernel(z_rows, x_rows, rows, mark):
     mark[...] = jnp.zeros_like(mark)
-    rows[:, :OUT_Z, :] = z_rows[...]
-    rows[:, OUT_Z:, :] = x_rows[:, OUT_X:, :]
-
-
-def join_kernel(pick, own, z_rows, x_rows, layer, grad, rows):
-    rows[:, :OUT_OWN, :] = own[...]
-    rows[:, OUT_OWN : OUT_OWN + OUT_Z, :] = z_rows[:, :OUT_Z, :]
-    rows[:, OUT_OWN + OUT_Z : OUT_ROWS - OUT_D, :] = x_rows[:, :OUT_X, :]
-    rows[:, OUT_ROWS - OUT_D :, :] = z_rows[:, OUT_Z:, :]
-    for at, single in enumerate((layer, grad)):
-        single[...] = dot_columns(pick[...], rows[at]).astype(BF16)
+    _, north, east, corner = group_sizes()
+    for at in range(2):
+        total = taken(NORTH_ROWS, z_rows[at], [(0, 0, north)])
+        total = total + taken(NORTH_ROWS, x_rows[at], [(north, east, corner)])
+        rows[at] = total.astype(BF16)
+
+
+def join_kernel(own, z_rows, x_rows, layer, grad):
+    stay, north, east, corner = group_sizes()
+    for at, joined in enumerate((layer, grad)):
+        total = taken(PART, own[at], [(0, 0, stay)])
+        spans = [(stay, 0, north), (stay + north + east, north, corner)]
+        total = total + taken(PART, z_rows[at], spans)
+        total = total + taken(PART, x_rows[at], [(stay + north, 0, east)])
+        joined[...] = total.astype(BF16)
+
+
+def pass_kernel(arrived, passed):
+    passed[...] = arrived[...]
 
 
 def spread_kernel(pick, *refs):
@@ -475,7 +498,9 @@
     owners = (head_index, head_index + sibling, over, over + sibling)
     for at, out in enumerate(outs):
         for owner, piece in zip(owners, arrived[at::2]):
-            gathered[at, pl.ds(pl.multiple_of(owner * PART, 16), PART), :] = piece[...]
+            start = pl.multiple_of(owner * STRIDE, 16)
+            gathered[at, pl.ds(start + STRIDE - 16, 16), :] = jnp.zeros_like(gathered[at, :16, :])
+            gathered[at, pl.ds(start, PART), :] = piece[...]
         out[...] = dot(pick[...], gathered[at]).astype(BF16)
 
 
@@ -553,8 +578,8 @@
             pltpu.VMEM((CELLS, 3 * group), BF16),
             pltpu.VMEM((CELLS, group), BF16),
             pltpu.VMEM((CELLS, 4 * group), BF16),
-            pltpu.VMEM((QUARTERS * PART, 4 * group), BF16),
-            pltpu.VMEM((2, QUARTERS * PART, width), BF16),
+            pltpu.VMEM((QUARTERS * STRIDE, 4 * group), BF16),
+            pltpu.VMEM((2, QUARTERS * STRIDE, width), BF16),
             pltpu.VMEM((width, 4 * group), BF16),
             pltpu.VMEM((width, 3 * group), BF16),
             pltpu.SemaphoreType.DMA((4,)),
@@ -587,7 +612,7 @@
     crossed = lax.ppermute(across, "head", chips)
     *pieces, norm_mark = call(
         norm_kernel,
-        [shaped(2, count, width) for count in (OUT_OWN, OUT_Z, OUT_X + OUT_D)] + [mark],
+        [shaped(2, count, width) for count in OUT_SIZES] + [mark],
         cost=cost(2 * 2 * OUT_ROWS * PART * width, 12 * PART * width),
         name="sum_over_heads",
     )(part_tokens, part_cotangent, gain, group_pick(), stay, swapped, crossed)
@@ -606,8 +631,8 @@
     from_west = rotated(pieces[2], "lon", 1)
     to_north, north_mark = call(
         north_kernel,
-        [shaped(2, OUT_Z + OUT_D, width), mark],
-        cost=cost(0, 8 * (OUT_Z + OUT_D) * width),
+        [shaped(2, NORTH_ROWS, width), mark],
+        cost=cost(0, 8 * NORTH_ROWS * width),
         name="rows_for_north",
         after=(second_mark,),
     )(pieces[1], from_west)
@@ -623,18 +648,20 @@
     each = call(
         join_kernel,
         [shaped(PART, width)] * 2,
-        [pltpu.VMEM((2, OUT_ROWS, width), BF16)],
         cost=cost(2 * 2 * OUT_ROWS * PART * width, 8 * OUT_ROWS * width),
         name="join_home",
         after=(third_mark,),
-    )(group_pick(), *home)
+    )(*home)
     far = [lax.ppermute(single, "head", chips) for single in each]
     near = [lax.ppermute(single, "head", pairs) for single in each]
-    across = [lax.ppermute(single, "head", pairs) for single in far]
+    held = call(
+        pass_kernel, shaped(PART, width), name="pass_on", after=(last,), cost=cost(0, 4 * PART * width)
+    )(far[1])
+    across = [lax.ppermute(single, "head", pairs) for single in (far[0], held)]
     layer_out, grad_tokens, spread_mark = call(
         spread_kernel,
         [shaped(CELLS, width)] * 2 + [mark],
-        [pltpu.VMEM((2, QUARTERS * PART, width), BF16)],
+        [pltpu.VMEM((2, QUARTERS * STRIDE, width), BF16)],
         cost=cost(2 * 2 * CELLS * CELLS * width, 8 * CELLS * width),
         name="spread_outputs",
     )(own_pick(), *each, *near, *far, *across)

time: 69.2 us -> 74.8 us (1.081)
  the two profiles are of different devices: /device:TPU:0 before, /device:TPU:17 now
where the time goes in v6:
time: 74.8 us; the launch traced here: 74.6 us
  starting transfers between devices  28.8 us (39%)
  waiting for transfers between devices  28.8 us (39%)
  Pallas kernels  15.4 us (21%)
  between operations  0.8 us (1%)
  local copies, waits for them, and re-layouts  0.75 us (1%)
    pallas_call x13, Pallas kernels, run(): pl.pallas_call(body, out_shape=outs, in_specs=[near] * len(args) + [outsi...  15.4 us
    ppermute x4, waiting for transfers between devices, rotated(): lax.ppermute(value, axis, [(i, (i + step) % count) for i in range(count)])  12.9 us
    ppermute x2, starting transfers between devices, body(): near = [lax.ppermute(single, 'head', pairs) for single in each]  10.7 us
    ppermute x1, waiting for transfers between devices, body(): crossed = lax.ppermute(across, 'head', chips)  6.59 us
    ppermute x3, waiting for transfers between devices, moved(): return lax.ppermute(value, ('lon', 'lat'), pairs)  5.04 us
    ppermute x2, starting transfers between devices, body(): across = [lax.ppermute(single, 'head', pairs) for single in (far[0], held)]  4.75 us
    ppermute x1, starting transfers between devices, body(): from_lat = lax.ppermute(lat_send, 'lat', neighbours)  3.09 us
    ppermute x4, starting transfers between devices, rotated(): lax.ppermute(value, axis, [(i, (i + step) % count) for i in range(count)])  2.28 us
  transfers between devices with their start and end apart: 19, of which 8 were waited for; matrix products, arithmetic and copies ran while one was open for 0% of the time, Pallas kernels for 4%

profile of v6, /device:TPU:17, one launch (start us, length us, event | category | flops | bytes accessed | tf_op | source)
XLA Modules:
  0.0 74.6 jit_solution(1031093662631719644)
XLA Ops:
  0.6 1.6 %pack_rims.1 = (bf16[112,1024]{1,0:T(8,128)(2,1)S(1)}, bf16[48,1024]{1,0:T(8,128)(2,1)S(1)}, bf16[48,1024]{1,0:T(8,128)(2,1)S(1)}) custom-call(bf16[288,1024]{1,0:T(8,128)(2,1)} %bitcast.6, bf16[288,1024]{1,0:T(8,128)(2,1)} %bitcast.8), custom_call_target="tpu_custom_call" | custom-call | flops 122683392 | bytes 1179648 | tf_op jit(solution)/shard_map/pack_rims/pallas_call | solution.py:160
  2.4 1.2 %collective-permute-start.1 = (bf16[48,1024]{1,0:T(8,128)(2,1)S(1)}, bf16[48,1024]{1,0:T(8,128)(2,1)S(1)}, u32[]{:S(2)}, u32[]{:S(2)}) collective-permute-start(bf16[48,1024]{1,0:T(8,128)(2,1)S(1)} %get-tuple-element.40), channel_id=1, source_target_pairs={{0,16},{4,20},{8,24},{12,28},{16,0},{20,4},{24,8},{28,12},{1,17},{... | collective-permute-start | bytes 294920 | tf_op jit(solution)/shard_map/ppermute | solution.py:523
  3.7 0.7 copy-done.7
  4.5 2.0 %window_bias.1 = (f32[4,144,144]{2,1,0:T(8,128)S(1)}, f32[8,128]{1,0:T(8,128)S(1)}) custom-call(f32[4,759]{1,0:T(4,128)S(1)} %bitcast.12), custom_call_target="tpu_custom_call" | custom-call | flops 1019215872 | bytes 1000000 | tf_op jit(solution)/shard_map/window_bias/pallas_call | solution.py:160
  6.4 5.0 %collective-permute-done.2.refs_2_ = bf16[48,1024]{1,0:T(8,128)(2,1)S(1)} collective-permute-done((bf16[48,1024]{1,0:T(8,128)(2,1)S(1)}, bf16[48,1024]{1,0:T(8,128)(2,1)S(1)}, u32[]{:S(2)}, u32[]{:S(2)}) %collective-permute-start.2) | collective-permute-done | bytes 98336 | tf_op jit(solution)/shard_map/ppermute | solution.py:523
  11.5 1.9 %collective-permute-start.3 = (bf16[208,1024]{1,0:T(8,128)(2,1)S(1)}, bf16[208,1024]{1,0:T(8,128)(2,1)S(1)}, u32[]{:S(2)}, u32[]{:S(2)}) collective-permute-start(bf16[208,1024]{1,0:T(8,128)(2,1)S(1)} %join_rims.1.refs_2_), channel_id=1, source_target_pairs={{0,1},{1,0},{2,3},{3,2},{4,5},{5,4},{6,7},{7,6},{8,9},{9,8},{10,11... | collective-permute-start | bytes 1277960 | tf_op jit(solution)/shard_map/ppermute | solution.py:562
  13.4 1.4 %collective-permute-done.3.refs_3_ = bf16[208,1024]{1,0:T(8,128)(2,1)S(1)} collective-permute-done((bf16[208,1024]{1,0:T(8,128)(2,1)S(1)}, bf16[208,1024]{1,0:T(8,128)(2,1)S(1)}, u32[]{:S(2)}, u32[]{:S(2)}) %collective-permute-start.3) | collective-permute-done | bytes 426016 | tf_op jit(solution)/shard_map/ppermute | solution.py:562
  14.9 7.7 %window_layer.1 = (bf16[512,512]{1,0:T(8,128)(2,1)S(1)}, bf16[512,512]{1,0:T(8,128)(2,1)S(1)}, bf16[512,512]{1,0:T(8,128)(2,1)S(1)}, bf16[512,512]{1,0:T(8,128)(...) custom-call(bf16[288,1024]{1,0:T(8,128)(2,1)S(1)} %bitcast.7, ...), custom_call_target="tpu_custom_call" | custom-call | flops 1811939328 | bytes 8000000 | tf_op jit(solution)/shard_map/window_layer/pallas_call | solution.py:160
  22.6 0.4 collective-permute-start.4
  23.0 0.2 collective-permute-start.7
  23.3 3.1 %collective-permute-start.8 = (bf16[512,512]{1,0:T(8,128)(2,1)S(1)}, bf16[512,512]{1,0:T(8,128)(2,1)S(1)}, u32[]{:S(2)}, u32[]{:S(2)}) collective-permute-start(bf16[512,512]{1,0:T(8,128)(2,1)S(1)} %get-tuple-element.55), channel_id=1, source_target_pairs={{0,4},{4,0},{8,12},{12,8},{1,5},{5,1},{9,13},{13,9},{2,6},{6,2},{1... | collective-permute-start | bytes 1572872 | tf_op jit(solution)/shard_map/ppermute | solution.py:606
  26.4 1.3 %collective-permute-start.5 = (bf16[2,72,1024]{2,1,0:T(8,128)(2,1)S(1)}, bf16[2,72,1024]{2,1,0:T(8,128)(2,1)S(1)}, u32[]{:S(2)}, u32[]{:S(2)}) collective-permute-start(bf16[2,72,1024]{2,1,0:T(8,128)(2,1)S(1)} %sum_over_cores.1), channel_id=1, source_target_pairs={{0,2},{1,3},{2,0},{3,1},{4,6},{5,7},{6,4},{7,5},{8,10},{9,11},{10,... | collective-permute-start | bytes 884744 | tf_op jit(solution)/shard_map/ppermute | solution.py:612
  27.7 6.6 %collective-permute-done.5.refs_6_ = bf16[2,72,1024]{2,1,0:T(8,128)(2,1)S(1)} collective-permute-done((bf16[2,72,1024]{2,1,0:T(8,128)(2,1)S(1)}, bf16[2,72,1024]{2,1,0:T(8,128)(2,1)S(1)}, u32[]{:S(2)}, u32[]{:S(2)}) %collective-permute-start.5) | collective-permute-done | bytes 294944 | tf_op jit(solution)/shard_map/ppermute | solution.py:612
  34.3 0.5 sum_over_heads.1
  34.9 1.5 %collective-permute-done.7.refs_1_ = bf16[512,512]{1,0:T(8,128)(2,1)S(1)} collective-permute-done((bf16[512,512]{1,0:T(8,128)(2,1)S(1)}, bf16[512,512]{1,0:T(8,128)(2,1)S(1)}, u32[]{:S(2)}, u32[]{:S(2)}) %collective-permute-start.7) | collective-permute-done | bytes 524320 | tf_op jit(solution)/shard_map/ppermute | solution.py:513
  36.4 1.9 %collective-permute-done.8.refs_3_ = bf16[512,512]{1,0:T(8,128)(2,1)S(1)} collective-permute-done((bf16[512,512]{1,0:T(8,128)(2,1)S(1)}, bf16[512,512]{1,0:T(8,128)(2,1)S(1)}, u32[]{:S(2)}, u32[]{:S(2)}) %collective-permute-start.8) | collective-permute-done | bytes 524320 | tf_op jit(solution)/shard_map/ppermute | solution.py:606
  38.3 0.2 second_step.1
  38.5 1.3 %collective-permute-start.10 = (bf16[256,512]{1,0:T(8,128)(2,1)S(1)}, bf16[256,512]{1,0:T(8,128)(2,1)S(1)}, u32[]{:S(2)}, u32[]{:S(2)}) collective-permute-start(bf16[256,512]{1,0:T(8,128)(2,1)S(1)} %get-tuple-element.60), channel_id=1, source_target_pairs={{0,4},{4,0},{8,12},{12,8},{1,5},{5,1},{9,13},{13,9},{2,6},{6,2},{1... | collective-permute-start | bytes 786440 | tf_op jit(solution)/shard_map/ppermute | solution.py:629
  39.8 1.1 %collective-permute-start.11 = (bf16[256,512]{1,0:T(8,128)(2,1)S(1)}, bf16[256,512]{1,0:T(8,128)(2,1)S(1)}, u32[]{:S(2)}, u32[]{:S(2)}) collective-permute-start(bf16[256,512]{1,0:T(8,128)(2,1)S(1)} %get-tuple-element.62), channel_id=1, source_target_pairs={{0,16},{16,0},{1,17},{17,1},{2,18},{18,2},{3,19},{19,3},{4,20},{20... | collective-permute-start | bytes 786440 | tf_op jit(solution)/shard_map/ppermute | solution.py:513
  41.0 0.3 collective-permute-start.6
  41.3 7.7 %collective-permute-done.6.refs_1_.refs_2_ = bf16[2,32,1024]{2,1,0:T(8,128)(2,1)S(1)} collective-permute-done((bf16[2,32,1024]{2,1,0:T(8,128)(2,1)S(1)}, bf16[2,32,1024]{2,1,0:T(8,128)(2,1)S(1)}, u32[]{:S(2)}, u32[]{:S(2)}) %collective-permute-start.6) | collective-permute-done | bytes 131104 | tf_op jit(solution)/shard_map/ppermute | solution.py:513
  48.9 0.2 rows_for_north.1
  49.2 0.6 collective-permute-start.9
  49.9 3.7 %collective-permute-done.9.refs_1_ = bf16[2,40,1024]{2,1,0:T(8,128)(2,1)S(1)} collective-permute-done((bf16[2,40,1024]{2,1,0:T(8,128)(2,1)S(1)}, bf16[2,40,1024]{2,1,0:T(8,128)(2,1)S(1)}, u32[]{:S(2)}, u32[]{:S(2)}) %collective-permute-start.9) | collective-permute-done | bytes 163872 | tf_op jit(solution)/shard_map/ppermute | solution.py:513
  53.6 0.4 join_home.1
  54.0 1.3 %collective-permute-start.14 = (bf16[72,1024]{1,0:T(8,128)(2,1)S(1)}, bf16[72,1024]{1,0:T(8,128)(2,1)S(1)}, u32[]{:S(2)}, u32[]{:S(2)}) collective-permute-start(bf16[72,1024]{1,0:T(8,128)(2,1)S(1)} %get-tuple-element.65.refs_1_), channel_id=1, source_target_pairs={{0,2},{1,3},{2,0},{3,1},{4,6},{5,7},{6,4},{7,5},{8,10},{9,11},{10,... | collective-permute-start | bytes 442376 | tf_op jit(solution)/shard_map/ppermute | solution.py:655
  55.6 10.7 %collective-permute-start.12 = (bf16[72,1024]{1,0:T(8,128)(2,1)S(1)}, bf16[72,1024]{1,0:T(8,128)(2,1)S(1)}, u32[]{:S(2)}, u32[]{:S(2)}) collective-permute-start(bf16[72,1024]{1,0:T(8,128)(2,1)S(1)} %get-tuple-element.65.refs_1_), channel_id=1, source_target_pairs={{0,1},{1,0},{2,3},{3,2},{4,5},{5,4},{6,7},{7,6},{8,9},{9,8},{10,11... | collective-permute-start | bytes 442376 | tf_op jit(solution)/shard_map/ppermute | solution.py:656
  66.2 3.1 %collective-permute-start.16 = (bf16[72,1024]{1,0:T(8,128)(2,1)S(1)}, bf16[72,1024]{1,0:T(8,128)(2,1)S(1)}, u32[]{:S(2)}, u32[]{:S(2)}) collective-permute-start(bf16[72,1024]{1,0:T(8,128)(2,1)S(1)} %collective-permute-done.14.refs_5_), channel_id=1, source_target_pairs={{0,1},{1,0},{2,3},{3,2},{4,5},{5,4},{6,7},{7,6},{8,9},{9,8},{10,11... | collective-permute-start | bytes 442376 | tf_op jit(solution)/shard_map/ppermute | solution.py:660
  69.4 1.6 %collective-permute-start.18 = (bf16[72,1024]{1,0:T(8,128)(2,1)S(1)}, bf16[72,1024]{1,0:T(8,128)(2,1)S(1)}, u32[]{:S(2)}, u32[]{:S(2)}) collective-permute-start(bf16[72,1024]{1,0:T(8,128)(2,1)S(1)} %pass_on.1), channel_id=1, source_target_pairs={{0,1},{1,0},{2,3},{3,2},{4,5},{5,4},{6,7},{7,6},{8,9},{9,8},{10,11... | collective-permute-start | bytes 442376 | tf_op jit(solution)/shard_map/ppermute | solution.py:660
  71.0 1.0 %collective-permute-done.18.refs_8_ = bf16[72,1024]{1,0:T(8,128)(2,1)S(1)} collective-permute-done((bf16[72,1024]{1,0:T(8,128)(2,1)S(1)}, bf16[72,1024]{1,0:T(8,128)(2,1)S(1)}, u32[]{:S(2)}, u32[]{:S(2)}) %collective-permute-start.18) | collective-permute-done | bytes 147488 | tf_op jit(solution)/shard_map/ppermute | solution.py:660
  72.0 1.7 %spread_outputs.1 = (bf16[288,1024]{1,0:T(8,128)(2,1)}, bf16[288,1024]{1,0:T(8,128)(2,1)}, f32[8,128]{1,0:T(8,128)S(1)}) custom-call(bf16[288,320]{1,0:T(8,128)(2,1)S(1)} %copy-done.2, bf16[72,1024]{1,0:T(8,128)(2,1)S(1)} %get-tuple-element.65.refs_1_, bf16[72,1024]{1,0:T(8,128)(2,1)S(1)} %get-tuple-element.66.refs_2_, ...), custom_call_target="tpu_custom_call" | custom-call | flops 339738624 | bytes 2359296 | tf_op jit(solution)/shard_map/spread_outputs/pallas_call | solution.py:160
  73.7 0.8 %sum_over_lat.1 = (f32[128,768]{1,0:T(8,128)}, f32[256,128]{1,0:T(8,128)}) custom-call(f32[2,128,512]{2,1,0:T(8,128)S(1)} %get-tuple-element.70.refs_0_, bf16[2,128,512]{2,1,0:T(8,128)(2,1)S(1)} %collective-permute-done.17.refs_1_, f32[8,128]{1,0:T(8,128)S(1)} %get-tuple-element.71.refs_2_), custom_call_target="tpu_custom_call" | custom-call | flops 524288 | bytes 2097152 | tf_op jit(solution)/shard_map/sum_over_lat/pallas_call | solution.py:160
  (39 shorter events, 0.8 us)
Async XLA Ops:
  2.2 9.3 %collective-permute-start = (bf16[112,1024]{1,0:T(8,128)(2,1)S(1)}, bf16[112,1024]{1,0:T(8,128)(2,1)S(1)}, u32[]{:S(2)}, u32[]{:S(2)}) collective-permute-start(bf16[112,1024]{1,0:T(8,128)(2,1)S(1)} %get-tuple-element.39), channel_id=1, source_target_pairs={{0,12},{4,0},{8,4},{12,8},{16,28},{20,16},{24,20},{28,24},{1,13},{... | collective-permute-start | bytes 688136 | tf_op jit(solution)/shard_map/ppermute | solution.py:523
  2.4 4.0 %collective-permute-start.1 = (bf16[48,1024]{1,0:T(8,128)(2,1)S(1)}, bf16[48,1024]{1,0:T(8,128)(2,1)S(1)}, u32[]{:S(2)}, u32[]{:S(2)}) collective-permute-start(bf16[48,1024]{1,0:T(8,128)(2,1)S(1)} %get-tuple-element.40), channel_id=1, source_target_pairs={{0,16},{4,20},{8,24},{12,28},{16,0},{20,4},{24,8},{28,12},{1,17},{... | collective-permute-start | bytes 294920 | tf_op jit(solution)/shard_map/ppermute | solution.py:523
  3.7 7.8 %collective-permute-start.2 = (bf16[48,1024]{1,0:T(8,128)(2,1)S(1)}, bf16[48,1024]{1,0:T(8,128)(2,1)S(1)}, u32[]{:S(2)}, u32[]{:S(2)}) collective-permute-start(bf16[48,1024]{1,0:T(8,128)(2,1)S(1)} %get-tuple-element.41), channel_id=1, source_target_pairs={{0,28},{4,16},{8,20},{12,24},{16,12},{20,0},{24,4},{28,8},{1,29},{... | collective-permute-start | bytes 294920 | tf_op jit(solution)/shard_map/ppermute | solution.py:523
  3.7 0.7 copy-start.7
  4.4 10.4 %copy-start = (bf16[2,6,24,1024]{3,2,1,0:T(8,128)(2,1)S(1)}, bf16[2,6,24,1024]{3,2,1,0:T(8,128)(2,1)}, u32[]{:S(2)}) copy-start(bf16[2,6,24,1024]{3,2,1,0:T(8,128)(2,1)} %param.10) | copy-start | bytes 1769476
  4.4 10.4 %copy-start.1 = (bf16[2,6,24,1024]{3,2,1,0:T(8,128)(2,1)S(1)}, bf16[2,6,24,1024]{3,2,1,0:T(8,128)(2,1)}, u32[]{:S(2)}) copy-start(bf16[2,6,24,1024]{3,2,1,0:T(8,128)(2,1)} %param.15) | copy-start | bytes 1769476
  4.4 10.4 %copy-start.4 = (f32[1024]{0:T(1024)S(1)}, f32[1024]{0:T(1024)}, u32[]{:S(2)}) copy-start(f32[1024]{0:T(1024)} %param.11) | copy-start | bytes 12292
  4.4 10.4 %copy-start.5 = (bf16[1024,768]{1,0:T(8,128)(2,1)S(1)}, bf16[1024,768]{1,0:T(8,128)(2,1)}, u32[]{:S(2)}) copy-start(bf16[1024,768]{1,0:T(8,128)(2,1)} %refs_9_.1) | copy-start | bytes 4718596
  4.4 10.4 %copy-start.6 = (bf16[256,1024]{1,0:T(8,128)(2,1)S(1)}, bf16[256,1024]{1,0:T(8,128)(2,1)}, u32[]{:S(2)}) copy-start(bf16[256,1024]{1,0:T(8,128)(2,1)} %refs_5_.1) | copy-start | bytes 1572868
  4.4 10.4 %copy-start.8 = (bf16[288,496]{1,0:T(8,128)(2,1)S(1)}, bf16[288,496]{1,0:T(8,128)(2,1)}, u32[]{:S(2)}) copy-start(bf16[288,496]{1,0:T(8,128)(2,1)} %constant.8.clone.refs_7_) | copy-start | bytes 857092
  4.5 10.4 %copy-start.9 = (bf16[320,288]{1,0:T(8,128)(2,1)S(1)}, bf16[320,288]{1,0:T(8,128)(2,1)}, u32[]{:S(2)}) copy-start(bf16[320,288]{1,0:T(8,128)(2,1)} %constant.9.clone.refs_8_) | copy-start | bytes 552964
  11.5 3.3 %collective-permute-start.3 = (bf16[208,1024]{1,0:T(8,128)(2,1)S(1)}, bf16[208,1024]{1,0:T(8,128)(2,1)S(1)}, u32[]{:S(2)}, u32[]{:S(2)}) collective-permute-start(bf16[208,1024]{1,0:T(8,128)(2,1)S(1)} %join_rims.1.refs_2_), channel_id=1, source_target_pairs={{0,1},{1,0},{2,3},{3,2},{4,5},{5,4},{6,7},{7,6},{8,9},{9,8},{10,11... | collective-permute-start | bytes 1277960 | tf_op jit(solution)/shard_map/ppermute | solution.py:562
  14.9 19.5 %copy-start.3 = (bf16[96,72]{1,0:T(8,128)(2,1)S(1)}, bf16[96,72]{1,0:T(8,128)(2,1)}, u32[]{:S(2)}) copy-start(bf16[96,72]{1,0:T(8,128)(2,1)} %constant.10.clone.refs_3_) | copy-start | bytes 41476
  22.6 3.8 %collective-permute-start.4 = (bf16[2,2,72,1024]{3,2,1,0:T(8,128)(2,1)S(1)}, bf16[2,2,72,1024]{3,2,1,0:T(8,128)(2,1)S(1)}, u32[]{:S(2)}, u32[]{:S(2)}) collective-permute-start(bf16[2,2,72,1024]{3,2,1,0:T(8,128)(2,1)S(1)} %get-tuple-element.47), channel_id=1, source_target_pairs={{0,1},{1,0},{2,3},{3,2},{4,5},{5,4},{6,7},{7,6},{8,9},{9,8},{10,11... | collective-permute-start | bytes 1769480 | tf_op jit(solution)/shard_map/ppermute | solution.py:607
  23.0 13.4 %collective-permute-start.7 = (bf16[512,512]{1,0:T(8,128)(2,1)S(1)}, bf16[512,512]{1,0:T(8,128)(2,1)S(1)}, u32[]{:S(2)}, u32[]{:S(2)}) collective-permute-start(bf16[512,512]{1,0:T(8,128)(2,1)S(1)} %get-tuple-element.53), channel_id=1, source_target_pairs={{0,16},{16,0},{1,17},{17,1},{2,18},{18,2},{3,19},{19,3},{4,20},{20... | collective-permute-start | bytes 1572872 | tf_op jit(solution)/shard_map/ppermute | solution.py:513
  23.3 15.0 %collective-permute-start.8 = (bf16[512,512]{1,0:T(8,128)(2,1)S(1)}, bf16[512,512]{1,0:T(8,128)(2,1)S(1)}, u32[]{:S(2)}, u32[]{:S(2)}) collective-permute-start(bf16[512,512]{1,0:T(8,128)(2,1)S(1)} %get-tuple-element.55), channel_id=1, source_target_pairs={{0,4},{4,0},{8,12},{12,8},{1,5},{5,1},{9,13},{13,9},{2,6},{6,2},{1... | collective-permute-start | bytes 1572872 | tf_op jit(solution)/shard_map/ppermute | solution.py:606
  26.4 7.9 %collective-permute-start.5 = (bf16[2,72,1024]{2,1,0:T(8,128)(2,1)S(1)}, bf16[2,72,1024]{2,1,0:T(8,128)(2,1)S(1)}, u32[]{:S(2)}, u32[]{:S(2)}) collective-permute-start(bf16[2,72,1024]{2,1,0:T(8,128)(2,1)S(1)} %sum_over_cores.1), channel_id=1, source_target_pairs={{0,2},{1,3},{2,0},{3,1},{4,6},{5,7},{6,4},{7,5},{8,10},{9,11},{10,... | collective-permute-start | bytes 884744 | tf_op jit(solution)/shard_map/ppermute | solution.py:612
  38.5 33.5 %copy-start.2 = (bf16[288,320]{1,0:T(8,128)(2,1)S(1)}, bf16[288,320]{1,0:T(8,128)(2,1)}, u32[]{:S(2)}) copy-start(bf16[288,320]{1,0:T(8,128)(2,1)} %constant.11.clone.refs_0_) | copy-start | bytes 552964
  38.5 11.2 %collective-permute-start.10 = (bf16[256,512]{1,0:T(8,128)(2,1)S(1)}, bf16[256,512]{1,0:T(8,128)(2,1)S(1)}, u32[]{:S(2)}, u32[]{:S(2)}) collective-permute-start(bf16[256,512]{1,0:T(8,128)(2,1)S(1)} %get-tuple-element.60), channel_id=1, source_target_pairs={{0,4},{4,0},{8,12},{12,8},{1,5},{5,1},{9,13},{13,9},{2,6},{6,2},{1... | collective-permute-start | bytes 786440 | tf_op jit(solution)/shard_map/ppermute | solution.py:629
  39.8 9.9 %collective-permute-start.11 = (bf16[256,512]{1,0:T(8,128)(2,1)S(1)}, bf16[256,512]{1,0:T(8,128)(2,1)S(1)}, u32[]{:S(2)}, u32[]{:S(2)}) collective-permute-start(bf16[256,512]{1,0:T(8,128)(2,1)S(1)} %get-tuple-element.62), channel_id=1, source_target_pairs={{0,16},{16,0},{1,17},{17,1},{2,18},{18,2},{3,19},{19,3},{4,20},{20... | collective-permute-start | bytes 786440 | tf_op jit(solution)/shard_map/ppermute | solution.py:513
  41.0 8.0 %collective-permute-start.6 = (bf16[2,32,1024]{2,1,0:T(8,128)(2,1)S(1)}, bf16[2,32,1024]{2,1,0:T(8,128)(2,1)S(1)}, u32[]{:S(2)}, u32[]{:S(2)}) collective-permute-start(bf16[2,32,1024]{2,1,0:T(8,128)(2,1)S(1)} %get-tuple-element.51), channel_id=1, source_target_pairs={{0,16},{16,0},{1,17},{17,1},{2,18},{18,2},{3,19},{19,3},{4,20},{20... | collective-permute-start | bytes 393224 | tf_op jit(solution)/shard_map/ppermute | solution.py:513
  49.2 4.4 %collective-permute-start.9 = (bf16[2,40,1024]{2,1,0:T(8,128)(2,1)S(1)}, bf16[2,40,1024]{2,1,0:T(8,128)(2,1)S(1)}, u32[]{:S(2)}, u32[]{:S(2)}) collective-permute-start(bf16[2,40,1024]{2,1,0:T(8,128)(2,1)S(1)} %get-tuple-element.58), channel_id=1, source_target_pairs={{0,4},{4,8},{8,12},{12,0},{1,5},{5,9},{9,13},{13,1},{2,6},{6,10},{... | collective-permute-start | bytes 491528 | tf_op jit(solution)/shard_map/ppermute | solution.py:513
  49.8 19.5 %collective-permute-start.17 = (bf16[2,128,512]{2,1,0:T(8,128)(2,1)S(1)}, bf16[2,128,512]{2,1,0:T(8,128)(2,1)S(1)}, u32[]{:S(2)}, u32[]{:S(2)}) collective-permute-start(bf16[2,128,512]{2,1,0:T(8,128)(2,1)S(1)} %get-tuple-element.67), channel_id=1, source_target_pairs={{0,8},{4,12},{8,0},{12,4},{1,9},{5,13},{9,1},{13,5},{2,10},{6,14},... | collective-permute-start | bytes 786440 | tf_op jit(solution)/shard_map/ppermute | solution.py:647
  54.0 12.2 %collective-permute-start.14 = (bf16[72,1024]{1,0:T(8,128)(2,1)S(1)}, bf16[72,1024]{1,0:T(8,128)(2,1)S(1)}, u32[]{:S(2)}, u32[]{:S(2)}) collective-permute-start(bf16[72,1024]{1,0:T(8,128)(2,1)S(1)} %get-tuple-element.65.refs_1_), channel_id=1, source_target_pairs={{0,2},{1,3},{2,0},{3,1},{4,6},{5,7},{6,4},{7,5},{8,10},{9,11},{10,... | collective-permute-start | bytes 442376 | tf_op jit(solution)/shard_map/ppermute | solution.py:655
  55.4 14.0 %collective-permute-start.15 = (bf16[72,1024]{1,0:T(8,128)(2,1)S(1)}, bf16[72,1024]{1,0:T(8,128)(2,1)S(1)}, u32[]{:S(2)}, u32[]{:S(2)}) collective-permute-start(bf16[72,1024]{1,0:T(8,128)(2,1)S(1)} %get-tuple-element.66.refs_2_), channel_id=1, source_target_pairs={{0,2},{1,3},{2,0},{3,1},{4,6},{5,7},{6,4},{7,5},{8,10},{9,11},{10,... | collective-permute-start | bytes 442376 | tf_op jit(solution)/shard_map/ppermute | solution.py:655
  55.6 15.4 %collective-permute-start.12 = (bf16[72,1024]{1,0:T(8,128)(2,1)S(1)}, bf16[72,1024]{1,0:T(8,128)(2,1)S(1)}, u32[]{:S(2)}, u32[]{:S(2)}) collective-permute-start(bf16[72,1024]{1,0:T(8,128)(2,1)S(1)} %get-tuple-element.65.refs_1_), channel_id=1, source_target_pairs={{0,1},{1,0},{2,3},{3,2},{4,5},{5,4},{6,7},{7,6},{8,9},{9,8},{10,11... | collective-permute-start | bytes 442376 | tf_op jit(solution)/shard_map/ppermute | solution.py:656
  66.2 4.8 %collective-permute-start.13 = (bf16[72,1024]{1,0:T(8,128)(2,1)S(1)}, bf16[72,1024]{1,0:T(8,128)(2,1)S(1)}, u32[]{:S(2)}, u32[]{:S(2)}) collective-permute-start(bf16[72,1024]{1,0:T(8,128)(2,1)S(1)} %get-tuple-element.66.refs_2_), channel_id=1, source_target_pairs={{0,1},{1,0},{2,3},{3,2},{4,5},{5,4},{6,7},{7,6},{8,9},{9,8},{10,11... | collective-permute-start | bytes 442376 | tf_op jit(solution)/shard_map/ppermute | solution.py:656
  66.2 4.8 %collective-permute-start.16 = (bf16[72,1024]{1,0:T(8,128)(2,1)S(1)}, bf16[72,1024]{1,0:T(8,128)(2,1)S(1)}, u32[]{:S(2)}, u32[]{:S(2)}) collective-permute-start(bf16[72,1024]{1,0:T(8,128)(2,1)S(1)} %collective-permute-done.14.refs_5_), channel_id=1, source_target_pairs={{0,1},{1,0},{2,3},{3,2},{4,5},{5,4},{6,7},{7,6},{8,9},{9,8},{10,11... | collective-permute-start | bytes 442376 | tf_op jit(solution)/shard_map/ppermute | solution.py:660
  69.4 2.6 %collective-permute-start.18 = (bf16[72,1024]{1,0:T(8,128)(2,1)S(1)}, bf16[72,1024]{1,0:T(8,128)(2,1)S(1)}, u32[]{:S(2)}, u32[]{:S(2)}) collective-permute-start(bf16[72,1024]{1,0:T(8,128)(2,1)S(1)} %pass_on.1), channel_id=1, source_target_pairs={{0,1},{1,0},{2,3},{3,2},{4,5},{5,4},{6,7},{7,6},{8,9},{9,8},{10,11... | collective-permute-start | bytes 442376 | tf_op jit(solution)/shard_map/ppermute | solution.py:660

commit v7 on v6

--- a/solution.py
+++ b/solution.py
@@ -483,10 +483,6 @@
         total = total + taken(PART, z_rows[at], spans)
         total = total + taken(PART, x_rows[at], [(stay + north, 0, east)])
         joined[...] = total.astype(BF16)
-
-
-def pass_kernel(arrived, passed):
-    passed[...] = arrived[...]
 
 
 def spread_kernel(pick, *refs):
@@ -654,10 +650,7 @@
     )(*home)
     far = [lax.ppermute(single, "head", chips) for single in each]
     near = [lax.ppermute(single, "head", pairs) for single in each]
-    held = call(
-        pass_kernel, shaped(PART, width), name="pass_on", after=(last,), cost=cost(0, 4 * PART * width)
-    )(far[1])
-    across = [lax.ppermute(single, "head", pairs) for single in (far[0], held)]
+    across = [lax.ppermute(single, "head", pairs) for single in far]
     layer_out, grad_tokens, spread_mark = call(
         spread_kernel,
         [shaped(CELLS, width)] * 2 + [mark],

time: 74.8 us -> 68.3 us (0.913)
  the two profiles are of different devices: /device:TPU:17 before, /device:TPU:0 now
where the time goes in v7:
time: 68.3 us; the launch traced here: 68.1 us
  waiting for transfers between devices  33.3 us (49%)
  starting transfers between devices  17.9 us (26%)
  Pallas kernels  15.4 us (23%)
  between operations  0.8 us (1%)
  local copies, waits for them, and re-layouts  0.75 us (1%)
    pallas_call x12, Pallas kernels, run(): pl.pallas_call(body, out_shape=outs, in_specs=[near] * len(args) + [outsi...  15.4 us
    ppermute x4, waiting for transfers between devices, rotated(): lax.ppermute(value, axis, [(i, (i + step) % count) for i in range(count)])  7.87 us
    ppermute x1, waiting for transfers between devices, body(): crossed = lax.ppermute(across, 'head', chips)  7.49 us
    ppermute x3, starting transfers between devices, moved(): return lax.ppermute(value, ('lon', 'lat'), pairs)  7 us
    ppermute x4, starting transfers between devices, rotated(): lax.ppermute(value, axis, [(i, (i + step) % count) for i in range(count)])  5.14 us
    ppermute x2, waiting for transfers between devices, body(): far = [lax.ppermute(single, 'head', chips) for single in each]  5 us
    ppermute x1, waiting for transfers between devices, body(): from_lat = lax.ppermute(send_first, 'lat', neighbours)  4.29 us
    ppermute x1, waiting for transfers between devices, body(): last = lax.ppermute(send, 'lat', [(i, i ^ 2) for i in range(lat_count)])  2.5 us
  transfers between devices with their start and end apart: 19, of which 13 were waited for; matrix products, arithmetic and copies ran while one was open for 0% of the time, Pallas kernels for 7%

profile of v7, /device:TPU:0, one launch (start us, length us, event | category | flops | bytes accessed | tf_op | source)
XLA Modules:
  0.0 68.1 jit_solution(14039437703408054717)
XLA Ops:
  0.6 1.6 %pack_rims.1 = (bf16[112,1024]{1,0:T(8,128)(2,1)S(1)}, bf16[48,1024]{1,0:T(8,128)(2,1)S(1)}, bf16[48,1024]{1,0:T(8,128)(2,1)S(1)}) custom-call(bf16[288,1024]{1,0:T(8,128)(2,1)} %bitcast.6, bf16[288,1024]{1,0:T(8,128)(2,1)} %bitcast.8), custom_call_target="tpu_custom_call" | custom-call | flops 122683392 | bytes 1179648 | tf_op jit(solution)/shard_map/pack_rims/pallas_call | solution.py:160
  2.2 5.1 %collective-permute-start = (bf16[112,1024]{1,0:T(8,128)(2,1)S(1)}, bf16[112,1024]{1,0:T(8,128)(2,1)S(1)}, u32[]{:S(2)}, u32[]{:S(2)}) collective-permute-start(bf16[112,1024]{1,0:T(8,128)(2,1)S(1)} %get-tuple-element.39), channel_id=1, source_target_pairs={{0,12},{4,0},{8,4},{12,8},{16,28},{20,16},{24,20},{28,24},{1,13},{... | collective-permute-start | bytes 688136 | tf_op jit(solution)/shard_map/ppermute | solution.py:519
  7.3 1.5 %collective-permute-start.1 = (bf16[48,1024]{1,0:T(8,128)(2,1)S(1)}, bf16[48,1024]{1,0:T(8,128)(2,1)S(1)}, u32[]{:S(2)}, u32[]{:S(2)}) collective-permute-start(bf16[48,1024]{1,0:T(8,128)(2,1)S(1)} %get-tuple-element.40), channel_id=1, source_target_pairs={{0,16},{4,20},{8,24},{12,28},{16,0},{20,4},{24,8},{28,12},{1,17},{... | collective-permute-start | bytes 294920 | tf_op jit(solution)/shard_map/ppermute | solution.py:519
  8.8 0.4 collective-permute-start.2
  9.2 0.7 %copy-done.7 = f32[759,4]{0,1:T(4,128)S(1)} copy-done((f32[759,4]{0,1:T(4,128)S(1)}, f32[759,4]{0,1:T(4,128)}, u32[]{:S(2)}) %copy-start.7) | copy-done | bytes 12168
  10.0 2.0 %window_bias.1 = (f32[4,144,144]{2,1,0:T(8,128)S(1)}, f32[8,128]{1,0:T(8,128)S(1)}) custom-call(f32[4,759]{1,0:T(4,128)S(1)} %bitcast.12), custom_call_target="tpu_custom_call" | custom-call | flops 1019215872 | bytes 1000000 | tf_op jit(solution)/shard_map/window_bias/pallas_call | solution.py:160
  12.0 1.0 %collective-permute-done.1.refs_1_ = bf16[48,1024]{1,0:T(8,128)(2,1)S(1)} collective-permute-done((bf16[48,1024]{1,0:T(8,128)(2,1)S(1)}, bf16[48,1024]{1,0:T(8,128)(2,1)S(1)}, u32[]{:S(2)}, u32[]{:S(2)}) %collective-permute-start.1) | collective-permute-done | bytes 98336 | tf_op jit(solution)/shard_map/ppermute | solution.py:519
  13.0 1.3 %collective-permute-done.2.refs_2_ = bf16[48,1024]{1,0:T(8,128)(2,1)S(1)} collective-permute-done((bf16[48,1024]{1,0:T(8,128)(2,1)S(1)}, bf16[48,1024]{1,0:T(8,128)(2,1)S(1)}, u32[]{:S(2)}, u32[]{:S(2)}) %collective-permute-start.2) | collective-permute-done | bytes 98336 | tf_op jit(solution)/shard_map/ppermute | solution.py:519
  14.4 1.8 %collective-permute-done.3.refs_3_ = bf16[208,1024]{1,0:T(8,128)(2,1)S(1)} collective-permute-done((bf16[208,1024]{1,0:T(8,128)(2,1)S(1)}, bf16[208,1024]{1,0:T(8,128)(2,1)S(1)}, u32[]{:S(2)}, u32[]{:S(2)}) %collective-permute-start.3) | collective-permute-done | bytes 426016 | tf_op jit(solution)/shard_map/ppermute | solution.py:558
  16.3 7.7 %window_layer.1 = (bf16[512,512]{1,0:T(8,128)(2,1)S(1)}, bf16[512,512]{1,0:T(8,128)(2,1)S(1)}, bf16[512,512]{1,0:T(8,128)(2,1)S(1)}, bf16[512,512]{1,0:T(8,128)(...) custom-call(bf16[288,1024]{1,0:T(8,128)(2,1)S(1)} %bitcast.7, ...), custom_call_target="tpu_custom_call" | custom-call | flops 1811939328 | bytes 8000000 | tf_op jit(solution)/shard_map/window_layer/pallas_call | solution.py:160
  24.1 1.5 %collective-permute-start.7 = (bf16[512,512]{1,0:T(8,128)(2,1)S(1)}, bf16[512,512]{1,0:T(8,128)(2,1)S(1)}, u32[]{:S(2)}, u32[]{:S(2)}) collective-permute-start(bf16[512,512]{1,0:T(8,128)(2,1)S(1)} %get-tuple-element.53), channel_id=1, source_target_pairs={{0,16},{16,0},{1,17},{17,1},{2,18},{18,2},{3,19},{19,3},{4,20},{20... | collective-permute-start | bytes 1572872 | tf_op jit(solution)/shard_map/ppermute | solution.py:509
  25.6 0.4 collective-permute-start.8
  26.1 1.6 %collective-permute-start.5 = (bf16[2,72,1024]{2,1,0:T(8,128)(2,1)S(1)}, bf16[2,72,1024]{2,1,0:T(8,128)(2,1)S(1)}, u32[]{:S(2)}, u32[]{:S(2)}) collective-permute-start(bf16[2,72,1024]{2,1,0:T(8,128)(2,1)S(1)} %sum_over_cores.1), channel_id=1, source_target_pairs={{0,2},{1,3},{2,0},{3,1},{4,6},{5,7},{6,4},{7,5},{8,10},{9,11},{10,... | collective-permute-start | bytes 884744 | tf_op jit(solution)/shard_map/ppermute | solution.py:608
  27.7 7.5 %collective-permute-done.5.refs_6_ = bf16[2,72,1024]{2,1,0:T(8,128)(2,1)S(1)} collective-permute-done((bf16[2,72,1024]{2,1,0:T(8,128)(2,1)S(1)}, bf16[2,72,1024]{2,1,0:T(8,128)(2,1)S(1)}, u32[]{:S(2)}, u32[]{:S(2)}) %collective-permute-start.5) | collective-permute-done | bytes 294944 | tf_op jit(solution)/shard_map/ppermute | solution.py:608
  35.2 0.5 sum_over_heads.1
  35.7 1.5 %collective-permute-start.6 = (bf16[2,32,1024]{2,1,0:T(8,128)(2,1)S(1)}, bf16[2,32,1024]{2,1,0:T(8,128)(2,1)S(1)}, u32[]{:S(2)}, u32[]{:S(2)}) collective-permute-start(bf16[2,32,1024]{2,1,0:T(8,128)(2,1)S(1)} %get-tuple-element.51), channel_id=1, source_target_pairs={{0,16},{16,0},{1,17},{17,1},{2,18},{18,2},{3,19},{19,3},{4,20},{20... | collective-permute-start | bytes 393224 | tf_op jit(solution)/shard_map/ppermute | solution.py:509
  37.3 1.6 %collective-permute-done.7.refs_1_ = bf16[512,512]{1,0:T(8,128)(2,1)S(1)} collective-permute-done((bf16[512,512]{1,0:T(8,128)(2,1)S(1)}, bf16[512,512]{1,0:T(8,128)(2,1)S(1)}, u32[]{:S(2)}, u32[]{:S(2)}) %collective-permute-start.7) | collective-permute-done | bytes 524320 | tf_op jit(solution)/shard_map/ppermute | solution.py:509
  38.9 0.6 collective-permute-done.8.refs_3_
  39.8 0.8 %collective-permute-start.10 = (bf16[256,512]{1,0:T(8,128)(2,1)S(1)}, bf16[256,512]{1,0:T(8,128)(2,1)S(1)}, u32[]{:S(2)}, u32[]{:S(2)}) collective-permute-start(bf16[256,512]{1,0:T(8,128)(2,1)S(1)} %get-tuple-element.60), channel_id=1, source_target_pairs={{0,4},{4,0},{8,12},{12,8},{1,5},{5,1},{9,13},{13,9},{2,6},{6,2},{1... | collective-permute-start | bytes 786440 | tf_op jit(solution)/shard_map/ppermute | solution.py:625
  40.6 1.2 %collective-permute-start.11 = (bf16[256,512]{1,0:T(8,128)(2,1)S(1)}, bf16[256,512]{1,0:T(8,128)(2,1)S(1)}, u32[]{:S(2)}, u32[]{:S(2)}) collective-permute-start(bf16[256,512]{1,0:T(8,128)(2,1)S(1)} %get-tuple-element.62), channel_id=1, source_target_pairs={{0,16},{16,0},{1,17},{17,1},{2,18},{18,2},{3,19},{19,3},{4,20},{20... | collective-permute-start | bytes 786440 | tf_op jit(solution)/shard_map/ppermute | solution.py:509
  42.0 1.0 %collective-permute-start.9 = (bf16[2,40,1024]{2,1,0:T(8,128)(2,1)S(1)}, bf16[2,40,1024]{2,1,0:T(8,128)(2,1)S(1)}, u32[]{:S(2)}, u32[]{:S(2)}) collective-permute-start(bf16[2,40,1024]{2,1,0:T(8,128)(2,1)S(1)} %get-tuple-element.58), channel_id=1, source_target_pairs={{0,4},{4,8},{8,12},{12,0},{1,5},{5,9},{9,13},{13,1},{2,6},{6,10},{... | collective-permute-start | bytes 491528 | tf_op jit(solution)/shard_map/ppermute | solution.py:509
  43.0 4.3 %collective-permute-done.10.refs_1_ = bf16[256,512]{1,0:T(8,128)(2,1)S(1)} collective-permute-done((bf16[256,512]{1,0:T(8,128)(2,1)S(1)}, bf16[256,512]{1,0:T(8,128)(2,1)S(1)}, u32[]{:S(2)}, u32[]{:S(2)}) %collective-permute-start.10) | collective-permute-done | bytes 262176 | tf_op jit(solution)/shard_map/ppermute | solution.py:625
  47.6 6.0 %collective-permute-done.9.refs_1_ = bf16[2,40,1024]{2,1,0:T(8,128)(2,1)S(1)} collective-permute-done((bf16[2,40,1024]{2,1,0:T(8,128)(2,1)S(1)}, bf16[2,40,1024]{2,1,0:T(8,128)(2,1)S(1)}, u32[]{:S(2)}, u32[]{:S(2)}) %collective-permute-start.9) | collective-permute-done | bytes 163872 | tf_op jit(solution)/shard_map/ppermute | solution.py:509
  54.0 1.6 %collective-permute-start.14 = (bf16[72,1024]{1,0:T(8,128)(2,1)S(1)}, bf16[72,1024]{1,0:T(8,128)(2,1)S(1)}, u32[]{:S(2)}, u32[]{:S(2)}) collective-permute-start(bf16[72,1024]{1,0:T(8,128)(2,1)S(1)} %get-tuple-element.65.refs_1_), channel_id=1, source_target_pairs={{0,2},{1,3},{2,0},{3,1},{4,6},{5,7},{6,4},{7,5},{8,10},{9,11},{10,... | collective-permute-start | bytes 442376 | tf_op jit(solution)/shard_map/ppermute | solution.py:651
  55.6 0.5 collective-permute-start.15
  56.1 0.5 collective-permute-start.13
  56.6 3.4 %collective-permute-done.14.refs_5_ = bf16[72,1024]{1,0:T(8,128)(2,1)S(1)} collective-permute-done((bf16[72,1024]{1,0:T(8,128)(2,1)S(1)}, bf16[72,1024]{1,0:T(8,128)(2,1)S(1)}, u32[]{:S(2)}, u32[]{:S(2)}) %collective-permute-start.14) | collective-permute-done | bytes 147488 | tf_op jit(solution)/shard_map/ppermute | solution.py:651
  60.1 1.6 %collective-permute-done.15.refs_6_ = bf16[72,1024]{1,0:T(8,128)(2,1)S(1)} collective-permute-done((bf16[72,1024]{1,0:T(8,128)(2,1)S(1)}, bf16[72,1024]{1,0:T(8,128)(2,1)S(1)}, u32[]{:S(2)}, u32[]{:S(2)}) %collective-permute-start.15) | collective-permute-done | bytes 147488 | tf_op jit(solution)/shard_map/ppermute | solution.py:651
  61.7 1.3 %collective-permute-done.17.refs_8_ = bf16[72,1024]{1,0:T(8,128)(2,1)S(1)} collective-permute-done((bf16[72,1024]{1,0:T(8,128)(2,1)S(1)}, bf16[72,1024]{1,0:T(8,128)(2,1)S(1)}, u32[]{:S(2)}, u32[]{:S(2)}) %collective-permute-start.17) | collective-permute-done | bytes 147488 | tf_op jit(solution)/shard_map/ppermute | solution.py:653
  63.0 1.7 %spread_outputs.1 = (bf16[288,1024]{1,0:T(8,128)(2,1)}, bf16[288,1024]{1,0:T(8,128)(2,1)}, f32[8,128]{1,0:T(8,128)S(1)}) custom-call(bf16[288,320]{1,0:T(8,128)(2,1)S(1)} %copy-done.2, bf16[72,1024]{1,0:T(8,128)(2,1)S(1)} %get-tuple-element.65.refs_1_, bf16[72,1024]{1,0:T(8,128)(2,1)S(1)} %get-tuple-element.66.refs_2_, ...), custom_call_target="tpu_custom_call" | custom-call | flops 339738624 | bytes 2359296 | tf_op jit(solution)/shard_map/spread_outputs/pallas_call | solution.py:160
  64.7 2.5 %collective-permute-done.18.refs_1_ = bf16[2,128,512]{2,1,0:T(8,128)(2,1)S(1)} collective-permute-done((bf16[2,128,512]{2,1,0:T(8,128)(2,1)S(1)}, bf16[2,128,512]{2,1,0:T(8,128)(2,1)S(1)}, u32[]{:S(2)}, u32[]{:S(2)}) %collective-permute-start.18) | collective-permute-done | bytes 262176 | tf_op jit(solution)/shard_map/ppermute | solution.py:643
  67.2 0.8 %sum_over_lat.1 = (f32[128,768]{1,0:T(8,128)}, f32[256,128]{1,0:T(8,128)}) custom-call(f32[2,128,512]{2,1,0:T(8,128)S(1)} %get-tuple-element.69.refs_0_, bf16[2,128,512]{2,1,0:T(8,128)(2,1)S(1)} %collective-permute-done.18.refs_1_, f32[8,128]{1,0:T(8,128)S(1)} %get-tuple-element.71.refs_2_), custom_call_target="tpu_custom_call" | custom-call | flops 524288 | bytes 2097152 | tf_op jit(solution)/shard_map/sum_over_lat/pallas_call | solution.py:160
  (38 shorter events, 1.7 us)
Async XLA Ops:
  2.2 12.1 %collective-permute-start = (bf16[112,1024]{1,0:T(8,128)(2,1)S(1)}, bf16[112,1024]{1,0:T(8,128)(2,1)S(1)}, u32[]{:S(2)}, u32[]{:S(2)}) collective-permute-start(bf16[112,1024]{1,0:T(8,128)(2,1)S(1)} %get-tuple-element.39), channel_id=1, source_target_pairs={{0,12},{4,0},{8,4},{12,8},{16,28},{20,16},{24,20},{28,24},{1,13},{... | collective-permute-start | bytes 688136 | tf_op jit(solution)/shard_map/ppermute | solution.py:519
  7.3 5.7 %collective-permute-start.1 = (bf16[48,1024]{1,0:T(8,128)(2,1)S(1)}, bf16[48,1024]{1,0:T(8,128)(2,1)S(1)}, u32[]{:S(2)}, u32[]{:S(2)}) collective-permute-start(bf16[48,1024]{1,0:T(8,128)(2,1)S(1)} %get-tuple-element.40), channel_id=1, source_target_pairs={{0,16},{4,20},{8,24},{12,28},{16,0},{20,4},{24,8},{28,12},{1,17},{... | collective-permute-start | bytes 294920 | tf_op jit(solution)/shard_map/ppermute | solution.py:519
  8.8 5.5 %collective-permute-start.2 = (bf16[48,1024]{1,0:T(8,128)(2,1)S(1)}, bf16[48,1024]{1,0:T(8,128)(2,1)S(1)}, u32[]{:S(2)}, u32[]{:S(2)}) collective-permute-start(bf16[48,1024]{1,0:T(8,128)(2,1)S(1)} %get-tuple-element.41), channel_id=1, source_target_pairs={{0,28},{4,16},{8,20},{12,24},{16,12},{20,0},{24,4},{28,8},{1,29},{... | collective-permute-start | bytes 294920 | tf_op jit(solution)/shard_map/ppermute | solution.py:519
  9.2 0.7 %copy-start.7 = (f32[759,4]{0,1:T(4,128)S(1)}, f32[759,4]{0,1:T(4,128)}, u32[]{:S(2)}) copy-start(f32[759,4]{0,1:T(4,128)} %param.14) | copy-start | bytes 36436
  9.9 6.3 %copy-start = (bf16[2,6,24,1024]{3,2,1,0:T(8,128)(2,1)S(1)}, bf16[2,6,24,1024]{3,2,1,0:T(8,128)(2,1)}, u32[]{:S(2)}) copy-start(bf16[2,6,24,1024]{3,2,1,0:T(8,128)(2,1)} %param.10) | copy-start | bytes 1769476
  9.9 6.3 %copy-start.1 = (bf16[2,6,24,1024]{3,2,1,0:T(8,128)(2,1)S(1)}, bf16[2,6,24,1024]{3,2,1,0:T(8,128)(2,1)}, u32[]{:S(2)}) copy-start(bf16[2,6,24,1024]{3,2,1,0:T(8,128)(2,1)} %param.15) | copy-start | bytes 1769476
  9.9 6.3 %copy-start.4 = (f32[1024]{0:T(1024)S(1)}, f32[1024]{0:T(1024)}, u32[]{:S(2)}) copy-start(f32[1024]{0:T(1024)} %param.11) | copy-start | bytes 12292
  9.9 6.3 %copy-start.5 = (bf16[1024,768]{1,0:T(8,128)(2,1)S(1)}, bf16[1024,768]{1,0:T(8,128)(2,1)}, u32[]{:S(2)}) copy-start(bf16[1024,768]{1,0:T(8,128)(2,1)} %refs_9_.1) | copy-start | bytes 4718596
  9.9 6.3 %copy-start.6 = (bf16[256,1024]{1,0:T(8,128)(2,1)S(1)}, bf16[256,1024]{1,0:T(8,128)(2,1)}, u32[]{:S(2)}) copy-start(bf16[256,1024]{1,0:T(8,128)(2,1)} %refs_5_.1) | copy-start | bytes 1572868
  10.0 6.3 %copy-start.8 = (bf16[288,496]{1,0:T(8,128)(2,1)S(1)}, bf16[288,496]{1,0:T(8,128)(2,1)}, u32[]{:S(2)}) copy-start(bf16[288,496]{1,0:T(8,128)(2,1)} %constant.8.clone.refs_7_) | copy-start | bytes 857092
  10.0 6.3 %copy-start.9 = (bf16[320,288]{1,0:T(8,128)(2,1)S(1)}, bf16[320,288]{1,0:T(8,128)(2,1)}, u32[]{:S(2)}) copy-start(bf16[320,288]{1,0:T(8,128)(2,1)} %constant.9.clone.refs_8_) | copy-start | bytes 552964
  14.4 1.8 %collective-permute-start.3 = (bf16[208,1024]{1,0:T(8,128)(2,1)S(1)}, bf16[208,1024]{1,0:T(8,128)(2,1)S(1)}, u32[]{:S(2)}, u32[]{:S(2)}) collective-permute-start(bf16[208,1024]{1,0:T(8,128)(2,1)S(1)} %join_rims.1.refs_2_), channel_id=1, source_target_pairs={{0,1},{1,0},{2,3},{3,2},{4,5},{5,4},{6,7},{7,6},{8,9},{9,8},{10,11... | collective-permute-start | bytes 1277960 | tf_op jit(solution)/shard_map/ppermute | solution.py:558
  16.2 19.0 %copy-start.3 = (bf16[96,72]{1,0:T(8,128)(2,1)S(1)}, bf16[96,72]{1,0:T(8,128)(2,1)}, u32[]{:S(2)}) copy-start(bf16[96,72]{1,0:T(8,128)(2,1)} %constant.10.clone.refs_3_) | copy-start | bytes 41476
  23.9 2.1 %collective-permute-start.4 = (bf16[2,2,72,1024]{3,2,1,0:T(8,128)(2,1)S(1)}, bf16[2,2,72,1024]{3,2,1,0:T(8,128)(2,1)S(1)}, u32[]{:S(2)}, u32[]{:S(2)}) collective-permute-start(bf16[2,2,72,1024]{3,2,1,0:T(8,128)(2,1)S(1)} %get-tuple-element.47), channel_id=1, source_target_pairs={{0,1},{1,0},{2,3},{3,2},{4,5},{5,4},{6,7},{7,6},{8,9},{9,8},{10,11... | collective-permute-start | bytes 1769480 | tf_op jit(solution)/shard_map/ppermute | solution.py:603
  24.1 14.8 %collective-permute-start.7 = (bf16[512,512]{1,0:T(8,128)(2,1)S(1)}, bf16[512,512]{1,0:T(8,128)(2,1)S(1)}, u32[]{:S(2)}, u32[]{:S(2)}) collective-permute-start(bf16[512,512]{1,0:T(8,128)(2,1)S(1)} %get-tuple-element.53), channel_id=1, source_target_pairs={{0,16},{16,0},{1,17},{17,1},{2,18},{18,2},{3,19},{19,3},{4,20},{20... | collective-permute-start | bytes 1572872 | tf_op jit(solution)/shard_map/ppermute | solution.py:509
  25.6 13.9 %collective-permute-start.8 = (bf16[512,512]{1,0:T(8,128)(2,1)S(1)}, bf16[512,512]{1,0:T(8,128)(2,1)S(1)}, u32[]{:S(2)}, u32[]{:S(2)}) collective-permute-start(bf16[512,512]{1,0:T(8,128)(2,1)S(1)} %get-tuple-element.55), channel_id=1, source_target_pairs={{0,4},{4,0},{8,12},{12,8},{1,5},{5,1},{9,13},{13,9},{2,6},{6,2},{1... | collective-permute-start | bytes 1572872 | tf_op jit(solution)/shard_map/ppermute | solution.py:602
  26.1 9.1 %collective-permute-start.5 = (bf16[2,72,1024]{2,1,0:T(8,128)(2,1)S(1)}, bf16[2,72,1024]{2,1,0:T(8,128)(2,1)S(1)}, u32[]{:S(2)}, u32[]{:S(2)}) collective-permute-start(bf16[2,72,1024]{2,1,0:T(8,128)(2,1)S(1)} %sum_over_cores.1), channel_id=1, source_target_pairs={{0,2},{1,3},{2,0},{3,1},{4,6},{5,7},{6,4},{7,5},{8,10},{9,11},{10,... | collective-permute-start | bytes 884744 | tf_op jit(solution)/shard_map/ppermute | solution.py:608
  35.7 6.0 %collective-permute-start.6 = (bf16[2,32,1024]{2,1,0:T(8,128)(2,1)S(1)}, bf16[2,32,1024]{2,1,0:T(8,128)(2,1)S(1)}, u32[]{:S(2)}, u32[]{:S(2)}) collective-permute-start(bf16[2,32,1024]{2,1,0:T(8,128)(2,1)S(1)} %get-tuple-element.51), channel_id=1, source_target_pairs={{0,16},{16,0},{1,17},{17,1},{2,18},{18,2},{3,19},{19,3},{4,20},{20... | collective-permute-start | bytes 393224 | tf_op jit(solution)/shard_map/ppermute | solution.py:509
  39.8 23.2 %copy-start.2 = (bf16[288,320]{1,0:T(8,128)(2,1)S(1)}, bf16[288,320]{1,0:T(8,128)(2,1)}, u32[]{:S(2)}) copy-start(bf16[288,320]{1,0:T(8,128)(2,1)} %constant.11.clone.refs_0_) | copy-start | bytes 552964
  39.8 7.5 %collective-permute-start.10 = (bf16[256,512]{1,0:T(8,128)(2,1)S(1)}, bf16[256,512]{1,0:T(8,128)(2,1)S(1)}, u32[]{:S(2)}, u32[]{:S(2)}) collective-permute-start(bf16[256,512]{1,0:T(8,128)(2,1)S(1)} %get-tuple-element.60), channel_id=1, source_target_pairs={{0,4},{4,0},{8,12},{12,8},{1,5},{5,1},{9,13},{13,9},{2,6},{6,2},{1... | collective-permute-start | bytes 786440 | tf_op jit(solution)/shard_map/ppermute | solution.py:625
  40.6 6.9 %collective-permute-start.11 = (bf16[256,512]{1,0:T(8,128)(2,1)S(1)}, bf16[256,512]{1,0:T(8,128)(2,1)S(1)}, u32[]{:S(2)}, u32[]{:S(2)}) collective-permute-start(bf16[256,512]{1,0:T(8,128)(2,1)S(1)} %get-tuple-element.62), channel_id=1, source_target_pairs={{0,16},{16,0},{1,17},{17,1},{2,18},{18,2},{3,19},{19,3},{4,20},{20... | collective-permute-start | bytes 786440 | tf_op jit(solution)/shard_map/ppermute | solution.py:509
  42.0 11.6 %collective-permute-start.9 = (bf16[2,40,1024]{2,1,0:T(8,128)(2,1)S(1)}, bf16[2,40,1024]{2,1,0:T(8,128)(2,1)S(1)}, u32[]{:S(2)}, u32[]{:S(2)}) collective-permute-start(bf16[2,40,1024]{2,1,0:T(8,128)(2,1)S(1)} %get-tuple-element.58), channel_id=1, source_target_pairs={{0,4},{4,8},{8,12},{12,0},{1,5},{5,9},{9,13},{13,1},{2,6},{6,10},{... | collective-permute-start | bytes 491528 | tf_op jit(solution)/shard_map/ppermute | solution.py:509
  54.0 6.0 %collective-permute-start.14 = (bf16[72,1024]{1,0:T(8,128)(2,1)S(1)}, bf16[72,1024]{1,0:T(8,128)(2,1)S(1)}, u32[]{:S(2)}, u32[]{:S(2)}) collective-permute-start(bf16[72,1024]{1,0:T(8,128)(2,1)S(1)} %get-tuple-element.65.refs_1_), channel_id=1, source_target_pairs={{0,2},{1,3},{2,0},{3,1},{4,6},{5,7},{6,4},{7,5},{8,10},{9,11},{10,... | collective-permute-start | bytes 442376 | tf_op jit(solution)/shard_map/ppermute | solution.py:651
  55.6 6.0 %collective-permute-start.15 = (bf16[72,1024]{1,0:T(8,128)(2,1)S(1)}, bf16[72,1024]{1,0:T(8,128)(2,1)S(1)}, u32[]{:S(2)}, u32[]{:S(2)}) collective-permute-start(bf16[72,1024]{1,0:T(8,128)(2,1)S(1)} %get-tuple-element.66.refs_2_), channel_id=1, source_target_pairs={{0,2},{1,3},{2,0},{3,1},{4,6},{5,7},{6,4},{7,5},{8,10},{9,11},{10,... | collective-permute-start | bytes 442376 | tf_op jit(solution)/shard_map/ppermute | solution.py:651
  56.1 11.1 %collective-permute-start.18 = (bf16[2,128,512]{2,1,0:T(8,128)(2,1)S(1)}, bf16[2,128,512]{2,1,0:T(8,128)(2,1)S(1)}, u32[]{:S(2)}, u32[]{:S(2)}) collective-permute-start(bf16[2,128,512]{2,1,0:T(8,128)(2,1)S(1)} %get-tuple-element.70), channel_id=1, source_target_pairs={{0,8},{4,12},{8,0},{12,4},{1,9},{5,13},{9,1},{13,5},{2,10},{6,14},... | collective-permute-start | bytes 786440 | tf_op jit(solution)/shard_map/ppermute | solution.py:643
  56.1 5.5 %collective-permute-start.12 = (bf16[72,1024]{1,0:T(8,128)(2,1)S(1)}, bf16[72,1024]{1,0:T(8,128)(2,1)S(1)}, u32[]{:S(2)}, u32[]{:S(2)}) collective-permute-start(bf16[72,1024]{1,0:T(8,128)(2,1)S(1)} %get-tuple-element.65.refs_1_), channel_id=1, source_target_pairs={{0,1},{1,0},{2,3},{3,2},{4,5},{5,4},{6,7},{7,6},{8,9},{9,8},{10,11... | collective-permute-start | bytes 442376 | tf_op jit(solution)/shard_map/ppermute | solution.py:652
  56.1 5.5 %collective-permute-start.13 = (bf16[72,1024]{1,0:T(8,128)(2,1)S(1)}, bf16[72,1024]{1,0:T(8,128)(2,1)S(1)}, u32[]{:S(2)}, u32[]{:S(2)}) collective-permute-start(bf16[72,1024]{1,0:T(8,128)(2,1)S(1)} %get-tuple-element.66.refs_2_), channel_id=1, source_target_pairs={{0,1},{1,0},{2,3},{3,2},{4,5},{5,4},{6,7},{7,6},{8,9},{9,8},{10,11... | collective-permute-start | bytes 442376 | tf_op jit(solution)/shard_map/ppermute | solution.py:652
  60.1 1.6 %collective-permute-start.16 = (bf16[72,1024]{1,0:T(8,128)(2,1)S(1)}, bf16[72,1024]{1,0:T(8,128)(2,1)S(1)}, u32[]{:S(2)}, u32[]{:S(2)}) collective-permute-start(bf16[72,1024]{1,0:T(8,128)(2,1)S(1)} %collective-permute-done.14.refs_5_), channel_id=1, source_target_pairs={{0,1},{1,0},{2,3},{3,2},{4,5},{5,4},{6,7},{7,6},{8,9},{9,8},{10,11... | collective-permute-start | bytes 442376 | tf_op jit(solution)/shard_map/ppermute | solution.py:653
  61.6 1.4 %collective-permute-start.17 = (bf16[72,1024]{1,0:T(8,128)(2,1)S(1)}, bf16[72,1024]{1,0:T(8,128)(2,1)S(1)}, u32[]{:S(2)}, u32[]{:S(2)}) collective-permute-start(bf16[72,1024]{1,0:T(8,128)(2,1)S(1)} %collective-permute-done.15.refs_6_), channel_id=1, source_target_pairs={{0,1},{1,0},{2,3},{3,2},{4,5},{5,4},{6,7},{7,6},{8,9},{9,8},{10,11... | collective-permute-start | bytes 442376 | tf_op jit(solution)/shard_map/ppermute | solution.py:653

commit v8 on v7

--- a/solution.py
+++ b/solution.py
@@ -32,7 +32,9 @@
 RIM = RIM_Z + RIM_X + RIM_D
 OUT_STARTS = (0, 32, 64)
 OUT_SIZES = (32, 32, 32)
-OUT_ROWS = 96
+OUT_ROWS = 112
+PIECES = 3
+SLOT = 32
 NORTH_ROWS = 40
 
 
@@ -116,8 +118,8 @@
         for at, (window, level, lat, lon) in enumerate(sum(quarter_cells(quarter), [])):
             column = (window * WLON + lon + MID_LON) % TILE_LON
             row = own_row(level, (lat + MID_LAT) % WLAT, column)
-            place[row] = quarter * STRIDE + at
-    return one_hot([place[row] for row in range(CELLS)], QUARTERS * STRIDE)
+            place[row] = (quarter * PIECES + at // (PART // PIECES)) * SLOT + at % (PART // PIECES)
+    return one_hot([place[row] for row in range(CELLS)], QUARTERS * PIECES * SLOT)
 
 
 def window_position(shape, dim):
@@ -215,10 +217,13 @@
     rim_d[...] = rim[RIM_Z + RIM_X :]
 
 
-def rims_kernel(rim_z, rim_x, rim_d, rim):
-    rim[:RIM_Z] = rim_z[...]
-    rim[RIM_Z : RIM_Z + RIM_X] = rim_x[...]
-    rim[RIM_Z + RIM_X :] = rim_d[...]
+def hold_kernel(rim, held):
+    held[...] = rim[...]
+
+
+def rims_kernel(x_rim, d_rim, rim):
+    rim[:RIM_X] = x_rim[...]
+    rim[RIM_X:] = d_rim[...]
 
 
 def bias_kernel(table, bias, mark, padded, shifted, parts):
@@ -318,8 +323,10 @@
 def layer_kernel(
     tokens,
     cotangent,
-    rim_here,
-    rim_there,
+    z_here,
+    xd_here,
+    z_there,
+    xd_there,
     gain,
     w_out,
     bias,
@@ -344,10 +351,13 @@
     core = lax.rem(head_index, 2)
     heads = bias.shape[0]
     group = heads * HEAD_DIM
-    source[CELLS:, :] = jnp.where(core == 0, rim_here[...], rim_there[...])
+    split = CELLS + RIM_Z
+    source[CELLS:split, :] = jnp.where(core == 0, z_here[...], z_there[...])
+    source[split:, :] = jnp.where(core == 0, xd_here[...], xd_there[...])
     source[:CELLS, :] = tokens[...]
     near_tokens[...] = dot(shift_pick[...], source[...]).astype(BF16)
-    source[CELLS:, :] = jnp.where(core == 0, rim_there[...], rim_here[...])
+    source[CELLS:split, :] = jnp.where(core == 0, z_there[...], z_here[...])
+    source[split:, :] = jnp.where(core == 0, xd_there[...], xd_here[...])
     source[:CELLS, :] = cotangent[...]
     near_grad[...] = dot(shift_pick[...], source[...]).astype(BF16)
     scaled, _ = scaled_rows(near_tokens[...])
@@ -475,28 +485,32 @@
         rows[at] = total.astype(BF16)
 
 
-def join_kernel(own, z_rows, x_rows, layer, grad):
+def join_kernel(own, z_rows, x_rows, *pieces):
     stay, north, east, corner = group_sizes()
-    for at, joined in enumerate((layer, grad)):
+    for at in range(2):
         total = taken(PART, own[at], [(0, 0, stay)])
         spans = [(stay, 0, north), (stay + north + east, north, corner)]
         total = total + taken(PART, z_rows[at], spans)
         total = total + taken(PART, x_rows[at], [(stay + north, 0, east)])
-        joined[...] = total.astype(BF16)
+        for number, piece in enumerate(pieces):
+            rows = piece.shape[1]
+            piece[at] = total[number * rows : (number + 1) * rows].astype(BF16)
 
 
 def spread_kernel(pick, *refs):
-    arrived, outs, (mark, gathered) = refs[:8], refs[8:10], refs[10:]
+    *arrived, layer, grad, mark, gathered = refs
     mark[...] = jnp.zeros_like(mark)
     head_index = lax.axis_index("head")
     sibling = 1 - 2 * lax.rem(head_index, 2)
     over = lax.rem(head_index + 2, QUARTERS)
     owners = (head_index, head_index + sibling, over, over + sibling)
-    for at, out in enumerate(outs):
-        for owner, piece in zip(owners, arrived[at::2]):
-            start = pl.multiple_of(owner * STRIDE, 16)
-            gathered[at, pl.ds(start + STRIDE - 16, 16), :] = jnp.zeros_like(gathered[at, :16, :])
-            gathered[at, pl.ds(start, PART), :] = piece[...]
+    for at, out in enumerate((layer, grad)):
+        for step, owner in enumerate(owners):
+            for number in range(PIECES):
+                start = pl.multiple_of((owner * PIECES + number) * SLOT, SLOT)
+                gathered[at, pl.ds(start + SLOT - 16, 16), :] = jnp.zeros_like(gathered[at, :16, :])
+                piece = arrived[step * PIECES + number][at]
+                gathered[at, pl.ds(start, PART // PIECES), :] = piece
         out[...] = dot(pick[...], gathered[at]).astype(BF16)
 
 
@@ -551,11 +565,19 @@
         cost=cost(2 * 192 * 768 * 144 * 12 * 2, 1000000),
         name="window_bias",
     )(bias_table.T)
-    rim_here = call(
-        rims_kernel, shaped(RIM, width), name="join_rims", cost=cost(0, 4 * RIM * width), after=(bias_mark,)
-    )(*arrived)
+    held = call(
+        hold_kernel, shaped(RIM_Z, width), name="hold_rim", cost=cost(0, 4 * RIM_Z * width), after=(bias_mark,)
+    )(arrived[0])
+    joined = call(
+        rims_kernel,
+        shaped(RIM_X + RIM_D, width),
+        name="join_rims",
+        cost=cost(0, 4 * (RIM_X + RIM_D) * width),
+        after=(bias_mark,),
+    )(*arrived[1:])
+    rims = [held, joined]
     pairs = [(i, i ^ 1) for i in range(QUARTERS)]
-    rim_there = lax.ppermute(rim_here, "head", pairs)
+    rims += [lax.ppermute(rim, "head", pairs) for rim in rims]
     lon_rows = width // lon_count
     rows = lon_rows // lat_count
     columns = 2 * group
@@ -589,8 +611,7 @@
     )(
         flat_tokens,
         flat_grad,
-        rim_here,
-        rim_there,
+        *rims,
         gain,
         w_out,
         bias,
@@ -643,7 +664,7 @@
     last = lax.ppermute(send, "lat", [(i, i ^ 2) for i in range(lat_count)])
     each = call(
         join_kernel,
-        [shaped(PART, width)] * 2,
+        [shaped(2, PART // PIECES, width)] * PIECES,
         cost=cost(2 * 2 * OUT_ROWS * PART * width, 8 * OUT_ROWS * width),
         name="join_home",
         after=(third_mark,),
@@ -654,7 +675,7 @@
     layer_out, grad_tokens, spread_mark = call(
         spread_kernel,
         [shaped(CELLS, width)] * 2 + [mark],
-        [pltpu.VMEM((2, QUARTERS * STRIDE, width), BF16)],
+        [pltpu.VMEM((2, QUARTERS * PIECES * SLOT, width), BF16)],
         cost=cost(2 * 2 * CELLS * CELLS * width, 8 * CELLS * width),
         name="spread_outputs",
     )(own_pick(), *each, *near, *far, *across)

time: 68.3 us -> 67.7 us (level)
  waiting for transfers between devices: 33.3 us -> 29.7 us
  starting transfers between devices: 17.9 us -> 20.7 us
    ppermute x2 -> x3, starting transfers between devices: 2.09 us -> 4.57 us  [body(): far = [lax.ppermute(single, 'head', chips) for single in each]]
    ppermute x1, waiting for transfers between devices: 2.5 us -> 0.03 us  [body(): last = lax.ppermute(send, 'lat', [(i, i ^ 2) for i in range(lat_count)])]
    ppermute x2 -> x3, waiting for transfers between devices: 5 us -> 4.42 us  [body(): far = [lax.ppermute(single, 'head', chips) for single in each]]
    ppermute x1 -> x2, waiting for transfers between devices: 1.76 us -> 1.43 us  [body(): rims += [lax.ppermute(rim, 'head', pairs) for rim in rims]]
    pallas_call x12 -> x13, Pallas kernels: 15.4 us -> 15.5 us  [run(): pl.pallas_call(body, out_shape=outs, in_specs=[near] * len(args) + [outsi...]
  transfers between devices with their start and end apart: 19 -> 23, of which waited for: 13 -> 12; matrix products, arithmetic and copies ran while one was open for 0% -> 0% of each run, Pallas kernels for 7% -> 7%
where the time goes in v8:
time: 67.7 us; the launch traced here: 67.5 us
  waiting for transfers between devices  29.7 us (44%)
  starting transfers between devices  20.7 us (31%)
  Pallas kernels  15.5 us (23%)
  between operations  0.84 us (1%)
  local copies, waits for them, and re-layouts  0.75 us (1%)
    pallas_call x13, Pallas kernels, run(): pl.pallas_call(body, out_shape=outs, in_specs=[near] * len(args) + [outsi...  15.5 us
    ppermute x4, waiting for transfers between devices, rotated(): lax.ppermute(value, axis, [(i, (i + step) % count) for i in range(count)])  7.85 us
    ppermute x1, waiting for transfers between devices, body(): crossed = lax.ppermute(across, 'head', chips)  7.49 us
    ppermute x3, starting transfers between devices, moved(): return lax.ppermute(value, ('lon', 'lat'), pairs)  7 us
    ppermute x4, starting transfers between devices, rotated(): lax.ppermute(value, axis, [(i, (i + step) % count) for i in range(count)])  5.16 us
    ppermute x3, starting transfers between devices, body(): far = [lax.ppermute(single, 'head', chips) for single in each]  4.57 us
    ppermute x3, waiting for transfers between devices, body(): far = [lax.ppermute(single, 'head', chips) for single in each]  4.42 us
    ppermute x1, waiting for transfers between devices, body(): from_lat = lax.ppermute(send_first, 'lat', neighbours)  4.3 us
  transfers between devices with their start and end apart: 23, of which 12 were waited for; matrix products, arithmetic and copies ran while one was open for 0% of the time, Pallas kernels for 7%

profile of v8, /device:TPU:0, one launch (start us, length us, event | category | flops | bytes accessed | tf_op | source)
XLA Modules:
  0.0 67.5 jit_solution(17204863441356551117)
XLA Ops:
  0.6 1.6 %pack_rims.1 = (bf16[112,1024]{1,0:T(8,128)(2,1)S(1)}, bf16[48,1024]{1,0:T(8,128)(2,1)S(1)}, bf16[48,1024]{1,0:T(8,128)(2,1)S(1)}) custom-call(bf16[288,1024]{1,0:T(8,128)(2,1)} %bitcast.6, bf16[288,1024]{1,0:T(8,128)(2,1)} %bitcast.8), custom_call_target="tpu_custom_call" | custom-call | flops 122683392 | bytes 1179648 | tf_op jit(solution)/shard_map/pack_rims/pallas_call | solution.py:162
  2.2 5.1 %collective-permute-start = (bf16[112,1024]{1,0:T(8,128)(2,1)S(1)}, bf16[112,1024]{1,0:T(8,128)(2,1)S(1)}, u32[]{:S(2)}, u32[]{:S(2)}) collective-permute-start(bf16[112,1024]{1,0:T(8,128)(2,1)S(1)} %get-tuple-element.40), channel_id=1, source_target_pairs={{0,12},{4,0},{8,4},{12,8},{16,28},{20,16},{24,20},{28,24},{1,13},{... | collective-permute-start | bytes 688136 | tf_op jit(solution)/shard_map/ppermute | solution.py:533
  7.3 1.5 %collective-permute-start.1 = (bf16[48,1024]{1,0:T(8,128)(2,1)S(1)}, bf16[48,1024]{1,0:T(8,128)(2,1)S(1)}, u32[]{:S(2)}, u32[]{:S(2)}) collective-permute-start(bf16[48,1024]{1,0:T(8,128)(2,1)S(1)} %get-tuple-element.42), channel_id=1, source_target_pairs={{0,16},{4,20},{8,24},{12,28},{16,0},{20,4},{24,8},{28,12},{1,17},{... | collective-permute-start | bytes 294920 | tf_op jit(solution)/shard_map/ppermute | solution.py:533
  8.8 0.4 collective-permute-start.2
  9.2 0.7 %copy-done.7 = f32[759,4]{0,1:T(4,128)S(1)} copy-done((f32[759,4]{0,1:T(4,128)S(1)}, f32[759,4]{0,1:T(4,128)}, u32[]{:S(2)}) %copy-start.7) | copy-done | bytes 12168
  10.0 2.0 %window_bias.1 = (f32[4,144,144]{2,1,0:T(8,128)S(1)}, f32[8,128]{1,0:T(8,128)S(1)}) custom-call(f32[4,759]{1,0:T(4,128)S(1)} %bitcast.12), custom_call_target="tpu_custom_call" | custom-call | flops 1019215872 | bytes 1000000 | tf_op jit(solution)/shard_map/window_bias/pallas_call | solution.py:162
  12.0 1.3 %collective-permute-done.refs_0_ = bf16[112,1024]{1,0:T(8,128)(2,1)S(1)} collective-permute-done((bf16[112,1024]{1,0:T(8,128)(2,1)S(1)}, bf16[112,1024]{1,0:T(8,128)(2,1)S(1)}, u32[]{:S(2)}, u32[]{:S(2)}) %collective-permute-start) | collective-permute-done | bytes 229408 | tf_op jit(solution)/shard_map/ppermute | solution.py:533
  13.4 1.0 %collective-permute-done.2.refs_1_ = bf16[48,1024]{1,0:T(8,128)(2,1)S(1)} collective-permute-done((bf16[48,1024]{1,0:T(8,128)(2,1)S(1)}, bf16[48,1024]{1,0:T(8,128)(2,1)S(1)}, u32[]{:S(2)}, u32[]{:S(2)}) %collective-permute-start.2) | collective-permute-done | bytes 98336 | tf_op jit(solution)/shard_map/ppermute | solution.py:533
  14.4 1.4 %collective-permute-done.4.refs_5_ = bf16[96,1024]{1,0:T(8,128)(2,1)S(1)} collective-permute-done((bf16[96,1024]{1,0:T(8,128)(2,1)S(1)}, bf16[96,1024]{1,0:T(8,128)(2,1)S(1)}, u32[]{:S(2)}, u32[]{:S(2)}) %collective-permute-start.4) | collective-permute-done | bytes 196640 | tf_op jit(solution)/shard_map/ppermute | solution.py:580
  15.9 7.7 %window_layer.1 = (bf16[512,512]{1,0:T(8,128)(2,1)S(1)}, bf16[512,512]{1,0:T(8,128)(2,1)S(1)}, bf16[512,512]{1,0:T(8,128)(2,1)S(1)}, bf16[512,512]{1,0:T(8,128)(...) custom-call(bf16[288,1024]{1,0:T(8,128)(2,1)S(1)} %bitcast.7, ...), custom_call_target="tpu_custom_call" | custom-call | flops 1811939328 | bytes 8000000 | tf_op jit(solution)/shard_map/window_layer/pallas_call | solution.py:162
  23.8 1.5 %collective-permute-start.8 = (bf16[512,512]{1,0:T(8,128)(2,1)S(1)}, bf16[512,512]{1,0:T(8,128)(2,1)S(1)}, u32[]{:S(2)}, u32[]{:S(2)}) collective-permute-start(bf16[512,512]{1,0:T(8,128)(2,1)S(1)} %get-tuple-element.54), channel_id=1, source_target_pairs={{0,16},{16,0},{1,17},{17,1},{2,18},{18,2},{3,19},{19,3},{4,20},{20... | collective-permute-start | bytes 1572872 | tf_op jit(solution)/shard_map/ppermute | solution.py:523
  25.3 0.4 collective-permute-start.9
  25.8 1.6 %collective-permute-start.6 = (bf16[2,72,1024]{2,1,0:T(8,128)(2,1)S(1)}, bf16[2,72,1024]{2,1,0:T(8,128)(2,1)S(1)}, u32[]{:S(2)}, u32[]{:S(2)}) collective-permute-start(bf16[2,72,1024]{2,1,0:T(8,128)(2,1)S(1)} %sum_over_cores.1), channel_id=1, source_target_pairs={{0,2},{1,3},{2,0},{3,1},{4,6},{5,7},{6,4},{7,5},{8,10},{9,11},{10,... | collective-permute-start | bytes 884744 | tf_op jit(solution)/shard_map/ppermute | solution.py:629
  27.4 7.5 %collective-permute-done.6.refs_6_ = bf16[2,72,1024]{2,1,0:T(8,128)(2,1)S(1)} collective-permute-done((bf16[2,72,1024]{2,1,0:T(8,128)(2,1)S(1)}, bf16[2,72,1024]{2,1,0:T(8,128)(2,1)S(1)}, u32[]{:S(2)}, u32[]{:S(2)}) %collective-permute-start.6) | collective-permute-done | bytes 294944 | tf_op jit(solution)/shard_map/ppermute | solution.py:629
  34.9 0.6 sum_over_heads.1
  35.4 1.5 %collective-permute-start.7 = (bf16[2,32,1024]{2,1,0:T(8,128)(2,1)S(1)}, bf16[2,32,1024]{2,1,0:T(8,128)(2,1)S(1)}, u32[]{:S(2)}, u32[]{:S(2)}) collective-permute-start(bf16[2,32,1024]{2,1,0:T(8,128)(2,1)S(1)} %get-tuple-element.52), channel_id=1, source_target_pairs={{0,16},{16,0},{1,17},{17,1},{2,18},{18,2},{3,19},{19,3},{4,20},{20... | collective-permute-start | bytes 393224 | tf_op jit(solution)/shard_map/ppermute | solution.py:523
  36.9 1.6 %collective-permute-done.8.refs_1_ = bf16[512,512]{1,0:T(8,128)(2,1)S(1)} collective-permute-done((bf16[512,512]{1,0:T(8,128)(2,1)S(1)}, bf16[512,512]{1,0:T(8,128)(2,1)S(1)}, u32[]{:S(2)}, u32[]{:S(2)}) %collective-permute-start.8) | collective-permute-done | bytes 524320 | tf_op jit(solution)/shard_map/ppermute | solution.py:523
  38.6 0.6 collective-permute-done.9.refs_3_
  39.4 0.8 %collective-permute-start.11 = (bf16[256,512]{1,0:T(8,128)(2,1)S(1)}, bf16[256,512]{1,0:T(8,128)(2,1)S(1)}, u32[]{:S(2)}, u32[]{:S(2)}) collective-permute-start(bf16[256,512]{1,0:T(8,128)(2,1)S(1)} %get-tuple-element.61), channel_id=1, source_target_pairs={{0,4},{4,0},{8,12},{12,8},{1,5},{5,1},{9,13},{13,9},{2,6},{6,2},{1... | collective-permute-start | bytes 786440 | tf_op jit(solution)/shard_map/ppermute | solution.py:646
  40.3 1.2 %collective-permute-start.12 = (bf16[256,512]{1,0:T(8,128)(2,1)S(1)}, bf16[256,512]{1,0:T(8,128)(2,1)S(1)}, u32[]{:S(2)}, u32[]{:S(2)}) collective-permute-start(bf16[256,512]{1,0:T(8,128)(2,1)S(1)} %get-tuple-element.63), channel_id=1, source_target_pairs={{0,16},{16,0},{1,17},{17,1},{2,18},{18,2},{3,19},{19,3},{4,20},{20... | collective-permute-start | bytes 786440 | tf_op jit(solution)/shard_map/ppermute | solution.py:523
  41.7 1.0 %collective-permute-start.10 = (bf16[2,40,1024]{2,1,0:T(8,128)(2,1)S(1)}, bf16[2,40,1024]{2,1,0:T(8,128)(2,1)S(1)}, u32[]{:S(2)}, u32[]{:S(2)}) collective-permute-start(bf16[2,40,1024]{2,1,0:T(8,128)(2,1)S(1)} %get-tuple-element.59), channel_id=1, source_target_pairs={{0,4},{4,8},{8,12},{12,0},{1,5},{5,9},{9,13},{13,1},{2,6},{6,10},{... | collective-permute-start | bytes 491528 | tf_op jit(solution)/shard_map/ppermute | solution.py:523
  42.7 4.3 %collective-permute-done.11.refs_1_ = bf16[256,512]{1,0:T(8,128)(2,1)S(1)} collective-permute-done((bf16[256,512]{1,0:T(8,128)(2,1)S(1)}, bf16[256,512]{1,0:T(8,128)(2,1)S(1)}, u32[]{:S(2)}, u32[]{:S(2)}) %collective-permute-start.11) | collective-permute-done | bytes 262176 | tf_op jit(solution)/shard_map/ppermute | solution.py:646
  47.3 6.0 %collective-permute-done.10.refs_1_ = bf16[2,40,1024]{2,1,0:T(8,128)(2,1)S(1)} collective-permute-done((bf16[2,40,1024]{2,1,0:T(8,128)(2,1)S(1)}, bf16[2,40,1024]{2,1,0:T(8,128)(2,1)S(1)}, u32[]{:S(2)}, u32[]{:S(2)}) %collective-permute-start.10) | collective-permute-done | bytes 163872 | tf_op jit(solution)/shard_map/ppermute | solution.py:523
  53.7 1.6 %collective-permute-start.16 = (bf16[2,24,1024]{2,1,0:T(8,128)(2,1)S(1)}, bf16[2,24,1024]{2,1,0:T(8,128)(2,1)S(1)}, u32[]{:S(2)}, u32[]{:S(2)}) collective-permute-start(bf16[2,24,1024]{2,1,0:T(8,128)(2,1)S(1)} %get-tuple-element.66.refs_1_), channel_id=1, source_target_pairs={{0,2},{1,3},{2,0},{3,1},{4,6},{5,7},{6,4},{7,5},{8,10},{9,11},{10,... | collective-permute-start | bytes 294920 | tf_op jit(solution)/shard_map/ppermute | solution.py:672
  55.3 0.5 collective-permute-start.17
  56.0 2.4 %collective-permute-done.16.refs_7_ = bf16[2,24,1024]{2,1,0:T(8,128)(2,1)S(1)} collective-permute-done((bf16[2,24,1024]{2,1,0:T(8,128)(2,1)S(1)}, bf16[2,24,1024]{2,1,0:T(8,128)(2,1)S(1)}, u32[]{:S(2)}, u32[]{:S(2)}) %collective-permute-start.16) | collective-permute-done | bytes 98336 | tf_op jit(solution)/shard_map/ppermute | solution.py:672
  58.4 2.5 %collective-permute-start.18 = (bf16[2,24,1024]{2,1,0:T(8,128)(2,1)S(1)}, bf16[2,24,1024]{2,1,0:T(8,128)(2,1)S(1)}, u32[]{:S(2)}, u32[]{:S(2)}) collective-permute-start(bf16[2,24,1024]{2,1,0:T(8,128)(2,1)S(1)} %get-tuple-element.68.refs_3_), channel_id=1, source_target_pairs={{0,2},{1,3},{2,0},{3,1},{4,6},{5,7},{6,4},{7,5},{8,10},{9,11},{10,... | collective-permute-start | bytes 294920 | tf_op jit(solution)/shard_map/ppermute | solution.py:672
  60.9 0.5 collective-permute-start.19
  61.5 2.0 %collective-permute-done.18.refs_9_ = bf16[2,24,1024]{2,1,0:T(8,128)(2,1)S(1)} collective-permute-done((bf16[2,24,1024]{2,1,0:T(8,128)(2,1)S(1)}, bf16[2,24,1024]{2,1,0:T(8,128)(2,1)S(1)}, u32[]{:S(2)}, u32[]{:S(2)}) %collective-permute-start.18) | collective-permute-done | bytes 98336 | tf_op jit(solution)/shard_map/ppermute | solution.py:672
  63.5 1.3 %collective-permute-done.21.refs_12_ = bf16[2,24,1024]{2,1,0:T(8,128)(2,1)S(1)} collective-permute-done((bf16[2,24,1024]{2,1,0:T(8,128)(2,1)S(1)}, bf16[2,24,1024]{2,1,0:T(8,128)(2,1)S(1)}, u32[]{:S(2)}, u32[]{:S(2)}) %collective-permute-start.21) | collective-permute-done | bytes 98336 | tf_op jit(solution)/shard_map/ppermute | solution.py:674
  64.8 1.8 %spread_outputs.1 = (bf16[288,1024]{1,0:T(8,128)(2,1)}, bf16[288,1024]{1,0:T(8,128)(2,1)}, f32[8,128]{1,0:T(8,128)S(1)}) custom-call(bf16[288,384]{1,0:T(8,128)(2,1)S(1)} %copy-done.2, bf16[2,24,1024]{2,1,0:T(8,128)(2,1)S(1)} %get-tuple-element.66.refs_1_, bf16[2,24,1024]{2,1,0:T(8,128)(2,1)S(1)} %get-tuple-element.67.refs_2_, ...), custom_call_target="tpu_custom_call" | custom-call | flops 339738624 | bytes 2359296 | tf_op jit(solution)/shard_map/spread_outputs/pallas_call | solution.py:162
  66.6 0.8 %sum_over_lat.1 = (f32[128,768]{1,0:T(8,128)}, f32[256,128]{1,0:T(8,128)}) custom-call(f32[2,128,512]{2,1,0:T(8,128)S(1)} %get-tuple-element.71.refs_0_, bf16[2,128,512]{2,1,0:T(8,128)(2,1)S(1)} %collective-permute-done.22.refs_1_, f32[8,128]{1,0:T(8,128)S(1)} %get-tuple-element.73.refs_2_), custom_call_target="tpu_custom_call" | custom-call | flops 524288 | bytes 2097152 | tf_op jit(solution)/shard_map/sum_over_lat/pallas_call | solution.py:162
  (47 shorter events, 2.0 us)
Async XLA Ops:
  2.2 11.0 %collective-permute-start = (bf16[112,1024]{1,0:T(8,128)(2,1)S(1)}, bf16[112,1024]{1,0:T(8,128)(2,1)S(1)}, u32[]{:S(2)}, u32[]{:S(2)}) collective-permute-start(bf16[112,1024]{1,0:T(8,128)(2,1)S(1)} %get-tuple-element.40), channel_id=1, source_target_pairs={{0,12},{4,0},{8,4},{12,8},{16,28},{20,16},{24,20},{28,24},{1,13},{... | collective-permute-start | bytes 688136 | tf_op jit(solution)/shard_map/ppermute | solution.py:533
  7.3 6.0 %collective-permute-start.1 = (bf16[48,1024]{1,0:T(8,128)(2,1)S(1)}, bf16[48,1024]{1,0:T(8,128)(2,1)S(1)}, u32[]{:S(2)}, u32[]{:S(2)}) collective-permute-start(bf16[48,1024]{1,0:T(8,128)(2,1)S(1)} %get-tuple-element.42), channel_id=1, source_target_pairs={{0,16},{4,20},{8,24},{12,28},{16,0},{20,4},{24,8},{28,12},{1,17},{... | collective-permute-start | bytes 294920 | tf_op jit(solution)/shard_map/ppermute | solution.py:533
  8.8 5.5 %collective-permute-start.2 = (bf16[48,1024]{1,0:T(8,128)(2,1)S(1)}, bf16[48,1024]{1,0:T(8,128)(2,1)S(1)}, u32[]{:S(2)}, u32[]{:S(2)}) collective-permute-start(bf16[48,1024]{1,0:T(8,128)(2,1)S(1)} %get-tuple-element.43), channel_id=1, source_target_pairs={{0,28},{4,16},{8,20},{12,24},{16,12},{20,0},{24,4},{28,8},{1,29},{... | collective-permute-start | bytes 294920 | tf_op jit(solution)/shard_map/ppermute | solution.py:533
  9.9 5.9 %copy-start = (bf16[2,6,24,1024]{3,2,1,0:T(8,128)(2,1)S(1)}, bf16[2,6,24,1024]{3,2,1,0:T(8,128)(2,1)}, u32[]{:S(2)}) copy-start(bf16[2,6,24,1024]{3,2,1,0:T(8,128)(2,1)} %param.10) | copy-start | bytes 1769476
  9.9 5.9 %copy-start.1 = (bf16[2,6,24,1024]{3,2,1,0:T(8,128)(2,1)S(1)}, bf16[2,6,24,1024]{3,2,1,0:T(8,128)(2,1)}, u32[]{:S(2)}) copy-start(bf16[2,6,24,1024]{3,2,1,0:T(8,128)(2,1)} %param.15) | copy-start | bytes 1769476
  9.9 5.9 %copy-start.4 = (f32[1024]{0:T(1024)S(1)}, f32[1024]{0:T(1024)}, u32[]{:S(2)}) copy-start(f32[1024]{0:T(1024)} %param.11) | copy-start | bytes 12292
  9.9 5.9 %copy-start.5 = (bf16[1024,768]{1,0:T(8,128)(2,1)S(1)}, bf16[1024,768]{1,0:T(8,128)(2,1)}, u32[]{:S(2)}) copy-start(bf16[1024,768]{1,0:T(8,128)(2,1)} %refs_11_.1) | copy-start | bytes 4718596
  9.9 5.9 %copy-start.6 = (bf16[256,1024]{1,0:T(8,128)(2,1)S(1)}, bf16[256,1024]{1,0:T(8,128)(2,1)}, u32[]{:S(2)}) copy-start(bf16[256,1024]{1,0:T(8,128)(2,1)} %refs_7_.1) | copy-start | bytes 1572868
  10.0 5.9 %copy-start.8 = (bf16[288,496]{1,0:T(8,128)(2,1)S(1)}, bf16[288,496]{1,0:T(8,128)(2,1)}, u32[]{:S(2)}) copy-start(bf16[288,496]{1,0:T(8,128)(2,1)} %constant.8.clone.refs_9_) | copy-start | bytes 857092
  10.0 5.9 %copy-start.9 = (bf16[320,288]{1,0:T(8,128)(2,1)S(1)}, bf16[320,288]{1,0:T(8,128)(2,1)}, u32[]{:S(2)}) copy-start(bf16[320,288]{1,0:T(8,128)(2,1)} %constant.9.clone.refs_10_) | copy-start | bytes 552964
  13.3 2.6 %collective-permute-start.3 = (bf16[112,1024]{1,0:T(8,128)(2,1)S(1)}, bf16[112,1024]{1,0:T(8,128)(2,1)S(1)}, u32[]{:S(2)}, u32[]{:S(2)}) collective-permute-start(bf16[112,1024]{1,0:T(8,128)(2,1)S(1)} %hold_rim.1.refs_2_), channel_id=1, source_target_pairs={{0,1},{1,0},{2,3},{3,2},{4,5},{5,4},{6,7},{7,6},{8,9},{9,8},{10,11... | collective-permute-start | bytes 688136 | tf_op jit(solution)/shard_map/ppermute | solution.py:580
  14.3 1.5 %collective-permute-start.4 = (bf16[96,1024]{1,0:T(8,128)(2,1)S(1)}, bf16[96,1024]{1,0:T(8,128)(2,1)S(1)}, u32[]{:S(2)}, u32[]{:S(2)}) collective-permute-start(bf16[96,1024]{1,0:T(8,128)(2,1)S(1)} %join_rims.1.refs_3_), channel_id=1, source_target_pairs={{0,1},{1,0},{2,3},{3,2},{4,5},{5,4},{6,7},{7,6},{8,9},{9,8},{10,11... | collective-permute-start | bytes 589832 | tf_op jit(solution)/shard_map/ppermute | solution.py:580
  15.9 18.9 %copy-start.3 = (bf16[112,72]{1,0:T(8,128)(2,1)S(1)}, bf16[112,72]{1,0:T(8,128)(2,1)}, u32[]{:S(2)}) copy-start(bf16[112,72]{1,0:T(8,128)(2,1)} %constant.10.clone.refs_3_) | copy-start | bytes 48388
  23.6 2.1 %collective-permute-start.5 = (bf16[2,2,72,1024]{3,2,1,0:T(8,128)(2,1)S(1)}, bf16[2,2,72,1024]{3,2,1,0:T(8,128)(2,1)S(1)}, u32[]{:S(2)}, u32[]{:S(2)}) collective-permute-start(bf16[2,2,72,1024]{3,2,1,0:T(8,128)(2,1)S(1)} %get-tuple-element.48), channel_id=1, source_target_pairs={{0,1},{1,0},{2,3},{3,2},{4,5},{5,4},{6,7},{7,6},{8,9},{9,8},{10,11... | collective-permute-start | bytes 1769480 | tf_op jit(solution)/shard_map/ppermute | solution.py:624
  23.8 14.8 %collective-permute-start.8 = (bf16[512,512]{1,0:T(8,128)(2,1)S(1)}, bf16[512,512]{1,0:T(8,128)(2,1)S(1)}, u32[]{:S(2)}, u32[]{:S(2)}) collective-permute-start(bf16[512,512]{1,0:T(8,128)(2,1)S(1)} %get-tuple-element.54), channel_id=1, source_target_pairs={{0,16},{16,0},{1,17},{17,1},{2,18},{18,2},{3,19},{19,3},{4,20},{20... | collective-permute-start | bytes 1572872 | tf_op jit(solution)/shard_map/ppermute | solution.py:523
  25.3 13.9 %collective-permute-start.9 = (bf16[512,512]{1,0:T(8,128)(2,1)S(1)}, bf16[512,512]{1,0:T(8,128)(2,1)S(1)}, u32[]{:S(2)}, u32[]{:S(2)}) collective-permute-start(bf16[512,512]{1,0:T(8,128)(2,1)S(1)} %get-tuple-element.56), channel_id=1, source_target_pairs={{0,4},{4,0},{8,12},{12,8},{1,5},{5,1},{9,13},{13,9},{2,6},{6,2},{1... | collective-permute-start | bytes 1572872 | tf_op jit(solution)/shard_map/ppermute | solution.py:623
  25.8 9.1 %collective-permute-start.6 = (bf16[2,72,1024]{2,1,0:T(8,128)(2,1)S(1)}, bf16[2,72,1024]{2,1,0:T(8,128)(2,1)S(1)}, u32[]{:S(2)}, u32[]{:S(2)}) collective-permute-start(bf16[2,72,1024]{2,1,0:T(8,128)(2,1)S(1)} %sum_over_cores.1), channel_id=1, source_target_pairs={{0,2},{1,3},{2,0},{3,1},{4,6},{5,7},{6,4},{7,5},{8,10},{9,11},{10,... | collective-permute-start | bytes 884744 | tf_op jit(solution)/shard_map/ppermute | solution.py:629
  35.4 6.0 %collective-permute-start.7 = (bf16[2,32,1024]{2,1,0:T(8,128)(2,1)S(1)}, bf16[2,32,1024]{2,1,0:T(8,128)(2,1)S(1)}, u32[]{:S(2)}, u32[]{:S(2)}) collective-permute-start(bf16[2,32,1024]{2,1,0:T(8,128)(2,1)S(1)} %get-tuple-element.52), channel_id=1, source_target_pairs={{0,16},{16,0},{1,17},{17,1},{2,18},{18,2},{3,19},{19,3},{4,20},{20... | collective-permute-start | bytes 393224 | tf_op jit(solution)/shard_map/ppermute | solution.py:523
  39.4 25.4 %copy-start.2 = (bf16[288,384]{1,0:T(8,128)(2,1)S(1)}, bf16[288,384]{1,0:T(8,128)(2,1)}, u32[]{:S(2)}) copy-start(bf16[288,384]{1,0:T(8,128)(2,1)} %constant.11.clone.refs_0_) | copy-start | bytes 663556
  39.4 7.5 %collective-permute-start.11 = (bf16[256,512]{1,0:T(8,128)(2,1)S(1)}, bf16[256,512]{1,0:T(8,128)(2,1)S(1)}, u32[]{:S(2)}, u32[]{:S(2)}) collective-permute-start(bf16[256,512]{1,0:T(8,128)(2,1)S(1)} %get-tuple-element.61), channel_id=1, source_target_pairs={{0,4},{4,0},{8,12},{12,8},{1,5},{5,1},{9,13},{13,9},{2,6},{6,2},{1... | collective-permute-start | bytes 786440 | tf_op jit(solution)/shard_map/ppermute | solution.py:646
  40.3 6.9 %collective-permute-start.12 = (bf16[256,512]{1,0:T(8,128)(2,1)S(1)}, bf16[256,512]{1,0:T(8,128)(2,1)S(1)}, u32[]{:S(2)}, u32[]{:S(2)}) collective-permute-start(bf16[256,512]{1,0:T(8,128)(2,1)S(1)} %get-tuple-element.63), channel_id=1, source_target_pairs={{0,16},{16,0},{1,17},{17,1},{2,18},{18,2},{3,19},{19,3},{4,20},{20... | collective-permute-start | bytes 786440 | tf_op jit(solution)/shard_map/ppermute | solution.py:523
  41.7 11.6 %collective-permute-start.10 = (bf16[2,40,1024]{2,1,0:T(8,128)(2,1)S(1)}, bf16[2,40,1024]{2,1,0:T(8,128)(2,1)S(1)}, u32[]{:S(2)}, u32[]{:S(2)}) collective-permute-start(bf16[2,40,1024]{2,1,0:T(8,128)(2,1)S(1)} %get-tuple-element.59), channel_id=1, source_target_pairs={{0,4},{4,8},{8,12},{12,0},{1,5},{5,9},{9,13},{13,1},{2,6},{6,10},{... | collective-permute-start | bytes 491528 | tf_op jit(solution)/shard_map/ppermute | solution.py:523
  53.7 4.7 %collective-permute-start.16 = (bf16[2,24,1024]{2,1,0:T(8,128)(2,1)S(1)}, bf16[2,24,1024]{2,1,0:T(8,128)(2,1)S(1)}, u32[]{:S(2)}, u32[]{:S(2)}) collective-permute-start(bf16[2,24,1024]{2,1,0:T(8,128)(2,1)S(1)} %get-tuple-element.66.refs_1_), channel_id=1, source_target_pairs={{0,2},{1,3},{2,0},{3,1},{4,6},{5,7},{6,4},{7,5},{8,10},{9,11},{10,... | collective-permute-start | bytes 294920 | tf_op jit(solution)/shard_map/ppermute | solution.py:672
  55.3 11.3 %collective-permute-start.22 = (bf16[2,128,512]{2,1,0:T(8,128)(2,1)S(1)}, bf16[2,128,512]{2,1,0:T(8,128)(2,1)S(1)}, u32[]{:S(2)}, u32[]{:S(2)}) collective-permute-start(bf16[2,128,512]{2,1,0:T(8,128)(2,1)S(1)} %get-tuple-element.72), channel_id=1, source_target_pairs={{0,8},{4,12},{8,0},{12,4},{1,9},{5,13},{9,1},{13,5},{2,10},{6,14},... | collective-permute-start | bytes 786440 | tf_op jit(solution)/shard_map/ppermute | solution.py:664
  55.3 5.6 %collective-permute-start.13 = (bf16[2,24,1024]{2,1,0:T(8,128)(2,1)S(1)}, bf16[2,24,1024]{2,1,0:T(8,128)(2,1)S(1)}, u32[]{:S(2)}, u32[]{:S(2)}) collective-permute-start(bf16[2,24,1024]{2,1,0:T(8,128)(2,1)S(1)} %get-tuple-element.66.refs_1_), channel_id=1, source_target_pairs={{0,1},{1,0},{2,3},{3,2},{4,5},{5,4},{6,7},{7,6},{8,9},{9,8},{10,11... | collective-permute-start | bytes 294920 | tf_op jit(solution)/shard_map/ppermute | solution.py:673
  55.3 5.6 %collective-permute-start.17 = (bf16[2,24,1024]{2,1,0:T(8,128)(2,1)S(1)}, bf16[2,24,1024]{2,1,0:T(8,128)(2,1)S(1)}, u32[]{:S(2)}, u32[]{:S(2)}) collective-permute-start(bf16[2,24,1024]{2,1,0:T(8,128)(2,1)S(1)} %get-tuple-element.67.refs_2_), channel_id=1, source_target_pairs={{0,2},{1,3},{2,0},{3,1},{4,6},{5,7},{6,4},{7,5},{8,10},{9,11},{10,... | collective-permute-start | bytes 294920 | tf_op jit(solution)/shard_map/ppermute | solution.py:672
  55.8 5.6 %collective-permute-start.14 = (bf16[2,24,1024]{2,1,0:T(8,128)(2,1)S(1)}, bf16[2,24,1024]{2,1,0:T(8,128)(2,1)S(1)}, u32[]{:S(2)}, u32[]{:S(2)}) collective-permute-start(bf16[2,24,1024]{2,1,0:T(8,128)(2,1)S(1)} %get-tuple-element.67.refs_2_), channel_id=1, source_target_pairs={{0,1},{1,0},{2,3},{3,2},{4,5},{5,4},{6,7},{7,6},{8,9},{9,8},{10,11... | collective-permute-start | bytes 294920 | tf_op jit(solution)/shard_map/ppermute | solution.py:673
  58.4 5.1 %collective-permute-start.18 = (bf16[2,24,1024]{2,1,0:T(8,128)(2,1)S(1)}, bf16[2,24,1024]{2,1,0:T(8,128)(2,1)S(1)}, u32[]{:S(2)}, u32[]{:S(2)}) collective-permute-start(bf16[2,24,1024]{2,1,0:T(8,128)(2,1)S(1)} %get-tuple-element.68.refs_3_), channel_id=1, source_target_pairs={{0,2},{1,3},{2,0},{3,1},{4,6},{5,7},{6,4},{7,5},{8,10},{9,11},{10,... | collective-permute-start | bytes 294920 | tf_op jit(solution)/shard_map/ppermute | solution.py:672
  60.9 2.6 %collective-permute-start.15 = (bf16[2,24,1024]{2,1,0:T(8,128)(2,1)S(1)}, bf16[2,24,1024]{2,1,0:T(8,128)(2,1)S(1)}, u32[]{:S(2)}, u32[]{:S(2)}) collective-permute-start(bf16[2,24,1024]{2,1,0:T(8,128)(2,1)S(1)} %get-tuple-element.68.refs_3_), channel_id=1, source_target_pairs={{0,1},{1,0},{2,3},{3,2},{4,5},{5,4},{6,7},{7,6},{8,9},{9,8},{10,11... | collective-permute-start | bytes 294920 | tf_op jit(solution)/shard_map/ppermute | solution.py:673
  60.9 2.6 %collective-permute-start.19 = (bf16[2,24,1024]{2,1,0:T(8,128)(2,1)S(1)}, bf16[2,24,1024]{2,1,0:T(8,128)(2,1)S(1)}, u32[]{:S(2)}, u32[]{:S(2)}) collective-permute-start(bf16[2,24,1024]{2,1,0:T(8,128)(2,1)S(1)} %collective-permute-done.16.refs_7_), channel_id=1, source_target_pairs={{0,1},{1,0},{2,3},{3,2},{4,5},{5,4},{6,7},{7,6},{8,9},{9,8},{10,11... | collective-permute-start | bytes 294920 | tf_op jit(solution)/shard_map/ppermute | solution.py:674
  61.4 2.1 %collective-permute-start.20 = (bf16[2,24,1024]{2,1,0:T(8,128)(2,1)S(1)}, bf16[2,24,1024]{2,1,0:T(8,128)(2,1)S(1)}, u32[]{:S(2)}, u32[]{:S(2)}) collective-permute-start(bf16[2,24,1024]{2,1,0:T(8,128)(2,1)S(1)} %collective-permute-done.17.refs_8_), channel_id=1, source_target_pairs={{0,1},{1,0},{2,3},{3,2},{4,5},{5,4},{6,7},{7,6},{8,9},{9,8},{10,11... | collective-permute-start | bytes 294920 | tf_op jit(solution)/shard_map/ppermute | solution.py:674
  63.5 1.3 %collective-permute-start.21 = (bf16[2,24,1024]{2,1,0:T(8,128)(2,1)S(1)}, bf16[2,24,1024]{2,1,0:T(8,128)(2,1)S(1)}, u32[]{:S(2)}, u32[]{:S(2)}) collective-permute-start(bf16[2,24,1024]{2,1,0:T(8,128)(2,1)S(1)} %collective-permute-done.18.refs_9_), channel_id=1, source_target_pairs={{0,1},{1,0},{2,3},{3,2},{4,5},{5,4},{6,7},{7,6},{8,9},{9,8},{10,11... | collective-permute-start | bytes 294920 | tf_op jit(solution)/shard_map/ppermute | solution.py:674
  (1 other events, 0.7 us)

commit v9 on v8

--- a/solution.py
+++ b/solution.py
@@ -498,7 +498,8 @@
 
 
 def spread_kernel(pick, *refs):
-    *arrived, layer, grad, mark, gathered = refs
+    *arrived, layer, grad, mark, gathered, staged, sems = refs
+    copies = []
     mark[...] = jnp.zeros_like(mark)
     head_index = lax.axis_index("head")
     sibling = 1 - 2 * lax.rem(head_index, 2)
@@ -511,7 +512,15 @@
                 gathered[at, pl.ds(start + SLOT - 16, 16), :] = jnp.zeros_like(gathered[at, :16, :])
                 piece = arrived[step * PIECES + number][at]
                 gathered[at, pl.ds(start, PART // PIECES), :] = piece
-        out[...] = dot(pick[...], gathered[at]).astype(BF16)
+        staged[at] = dot(pick[...], gathered[at]).astype(BF16)
+        for number in range(PIECES):
+            rows = CELLS // PIECES
+            part = pl.ds(number * rows, rows)
+            sem = sems.at[at * PIECES + number]
+            copies.append(pltpu.make_async_copy(staged.at[at, part], out.at[part], sem))
+            copies[-1].start()
+    for copy in copies:
+        copy.wait()
 
 
 def shaped(*shape, dtype=BF16):
@@ -675,9 +684,14 @@
     layer_out, grad_tokens, spread_mark = call(
         spread_kernel,
         [shaped(CELLS, width)] * 2 + [mark],
-        [pltpu.VMEM((2, QUARTERS * PIECES * SLOT, width), BF16)],
+        [
+            pltpu.VMEM((2, QUARTERS * PIECES * SLOT, width), BF16),
+            pltpu.VMEM((2, CELLS, width), BF16),
+            pltpu.SemaphoreType.DMA((2 * PIECES,)),
+        ],
         cost=cost(2 * 2 * CELLS * CELLS * width, 8 * CELLS * width),
         name="spread_outputs",
+        far_outs=2,
     )(own_pick(), *each, *near, *far, *across)
     flip = rows % 128 == 0
     grad_qkv, grad_out = call(

time: 67.7 us -> 67.7 us (level)
  no operation moved by 1% of the time
where the time goes in v9:
time: 67.7 us; the launch traced here: 67.5 us
  waiting for transfers between devices  29.7 us (44%)
  starting transfers between devices  20.7 us (31%)
  Pallas kernels  15.5 us (23%)
  between operations  0.85 us (1%)
  local copies, waits for them, and re-layouts  0.75 us (1%)
    pallas_call x13, Pallas kernels, run(): pl.pallas_call(body, out_shape=outs, in_specs=[near] * len(args) + [outsi...  15.5 us
    ppermute x4, waiting for transfers between devices, rotated(): lax.ppermute(value, axis, [(i, (i + step) % count) for i in range(count)])  7.85 us
    ppermute x1, waiting for transfers between devices, body(): crossed = lax.ppermute(across, 'head', chips)  7.49 us
    ppermute x3, starting transfers between devices, moved(): return lax.ppermute(value, ('lon', 'lat'), pairs)  7 us
    ppermute x4, starting transfers between devices, rotated(): lax.ppermute(value, axis, [(i, (i + step) % count) for i in range(count)])  5.16 us
    ppermute x3, starting transfers between devices, body(): far = [lax.ppermute(single, 'head', chips) for single in each]  4.57 us
    ppermute x3, waiting for transfers between devices, body(): far = [lax.ppermute(single, 'head', chips) for single in each]  4.42 us
    ppermute x1, waiting for transfers between devices, body(): from_lat = lax.ppermute(send_first, 'lat', neighbours)  4.3 us
  transfers between devices with their start and end apart: 23, of which 12 were waited for; matrix products, arithmetic and copies ran while one was open for 0% of the time, Pallas kernels for 7%

profile of v9, /device:TPU:0, one launch (start us, length us, event | category | flops | bytes accessed | tf_op | source)
XLA Modules:
  0.0 67.5 jit_solution(10289715116136618338)
XLA Ops:
  0.6 1.6 %pack_rims.1 = (bf16[112,1024]{1,0:T(8,128)(2,1)S(1)}, bf16[48,1024]{1,0:T(8,128)(2,1)S(1)}, bf16[48,1024]{1,0:T(8,128)(2,1)S(1)}) custom-call(bf16[288,1024]{1,0:T(8,128)(2,1)} %bitcast.6, bf16[288,1024]{1,0:T(8,128)(2,1)} %bitcast.8), custom_call_target="tpu_custom_call" | custom-call | flops 122683392 | bytes 1179648 | tf_op jit(solution)/shard_map/pack_rims/pallas_call | solution.py:162
  2.2 5.1 %collective-permute-start = (bf16[112,1024]{1,0:T(8,128)(2,1)S(1)}, bf16[112,1024]{1,0:T(8,128)(2,1)S(1)}, u32[]{:S(2)}, u32[]{:S(2)}) collective-permute-start(bf16[112,1024]{1,0:T(8,128)(2,1)S(1)} %get-tuple-element.40), channel_id=1, source_target_pairs={{0,12},{4,0},{8,4},{12,8},{16,28},{20,16},{24,20},{28,24},{1,13},{... | collective-permute-start | bytes 688136 | tf_op jit(solution)/shard_map/ppermute | solution.py:542
  7.3 1.5 %collective-permute-start.1 = (bf16[48,1024]{1,0:T(8,128)(2,1)S(1)}, bf16[48,1024]{1,0:T(8,128)(2,1)S(1)}, u32[]{:S(2)}, u32[]{:S(2)}) collective-permute-start(bf16[48,1024]{1,0:T(8,128)(2,1)S(1)} %get-tuple-element.42), channel_id=1, source_target_pairs={{0,16},{4,20},{8,24},{12,28},{16,0},{20,4},{24,8},{28,12},{1,17},{... | collective-permute-start | bytes 294920 | tf_op jit(solution)/shard_map/ppermute | solution.py:542
  8.8 0.4 collective-permute-start.2
  9.2 0.7 %copy-done.7 = f32[759,4]{0,1:T(4,128)S(1)} copy-done((f32[759,4]{0,1:T(4,128)S(1)}, f32[759,4]{0,1:T(4,128)}, u32[]{:S(2)}) %copy-start.7) | copy-done | bytes 12168
  10.0 2.0 %window_bias.1 = (f32[4,144,144]{2,1,0:T(8,128)S(1)}, f32[8,128]{1,0:T(8,128)S(1)}) custom-call(f32[4,759]{1,0:T(4,128)S(1)} %bitcast.12), custom_call_target="tpu_custom_call" | custom-call | flops 1019215872 | bytes 1000000 | tf_op jit(solution)/shard_map/window_bias/pallas_call | solution.py:162
  12.0 1.3 %collective-permute-done.refs_0_ = bf16[112,1024]{1,0:T(8,128)(2,1)S(1)} collective-permute-done((bf16[112,1024]{1,0:T(8,128)(2,1)S(1)}, bf16[112,1024]{1,0:T(8,128)(2,1)S(1)}, u32[]{:S(2)}, u32[]{:S(2)}) %collective-permute-start) | collective-permute-done | bytes 229408 | tf_op jit(solution)/shard_map/ppermute | solution.py:542
  13.4 1.0 %collective-permute-done.2.refs_1_ = bf16[48,1024]{1,0:T(8,128)(2,1)S(1)} collective-permute-done((bf16[48,1024]{1,0:T(8,128)(2,1)S(1)}, bf16[48,1024]{1,0:T(8,128)(2,1)S(1)}, u32[]{:S(2)}, u32[]{:S(2)}) %collective-permute-start.2) | collective-permute-done | bytes 98336 | tf_op jit(solution)/shard_map/ppermute | solution.py:542
  14.4 1.4 %collective-permute-done.4.refs_5_ = bf16[96,1024]{1,0:T(8,128)(2,1)S(1)} collective-permute-done((bf16[96,1024]{1,0:T(8,128)(2,1)S(1)}, bf16[96,1024]{1,0:T(8,128)(2,1)S(1)}, u32[]{:S(2)}, u32[]{:S(2)}) %collective-permute-start.4) | collective-permute-done | bytes 196640 | tf_op jit(solution)/shard_map/ppermute | solution.py:589
  15.9 7.7 %window_layer.1 = (bf16[512,512]{1,0:T(8,128)(2,1)S(1)}, bf16[512,512]{1,0:T(8,128)(2,1)S(1)}, bf16[512,512]{1,0:T(8,128)(2,1)S(1)}, bf16[512,512]{1,0:T(8,128)(...) custom-call(bf16[288,1024]{1,0:T(8,128)(2,1)S(1)} %bitcast.7, ...), custom_call_target="tpu_custom_call" | custom-call | flops 1811939328 | bytes 8000000 | tf_op jit(solution)/shard_map/window_layer/pallas_call | solution.py:162
  23.8 1.5 %collective-permute-start.8 = (bf16[512,512]{1,0:T(8,128)(2,1)S(1)}, bf16[512,512]{1,0:T(8,128)(2,1)S(1)}, u32[]{:S(2)}, u32[]{:S(2)}) collective-permute-start(bf16[512,512]{1,0:T(8,128)(2,1)S(1)} %get-tuple-element.54), channel_id=1, source_target_pairs={{0,16},{16,0},{1,17},{17,1},{2,18},{18,2},{3,19},{19,3},{4,20},{20... | collective-permute-start | bytes 1572872 | tf_op jit(solution)/shard_map/ppermute | solution.py:532
  25.3 0.4 collective-permute-start.9
  25.8 1.6 %collective-permute-start.6 = (bf16[2,72,1024]{2,1,0:T(8,128)(2,1)S(1)}, bf16[2,72,1024]{2,1,0:T(8,128)(2,1)S(1)}, u32[]{:S(2)}, u32[]{:S(2)}) collective-permute-start(bf16[2,72,1024]{2,1,0:T(8,128)(2,1)S(1)} %sum_over_cores.1), channel_id=1, source_target_pairs={{0,2},{1,3},{2,0},{3,1},{4,6},{5,7},{6,4},{7,5},{8,10},{9,11},{10,... | collective-permute-start | bytes 884744 | tf_op jit(solution)/shard_map/ppermute | solution.py:638
  27.4 7.5 %collective-permute-done.6.refs_6_ = bf16[2,72,1024]{2,1,0:T(8,128)(2,1)S(1)} collective-permute-done((bf16[2,72,1024]{2,1,0:T(8,128)(2,1)S(1)}, bf16[2,72,1024]{2,1,0:T(8,128)(2,1)S(1)}, u32[]{:S(2)}, u32[]{:S(2)}) %collective-permute-start.6) | collective-permute-done | bytes 294944 | tf_op jit(solution)/shard_map/ppermute | solution.py:638
  34.9 0.6 sum_over_heads.1
  35.4 1.5 %collective-permute-start.7 = (bf16[2,32,1024]{2,1,0:T(8,128)(2,1)S(1)}, bf16[2,32,1024]{2,1,0:T(8,128)(2,1)S(1)}, u32[]{:S(2)}, u32[]{:S(2)}) collective-permute-start(bf16[2,32,1024]{2,1,0:T(8,128)(2,1)S(1)} %get-tuple-element.52), channel_id=1, source_target_pairs={{0,16},{16,0},{1,17},{17,1},{2,18},{18,2},{3,19},{19,3},{4,20},{20... | collective-permute-start | bytes 393224 | tf_op jit(solution)/shard_map/ppermute | solution.py:532
  36.9 1.6 %collective-permute-done.8.refs_1_ = bf16[512,512]{1,0:T(8,128)(2,1)S(1)} collective-permute-done((bf16[512,512]{1,0:T(8,128)(2,1)S(1)}, bf16[512,512]{1,0:T(8,128)(2,1)S(1)}, u32[]{:S(2)}, u32[]{:S(2)}) %collective-permute-start.8) | collective-permute-done | bytes 524320 | tf_op jit(solution)/shard_map/ppermute | solution.py:532
  38.6 0.6 collective-permute-done.9.refs_3_
  39.4 0.8 %collective-permute-start.11 = (bf16[256,512]{1,0:T(8,128)(2,1)S(1)}, bf16[256,512]{1,0:T(8,128)(2,1)S(1)}, u32[]{:S(2)}, u32[]{:S(2)}) collective-permute-start(bf16[256,512]{1,0:T(8,128)(2,1)S(1)} %get-tuple-element.61), channel_id=1, source_target_pairs={{0,4},{4,0},{8,12},{12,8},{1,5},{5,1},{9,13},{13,9},{2,6},{6,2},{1... | collective-permute-start | bytes 786440 | tf_op jit(solution)/shard_map/ppermute | solution.py:655
  40.3 1.2 %collective-permute-start.12 = (bf16[256,512]{1,0:T(8,128)(2,1)S(1)}, bf16[256,512]{1,0:T(8,128)(2,1)S(1)}, u32[]{:S(2)}, u32[]{:S(2)}) collective-permute-start(bf16[256,512]{1,0:T(8,128)(2,1)S(1)} %get-tuple-element.63), channel_id=1, source_target_pairs={{0,16},{16,0},{1,17},{17,1},{2,18},{18,2},{3,19},{19,3},{4,20},{20... | collective-permute-start | bytes 786440 | tf_op jit(solution)/shard_map/ppermute | solution.py:532
  41.7 1.0 %collective-permute-start.10 = (bf16[2,40,1024]{2,1,0:T(8,128)(2,1)S(1)}, bf16[2,40,1024]{2,1,0:T(8,128)(2,1)S(1)}, u32[]{:S(2)}, u32[]{:S(2)}) collective-permute-start(bf16[2,40,1024]{2,1,0:T(8,128)(2,1)S(1)} %get-tuple-element.59), channel_id=1, source_target_pairs={{0,4},{4,8},{8,12},{12,0},{1,5},{5,9},{9,13},{13,1},{2,6},{6,10},{... | collective-permute-start | bytes 491528 | tf_op jit(solution)/shard_map/ppermute | solution.py:532
  42.7 4.3 %collective-permute-done.11.refs_1_ = bf16[256,512]{1,0:T(8,128)(2,1)S(1)} collective-permute-done((bf16[256,512]{1,0:T(8,128)(2,1)S(1)}, bf16[256,512]{1,0:T(8,128)(2,1)S(1)}, u32[]{:S(2)}, u32[]{:S(2)}) %collective-permute-start.11) | collective-permute-done | bytes 262176 | tf_op jit(solution)/shard_map/ppermute | solution.py:655
  47.3 6.0 %collective-permute-done.10.refs_1_ = bf16[2,40,1024]{2,1,0:T(8,128)(2,1)S(1)} collective-permute-done((bf16[2,40,1024]{2,1,0:T(8,128)(2,1)S(1)}, bf16[2,40,1024]{2,1,0:T(8,128)(2,1)S(1)}, u32[]{:S(2)}, u32[]{:S(2)}) %collective-permute-start.10) | collective-permute-done | bytes 163872 | tf_op jit(solution)/shard_map/ppermute | solution.py:532
  53.7 1.6 %collective-permute-start.16 = (bf16[2,24,1024]{2,1,0:T(8,128)(2,1)S(1)}, bf16[2,24,1024]{2,1,0:T(8,128)(2,1)S(1)}, u32[]{:S(2)}, u32[]{:S(2)}) collective-permute-start(bf16[2,24,1024]{2,1,0:T(8,128)(2,1)S(1)} %get-tuple-element.66.refs_1_), channel_id=1, source_target_pairs={{0,2},{1,3},{2,0},{3,1},{4,6},{5,7},{6,4},{7,5},{8,10},{9,11},{10,... | collective-permute-start | bytes 294920 | tf_op jit(solution)/shard_map/ppermute | solution.py:681
  55.3 0.5 collective-permute-start.17
  56.0 2.4 %collective-permute-done.16.refs_7_ = bf16[2,24,1024]{2,1,0:T(8,128)(2,1)S(1)} collective-permute-done((bf16[2,24,1024]{2,1,0:T(8,128)(2,1)S(1)}, bf16[2,24,1024]{2,1,0:T(8,128)(2,1)S(1)}, u32[]{:S(2)}, u32[]{:S(2)}) %collective-permute-start.16) | collective-permute-done | bytes 98336 | tf_op jit(solution)/shard_map/ppermute | solution.py:681
  58.4 2.5 %collective-permute-start.18 = (bf16[2,24,1024]{2,1,0:T(8,128)(2,1)S(1)}, bf16[2,24,1024]{2,1,0:T(8,128)(2,1)S(1)}, u32[]{:S(2)}, u32[]{:S(2)}) collective-permute-start(bf16[2,24,1024]{2,1,0:T(8,128)(2,1)S(1)} %get-tuple-element.68.refs_3_), channel_id=1, source_target_pairs={{0,2},{1,3},{2,0},{3,1},{4,6},{5,7},{6,4},{7,5},{8,10},{9,11},{10,... | collective-permute-start | bytes 294920 | tf_op jit(solution)/shard_map/ppermute | solution.py:681
  60.9 0.5 collective-permute-start.19
  61.5 2.0 %collective-permute-done.18.refs_9_ = bf16[2,24,1024]{2,1,0:T(8,128)(2,1)S(1)} collective-permute-done((bf16[2,24,1024]{2,1,0:T(8,128)(2,1)S(1)}, bf16[2,24,1024]{2,1,0:T(8,128)(2,1)S(1)}, u32[]{:S(2)}, u32[]{:S(2)}) %collective-permute-start.18) | collective-permute-done | bytes 98336 | tf_op jit(solution)/shard_map/ppermute | solution.py:681
  63.5 1.3 %collective-permute-done.21.refs_12_ = bf16[2,24,1024]{2,1,0:T(8,128)(2,1)S(1)} collective-permute-done((bf16[2,24,1024]{2,1,0:T(8,128)(2,1)S(1)}, bf16[2,24,1024]{2,1,0:T(8,128)(2,1)S(1)}, u32[]{:S(2)}, u32[]{:S(2)}) %collective-permute-start.21) | collective-permute-done | bytes 98336 | tf_op jit(solution)/shard_map/ppermute | solution.py:683
  64.8 1.8 %spread_outputs.1 = (bf16[288,1024]{1,0:T(8,128)(2,1)}, bf16[288,1024]{1,0:T(8,128)(2,1)}, f32[8,128]{1,0:T(8,128)S(1)}) custom-call(bf16[288,384]{1,0:T(8,128)(2,1)S(1)} %copy-done.2, bf16[2,24,1024]{2,1,0:T(8,128)(2,1)S(1)} %get-tuple-element.66.refs_1_, bf16[2,24,1024]{2,1,0:T(8,128)(2,1)S(1)} %get-tuple-element.67.refs_2_, ...), custom_call_target="tpu_custom_call" | custom-call | flops 339738624 | bytes 2359296 | tf_op jit(solution)/shard_map/spread_outputs/pallas_call | solution.py:162
  66.6 0.8 %sum_over_lat.1 = (f32[128,768]{1,0:T(8,128)}, f32[256,128]{1,0:T(8,128)}) custom-call(f32[2,128,512]{2,1,0:T(8,128)S(1)} %get-tuple-element.71.refs_0_, bf16[2,128,512]{2,1,0:T(8,128)(2,1)S(1)} %collective-permute-done.22.refs_1_, f32[8,128]{1,0:T(8,128)S(1)} %get-tuple-element.73.refs_2_), custom_call_target="tpu_custom_call" | custom-call | flops 524288 | bytes 2097152 | tf_op jit(solution)/shard_map/sum_over_lat/pallas_call | solution.py:162
  (47 shorter events, 2.0 us)
Async XLA Ops:
  2.2 11.0 %collective-permute-start = (bf16[112,1024]{1,0:T(8,128)(2,1)S(1)}, bf16[112,1024]{1,0:T(8,128)(2,1)S(1)}, u32[]{:S(2)}, u32[]{:S(2)}) collective-permute-start(bf16[112,1024]{1,0:T(8,128)(2,1)S(1)} %get-tuple-element.40), channel_id=1, source_target_pairs={{0,12},{4,0},{8,4},{12,8},{16,28},{20,16},{24,20},{28,24},{1,13},{... | collective-permute-start | bytes 688136 | tf_op jit(solution)/shard_map/ppermute | solution.py:542
  7.3 6.0 %collective-permute-start.1 = (bf16[48,1024]{1,0:T(8,128)(2,1)S(1)}, bf16[48,1024]{1,0:T(8,128)(2,1)S(1)}, u32[]{:S(2)}, u32[]{:S(2)}) collective-permute-start(bf16[48,1024]{1,0:T(8,128)(2,1)S(1)} %get-tuple-element.42), channel_id=1, source_target_pairs={{0,16},{4,20},{8,24},{12,28},{16,0},{20,4},{24,8},{28,12},{1,17},{... | collective-permute-start | bytes 294920 | tf_op jit(solution)/shard_map/ppermute | solution.py:542
  8.8 5.5 %collective-permute-start.2 = (bf16[48,1024]{1,0:T(8,128)(2,1)S(1)}, bf16[48,1024]{1,0:T(8,128)(2,1)S(1)}, u32[]{:S(2)}, u32[]{:S(2)}) collective-permute-start(bf16[48,1024]{1,0:T(8,128)(2,1)S(1)} %get-tuple-element.43), channel_id=1, source_target_pairs={{0,28},{4,16},{8,20},{12,24},{16,12},{20,0},{24,4},{28,8},{1,29},{... | collective-permute-start | bytes 294920 | tf_op jit(solution)/shard_map/ppermute | solution.py:542
  9.9 5.9 %copy-start = (bf16[2,6,24,1024]{3,2,1,0:T(8,128)(2,1)S(1)}, bf16[2,6,24,1024]{3,2,1,0:T(8,128)(2,1)}, u32[]{:S(2)}) copy-start(bf16[2,6,24,1024]{3,2,1,0:T(8,128)(2,1)} %param.10) | copy-start | bytes 1769476
  9.9 5.9 %copy-start.1 = (bf16[2,6,24,1024]{3,2,1,0:T(8,128)(2,1)S(1)}, bf16[2,6,24,1024]{3,2,1,0:T(8,128)(2,1)}, u32[]{:S(2)}) copy-start(bf16[2,6,24,1024]{3,2,1,0:T(8,128)(2,1)} %param.15) | copy-start | bytes 1769476
  9.9 5.9 %copy-start.4 = (f32[1024]{0:T(1024)S(1)}, f32[1024]{0:T(1024)}, u32[]{:S(2)}) copy-start(f32[1024]{0:T(1024)} %param.11) | copy-start | bytes 12292
  9.9 5.9 %copy-start.5 = (bf16[1024,768]{1,0:T(8,128)(2,1)S(1)}, bf16[1024,768]{1,0:T(8,128)(2,1)}, u32[]{:S(2)}) copy-start(bf16[1024,768]{1,0:T(8,128)(2,1)} %refs_11_.1) | copy-start | bytes 4718596
  9.9 5.9 %copy-start.6 = (bf16[256,1024]{1,0:T(8,128)(2,1)S(1)}, bf16[256,1024]{1,0:T(8,128)(2,1)}, u32[]{:S(2)}) copy-start(bf16[256,1024]{1,0:T(8,128)(2,1)} %refs_7_.1) | copy-start | bytes 1572868
  10.0 5.9 %copy-start.8 = (bf16[288,496]{1,0:T(8,128)(2,1)S(1)}, bf16[288,496]{1,0:T(8,128)(2,1)}, u32[]{:S(2)}) copy-start(bf16[288,496]{1,0:T(8,128)(2,1)} %constant.8.clone.refs_9_) | copy-start | bytes 857092
  10.0 5.9 %copy-start.9 = (bf16[320,288]{1,0:T(8,128)(2,1)S(1)}, bf16[320,288]{1,0:T(8,128)(2,1)}, u32[]{:S(2)}) copy-start(bf16[320,288]{1,0:T(8,128)(2,1)} %constant.9.clone.refs_10_) | copy-start | bytes 552964
  13.3 2.6 %collective-permute-start.3 = (bf16[112,1024]{1,0:T(8,128)(2,1)S(1)}, bf16[112,1024]{1,0:T(8,128)(2,1)S(1)}, u32[]{:S(2)}, u32[]{:S(2)}) collective-permute-start(bf16[112,1024]{1,0:T(8,128)(2,1)S(1)} %hold_rim.1.refs_2_), channel_id=1, source_target_pairs={{0,1},{1,0},{2,3},{3,2},{4,5},{5,4},{6,7},{7,6},{8,9},{9,8},{10,11... | collective-permute-start | bytes 688136 | tf_op jit(solution)/shard_map/ppermute | solution.py:589
  14.3 1.5 %collective-permute-start.4 = (bf16[96,1024]{1,0:T(8,128)(2,1)S(1)}, bf16[96,1024]{1,0:T(8,128)(2,1)S(1)}, u32[]{:S(2)}, u32[]{:S(2)}) collective-permute-start(bf16[96,1024]{1,0:T(8,128)(2,1)S(1)} %join_rims.1.refs_3_), channel_id=1, source_target_pairs={{0,1},{1,0},{2,3},{3,2},{4,5},{5,4},{6,7},{7,6},{8,9},{9,8},{10,11... | collective-permute-start | bytes 589832 | tf_op jit(solution)/shard_map/ppermute | solution.py:589
  15.9 18.9 %copy-start.3 = (bf16[112,72]{1,0:T(8,128)(2,1)S(1)}, bf16[112,72]{1,0:T(8,128)(2,1)}, u32[]{:S(2)}) copy-start(bf16[112,72]{1,0:T(8,128)(2,1)} %constant.10.clone.refs_3_) | copy-start | bytes 48388
  23.6 2.1 %collective-permute-start.5 = (bf16[2,2,72,1024]{3,2,1,0:T(8,128)(2,1)S(1)}, bf16[2,2,72,1024]{3,2,1,0:T(8,128)(2,1)S(1)}, u32[]{:S(2)}, u32[]{:S(2)}) collective-permute-start(bf16[2,2,72,1024]{3,2,1,0:T(8,128)(2,1)S(1)} %get-tuple-element.48), channel_id=1, source_target_pairs={{0,1},{1,0},{2,3},{3,2},{4,5},{5,4},{6,7},{7,6},{8,9},{9,8},{10,11... | collective-permute-start | bytes 1769480 | tf_op jit(solution)/shard_map/ppermute | solution.py:633
  23.8 14.8 %collective-permute-start.8 = (bf16[512,512]{1,0:T(8,128)(2,1)S(1)}, bf16[512,512]{1,0:T(8,128)(2,1)S(1)}, u32[]{:S(2)}, u32[]{:S(2)}) collective-permute-start(bf16[512,512]{1,0:T(8,128)(2,1)S(1)} %get-tuple-element.54), channel_id=1, source_target_pairs={{0,16},{16,0},{1,17},{17,1},{2,18},{18,2},{3,19},{19,3},{4,20},{20... | collective-permute-start | bytes 1572872 | tf_op jit(solution)/shard_map/ppermute | solution.py:532
  25.3 13.9 %collective-permute-start.9 = (bf16[512,512]{1,0:T(8,128)(2,1)S(1)}, bf16[512,512]{1,0:T(8,128)(2,1)S(1)}, u32[]{:S(2)}, u32[]{:S(2)}) collective-permute-start(bf16[512,512]{1,0:T(8,128)(2,1)S(1)} %get-tuple-element.56), channel_id=1, source_target_pairs={{0,4},{4,0},{8,12},{12,8},{1,5},{5,1},{9,13},{13,9},{2,6},{6,2},{1... | collective-permute-start | bytes 1572872 | tf_op jit(solution)/shard_map/ppermute | solution.py:632
  25.8 9.1 %collective-permute-start.6 = (bf16[2,72,1024]{2,1,0:T(8,128)(2,1)S(1)}, bf16[2,72,1024]{2,1,0:T(8,128)(2,1)S(1)}, u32[]{:S(2)}, u32[]{:S(2)}) collective-permute-start(bf16[2,72,1024]{2,1,0:T(8,128)(2,1)S(1)} %sum_over_cores.1), channel_id=1, source_target_pairs={{0,2},{1,3},{2,0},{3,1},{4,6},{5,7},{6,4},{7,5},{8,10},{9,11},{10,... | collective-permute-start | bytes 884744 | tf_op jit(solution)/shard_map/ppermute | solution.py:638
  35.4 6.0 %collective-permute-start.7 = (bf16[2,32,1024]{2,1,0:T(8,128)(2,1)S(1)}, bf16[2,32,1024]{2,1,0:T(8,128)(2,1)S(1)}, u32[]{:S(2)}, u32[]{:S(2)}) collective-permute-start(bf16[2,32,1024]{2,1,0:T(8,128)(2,1)S(1)} %get-tuple-element.52), channel_id=1, source_target_pairs={{0,16},{16,0},{1,17},{17,1},{2,18},{18,2},{3,19},{19,3},{4,20},{20... | collective-permute-start | bytes 393224 | tf_op jit(solution)/shard_map/ppermute | solution.py:532
  39.4 25.4 %copy-start.2 = (bf16[288,384]{1,0:T(8,128)(2,1)S(1)}, bf16[288,384]{1,0:T(8,128)(2,1)}, u32[]{:S(2)}) copy-start(bf16[288,384]{1,0:T(8,128)(2,1)} %constant.11.clone.refs_0_) | copy-start | bytes 663556
  39.4 7.5 %collective-permute-start.11 = (bf16[256,512]{1,0:T(8,128)(2,1)S(1)}, bf16[256,512]{1,0:T(8,128)(2,1)S(1)}, u32[]{:S(2)}, u32[]{:S(2)}) collective-permute-start(bf16[256,512]{1,0:T(8,128)(2,1)S(1)} %get-tuple-element.61), channel_id=1, source_target_pairs={{0,4},{4,0},{8,12},{12,8},{1,5},{5,1},{9,13},{13,9},{2,6},{6,2},{1... | collective-permute-start | bytes 786440 | tf_op jit(solution)/shard_map/ppermute | solution.py:655
  40.3 6.9 %collective-permute-start.12 = (bf16[256,512]{1,0:T(8,128)(2,1)S(1)}, bf16[256,512]{1,0:T(8,128)(2,1)S(1)}, u32[]{:S(2)}, u32[]{:S(2)}) collective-permute-start(bf16[256,512]{1,0:T(8,128)(2,1)S(1)} %get-tuple-element.63), channel_id=1, source_target_pairs={{0,16},{16,0},{1,17},{17,1},{2,18},{18,2},{3,19},{19,3},{4,20},{20... | collective-permute-start | bytes 786440 | tf_op jit(solution)/shard_map/ppermute | solution.py:532
  41.7 11.6 %collective-permute-start.10 = (bf16[2,40,1024]{2,1,0:T(8,128)(2,1)S(1)}, bf16[2,40,1024]{2,1,0:T(8,128)(2,1)S(1)}, u32[]{:S(2)}, u32[]{:S(2)}) collective-permute-start(bf16[2,40,1024]{2,1,0:T(8,128)(2,1)S(1)} %get-tuple-element.59), channel_id=1, source_target_pairs={{0,4},{4,8},{8,12},{12,0},{1,5},{5,9},{9,13},{13,1},{2,6},{6,10},{... | collective-permute-start | bytes 491528 | tf_op jit(solution)/shard_map/ppermute | solution.py:532
  53.7 4.7 %collective-permute-start.16 = (bf16[2,24,1024]{2,1,0:T(8,128)(2,1)S(1)}, bf16[2,24,1024]{2,1,0:T(8,128)(2,1)S(1)}, u32[]{:S(2)}, u32[]{:S(2)}) collective-permute-start(bf16[2,24,1024]{2,1,0:T(8,128)(2,1)S(1)} %get-tuple-element.66.refs_1_), channel_id=1, source_target_pairs={{0,2},{1,3},{2,0},{3,1},{4,6},{5,7},{6,4},{7,5},{8,10},{9,11},{10,... | collective-permute-start | bytes 294920 | tf_op jit(solution)/shard_map/ppermute | solution.py:681
  55.3 11.4 %collective-permute-start.22 = (bf16[2,128,512]{2,1,0:T(8,128)(2,1)S(1)}, bf16[2,128,512]{2,1,0:T(8,128)(2,1)S(1)}, u32[]{:S(2)}, u32[]{:S(2)}) collective-permute-start(bf16[2,128,512]{2,1,0:T(8,128)(2,1)S(1)} %get-tuple-element.72), channel_id=1, source_target_pairs={{0,8},{4,12},{8,0},{12,4},{1,9},{5,13},{9,1},{13,5},{2,10},{6,14},... | collective-permute-start | bytes 786440 | tf_op jit(solution)/shard_map/ppermute | solution.py:673
  55.3 5.6 %collective-permute-start.13 = (bf16[2,24,1024]{2,1,0:T(8,128)(2,1)S(1)}, bf16[2,24,1024]{2,1,0:T(8,128)(2,1)S(1)}, u32[]{:S(2)}, u32[]{:S(2)}) collective-permute-start(bf16[2,24,1024]{2,1,0:T(8,128)(2,1)S(1)} %get-tuple-element.66.refs_1_), channel_id=1, source_target_pairs={{0,1},{1,0},{2,3},{3,2},{4,5},{5,4},{6,7},{7,6},{8,9},{9,8},{10,11... | collective-permute-start | bytes 294920 | tf_op jit(solution)/shard_map/ppermute | solution.py:682
  55.3 5.6 %collective-permute-start.17 = (bf16[2,24,1024]{2,1,0:T(8,128)(2,1)S(1)}, bf16[2,24,1024]{2,1,0:T(8,128)(2,1)S(1)}, u32[]{:S(2)}, u32[]{:S(2)}) collective-permute-start(bf16[2,24,1024]{2,1,0:T(8,128)(2,1)S(1)} %get-tuple-element.67.refs_2_), channel_id=1, source_target_pairs={{0,2},{1,3},{2,0},{3,1},{4,6},{5,7},{6,4},{7,5},{8,10},{9,11},{10,... | collective-permute-start | bytes 294920 | tf_op jit(solution)/shard_map/ppermute | solution.py:681
  55.8 5.6 %collective-permute-start.14 = (bf16[2,24,1024]{2,1,0:T(8,128)(2,1)S(1)}, bf16[2,24,1024]{2,1,0:T(8,128)(2,1)S(1)}, u32[]{:S(2)}, u32[]{:S(2)}) collective-permute-start(bf16[2,24,1024]{2,1,0:T(8,128)(2,1)S(1)} %get-tuple-element.67.refs_2_), channel_id=1, source_target_pairs={{0,1},{1,0},{2,3},{3,2},{4,5},{5,4},{6,7},{7,6},{8,9},{9,8},{10,11... | collective-permute-start | bytes 294920 | tf_op jit(solution)/shard_map/ppermute | solution.py:682
  58.4 5.1 %collective-permute-start.18 = (bf16[2,24,1024]{2,1,0:T(8,128)(2,1)S(1)}, bf16[2,24,1024]{2,1,0:T(8,128)(2,1)S(1)}, u32[]{:S(2)}, u32[]{:S(2)}) collective-permute-start(bf16[2,24,1024]{2,1,0:T(8,128)(2,1)S(1)} %get-tuple-element.68.refs_3_), channel_id=1, source_target_pairs={{0,2},{1,3},{2,0},{3,1},{4,6},{5,7},{6,4},{7,5},{8,10},{9,11},{10,... | collective-permute-start | bytes 294920 | tf_op jit(solution)/shard_map/ppermute | solution.py:681
  60.9 2.6 %collective-permute-start.15 = (bf16[2,24,1024]{2,1,0:T(8,128)(2,1)S(1)}, bf16[2,24,1024]{2,1,0:T(8,128)(2,1)S(1)}, u32[]{:S(2)}, u32[]{:S(2)}) collective-permute-start(bf16[2,24,1024]{2,1,0:T(8,128)(2,1)S(1)} %get-tuple-element.68.refs_3_), channel_id=1, source_target_pairs={{0,1},{1,0},{2,3},{3,2},{4,5},{5,4},{6,7},{7,6},{8,9},{9,8},{10,11... | collective-permute-start | bytes 294920 | tf_op jit(solution)/shard_map/ppermute | solution.py:682
  60.9 2.6 %collective-permute-start.19 = (bf16[2,24,1024]{2,1,0:T(8,128)(2,1)S(1)}, bf16[2,24,1024]{2,1,0:T(8,128)(2,1)S(1)}, u32[]{:S(2)}, u32[]{:S(2)}) collective-permute-start(bf16[2,24,1024]{2,1,0:T(8,128)(2,1)S(1)} %collective-permute-done.16.refs_7_), channel_id=1, source_target_pairs={{0,1},{1,0},{2,3},{3,2},{4,5},{5,4},{6,7},{7,6},{8,9},{9,8},{10,11... | collective-permute-start | bytes 294920 | tf_op jit(solution)/shard_map/ppermute | solution.py:683
  61.4 2.1 %collective-permute-start.20 = (bf16[2,24,1024]{2,1,0:T(8,128)(2,1)S(1)}, bf16[2,24,1024]{2,1,0:T(8,128)(2,1)S(1)}, u32[]{:S(2)}, u32[]{:S(2)}) collective-permute-start(bf16[2,24,1024]{2,1,0:T(8,128)(2,1)S(1)} %collective-permute-done.17.refs_8_), channel_id=1, source_target_pairs={{0,1},{1,0},{2,3},{3,2},{4,5},{5,4},{6,7},{7,6},{8,9},{9,8},{10,11... | collective-permute-start | bytes 294920 | tf_op jit(solution)/shard_map/ppermute | solution.py:683
  63.5 1.3 %collective-permute-start.21 = (bf16[2,24,1024]{2,1,0:T(8,128)(2,1)S(1)}, bf16[2,24,1024]{2,1,0:T(8,128)(2,1)S(1)}, u32[]{:S(2)}, u32[]{:S(2)}) collective-permute-start(bf16[2,24,1024]{2,1,0:T(8,128)(2,1)S(1)} %collective-permute-done.18.refs_9_), channel_id=1, source_target_pairs={{0,1},{1,0},{2,3},{3,2},{4,5},{5,4},{6,7},{7,6},{8,9},{9,8},{10,11... | collective-permute-start | bytes 294920 | tf_op jit(solution)/shard_map/ppermute | solution.py:683
  (1 other events, 0.7 us)

commit v10 on v8

--- a/solution.py
+++ b/solution.py
@@ -30,6 +30,7 @@
 
 RIM_Z, RIM_X, RIM_D = 112, 48, 48
 RIM = RIM_Z + RIM_X + RIM_D
+RIM_SENT = 40
 OUT_STARTS = (0, 32, 64)
 OUT_SIZES = (32, 32, 32)
 OUT_ROWS = 112
@@ -213,8 +214,8 @@
     wanted = lax.broadcasted_iota(jnp.int32, (RIM, CELLS), 0) == rim_rows((RIM, CELLS))
     rim = dot(wanted.astype(F32).astype(BF16), source[...]).astype(BF16)
     rim_z[...] = rim[:RIM_Z]
-    rim_x[...] = rim[RIM_Z : RIM_Z + RIM_X]
-    rim_d[...] = rim[RIM_Z + RIM_X :]
+    rim_x[...] = rim[RIM_Z : RIM_Z + RIM_SENT]
+    rim_d[...] = rim[RIM_Z + RIM_X : RIM_Z + RIM_X + RIM_SENT]
 
 
 def hold_kernel(rim, held):
@@ -222,8 +223,9 @@
 
 
 def rims_kernel(x_rim, d_rim, rim):
-    rim[:RIM_X] = x_rim[...]
-    rim[RIM_X:] = d_rim[...]
+    rim[...] = jnp.zeros_like(rim)
+    rim[:RIM_SENT] = x_rim[...]
+    rim[RIM_X : RIM_X + RIM_SENT] = d_rim[...]
 
 
 def bias_kernel(table, bias, mark, padded, shifted, parts):
@@ -544,7 +546,7 @@
     mark = shaped(8, 128, dtype=F32)
     rims = call(
         pack_kernel,
-        [shaped(RIM_Z, width), shaped(RIM_X, width), shaped(RIM_D, width)],
+        [shaped(RIM_Z, width)] + [shaped(RIM_SENT, width)] * 2,
         [pltpu.VMEM((CELLS, width), BF16), pltpu.SemaphoreType.DMA((6,))],
         cost=cost(2 * RIM * CELLS * width, 4 * CELLS * width),
         name="pack_rims",

time: 67.7 us -> 67.4 us (level)
  transfers between devices with their start and end apart: 23 -> 23, of which waited for: 12 -> 14; matrix products, arithmetic and copies ran while one was open for 0% -> 0% of each run, Pallas kernels for 7% -> 7%
where the time goes in v10:
time: 67.4 us; the launch traced here: 67.2 us
  waiting for transfers between devices  29.7 us (44%)
  starting transfers between devices  20.4 us (30%)
  Pallas kernels  15.5 us (23%)
  between operations  0.84 us (1%)
  local copies, waits for them, and re-layouts  0.75 us (1%)
    pallas_call x13, Pallas kernels, run(): pl.pallas_call(body, out_shape=outs, in_specs=[near] * len(args) + [outsi...  15.5 us
    ppermute x4, waiting for transfers between devices, rotated(): lax.ppermute(value, axis, [(i, (i + step) % count) for i in range(count)])  8.01 us
    ppermute x1, waiting for transfers between devices, body(): crossed = lax.ppermute(across, 'head', chips)  7.52 us
    ppermute x3, starting transfers between devices, moved(): return lax.ppermute(value, ('lon', 'lat'), pairs)  7 us
    ppermute x4, starting transfers between devices, rotated(): lax.ppermute(value, axis, [(i, (i + step) % count) for i in range(count)])  4.85 us
    ppermute x3, starting transfers between devices, body(): far = [lax.ppermute(single, 'head', chips) for single in each]  4.57 us
    ppermute x3, waiting for transfers between devices, body(): far = [lax.ppermute(single, 'head', chips) for single in each]  4.45 us
    ppermute x1, waiting for transfers between devices, body(): from_lat = lax.ppermute(send_first, 'lat', neighbours)  4.26 us
  transfers between devices with their start and end apart: 23, of which 14 were waited for; matrix products, arithmetic and copies ran while one was open for 0% of the time, Pallas kernels for 7%

profile of v10, /device:TPU:0, one launch (start us, length us, event | category | flops | bytes accessed | tf_op | source)
XLA Modules:
  0.0 67.2 jit_solution(17874248853721288863)
XLA Ops:
  0.6 1.6 %pack_rims.1 = (bf16[112,1024]{1,0:T(8,128)(2,1)S(1)}, bf16[40,1024]{1,0:T(8,128)(2,1)S(1)}, bf16[40,1024]{1,0:T(8,128)(2,1)S(1)}) custom-call(bf16[288,1024]{1,0:T(8,128)(2,1)} %bitcast.6, bf16[288,1024]{1,0:T(8,128)(2,1)} %bitcast.8), custom_call_target="tpu_custom_call" | custom-call | flops 122683392 | bytes 1179648 | tf_op jit(solution)/shard_map/pack_rims/pallas_call | solution.py:163
  2.2 5.1 %collective-permute-start = (bf16[112,1024]{1,0:T(8,128)(2,1)S(1)}, bf16[112,1024]{1,0:T(8,128)(2,1)S(1)}, u32[]{:S(2)}, u32[]{:S(2)}) collective-permute-start(bf16[112,1024]{1,0:T(8,128)(2,1)S(1)} %get-tuple-element.40), channel_id=1, source_target_pairs={{0,12},{4,0},{8,4},{12,8},{16,28},{20,16},{24,20},{28,24},{1,13},{... | collective-permute-start | bytes 688136 | tf_op jit(solution)/shard_map/ppermute | solution.py:535
  7.3 1.5 %collective-permute-start.1 = (bf16[40,1024]{1,0:T(8,128)(2,1)S(1)}, bf16[40,1024]{1,0:T(8,128)(2,1)S(1)}, u32[]{:S(2)}, u32[]{:S(2)}) collective-permute-start(bf16[40,1024]{1,0:T(8,128)(2,1)S(1)} %get-tuple-element.42), channel_id=1, source_target_pairs={{0,16},{4,20},{8,24},{12,28},{16,0},{20,4},{24,8},{28,12},{1,17},{... | collective-permute-start | bytes 245768 | tf_op jit(solution)/shard_map/ppermute | solution.py:535
  8.8 0.4 collective-permute-start.2
  9.2 0.7 %copy-done.7 = f32[759,4]{0,1:T(4,128)S(1)} copy-done((f32[759,4]{0,1:T(4,128)S(1)}, f32[759,4]{0,1:T(4,128)}, u32[]{:S(2)}) %copy-start.7) | copy-done | bytes 12168
  10.0 2.0 %window_bias.1 = (f32[4,144,144]{2,1,0:T(8,128)S(1)}, f32[8,128]{1,0:T(8,128)S(1)}) custom-call(f32[4,759]{1,0:T(4,128)S(1)} %bitcast.12), custom_call_target="tpu_custom_call" | custom-call | flops 1019215872 | bytes 1000000 | tf_op jit(solution)/shard_map/window_bias/pallas_call | solution.py:163
  12.0 1.1 %collective-permute-done.refs_0_ = bf16[112,1024]{1,0:T(8,128)(2,1)S(1)} collective-permute-done((bf16[112,1024]{1,0:T(8,128)(2,1)S(1)}, bf16[112,1024]{1,0:T(8,128)(2,1)S(1)}, u32[]{:S(2)}, u32[]{:S(2)}) %collective-permute-start) | collective-permute-done | bytes 229408 | tf_op jit(solution)/shard_map/ppermute | solution.py:535
  13.2 1.0 %collective-permute-done.2.refs_1_ = bf16[40,1024]{1,0:T(8,128)(2,1)S(1)} collective-permute-done((bf16[40,1024]{1,0:T(8,128)(2,1)S(1)}, bf16[40,1024]{1,0:T(8,128)(2,1)S(1)}, u32[]{:S(2)}, u32[]{:S(2)}) %collective-permute-start.2) | collective-permute-done | bytes 81952 | tf_op jit(solution)/shard_map/ppermute | solution.py:535
  14.2 1.4 %collective-permute-done.4.refs_5_ = bf16[96,1024]{1,0:T(8,128)(2,1)S(1)} collective-permute-done((bf16[96,1024]{1,0:T(8,128)(2,1)S(1)}, bf16[96,1024]{1,0:T(8,128)(2,1)S(1)}, u32[]{:S(2)}, u32[]{:S(2)}) %collective-permute-start.4) | collective-permute-done | bytes 196640 | tf_op jit(solution)/shard_map/ppermute | solution.py:582
  15.7 7.7 %window_layer.1 = (bf16[512,512]{1,0:T(8,128)(2,1)S(1)}, bf16[512,512]{1,0:T(8,128)(2,1)S(1)}, bf16[512,512]{1,0:T(8,128)(2,1)S(1)}, bf16[512,512]{1,0:T(8,128)(...) custom-call(bf16[288,1024]{1,0:T(8,128)(2,1)S(1)} %bitcast.7, ...), custom_call_target="tpu_custom_call" | custom-call | flops 1811939328 | bytes 8000000 | tf_op jit(solution)/shard_map/window_layer/pallas_call | solution.py:163
  23.6 1.3 %collective-permute-start.8 = (bf16[512,512]{1,0:T(8,128)(2,1)S(1)}, bf16[512,512]{1,0:T(8,128)(2,1)S(1)}, u32[]{:S(2)}, u32[]{:S(2)}) collective-permute-start(bf16[512,512]{1,0:T(8,128)(2,1)S(1)} %get-tuple-element.54), channel_id=1, source_target_pairs={{0,16},{16,0},{1,17},{17,1},{2,18},{18,2},{3,19},{19,3},{4,20},{20... | collective-permute-start | bytes 1572872 | tf_op jit(solution)/shard_map/ppermute | solution.py:525
  24.9 0.4 collective-permute-start.9
  25.6 1.6 %collective-permute-start.6 = (bf16[2,72,1024]{2,1,0:T(8,128)(2,1)S(1)}, bf16[2,72,1024]{2,1,0:T(8,128)(2,1)S(1)}, u32[]{:S(2)}, u32[]{:S(2)}) collective-permute-start(bf16[2,72,1024]{2,1,0:T(8,128)(2,1)S(1)} %sum_over_cores.1), channel_id=1, source_target_pairs={{0,2},{1,3},{2,0},{3,1},{4,6},{5,7},{6,4},{7,5},{8,10},{9,11},{10,... | collective-permute-start | bytes 884744 | tf_op jit(solution)/shard_map/ppermute | solution.py:631
  27.2 7.5 %collective-permute-done.6.refs_6_ = bf16[2,72,1024]{2,1,0:T(8,128)(2,1)S(1)} collective-permute-done((bf16[2,72,1024]{2,1,0:T(8,128)(2,1)S(1)}, bf16[2,72,1024]{2,1,0:T(8,128)(2,1)S(1)}, u32[]{:S(2)}, u32[]{:S(2)}) %collective-permute-start.6) | collective-permute-done | bytes 294944 | tf_op jit(solution)/shard_map/ppermute | solution.py:631
  34.7 0.6 sum_over_heads.1
  35.2 1.4 %collective-permute-start.7 = (bf16[2,32,1024]{2,1,0:T(8,128)(2,1)S(1)}, bf16[2,32,1024]{2,1,0:T(8,128)(2,1)S(1)}, u32[]{:S(2)}, u32[]{:S(2)}) collective-permute-start(bf16[2,32,1024]{2,1,0:T(8,128)(2,1)S(1)} %get-tuple-element.52), channel_id=1, source_target_pairs={{0,16},{16,0},{1,17},{17,1},{2,18},{18,2},{3,19},{19,3},{4,20},{20... | collective-permute-start | bytes 393224 | tf_op jit(solution)/shard_map/ppermute | solution.py:525
  36.6 1.8 %collective-permute-done.8.refs_1_ = bf16[512,512]{1,0:T(8,128)(2,1)S(1)} collective-permute-done((bf16[512,512]{1,0:T(8,128)(2,1)S(1)}, bf16[512,512]{1,0:T(8,128)(2,1)S(1)}, u32[]{:S(2)}, u32[]{:S(2)}) %collective-permute-start.8) | collective-permute-done | bytes 524320 | tf_op jit(solution)/shard_map/ppermute | solution.py:525
  38.4 0.5 collective-permute-done.9.refs_3_
  39.1 0.8 %collective-permute-start.11 = (bf16[256,512]{1,0:T(8,128)(2,1)S(1)}, bf16[256,512]{1,0:T(8,128)(2,1)S(1)}, u32[]{:S(2)}, u32[]{:S(2)}) collective-permute-start(bf16[256,512]{1,0:T(8,128)(2,1)S(1)} %get-tuple-element.61), channel_id=1, source_target_pairs={{0,4},{4,0},{8,12},{12,8},{1,5},{5,1},{9,13},{13,9},{2,6},{6,2},{1... | collective-permute-start | bytes 786440 | tf_op jit(solution)/shard_map/ppermute | solution.py:648
  39.9 1.2 %collective-permute-start.12 = (bf16[256,512]{1,0:T(8,128)(2,1)S(1)}, bf16[256,512]{1,0:T(8,128)(2,1)S(1)}, u32[]{:S(2)}, u32[]{:S(2)}) collective-permute-start(bf16[256,512]{1,0:T(8,128)(2,1)S(1)} %get-tuple-element.63), channel_id=1, source_target_pairs={{0,16},{16,0},{1,17},{17,1},{2,18},{18,2},{3,19},{19,3},{4,20},{20... | collective-permute-start | bytes 786440 | tf_op jit(solution)/shard_map/ppermute | solution.py:525
  41.3 1.0 %collective-permute-start.10 = (bf16[2,40,1024]{2,1,0:T(8,128)(2,1)S(1)}, bf16[2,40,1024]{2,1,0:T(8,128)(2,1)S(1)}, u32[]{:S(2)}, u32[]{:S(2)}) collective-permute-start(bf16[2,40,1024]{2,1,0:T(8,128)(2,1)S(1)} %get-tuple-element.59), channel_id=1, source_target_pairs={{0,4},{4,8},{8,12},{12,0},{1,5},{5,9},{9,13},{13,1},{2,6},{6,10},{... | collective-permute-start | bytes 491528 | tf_op jit(solution)/shard_map/ppermute | solution.py:525
  42.3 4.3 %collective-permute-done.11.refs_1_ = bf16[256,512]{1,0:T(8,128)(2,1)S(1)} collective-permute-done((bf16[256,512]{1,0:T(8,128)(2,1)S(1)}, bf16[256,512]{1,0:T(8,128)(2,1)S(1)}, u32[]{:S(2)}, u32[]{:S(2)}) %collective-permute-start.11) | collective-permute-done | bytes 262176 | tf_op jit(solution)/shard_map/ppermute | solution.py:648
  46.9 6.0 %collective-permute-done.10.refs_1_ = bf16[2,40,1024]{2,1,0:T(8,128)(2,1)S(1)} collective-permute-done((bf16[2,40,1024]{2,1,0:T(8,128)(2,1)S(1)}, bf16[2,40,1024]{2,1,0:T(8,128)(2,1)S(1)}, u32[]{:S(2)}, u32[]{:S(2)}) %collective-permute-start.10) | collective-permute-done | bytes 163872 | tf_op jit(solution)/shard_map/ppermute | solution.py:525
  53.3 1.6 %collective-permute-start.16 = (bf16[2,24,1024]{2,1,0:T(8,128)(2,1)S(1)}, bf16[2,24,1024]{2,1,0:T(8,128)(2,1)S(1)}, u32[]{:S(2)}, u32[]{:S(2)}) collective-permute-start(bf16[2,24,1024]{2,1,0:T(8,128)(2,1)S(1)} %get-tuple-element.66.refs_1_), channel_id=1, source_target_pairs={{0,2},{1,3},{2,0},{3,1},{4,6},{5,7},{6,4},{7,5},{8,10},{9,11},{10,... | collective-permute-start | bytes 294920 | tf_op jit(solution)/shard_map/ppermute | solution.py:674
  54.9 0.5 collective-permute-start.17
  55.6 2.4 %collective-permute-done.16.refs_7_ = bf16[2,24,1024]{2,1,0:T(8,128)(2,1)S(1)} collective-permute-done((bf16[2,24,1024]{2,1,0:T(8,128)(2,1)S(1)}, bf16[2,24,1024]{2,1,0:T(8,128)(2,1)S(1)}, u32[]{:S(2)}, u32[]{:S(2)}) %collective-permute-start.16) | collective-permute-done | bytes 98336 | tf_op jit(solution)/shard_map/ppermute | solution.py:674
  58.1 2.5 %collective-permute-start.18 = (bf16[2,24,1024]{2,1,0:T(8,128)(2,1)S(1)}, bf16[2,24,1024]{2,1,0:T(8,128)(2,1)S(1)}, u32[]{:S(2)}, u32[]{:S(2)}) collective-permute-start(bf16[2,24,1024]{2,1,0:T(8,128)(2,1)S(1)} %get-tuple-element.68.refs_3_), channel_id=1, source_target_pairs={{0,2},{1,3},{2,0},{3,1},{4,6},{5,7},{6,4},{7,5},{8,10},{9,11},{10,... | collective-permute-start | bytes 294920 | tf_op jit(solution)/shard_map/ppermute | solution.py:674
  60.6 0.5 collective-permute-start.19
  61.2 2.0 %collective-permute-done.18.refs_9_ = bf16[2,24,1024]{2,1,0:T(8,128)(2,1)S(1)} collective-permute-done((bf16[2,24,1024]{2,1,0:T(8,128)(2,1)S(1)}, bf16[2,24,1024]{2,1,0:T(8,128)(2,1)S(1)}, u32[]{:S(2)}, u32[]{:S(2)}) %collective-permute-start.18) | collective-permute-done | bytes 98336 | tf_op jit(solution)/shard_map/ppermute | solution.py:674
  63.2 1.3 %collective-permute-done.21.refs_12_ = bf16[2,24,1024]{2,1,0:T(8,128)(2,1)S(1)} collective-permute-done((bf16[2,24,1024]{2,1,0:T(8,128)(2,1)S(1)}, bf16[2,24,1024]{2,1,0:T(8,128)(2,1)S(1)}, u32[]{:S(2)}, u32[]{:S(2)}) %collective-permute-start.21) | collective-permute-done | bytes 98336 | tf_op jit(solution)/shard_map/ppermute | solution.py:676
  64.5 1.8 %spread_outputs.1 = (bf16[288,1024]{1,0:T(8,128)(2,1)}, bf16[288,1024]{1,0:T(8,128)(2,1)}, f32[8,128]{1,0:T(8,128)S(1)}) custom-call(bf16[288,384]{1,0:T(8,128)(2,1)S(1)} %copy-done.2, bf16[2,24,1024]{2,1,0:T(8,128)(2,1)S(1)} %get-tuple-element.66.refs_1_, bf16[2,24,1024]{2,1,0:T(8,128)(2,1)S(1)} %get-tuple-element.67.refs_2_, ...), custom_call_target="tpu_custom_call" | custom-call | flops 339738624 | bytes 2359296 | tf_op jit(solution)/shard_map/spread_outputs/pallas_call | solution.py:163
  66.3 0.8 %sum_over_lat.1 = (f32[128,768]{1,0:T(8,128)}, f32[256,128]{1,0:T(8,128)}) custom-call(f32[2,128,512]{2,1,0:T(8,128)S(1)} %get-tuple-element.71.refs_0_, bf16[2,128,512]{2,1,0:T(8,128)(2,1)S(1)} %collective-permute-done.22.refs_1_, f32[8,128]{1,0:T(8,128)S(1)} %get-tuple-element.73.refs_2_), custom_call_target="tpu_custom_call" | custom-call | flops 524288 | bytes 2097152 | tf_op jit(solution)/shard_map/sum_over_lat/pallas_call | solution.py:163
  (47 shorter events, 2.3 us)
Async XLA Ops:
  2.2 10.8 %collective-permute-start = (bf16[112,1024]{1,0:T(8,128)(2,1)S(1)}, bf16[112,1024]{1,0:T(8,128)(2,1)S(1)}, u32[]{:S(2)}, u32[]{:S(2)}) collective-permute-start(bf16[112,1024]{1,0:T(8,128)(2,1)S(1)} %get-tuple-element.40), channel_id=1, source_target_pairs={{0,12},{4,0},{8,4},{12,8},{16,28},{20,16},{24,20},{28,24},{1,13},{... | collective-permute-start | bytes 688136 | tf_op jit(solution)/shard_map/ppermute | solution.py:535
  7.3 5.8 %collective-permute-start.1 = (bf16[40,1024]{1,0:T(8,128)(2,1)S(1)}, bf16[40,1024]{1,0:T(8,128)(2,1)S(1)}, u32[]{:S(2)}, u32[]{:S(2)}) collective-permute-start(bf16[40,1024]{1,0:T(8,128)(2,1)S(1)} %get-tuple-element.42), channel_id=1, source_target_pairs={{0,16},{4,20},{8,24},{12,28},{16,0},{20,4},{24,8},{28,12},{1,17},{... | collective-permute-start | bytes 245768 | tf_op jit(solution)/shard_map/ppermute | solution.py:535
  8.8 5.3 %collective-permute-start.2 = (bf16[40,1024]{1,0:T(8,128)(2,1)S(1)}, bf16[40,1024]{1,0:T(8,128)(2,1)S(1)}, u32[]{:S(2)}, u32[]{:S(2)}) collective-permute-start(bf16[40,1024]{1,0:T(8,128)(2,1)S(1)} %get-tuple-element.43), channel_id=1, source_target_pairs={{0,28},{4,16},{8,20},{12,24},{16,12},{20,0},{24,4},{28,8},{1,29},{... | collective-permute-start | bytes 245768 | tf_op jit(solution)/shard_map/ppermute | solution.py:535
  9.9 5.7 %copy-start = (bf16[2,6,24,1024]{3,2,1,0:T(8,128)(2,1)S(1)}, bf16[2,6,24,1024]{3,2,1,0:T(8,128)(2,1)}, u32[]{:S(2)}) copy-start(bf16[2,6,24,1024]{3,2,1,0:T(8,128)(2,1)} %param.10) | copy-start | bytes 1769476
  9.9 5.7 %copy-start.1 = (bf16[2,6,24,1024]{3,2,1,0:T(8,128)(2,1)S(1)}, bf16[2,6,24,1024]{3,2,1,0:T(8,128)(2,1)}, u32[]{:S(2)}) copy-start(bf16[2,6,24,1024]{3,2,1,0:T(8,128)(2,1)} %param.15) | copy-start | bytes 1769476
  9.9 5.7 %copy-start.4 = (f32[1024]{0:T(1024)S(1)}, f32[1024]{0:T(1024)}, u32[]{:S(2)}) copy-start(f32[1024]{0:T(1024)} %param.11) | copy-start | bytes 12292
  9.9 5.8 %copy-start.5 = (bf16[1024,768]{1,0:T(8,128)(2,1)S(1)}, bf16[1024,768]{1,0:T(8,128)(2,1)}, u32[]{:S(2)}) copy-start(bf16[1024,768]{1,0:T(8,128)(2,1)} %refs_11_.1) | copy-start | bytes 4718596
  9.9 5.8 %copy-start.6 = (bf16[256,1024]{1,0:T(8,128)(2,1)S(1)}, bf16[256,1024]{1,0:T(8,128)(2,1)}, u32[]{:S(2)}) copy-start(bf16[256,1024]{1,0:T(8,128)(2,1)} %refs_7_.1) | copy-start | bytes 1572868
  10.0 5.8 %copy-start.8 = (bf16[288,496]{1,0:T(8,128)(2,1)S(1)}, bf16[288,496]{1,0:T(8,128)(2,1)}, u32[]{:S(2)}) copy-start(bf16[288,496]{1,0:T(8,128)(2,1)} %constant.8.clone.refs_9_) | copy-start | bytes 857092
  10.0 5.8 %copy-start.9 = (bf16[320,288]{1,0:T(8,128)(2,1)S(1)}, bf16[320,288]{1,0:T(8,128)(2,1)}, u32[]{:S(2)}) copy-start(bf16[320,288]{1,0:T(8,128)(2,1)} %constant.9.clone.refs_10_) | copy-start | bytes 552964
  13.1 2.6 %collective-permute-start.3 = (bf16[112,1024]{1,0:T(8,128)(2,1)S(1)}, bf16[112,1024]{1,0:T(8,128)(2,1)S(1)}, u32[]{:S(2)}, u32[]{:S(2)}) collective-permute-start(bf16[112,1024]{1,0:T(8,128)(2,1)S(1)} %hold_rim.1.refs_2_), channel_id=1, source_target_pairs={{0,1},{1,0},{2,3},{3,2},{4,5},{5,4},{6,7},{7,6},{8,9},{9,8},{10,11... | collective-permute-start | bytes 688136 | tf_op jit(solution)/shard_map/ppermute | solution.py:582
  14.2 1.5 %collective-permute-start.4 = (bf16[96,1024]{1,0:T(8,128)(2,1)S(1)}, bf16[96,1024]{1,0:T(8,128)(2,1)S(1)}, u32[]{:S(2)}, u32[]{:S(2)}) collective-permute-start(bf16[96,1024]{1,0:T(8,128)(2,1)S(1)} %join_rims.1.refs_3_), channel_id=1, source_target_pairs={{0,1},{1,0},{2,3},{3,2},{4,5},{5,4},{6,7},{7,6},{8,9},{9,8},{10,11... | collective-permute-start | bytes 589832 | tf_op jit(solution)/shard_map/ppermute | solution.py:582
  15.7 18.9 %copy-start.3 = (bf16[112,72]{1,0:T(8,128)(2,1)S(1)}, bf16[112,72]{1,0:T(8,128)(2,1)}, u32[]{:S(2)}) copy-start(bf16[112,72]{1,0:T(8,128)(2,1)} %constant.10.clone.refs_3_) | copy-start | bytes 48388
  23.4 2.1 %collective-permute-start.5 = (bf16[2,2,72,1024]{3,2,1,0:T(8,128)(2,1)S(1)}, bf16[2,2,72,1024]{3,2,1,0:T(8,128)(2,1)S(1)}, u32[]{:S(2)}, u32[]{:S(2)}) collective-permute-start(bf16[2,2,72,1024]{3,2,1,0:T(8,128)(2,1)S(1)} %get-tuple-element.48), channel_id=1, source_target_pairs={{0,1},{1,0},{2,3},{3,2},{4,5},{5,4},{6,7},{7,6},{8,9},{9,8},{10,11... | collective-permute-start | bytes 1769480 | tf_op jit(solution)/shard_map/ppermute | solution.py:626
  23.6 14.8 %collective-permute-start.8 = (bf16[512,512]{1,0:T(8,128)(2,1)S(1)}, bf16[512,512]{1,0:T(8,128)(2,1)S(1)}, u32[]{:S(2)}, u32[]{:S(2)}) collective-permute-start(bf16[512,512]{1,0:T(8,128)(2,1)S(1)} %get-tuple-element.54), channel_id=1, source_target_pairs={{0,16},{16,0},{1,17},{17,1},{2,18},{18,2},{3,19},{19,3},{4,20},{20... | collective-permute-start | bytes 1572872 | tf_op jit(solution)/shard_map/ppermute | solution.py:525
  24.9 13.9 %collective-permute-start.9 = (bf16[512,512]{1,0:T(8,128)(2,1)S(1)}, bf16[512,512]{1,0:T(8,128)(2,1)S(1)}, u32[]{:S(2)}, u32[]{:S(2)}) collective-permute-start(bf16[512,512]{1,0:T(8,128)(2,1)S(1)} %get-tuple-element.56), channel_id=1, source_target_pairs={{0,4},{4,0},{8,12},{12,8},{1,5},{5,1},{9,13},{13,9},{2,6},{6,2},{1... | collective-permute-start | bytes 1572872 | tf_op jit(solution)/shard_map/ppermute | solution.py:625
  25.6 9.1 %collective-permute-start.6 = (bf16[2,72,1024]{2,1,0:T(8,128)(2,1)S(1)}, bf16[2,72,1024]{2,1,0:T(8,128)(2,1)S(1)}, u32[]{:S(2)}, u32[]{:S(2)}) collective-permute-start(bf16[2,72,1024]{2,1,0:T(8,128)(2,1)S(1)} %sum_over_cores.1), channel_id=1, source_target_pairs={{0,2},{1,3},{2,0},{3,1},{4,6},{5,7},{6,4},{7,5},{8,10},{9,11},{10,... | collective-permute-start | bytes 884744 | tf_op jit(solution)/shard_map/ppermute | solution.py:631
  35.2 5.9 %collective-permute-start.7 = (bf16[2,32,1024]{2,1,0:T(8,128)(2,1)S(1)}, bf16[2,32,1024]{2,1,0:T(8,128)(2,1)S(1)}, u32[]{:S(2)}, u32[]{:S(2)}) collective-permute-start(bf16[2,32,1024]{2,1,0:T(8,128)(2,1)S(1)} %get-tuple-element.52), channel_id=1, source_target_pairs={{0,16},{16,0},{1,17},{17,1},{2,18},{18,2},{3,19},{19,3},{4,20},{20... | collective-permute-start | bytes 393224 | tf_op jit(solution)/shard_map/ppermute | solution.py:525
  39.1 25.4 %copy-start.2 = (bf16[288,384]{1,0:T(8,128)(2,1)S(1)}, bf16[288,384]{1,0:T(8,128)(2,1)}, u32[]{:S(2)}) copy-start(bf16[288,384]{1,0:T(8,128)(2,1)} %constant.11.clone.refs_0_) | copy-start | bytes 663556
  39.1 7.5 %collective-permute-start.11 = (bf16[256,512]{1,0:T(8,128)(2,1)S(1)}, bf16[256,512]{1,0:T(8,128)(2,1)S(1)}, u32[]{:S(2)}, u32[]{:S(2)}) collective-permute-start(bf16[256,512]{1,0:T(8,128)(2,1)S(1)} %get-tuple-element.61), channel_id=1, source_target_pairs={{0,4},{4,0},{8,12},{12,8},{1,5},{5,1},{9,13},{13,9},{2,6},{6,2},{1... | collective-permute-start | bytes 786440 | tf_op jit(solution)/shard_map/ppermute | solution.py:648
  39.9 6.9 %collective-permute-start.12 = (bf16[256,512]{1,0:T(8,128)(2,1)S(1)}, bf16[256,512]{1,0:T(8,128)(2,1)S(1)}, u32[]{:S(2)}, u32[]{:S(2)}) collective-permute-start(bf16[256,512]{1,0:T(8,128)(2,1)S(1)} %get-tuple-element.63), channel_id=1, source_target_pairs={{0,16},{16,0},{1,17},{17,1},{2,18},{18,2},{3,19},{19,3},{4,20},{20... | collective-permute-start | bytes 786440 | tf_op jit(solution)/shard_map/ppermute | solution.py:525
  41.3 11.6 %collective-permute-start.10 = (bf16[2,40,1024]{2,1,0:T(8,128)(2,1)S(1)}, bf16[2,40,1024]{2,1,0:T(8,128)(2,1)S(1)}, u32[]{:S(2)}, u32[]{:S(2)}) collective-permute-start(bf16[2,40,1024]{2,1,0:T(8,128)(2,1)S(1)} %get-tuple-element.59), channel_id=1, source_target_pairs={{0,4},{4,8},{8,12},{12,0},{1,5},{5,9},{9,13},{13,1},{2,6},{6,10},{... | collective-permute-start | bytes 491528 | tf_op jit(solution)/shard_map/ppermute | solution.py:525
  53.3 4.8 %collective-permute-start.16 = (bf16[2,24,1024]{2,1,0:T(8,128)(2,1)S(1)}, bf16[2,24,1024]{2,1,0:T(8,128)(2,1)S(1)}, u32[]{:S(2)}, u32[]{:S(2)}) collective-permute-start(bf16[2,24,1024]{2,1,0:T(8,128)(2,1)S(1)} %get-tuple-element.66.refs_1_), channel_id=1, source_target_pairs={{0,2},{1,3},{2,0},{3,1},{4,6},{5,7},{6,4},{7,5},{8,10},{9,11},{10,... | collective-permute-start | bytes 294920 | tf_op jit(solution)/shard_map/ppermute | solution.py:674
  54.9 11.4 %collective-permute-start.22 = (bf16[2,128,512]{2,1,0:T(8,128)(2,1)S(1)}, bf16[2,128,512]{2,1,0:T(8,128)(2,1)S(1)}, u32[]{:S(2)}, u32[]{:S(2)}) collective-permute-start(bf16[2,128,512]{2,1,0:T(8,128)(2,1)S(1)} %get-tuple-element.72), channel_id=1, source_target_pairs={{0,8},{4,12},{8,0},{12,4},{1,9},{5,13},{9,1},{13,5},{2,10},{6,14},... | collective-permute-start | bytes 786440 | tf_op jit(solution)/shard_map/ppermute | solution.py:666
  54.9 5.6 %collective-permute-start.13 = (bf16[2,24,1024]{2,1,0:T(8,128)(2,1)S(1)}, bf16[2,24,1024]{2,1,0:T(8,128)(2,1)S(1)}, u32[]{:S(2)}, u32[]{:S(2)}) collective-permute-start(bf16[2,24,1024]{2,1,0:T(8,128)(2,1)S(1)} %get-tuple-element.66.refs_1_), channel_id=1, source_target_pairs={{0,1},{1,0},{2,3},{3,2},{4,5},{5,4},{6,7},{7,6},{8,9},{9,8},{10,11... | collective-permute-start | bytes 294920 | tf_op jit(solution)/shard_map/ppermute | solution.py:675
  54.9 5.6 %collective-permute-start.17 = (bf16[2,24,1024]{2,1,0:T(8,128)(2,1)S(1)}, bf16[2,24,1024]{2,1,0:T(8,128)(2,1)S(1)}, u32[]{:S(2)}, u32[]{:S(2)}) collective-permute-start(bf16[2,24,1024]{2,1,0:T(8,128)(2,1)S(1)} %get-tuple-element.67.refs_2_), channel_id=1, source_target_pairs={{0,2},{1,3},{2,0},{3,1},{4,6},{5,7},{6,4},{7,5},{8,10},{9,11},{10,... | collective-permute-start | bytes 294920 | tf_op jit(solution)/shard_map/ppermute | solution.py:674
  55.4 5.7 %collective-permute-start.14 = (bf16[2,24,1024]{2,1,0:T(8,128)(2,1)S(1)}, bf16[2,24,1024]{2,1,0:T(8,128)(2,1)S(1)}, u32[]{:S(2)}, u32[]{:S(2)}) collective-permute-start(bf16[2,24,1024]{2,1,0:T(8,128)(2,1)S(1)} %get-tuple-element.67.refs_2_), channel_id=1, source_target_pairs={{0,1},{1,0},{2,3},{3,2},{4,5},{5,4},{6,7},{7,6},{8,9},{9,8},{10,11... | collective-permute-start | bytes 294920 | tf_op jit(solution)/shard_map/ppermute | solution.py:675
  58.1 5.1 %collective-permute-start.18 = (bf16[2,24,1024]{2,1,0:T(8,128)(2,1)S(1)}, bf16[2,24,1024]{2,1,0:T(8,128)(2,1)S(1)}, u32[]{:S(2)}, u32[]{:S(2)}) collective-permute-start(bf16[2,24,1024]{2,1,0:T(8,128)(2,1)S(1)} %get-tuple-element.68.refs_3_), channel_id=1, source_target_pairs={{0,2},{1,3},{2,0},{3,1},{4,6},{5,7},{6,4},{7,5},{8,10},{9,11},{10,... | collective-permute-start | bytes 294920 | tf_op jit(solution)/shard_map/ppermute | solution.py:674
  60.6 2.6 %collective-permute-start.15 = (bf16[2,24,1024]{2,1,0:T(8,128)(2,1)S(1)}, bf16[2,24,1024]{2,1,0:T(8,128)(2,1)S(1)}, u32[]{:S(2)}, u32[]{:S(2)}) collective-permute-start(bf16[2,24,1024]{2,1,0:T(8,128)(2,1)S(1)} %get-tuple-element.68.refs_3_), channel_id=1, source_target_pairs={{0,1},{1,0},{2,3},{3,2},{4,5},{5,4},{6,7},{7,6},{8,9},{9,8},{10,11... | collective-permute-start | bytes 294920 | tf_op jit(solution)/shard_map/ppermute | solution.py:675
  60.6 2.6 %collective-permute-start.19 = (bf16[2,24,1024]{2,1,0:T(8,128)(2,1)S(1)}, bf16[2,24,1024]{2,1,0:T(8,128)(2,1)S(1)}, u32[]{:S(2)}, u32[]{:S(2)}) collective-permute-start(bf16[2,24,1024]{2,1,0:T(8,128)(2,1)S(1)} %collective-permute-done.16.refs_7_), channel_id=1, source_target_pairs={{0,1},{1,0},{2,3},{3,2},{4,5},{5,4},{6,7},{7,6},{8,9},{9,8},{10,11... | collective-permute-start | bytes 294920 | tf_op jit(solution)/shard_map/ppermute | solution.py:676
  61.1 2.1 %collective-permute-start.20 = (bf16[2,24,1024]{2,1,0:T(8,128)(2,1)S(1)}, bf16[2,24,1024]{2,1,0:T(8,128)(2,1)S(1)}, u32[]{:S(2)}, u32[]{:S(2)}) collective-permute-start(bf16[2,24,1024]{2,1,0:T(8,128)(2,1)S(1)} %collective-permute-done.17.refs_8_), channel_id=1, source_target_pairs={{0,1},{1,0},{2,3},{3,2},{4,5},{5,4},{6,7},{7,6},{8,9},{9,8},{10,11... | collective-permute-start | bytes 294920 | tf_op jit(solution)/shard_map/ppermute | solution.py:676
  63.2 1.3 %collective-permute-start.21 = (bf16[2,24,1024]{2,1,0:T(8,128)(2,1)S(1)}, bf16[2,24,1024]{2,1,0:T(8,128)(2,1)S(1)}, u32[]{:S(2)}, u32[]{:S(2)}) collective-permute-start(bf16[2,24,1024]{2,1,0:T(8,128)(2,1)S(1)} %collective-permute-done.18.refs_9_), channel_id=1, source_target_pairs={{0,1},{1,0},{2,3},{3,2},{4,5},{5,4},{6,7},{7,6},{8,9},{9,8},{10,11... | collective-permute-start | bytes 294920 | tf_op jit(solution)/shard_map/ppermute | solution.py:676
  (1 other events, 0.7 us)
